TPU v7x, 32 devices: a whole 2x2x4 slice. The times are simulated.
32 devices in a mesh: ens: 4 (over y, core), slab: 8 (over z, x).
Axes of the slice: x: 2, y: 2, z: 4, core: 2. Of those that a mesh axis runs over, the one named last changes fastest.
Arguments:
- tracer: float32 [32, 128, 4096], P('ens', 'slab'), may hold values from -6 to 6
- coefficients: float32 [4, 128, 4096], P(None, 'slab'), may hold values from -1.5 to 1.5, as said below
- parameters: float32 [32, 4096], P('ens'), may hold values from -6 to 6
- obs_index: int32 [16384], P('slab'), may hold values from 0 to 65535, as said below
- obs_values: float32 [32, 16384], P('ens', 'slab'), may hold values from -6 to 6
- obs_variance: float32 [16384], P('slab'), may hold values from 0.1 to 1
- member_group: int32 [32], replicated, may hold values from 0 to 7, as said below
Outputs:
- final_field: float32 [32, 128, 4096], P('ens', 'slab')
- updated_params: float32 [32, 4096], P('ens')
Inputs may be any that keep to these rules, and one draw needn't show every extreme that they name: `obs_index`: every slab has an observation at flat index 0 and one at 65535; indices may repeat. `member_group`: every group holds exactly 4 members. `coefficients`: the Courant numbers lie within -0.3 to 0.3, the diffusion number within 0.02 to 0.1.
All inputs are finite; a program needn't handle non-finite values.
Results may differ from a plain program's by a relative error of at most 0.0003.
Values sent between devices are 32-bit elements; how exact they have to be, the bound alone decides.
No kernel may reach another device: no remote copies, remote signals or barrier semaphores. Data moves between devices by JAX's collectives and lax.ppermute only.
A program may use at most 128 MiB of HBM per device.

v0:
```python
import math

import jax
import jax.numpy as jnp
from jax import lax
from jax.sharding import PartitionSpec as P

STEPS = 4
GROUPS = 8


def padded_2(block, sides, width):
    for axis, dim in sides:
        count = lax.axis_size(axis)
        forward = [(i, i + 1) for i in range(count - 1)]
        backward = [(target, source) for source, target in forward]
        low = lax.ppermute(
            lax.slice_in_dim(block, block.shape[dim] - width, None, axis=dim), axis, forward
        )
        high = lax.ppermute(lax.slice_in_dim(block, 0, width, axis=dim), axis, backward)
        block = jnp.concatenate([low, block, high], axis=dim)
    return block


def hdot(left, right):
    return jnp.dot(left, right, precision=lax.Precision.HIGHEST, preferred_element_type=jnp.float32)


def minmod(left, right):
    return jnp.where(
        left * right > 0.0, jnp.where(jnp.abs(left) < jnp.abs(right), left, right), 0.0
    )


def upwind(minus_two, minus_one, centre, plus_one, plus_two, speed):
    slope_back = minmod(minus_one - minus_two, centre - minus_one)
    slope_here = minmod(centre - minus_one, plus_one - centre)
    slope_next = minmod(plus_one - centre, plus_two - plus_one)
    forward = centre + 0.5 * slope_here - (minus_one + 0.5 * slope_back)
    backward = plus_one - 0.5 * slope_next - (centre - 0.5 * slope_here)
    return speed * jnp.where(speed > 0.0, forward, backward)


def advance(padded, coefficients, params):
    out_rows = padded.shape[-2] - 4
    along_x = [
        lax.slice_in_dim(padded, offset, offset + out_rows, axis=padded.ndim - 2)
        for offset in range(5)
    ]
    centre = along_x[2]
    along_y = [jnp.roll(centre, shift, axis=-1) for shift in (2, 1, 0, -1, -2)]
    advection = upwind(*along_x, coefficients[0]) + upwind(*along_y, coefficients[1])
    laplace = along_x[1] + along_x[3] + along_y[1] + along_y[3] - 4.0 * centre
    source = jnp.expand_dims(params, -2) * coefficients[3]
    return centre - advection + coefficients[2] * laplace + source


def eliminate(system, right_side):
    order = system.shape[0]
    augmented = jnp.concatenate([system, right_side], axis=1)
    positions = jnp.arange(order, dtype=jnp.int32)

    def one_pivot(pivot, current):
        pivot_row = lax.dynamic_slice_in_dim(current, pivot, 1, 0)
        pivot_col = lax.dynamic_slice_in_dim(current, pivot, 1, 1)
        pivot_val = lax.dynamic_slice_in_dim(pivot_row, pivot, 1, 1)
        scaled_row = pivot_row / pivot_val
        is_pivot = (positions == pivot).astype(jnp.float32)[:, None]
        factors = pivot_col * (1.0 - is_pivot)
        current = current - factors * scaled_row
        return current * (1.0 - is_pivot) + is_pivot * scaled_row

    finished = lax.fori_loop(0, order, one_pivot, augmented)
    return finished[:, order:]


def local(tracer, coefficients, parameters, obs_index, obs_values, obs_variance, member_group):
    local_members = tracer.shape[0]
    slab_rows = tracer.shape[1]
    columns = tracer.shape[2]
    ens_pos = lax.axis_index("ens")
    slab_count = lax.axis_size("slab")
    field_now = tracer
    for step_index in range(STEPS):
        padded = padded_2(field_now, (("slab", 1),), 2)
        field_now = advance(padded, coefficients, parameters)
    flat_state = field_now.reshape(local_members, slab_rows * columns)
    predicted = jnp.take(flat_state, obs_index, axis=1)
    total_obs = obs_variance.shape[0] * slab_count
    weight = 1.0 / (obs_variance * total_obs)
    innovation = (obs_values - predicted) * weight[None, :]
    all_predicted, all_params = (
        lax.all_gather(predicted, "ens", axis=0, tiled=True),
        lax.all_gather(parameters, "ens", axis=0, tiled=True),
    )
    members = member_group.shape[0]
    same_group = (member_group[:, None] == member_group[None, :]).astype(jnp.float32)
    per_group = members // GROUPS
    spread = 1.0 / math.sqrt(per_group - 1)
    anomalies = (all_predicted - hdot(same_group, all_predicted) / per_group) * spread
    weighted = anomalies * weight[None, :]
    gram_part = hdot(weighted, anomalies.T)
    mixed_part = hdot(anomalies, innovation.T)
    gram_sum, mixed_sum = lax.psum((gram_part, mixed_part), "slab")
    own_same = lax.dynamic_slice_in_dim(same_group, ens_pos * local_members, local_members, 1)
    system = jnp.eye(members, dtype=jnp.float32) + same_group * gram_sum
    solved = eliminate(system, own_same * mixed_sum)
    param_anomalies = (all_params - hdot(same_group, all_params) / per_group) * spread
    updated_params = parameters + hdot(solved.T, param_anomalies)
    return (field_now, updated_params)


def solution(mesh):
    in_specs = (
        P("ens", "slab", None),
        P(None, "slab", None),
        P("ens", None),
        P("slab"),
        P("ens", "slab"),
        P("slab"),
        P(),
    )
    out_specs = (P("ens", "slab", None), P("ens", None))
    return jax.shard_map(local, mesh=mesh, in_specs=in_specs, out_specs=out_specs, check_vma=False)
```

profile of v0, /device:TPU:0, one launch (start us, length us, event | category | flops | bytes accessed | tf_op | source)
XLA Modules:
  0.0 258.1 jit_solution(16291240644653546658)
XLA Ops:
  0.6 1.8 fusion.75
  2.5 0.8 copy.53
  3.3 5.5 %collective-permute-start = (f32[8,2,4096]{2,0,1:T(8,128)}, f32[8,2,4096]{2,0,1:T(8,128)}, u32[]{:S(2)}, u32[]{:S(2)}) collective-permute-start(f32[8,2,4096]{2,0,1:T(8,128)} %copy.53), channel_id=1, source_target_pairs={{0,1},{1,2},{2,3},{3,4},{4,5},{5,6},{6,7},{8,9},{9,10},{10,11},{11... | collective-permute-start | bytes 786440 | tf_op jit(solution)/shard_map/ppermute | solution.py:17
  8.9 0.9 copy.52
  9.7 1.3 collective-permute-start.1
  14.8 7.8 %all_gather.7 = f32[32,4096]{1,0:T(8,128)} all-gather(f32[8,4096]{1,0:T(8,128)S(1)} %copy-done.5), channel_id=1, replica_groups=mesh['ens'=4,'slab'=8] {'ens'}, dimensions={0}, use_global_device_ids=true | all-gather | bytes 655360 | tf_op jit(solution)/shard_map/all_gather | solution.py:94
  22.6 2.5 copy.45
  25.1 2.6 copy.46
  27.7 2.5 copy.49
  30.2 2.6 %copy.50 = f32[8,16,4095]{2,0,1:T(8,128)} copy(f32[8,16,4095]{2,1,0:T(8,128)S(1)} %get-tuple-element.155) | data formatting | bytes 4193280
  34.2 2.6 %fusion.5 = f32[32,4096]{1,0:T(8,128)} fusion(f32[32,4096]{1,0:T(8,128)} %all_gather.7, s32[32]{0:T(128)S(1)} %copy-done.9), kind=kOutput, calls=%fused_computation.15 | convolution fusion | flops 50725888 | bytes 1048704 | tf_op jit(solution)/shard_map/dot_general | solution.py:26
  36.8 1.0 constant_dynamic-update-slice_fusion.1
  37.8 1.2 constant_dynamic-update-slice_fusion
  39.0 1.6 constant_dynamic-update-slice_fusion.2
  40.6 8.8 %multiply_add_fusion.4 = f32[8,16,4096]{2,0,1:T(8,128)S(1)} fusion(f32[8,16,2]{2,0,1:T(8,128)S(1)} %copy.44, f32[8,16,4094]{2,0,1:T(8,128)S(1)} %copy-done.1, f32[8,16,4094]{2,0,1:T(8,128)S(1)} %copy-done.2, f32[8,16,2]{2,0,1:T(8,128)S(1)} %copy.47, f32[8,16,1]{2,0,1:T(8,128)} %copy.48, f32[8,16,4095]{2,0,1:T(8,128)S(1)} %copy-done.3, ...), kind=kLoop, calls=%fused_computation.12 | loop fusion | flops 43515904 | bytes 22282240 | tf_op jit(solution)/shard_map/add | solution.py:55
  50.9 4.6 %collective-permute-start.2 = (f32[8,2,4096]{2,0,1:T(8,128)S(1)}, f32[8,2,4096]{2,0,1:T(8,128)S(1)}, u32[]{:S(2)}, u32[]{:S(2)}) collective-permute-start(f32[8,2,4096]{2,0,1:T(8,128)S(1)} %get-tuple-element.139), channel_id=1, source_target_pairs={{0,1},{1,2},{2,3},{3,4},{4,5},{5,6},{6,7},{8,9},{9,10},{10,11},{11... | collective-permute-start | bytes 786440 | tf_op jit(solution)/shard_map/ppermute | solution.py:17
  55.5 1.5 collective-permute-start.3
  57.2 10.0 %collective-permute-done.2 = f32[8,2,4096]{2,0,1:T(8,128)S(1)} collective-permute-done((f32[8,2,4096]{2,0,1:T(8,128)S(1)}, f32[8,2,4096]{2,0,1:T(8,128)S(1)}, u32[]{:S(2)}, u32[]{:S(2)}) %collective-permute-start.2) | collective-permute-done | bytes 262176 | tf_op jit(solution)/shard_map/ppermute | solution.py:17
  67.2 8.5 %multiply_add_fusion.3 = f32[8,16,4096]{2,0,1:T(8,128)S(1)} fusion(f32[8,16,4096]{2,0,1:T(8,128)S(1)} %multiply_add_fusion.4, f32[8,16,2]{2,0,1:T(8,128)S(1)} %get-tuple-element.146, f32[8,16,4094]{2,0,1:T(8,128)S(1)} %get-tuple-element.148, f32[8,16,4094]{2,0,1:T(8,128)S(1)} %get-tuple-element.147, f32[8,16,2]{2,0,1:T(8,128)S(1)} %get-tuple-element.145, ...), kind=kLoop, calls=%fused_computation.11 | loop fusion | flops 45613056 | bytes 14417920 | tf_op jit(solution)/shard_map/add | solution.py:55
  77.2 4.4 %collective-permute-start.4 = (f32[8,2,4096]{2,0,1:T(8,128)S(1)}, f32[8,2,4096]{2,0,1:T(8,128)S(1)}, u32[]{:S(2)}, u32[]{:S(2)}) collective-permute-start(f32[8,2,4096]{2,0,1:T(8,128)S(1)} %get-tuple-element.129), channel_id=1, source_target_pairs={{0,1},{1,2},{2,3},{3,4},{4,5},{5,6},{6,7},{8,9},{9,10},{10,11},{11... | collective-permute-start | bytes 786440 | tf_op jit(solution)/shard_map/ppermute | solution.py:17
  81.6 1.3 collective-permute-start.5
  83.0 3.8 %collective-permute-done.4 = f32[8,2,4096]{2,0,1:T(8,128)S(1)} collective-permute-done((f32[8,2,4096]{2,0,1:T(8,128)S(1)}, f32[8,2,4096]{2,0,1:T(8,128)S(1)}, u32[]{:S(2)}, u32[]{:S(2)}) %collective-permute-start.4) | collective-permute-done | bytes 262176 | tf_op jit(solution)/shard_map/ppermute | solution.py:17
  86.8 5.5 %collective-permute-done.5 = f32[8,2,4096]{2,0,1:T(8,128)S(1)} collective-permute-done((f32[8,2,4096]{2,0,1:T(8,128)S(1)}, f32[8,2,4096]{2,0,1:T(8,128)S(1)}, u32[]{:S(2)}, u32[]{:S(2)}) %collective-permute-start.5) | collective-permute-done | bytes 262176 | tf_op jit(solution)/shard_map/ppermute | solution.py:20
  92.4 8.5 %multiply_add_fusion.2 = f32[8,16,4096]{2,0,1:T(8,128)S(1)} fusion(f32[8,16,4096]{2,0,1:T(8,128)S(1)} %multiply_add_fusion.3, f32[8,16,2]{2,0,1:T(8,128)S(1)} %get-tuple-element.136, f32[8,16,4094]{2,0,1:T(8,128)S(1)} %get-tuple-element.138, f32[8,16,4094]{2,0,1:T(8,128)S(1)} %get-tuple-element.137, f32[8,16,2]{2,0,1:T(8,128)S(1)} %get-tuple-element.135, ...), kind=kLoop, calls=%fused_computation.10 | loop fusion | flops 45613056 | bytes 14417920 | tf_op jit(solution)/shard_map/add | solution.py:55
  102.4 4.6 %collective-permute-start.6 = (f32[8,2,4096]{2,0,1:T(8,128)S(1)}, f32[8,2,4096]{2,0,1:T(8,128)S(1)}, u32[]{:S(2)}, u32[]{:S(2)}) collective-permute-start(f32[8,2,4096]{2,0,1:T(8,128)S(1)} %get-tuple-element.119), channel_id=1, source_target_pairs={{0,1},{1,2},{2,3},{3,4},{4,5},{5,6},{6,7},{8,9},{9,10},{10,11},{11... | collective-permute-start | bytes 786440 | tf_op jit(solution)/shard_map/ppermute | solution.py:17
  106.9 1.3 collective-permute-start.7
  108.4 3.1 %collective-permute-done.6 = f32[8,2,4096]{2,0,1:T(8,128)S(1)} collective-permute-done((f32[8,2,4096]{2,0,1:T(8,128)S(1)}, f32[8,2,4096]{2,0,1:T(8,128)S(1)}, u32[]{:S(2)}, u32[]{:S(2)}) %collective-permute-start.6) | collective-permute-done | bytes 262176 | tf_op jit(solution)/shard_map/ppermute | solution.py:17
  111.5 7.5 %collective-permute-done.7 = f32[8,2,4096]{2,0,1:T(8,128)S(1)} collective-permute-done((f32[8,2,4096]{2,0,1:T(8,128)S(1)}, f32[8,2,4096]{2,0,1:T(8,128)S(1)}, u32[]{:S(2)}, u32[]{:S(2)}) %collective-permute-start.7) | collective-permute-done | bytes 262176 | tf_op jit(solution)/shard_map/ppermute | solution.py:20
  119.0 8.5 %multiply_add_fusion.1 = f32[8,16,4096]{2,0,1:T(8,128)S(1)} fusion(f32[8,16,4096]{2,0,1:T(8,128)S(1)} %multiply_add_fusion.2, f32[8,16,2]{2,0,1:T(8,128)S(1)} %get-tuple-element.126, f32[8,16,4094]{2,0,1:T(8,128)S(1)} %get-tuple-element.128, f32[8,16,4094]{2,0,1:T(8,128)S(1)} %get-tuple-element.127, f32[8,16,2]{2,0,1:T(8,128)S(1)} %get-tuple-element.125, ...), kind=kLoop, calls=%fused_computation.9 | loop fusion | flops 45613056 | bytes 14417920 | tf_op jit(solution)/shard_map/add | solution.py:55
  127.5 15.6 %copy.35 = f32[8,16,4096]{0,2,1:T(8,128)} copy(f32[8,16,4096]{2,0,1:T(8,128)S(1)} %multiply_add_fusion.1) | data formatting | bytes 4194304 | tf_op jit(solution)/shard_map/add | solution.py:55
  143.1 2.5 copy.39
  145.6 16.1 %gather_fusion = f32[2048,8]{1,0:T(8,128)S(1)} fusion(f32[8,65536]{0,1:T(8,128)} %bitcast.31, s32[2048]{0:T(1024)S(1)} %copy-done.10), kind=kCustom, calls=%fused_computation | custom fusion | bytes 139264 | tf_op jit(solution)/shard_map/jit(_take)/gather | solution.py:88
  162.0 5.8 %all_gather.6 = f32[32,2048]{1,0:T(8,128)S(1)} all-gather(f32[8,2048]{1,0:T(8,128)S(1)} %select_bitcast_fusion), channel_id=1, replica_groups=mesh['ens'=4,'slab'=8] {'ens'}, dimensions={0}, use_global_device_ids=true | all-gather | bytes 327680 | tf_op jit(solution)/shard_map/all_gather | solution.py:93
  168.8 39.0 %all-reduce = (f32[32,8]{1,0:T(8,128)S(1)}, f32[32,32]{1,0:T(8,128)S(1)}) all-reduce(f32[32,8]{1,0:T(8,128)S(1)} %fusion.41, f32[32,32]{1,0:T(8,128)S(1)} %fusion.39), channel_id=1, replica_groups=mesh['ens'=4,'slab'=8] {'slab'}, use_global_device_ids=true, to_apply=%region_1.2 | all-reduce | flops 1280 | bytes 10240 | tf_op jit(solution)/shard_map/psum | solution.py:104
  208.2 48.9 %while.17 = (s32[]{:T(128)}, f32[32,40]{0,1:T(8,128)S(1)}, s32[]{:T(128)}, s32[]{:T(128)}, s32[]{:T(128)}, /*index=5*/s32[]{:T(128)}) while((s32[]{:T(128)}, f32[32,40]{0,1:T(8,128)S(1)}, s32[]{:T(128)}, s32[]{:T(128)}, s32[]{:T(128)}, /*index=5*/s32[]{:T(128)}) %tuple.74), condition=%wide.region_3.4_spmd.clone, body=%wide.region_2.3_spmd.clone.sunk | while | flops 6732 | bytes 12769 | solution.py:73
  208.8 0.8 fusion.85
  210.3 0.8 fusion.85
  211.8 0.8 fusion.85
  213.3 0.8 fusion.85
  214.9 0.8 fusion.85
  216.4 0.8 fusion.85
  217.9 0.8 fusion.85
  219.5 0.8 fusion.85
  221.0 0.8 fusion.85
  222.5 0.8 fusion.85
  224.0 0.8 fusion.85
  225.6 0.8 fusion.85
  227.1 0.8 fusion.85
  228.6 0.8 fusion.85
  230.2 0.8 fusion.85
  231.7 0.8 fusion.85
  233.2 0.8 fusion.85
  234.8 0.8 fusion.85
  236.3 0.8 fusion.85
  237.8 0.8 fusion.85
  239.3 0.8 fusion.85
  240.9 0.8 fusion.85
  242.4 0.8 fusion.85
  243.9 0.8 fusion.85
  247.0 0.8 fusion.85
  251.6 0.8 fusion.85
  253.1 0.8 fusion.85
  256.2 0.8 fusion.85
  257.1 1.0 convolution_add_fusion
  (235 shorter events, 36.7 us)
Async XLA Ops:
  0.6 10.4 %copy-start.6 = (f32[4,16,4096]{2,1,0:T(8,128)S(1)}, f32[4,16,4096]{2,1,0:T(8,128)}, u32[]{:S(2)}) copy-start(f32[4,16,4096]{2,1,0:T(8,128)} %param.10) | copy-start | bytes 3145732
  2.5 8.7 %copy-start = (f32[8,16,4096]{2,1,0:T(8,128)S(1)}, f32[8,16,4096]{2,1,0:T(8,128)}, u32[]{:S(2)}) copy-start(f32[8,16,4096]{2,1,0:T(8,128)} %param.9) | copy-start | bytes 6291460
  3.3 33.5 %collective-permute-start = (f32[8,2,4096]{2,0,1:T(8,128)}, f32[8,2,4096]{2,0,1:T(8,128)}, u32[]{:S(2)}, u32[]{:S(2)}) collective-permute-start(f32[8,2,4096]{2,0,1:T(8,128)} %copy.53), channel_id=1, source_target_pairs={{0,1},{1,2},{2,3},{3,4},{4,5},{5,6},{6,7},{8,9},{9,10},{10,11},{11... | collective-permute-start | bytes 786440 | tf_op jit(solution)/shard_map/ppermute | solution.py:17
  9.7 29.3 %collective-permute-start.1 = (f32[8,2,4096]{2,0,1:T(8,128)}, f32[8,2,4096]{2,0,1:T(8,128)}, u32[]{:S(2)}, u32[]{:S(2)}) collective-permute-start(f32[8,2,4096]{2,0,1:T(8,128)} %copy.52), channel_id=1, source_target_pairs={{1,0},{2,1},{3,2},{4,3},{5,4},{6,5},{7,6},{9,8},{10,9},{11,10},{12... | collective-permute-start | bytes 786440 | tf_op jit(solution)/shard_map/ppermute | solution.py:20
  11.9 0.9 copy-start.12
  11.9 2.1 copy-start.14
  11.9 2.7 %copy-start.9 = (s32[32]{0:T(128)S(1)}, s32[32]{0:T(128)}, u32[]{:S(2)}) copy-start(s32[32]{0:T(128)} %param.15) | copy-start | bytes 388
  12.0 2.8 %copy-start.5 = (f32[8,4096]{1,0:T(8,128)S(1)}, f32[8,4096]{1,0:T(8,128)}, u32[]{:S(2)}) copy-start(f32[8,4096]{1,0:T(8,128)} %param.11) | copy-start | bytes 393220
  34.2 6.4 %copy-start.4 = (f32[8,16,4095]{2,0,1:T(8,128)S(1)}, f32[8,16,4095]{2,0,1:T(8,128)}, u32[]{:S(2)}) copy-start(f32[8,16,4095]{2,0,1:T(8,128)} %copy.50) | copy-start | bytes 6289924
  37.8 2.9 %copy-start.1 = (f32[8,16,4094]{2,0,1:T(8,128)S(1)}, f32[8,16,4094]{2,0,1:T(8,128)}, u32[]{:S(2)}) copy-start(f32[8,16,4094]{2,0,1:T(8,128)} %copy.45) | copy-start | bytes 6288388
  37.8 2.8 %copy-start.2 = (f32[8,16,4094]{2,0,1:T(8,128)S(1)}, f32[8,16,4094]{2,0,1:T(8,128)}, u32[]{:S(2)}) copy-start(f32[8,16,4094]{2,0,1:T(8,128)} %copy.46) | copy-start | bytes 6288388
  37.8 2.8 %copy-start.3 = (f32[8,16,4095]{2,0,1:T(8,128)S(1)}, f32[8,16,4095]{2,0,1:T(8,128)}, u32[]{:S(2)}) copy-start(f32[8,16,4095]{2,0,1:T(8,128)} %copy.49) | copy-start | bytes 6289924
  50.9 16.2 %collective-permute-start.2 = (f32[8,2,4096]{2,0,1:T(8,128)S(1)}, f32[8,2,4096]{2,0,1:T(8,128)S(1)}, u32[]{:S(2)}, u32[]{:S(2)}) collective-permute-start(f32[8,2,4096]{2,0,1:T(8,128)S(1)} %get-tuple-element.139), channel_id=1, source_target_pairs={{0,1},{1,2},{2,3},{3,4},{4,5},{5,6},{6,7},{8,9},{9,10},{10,11},{11... | collective-permute-start | bytes 786440 | tf_op jit(solution)/shard_map/ppermute | solution.py:17
  55.5 11.7 %collective-permute-start.3 = (f32[8,2,4096]{2,0,1:T(8,128)S(1)}, f32[8,2,4096]{2,0,1:T(8,128)S(1)}, u32[]{:S(2)}, u32[]{:S(2)}) collective-permute-start(f32[8,2,4096]{2,0,1:T(8,128)S(1)} %get-tuple-element.140), channel_id=1, source_target_pairs={{1,0},{2,1},{3,2},{4,3},{5,4},{6,5},{7,6},{9,8},{10,9},{11,10},{12... | collective-permute-start | bytes 786440 | tf_op jit(solution)/shard_map/ppermute | solution.py:20
  77.2 9.7 %collective-permute-start.4 = (f32[8,2,4096]{2,0,1:T(8,128)S(1)}, f32[8,2,4096]{2,0,1:T(8,128)S(1)}, u32[]{:S(2)}, u32[]{:S(2)}) collective-permute-start(f32[8,2,4096]{2,0,1:T(8,128)S(1)} %get-tuple-element.129), channel_id=1, source_target_pairs={{0,1},{1,2},{2,3},{3,4},{4,5},{5,6},{6,7},{8,9},{9,10},{10,11},{11... | collective-permute-start | bytes 786440 | tf_op jit(solution)/shard_map/ppermute | solution.py:17
  81.6 10.8 %collective-permute-start.5 = (f32[8,2,4096]{2,0,1:T(8,128)S(1)}, f32[8,2,4096]{2,0,1:T(8,128)S(1)}, u32[]{:S(2)}, u32[]{:S(2)}) collective-permute-start(f32[8,2,4096]{2,0,1:T(8,128)S(1)} %get-tuple-element.130), channel_id=1, source_target_pairs={{1,0},{2,1},{3,2},{4,3},{5,4},{6,5},{7,6},{9,8},{10,9},{11,10},{12... | collective-permute-start | bytes 786440 | tf_op jit(solution)/shard_map/ppermute | solution.py:20
  102.4 9.1 %collective-permute-start.6 = (f32[8,2,4096]{2,0,1:T(8,128)S(1)}, f32[8,2,4096]{2,0,1:T(8,128)S(1)}, u32[]{:S(2)}, u32[]{:S(2)}) collective-permute-start(f32[8,2,4096]{2,0,1:T(8,128)S(1)} %get-tuple-element.119), channel_id=1, source_target_pairs={{0,1},{1,2},{2,3},{3,4},{4,5},{5,6},{6,7},{8,9},{9,10},{10,11},{11... | collective-permute-start | bytes 786440 | tf_op jit(solution)/shard_map/ppermute | solution.py:17
  106.9 12.1 %collective-permute-start.7 = (f32[8,2,4096]{2,0,1:T(8,128)S(1)}, f32[8,2,4096]{2,0,1:T(8,128)S(1)}, u32[]{:S(2)}, u32[]{:S(2)}) collective-permute-start(f32[8,2,4096]{2,0,1:T(8,128)S(1)} %get-tuple-element.120), channel_id=1, source_target_pairs={{1,0},{2,1},{3,2},{4,3},{5,4},{6,5},{7,6},{9,8},{10,9},{11,10},{12... | collective-permute-start | bytes 786440 | tf_op jit(solution)/shard_map/ppermute | solution.py:20
  143.1 2.5 copy-start.10
  143.1 18.9 %copy-start.13 = (pred[2048]{0:T(1024)(128)(4,1)S(1)}, pred[2048]{0:T(1024)(128)(4,1)}, u32[]{:S(2)}) copy-start(pred[2048]{0:T(1024)(128)(4,1)} %compare_and_fusion) | copy-start | bytes 6148
  145.6 22.9 %copy-start.8 = (f32[8,2048]{1,0:T(8,128)S(1)}, f32[8,2048]{1,0:T(8,128)}, u32[]{:S(2)}) copy-start(f32[8,2048]{1,0:T(8,128)} %param.13) | copy-start | bytes 196612
  145.6 22.9 %copy-start.11 = (f32[2048]{0:T(1024)S(1)}, f32[2048]{0:T(1024)}, u32[]{:S(2)}) copy-start(f32[2048]{0:T(1024)} %get-tuple-element.168) | copy-start | bytes 24580
  145.6 111.5 %copy-start.7 = (f32[32,4096]{1,0:T(8,128)S(1)}, f32[32,4096]{1,0:T(8,128)}, u32[]{:S(2)}) copy-start(f32[32,4096]{1,0:T(8,128)} %fusion.5) | copy-start | bytes 1572868
where the time goes:
time: 259 us; the launch traced here: 258 us
  local copies, waits for them, and re-layouts  78.8 us (30%)
  other arithmetic  66 us (25%)
  blocking collectives  52.6 us (20%)
  waiting for transfers between devices  29.9 us (12%)
  starting transfers between devices  24.4 us (9%)
  matrix products  4.56 us (2%)
    psum x1, blocking collectives, local(): gram_sum, mixed_sum = lax.psum((gram_part, mixed_part), 'slab')  39 us
    add x4, other arithmetic, advance(): return centre - advection + coefficients[2] * laplace + source  34.3 us
    div x32, other arithmetic, one_pivot(): scaled_row = pivot_row / pivot_val  26.3 us
    ppermute x4, starting transfers between devices, padded_2(): lax.ppermute(lax.slice_in_dim(block, block.shape[dim] - width, None, axis...  19.1 us
    dynamic_slice x32, local copies, waits for them, and re-layouts, one_pivot(): pivot_val = lax.dynamic_slice_in_dim(pivot_row, pivot, 1, 1)  18.7 us
    unnamed x43, local copies, waits for them, and re-layouts  17 us
    ppermute x4, waiting for transfers between devices, padded_2(): lax.ppermute(lax.slice_in_dim(block, block.shape[dim] - width, None, axis...  16.9 us
    gather x2, local copies, waits for them, and re-layouts, local(): predicted = jnp.take(flat_state, obs_index, axis=1)  16.4 us
  transfers between devices with their start and end apart: 8, of which 5 were waited for; matrix products, arithmetic and copies ran while one was open for 8% of the time, Pallas kernels for 0%

commit v1 on v0

v1 whole, which is shorter than its diff:
```python
import functools
import math

import jax
import jax.numpy as jnp
from jax import lax
from jax.experimental import pallas as pl
from jax.experimental.pallas import tpu as pltpu
from jax.sharding import PartitionSpec as P

STEPS = 4
GROUPS = 8
HALO = 2 * STEPS
LANES = 128
SUBLANES = 8
ROWS = 16
GROUP = 4
LAG = 3
WIDE = 4
VMEM_LIMIT = 48 * 1024 * 1024
ANYWHERE = pl.BlockSpec(memory_space=pl.ANY)
IN_VMEM = pl.BlockSpec(memory_space=pltpu.VMEM)
IN_SMEM = pl.BlockSpec(memory_space=pltpu.SMEM)


def hdot(left, right):
    return jnp.dot(left, right, precision=lax.Precision.HIGHEST, preferred_element_type=jnp.float32)


def limited(left, right):
    return jnp.minimum(jnp.maximum(left, jnp.minimum(right, 0.0)), jnp.maximum(right, 0.0))


def block_at(block):
    return pl.ds(pl.multiple_of(block * LANES, LANES), LANES)


def wide(row):
    return jnp.broadcast_to(row, (SUBLANES, LANES))


def columns_pass(level, row, levels, coef, params, blocks):
    lane = lax.broadcasted_iota(jnp.int32, (SUBLANES, LANES), 1)
    first, last = lane == 0, lane == LANES - 1
    c, c_rolled, d, d_rolled, slope, twice, left, right, laplace = ({} for _ in range(9))
    for tick in range(blocks + 2 * LAG + 4):
        b = tick - 1
        if b <= blocks:
            c[b] = levels[level, row, :, block_at(b % blocks)]
            c_rolled[b] = pltpu.roll(c[b], LANES - 1, 1)
        b = tick - 2 if tick - 2 < blocks else tick - 2
        if -1 <= b <= blocks:
            c_next = jnp.where(last, c_rolled[b + 1], c_rolled[b]) if b < blocks else c_rolled[b]
            d[b] = c_next - c[b]
            d_rolled[b] = pltpu.roll(d[b], 1, 1)
        b = tick - 2 - LAG
        if -1 <= b <= blocks:
            d_back = jnp.where(first, d_rolled[b - 1], d_rolled[b]) if b >= 0 else d_rolled[b]
            slope[b] = limited(d_back, d[b])
            twice[b] = d[b] + d[b]
            laplace[b] = d[b] - d_back
            left[b] = pltpu.roll(twice[b] - slope[b], 1, 1)
            right[b] = pltpu.roll(slope[b], LANES - 1, 1)
        b = tick - 3 - 2 * LAG
        if 0 <= b < blocks:
            at = block_at(b)
            speed = wide(coef[1, row, :, at])
            forward = jnp.where(first, left[b - 1], left[b])
            backward = twice[b] - jnp.where(last, right[b + 1], right[b])
            value = c[b] - speed * (jnp.where(speed > 0.0, forward, backward) + slope[b])
            value = value + wide(coef[2, row, :, at]) * laplace[b]
            value = value + params[:, at] * wide(coef[3, row, :, at])
            levels[level + 1, row, :, at] = value


def rows_pass(level, row, levels, coef, at):
    c = [levels[level, row - 2 + i, :, at] for i in range(GROUP + 4)]
    d = [c[i + 1] - c[i] for i in range(GROUP + 3)]
    slope = [None] + [limited(d[i - 1], d[i]) for i in range(1, GROUP + 3)]
    twice = [None] + [d[i] + d[i] for i in range(1, GROUP + 2)]
    for i in range(2, GROUP + 2):
        here = row - 2 + i
        speed = wide(coef[0, here, :, at])
        forward = twice[i - 1] - slope[i - 1]
        backward = twice[i] - slope[i + 1]
        change = wide(coef[2, here, :, at]) * (d[i] - d[i - 1])
        change = change - speed * (jnp.where(speed > 0.0, forward, backward) + slope[i])
        levels[level + 1, here, :, at] = levels[level + 1, here, :, at] + change


def advance_group(level, row, levels, coef, params, blocks):
    @pl.loop(0, GROUP)
    def _(i):
        columns_pass(level, row + i, levels, coef, params, blocks)

    @pl.loop(0, blocks // WIDE)
    def _(wide_block):
        for i in range(WIDE):
            rows_pass(level, row, levels, coef, block_at(wide_block * WIDE + i))


class Copies:
    def __init__(self, sems):
        self.sems, self.used = sems, 0

    def start(self, source, target):
        copy = pltpu.make_async_copy(source, target, self.sems.at[self.used])
        self.used += 1
        copy.start()
        return copy


def place(row):
    return pl.ds(row + HALO, GROUP)


def to_rows_kernel(blocks, tracer, *rest):
    outs, (staged, sems) = rest[: ROWS // GROUP], rest[ROWS // GROUP :]

    def copy(block):
        return pltpu.make_async_copy(tracer.at[:, block_at(block)], staged.at[block], sems.at[block])

    @pl.loop(0, blocks)
    def _(block):
        copy(block).start()

    @pl.loop(0, blocks)
    def _(block):
        copy(block).wait()
        for row in range(ROWS):
            outs[row // GROUP][row % GROUP, :, block_at(block)] = staged[
                block, pl.ds(row, SUBLANES, stride=ROWS), :
            ]


def interior_kernel(blocks, own0, own1, own2, own3, own_coef, params, *rest):
    outs, (levels, coef, sems) = rest[:5], rest[5:]
    copies = Copies(sems)
    waits = [
        copies.start(own, levels.at[0, place(GROUP * i)])
        for i, own in enumerate((own0, own1, own2, own3))
    ]
    waits.append(copies.start(own_coef, coef.at[:, HALO : HALO + ROWS]))
    for copy in waits:
        copy.wait()
    for level, start, count in ((0, 2, 3), (1, 4, 2), (2, 6, 1)):
        @pl.loop(0, count)
        def _(i):
            advance_group(level, start + HALO + GROUP * i, levels, coef, params, blocks)

    waits = [
        copies.start(levels.at[level, place(row)], out)
        for out, (level, row) in zip(outs, ((1, 2), (1, 10), (2, 4), (2, 8), (3, 6)))
    ]
    for copy in waits:
        copy.wait()


def edge_steps(outer, blocks, copies, waits, levels, coef, params, ready):
    for level in range(STEPS):
        for copy in waits[level]:
            copy.wait()
        low, high = 2 * level - outer, ROWS + outer - GROUP - 2 * level

        @pl.loop(0, 2)
        def _(side):
            advance_group(
                level, low + HALO + side * (high - low), levels, coef, params, blocks
            )

        ready(level, low, high)


def load_coef(copies, own_coef, gathered, coef):
    return [
        copies.start(own_coef, coef.at[:, HALO : HALO + ROWS]),
        copies.start(gathered.at[:, 0:HALO], coef.at[:, 0:HALO]),
        copies.start(gathered.at[:, HALO : 2 * HALO], coef.at[:, HALO + ROWS :]),
    ]


def middle_kernel(blocks, *refs):
    sources, refs = refs[:9], refs[9:]
    own_coef, gathered, params = refs[:3]
    outs, (levels, coef, sems) = refs[3:11], refs[11:]
    copies = Copies(sems)
    places = ((0, -4), (0, 0), (0, 12), (0, 16), (1, 2), (1, 10), (2, 4), (2, 8), (3, 6))
    waits = [[] for _ in range(STEPS)]
    for source, (level, row) in zip(sources, places):
        waits[level].append(copies.start(source, levels.at[level, place(row)]))
    waits[0] += load_coef(copies, own_coef, gathered, coef)
    sends = []

    def ready(level, low, high):
        for row, out in ((low, outs[2 * level]), (high, outs[2 * level + 1])):
            sends.append(copies.start(levels.at[level + 1, place(row)], out))

    edge_steps(2, blocks, copies, waits, levels, coef, params, ready)
    for copy in sends:
        copy.wait()


def last_kernel(blocks, *refs):
    sources, refs = refs[:12], refs[12:]
    own_coef, gathered, params, row_of, offset_of, shift_of = refs[:6]
    out, predicted, levels, coef, staged, sems, out_sems = refs[6:]
    copies = Copies(sems)
    places = (
        (0, -8), (0, -4), (0, 16), (0, 20),
        (1, -2), (1, 14), (2, 0), (2, 12), (3, 2), (3, 10), (4, 4), (4, 8),
    )
    waits = [[] for _ in range(STEPS + 1)]
    for source, (level, row) in zip(sources, places):
        waits[level].append(copies.start(source, levels.at[level, place(row)]))
    waits[0] += load_coef(copies, own_coef, gathered, coef)
    edge_steps(6, blocks, copies, waits, levels, coef, params, lambda *_: None)
    for copy in waits[STEPS]:
        copy.wait()

    def out_copy(block):
        return pltpu.make_async_copy(staged.at[block], out.at[:, block_at(block)], out_sems.at[block])

    @pl.loop(0, blocks)
    def _(block):
        for row in range(ROWS):
            staged[block, pl.ds(row, SUBLANES, stride=ROWS), :] = levels[
                STEPS, HALO + row, :, block_at(block)
            ]
        out_copy(block).start()

    lane = lax.broadcasted_iota(jnp.int32, (SUBLANES, LANES), 1)

    @pl.loop(0, predicted.shape[1] // LANES)
    def _(block):
        base = block * LANES
        found = jnp.zeros((SUBLANES, LANES), jnp.float32)
        for i in range(LANES):
            at = pl.ds(pl.multiple_of(offset_of[base + i], LANES), LANES)
            value = levels[STEPS, row_of[base + i], :, at]
            found = jnp.where(lane == i, pltpu.roll(value, shift_of[base + i], 1), found)
        predicted[:, block_at(block)] = found

    @pl.loop(0, blocks)
    def _(block):
        out_copy(block).wait()


def scratch(columns, sems):
    return [
        pltpu.VMEM((STEPS + 1, ROWS + 2 * HALO, SUBLANES, columns), jnp.float32),
        pltpu.VMEM((4, ROWS + 2 * HALO, 1, columns), jnp.float32),
    ], pltpu.SemaphoreType.DMA((sems,))


def kernel_call(body, name, outs, specs, out_specs, scratches, units, operands):
    return pl.pallas_call(
        body,
        out_shape=tuple(jax.ShapeDtypeStruct(shape, jnp.float32) for shape in outs),
        in_specs=specs,
        out_specs=out_specs,
        scratch_shapes=scratches,
        compiler_params=pltpu.CompilerParams(vmem_limit_bytes=VMEM_LIMIT),
        cost_estimate=pl.CostEstimate(
            flops=units * 40 * 32768, bytes_accessed=8 << 20, transcendentals=0
        ),
        name=name,
    )(*operands)


def transport(tracer, own_coef, halo_coef, params, obs_index, halos):
    members, rows, columns = tracer.shape
    if members != SUBLANES or rows != ROWS:
        raise ValueError("block shape")
    blocks = columns // LANES
    group = (GROUP, members, columns)
    flat = (members * rows, columns)
    own = kernel_call(
        functools.partial(to_rows_kernel, blocks), "to_rows",
        [group] * 4, [ANYWHERE], (IN_VMEM,) * 4,
        [pltpu.VMEM((blocks, members * rows, LANES), jnp.float32), pltpu.SemaphoreType.DMA((blocks,))],
        4, [tracer.reshape(flat)],
    )
    low0, high0, low1, high1 = halos(own)
    buffers, sems = scratch(columns, 10)
    inner = kernel_call(
        functools.partial(interior_kernel, blocks), "interior",
        [group] * 5, [ANYWHERE] * 5 + [IN_VMEM], (ANYWHERE,) * 5,
        buffers + [sems], 24, [*own, own_coef, params],
    )
    buffers, sems = scratch(columns, 20)
    first = kernel_call(
        functools.partial(middle_kernel, blocks), "edge_first",
        [group] * 8, [ANYWHERE] * 11 + [IN_VMEM], (ANYWHERE,) * 8,
        buffers + [sems], 32,
        [low0, own[0], own[3], high0, *inner, own_coef, halo_coef, params],
    )
    row_of = obs_index // columns + HALO
    lane_of = obs_index % LANES
    offset_of = obs_index % columns - lane_of
    shift_of = (jnp.arange(obs_index.shape[0], dtype=jnp.int32) - lane_of) % LANES
    buffers, sems = scratch(columns, 15)
    field, predicted = kernel_call(
        functools.partial(last_kernel, blocks), "edge_last",
        [flat, (members, obs_index.shape[0])],
        [ANYWHERE] * 14 + [IN_VMEM] + [IN_SMEM] * 3, (ANYWHERE, IN_VMEM),
        buffers + [pltpu.VMEM((blocks, members * rows, LANES), jnp.float32), sems, pltpu.SemaphoreType.DMA((blocks,))],
        40,
        [low1, low0, high0, high1, *first, own_coef, halo_coef, params, row_of, offset_of, shift_of],
    )
    return field.reshape(tracer.shape), predicted


def products_kernel(total_obs, per_group, spread, everyone, own, values, variance, same, out):
    weight = 1.0 / (variance[...] * total_obs)
    innovation = (values[...] - own[...]) * weight
    predicted = everyone[...]
    anomalies = (predicted - hdot(same[...], predicted) / per_group) * spread
    right = jnp.concatenate([anomalies * weight, innovation], axis=0)
    out[...] = lax.dot_general(
        anomalies,
        right,
        (((1,), (1,)), ((), ())),
        precision=lax.Precision.HIGHEST,
        preferred_element_type=jnp.float32,
    )


def update_kernel(per_group, summands, same, own_same, rank_row, rank_col, anomalies, own, out):
    members = same.shape[0]
    total = summands[0]
    for index in range(1, summands.shape[0]):
        total = total + summands[index]
    together = same[...]
    row = lax.broadcasted_iota(jnp.int32, (members, members), 0)
    col = lax.broadcasted_iota(jnp.int32, (members, members), 1)
    system = jnp.where(row == col, 1.0, 0.0) + together * total[:, 0:members]
    right = own_same[...] * total[:, members:]
    for pivot in range(per_group):
        pick = jnp.where(rank_row[...] == pivot, together, 0.0)
        pivot_system = hdot(pick, system)
        pivot_right = hdot(pick, right)
        pivot_value = jnp.sum(pick * pivot_system, axis=1, keepdims=True)
        factor = jnp.sum(pick * system, axis=1, keepdims=True)
        is_pivot = rank_col[...] == pivot
        scale = 1.0 / pivot_value
        scaled_system, scaled_right = pivot_system * scale, pivot_right * scale
        system = jnp.where(is_pivot, scaled_system, system - factor * scaled_system)
        right = jnp.where(is_pivot, scaled_right, right - factor * scaled_right)
    change = lax.dot_general(
        right,
        anomalies[...],
        (((0,), (0,)), ((), ())),
        precision=lax.Precision.HIGHEST,
        preferred_element_type=jnp.float32,
    )
    out[...] = own[...] + change


def local(tracer, coefficients, parameters, obs_index, obs_values, obs_variance, member_group):
    local_members, rows, columns = tracer.shape
    ens_pos = lax.axis_index("ens")
    ens_count = lax.axis_size("ens")
    slab_count = lax.axis_size("slab")
    if ens_count != coefficients.shape[0] or slab_count & (slab_count - 1):
        raise ValueError("mesh shape")
    forward = [(i, i + 1) for i in range(slab_count - 1)]
    backward = [(target, source) for source, target in forward]

    halving = jnp.array([0.5, 0.5, 1.0, 1.0], jnp.float32)[:, None, None]
    own_array = lax.dynamic_slice_in_dim(coefficients, ens_pos, 1, 0)[0]
    coef_low = lax.ppermute(own_array[rows - HALO :], "slab", forward)
    coef_high = lax.ppermute(own_array[:HALO], "slab", backward)
    shared = jnp.concatenate([coef_low, coef_high, parameters], axis=0)
    gathered = lax.all_gather(shared, "ens", axis=0, tiled=False)
    own_coef = (coefficients * halving)[:, :, None, :]
    halo_coef = (gathered[:, : 2 * HALO] * halving)[:, :, None, :]

    def halos(own):
        low0 = lax.ppermute(own[3], "slab", forward)
        high0 = lax.ppermute(own[0], "slab", backward)
        low1 = lax.ppermute(own[2], "slab", forward)
        high1 = lax.ppermute(own[1], "slab", backward)
        return low0, high0, low1, high1

    members = member_group.shape[0]
    per_group = members // GROUPS
    spread = 1.0 / math.sqrt(per_group - 1)
    same_bool = member_group[:, None] == member_group[None, :]
    same = same_bool.astype(jnp.float32)
    earlier = jnp.arange(members)[None, :] < jnp.arange(members)[:, None]
    rank = jnp.sum((same_bool & earlier).astype(jnp.int32), axis=1)
    own_same = lax.dynamic_slice_in_dim(same, ens_pos * local_members, local_members, 1)
    all_params = gathered[:, 2 * HALO :, :].reshape(members, columns)
    param_anomalies = (all_params - hdot(same, all_params) / per_group) * spread

    field, predicted = transport(tracer, own_coef, halo_coef, parameters, obs_index, halos)
    everyone = lax.all_gather(predicted, "ens", axis=0, tiled=True)
    total_obs = obs_variance.shape[0] * slab_count
    products = pl.pallas_call(
        functools.partial(products_kernel, float(total_obs), per_group, spread),
        out_shape=jax.ShapeDtypeStruct((members, members + local_members), jnp.float32),
        compiler_params=pltpu.CompilerParams(vmem_limit_bytes=VMEM_LIMIT),
        name="products",
    )(everyone, predicted, obs_values, obs_variance[None, :], same)
    distance = 1
    while distance < slab_count:
        pairs = [(i, i ^ distance) for i in range(slab_count)]
        products = products + lax.ppermute(products, "slab", pairs)
        distance *= 2
    updated = pl.pallas_call(
        functools.partial(update_kernel, per_group),
        out_shape=jax.ShapeDtypeStruct(parameters.shape, jnp.float32),
        compiler_params=pltpu.CompilerParams(vmem_limit_bytes=VMEM_LIMIT),
        name="update",
    )(products[None], same, own_same, rank[None, :], rank[:, None], param_anomalies, parameters)
    return (field, updated)


def solution(mesh):
    in_specs = (
        P("ens", "slab", None),
        P(None, "slab", None),
        P("ens", None),
        P("slab"),
        P("ens", "slab"),
        P("slab"),
        P(),
    )
    out_specs = (P("ens", "slab", None), P("ens", None))
    return jax.shard_map(local, mesh=mesh, in_specs=in_specs, out_specs=out_specs, check_vma=False)
```

time: 259 us -> 151 us (0.58)
  local copies, waits for them, and re-layouts: 78.8 us -> 12.6 us
  Pallas kernels: 0 us -> 62.7 us
  other arithmetic: 66 us -> 3.77 us
  blocking collectives: 52.6 us -> 5.79 us
  between operations: 1.06 us -> 14.2 us
  waiting for transfers between devices: 29.9 us -> 22.9 us
  matrix products: 4.56 us -> 1.64 us
    pallas_call x0 -> x6, Pallas kernels: none -> 62.7 us  [the longest x4 60 us: kernel_call(): pl.pallas_call(body, out_shape=tuple((jax.ShapeDtypeStruct(shape, jnp.flo...]
    psum x1 -> x0, blocking collectives: 39 us -> none  [local(): gram_sum, mixed_sum = lax.psum((gram_part, mixed_part), 'slab')]
    add x37 -> x2, other arithmetic: 36.9 us -> 0.01 us  [local(): products = products + lax.ppermute(products, 'slab', pairs)]
    div x32 -> x0, other arithmetic: 26.3 us -> none  [one_pivot(): scaled_row = pivot_row / pivot_val]
    dynamic_slice x32 -> x1, local copies, waits for them, and re-layouts: 18.7 us -> 0.07 us  [local(): lax.dynamic_slice_in_dim(same, ens_pos * local_members, local_members, 1)]
    gather x2 -> x0, local copies, waits for them, and re-layouts: 16.4 us -> none  [local(): predicted = jnp.take(flat_state, obs_index, axis=1)]
    add x1 -> x0, local copies, waits for them, and re-layouts: 15.6 us -> none  [advance(): return centre - advection + coefficients[2] * laplace + source]
    ppermute x8 -> x9, waiting for transfers between devices: 29.9 us -> 17.7 us  [the longest x1 8.98 us: halos(): low0 = lax.ppermute(own[3], 'slab', forward)]
  transfers between devices with their start and end apart: 8 -> 10, of which waited for: 5 -> 7; matrix products, arithmetic and copies ran while one was open for 8% -> 5% of each run, Pallas kernels for 0% -> 22%
where the time goes in v1:
time: 151 us; the launch traced here: 150 us
  Pallas kernels  62.7 us (42%)
  starting transfers between devices  26.5 us (18%)
  waiting for transfers between devices  22.9 us (15%)
  between operations  14.2 us (9%)
  local copies, waits for them, and re-layouts  12.6 us (8%)
  blocking collectives  5.79 us (4%)
  other arithmetic  3.77 us (2%)
  matrix products  1.64 us (1%)
    pallas_call x4, Pallas kernels, kernel_call(): pl.pallas_call(body, out_shape=tuple((jax.ShapeDtypeStruct(shape, jnp.flo...  60 us
    ppermute x1, waiting for transfers between devices, halos(): low0 = lax.ppermute(own[3], 'slab', forward)  8.98 us
    ppermute x3, starting transfers between devices, local(): products = products + lax.ppermute(products, 'slab', pairs)  8.66 us
    unnamed x32, local copies, waits for them, and re-layouts  8.27 us
    all_gather x1, blocking collectives, local(): everyone = lax.all_gather(predicted, 'ens', axis=0, tiled=True)  5.79 us
    all_gather x1, waiting for transfers between devices, local(): gathered = lax.all_gather(shared, 'ens', axis=0, tiled=False)  5.14 us
    ppermute x1, starting transfers between devices, local(): coef_low = lax.ppermute(own_array[rows - HALO:], 'slab', forward)  4.85 us
    ppermute x1, starting transfers between devices, halos(): low0 = lax.ppermute(own[3], 'slab', forward)  4.58 us
  transfers between devices with their start and end apart: 10, of which 7 were waited for; matrix products, arithmetic and copies ran while one was open for 5% of the time, Pallas kernels for 22%

profile of v1, /device:TPU:0, one launch (start us, length us, event | category | flops | bytes accessed | tf_op | source)
XLA Modules:
  0.0 150.2 jit_solution(13169235423440253587)
XLA Ops:
  7.2 0.0 all-gather.3.cloned.1.call-start
  7.2 1.0 dynamic-slice_bitcast_fusion.1
  8.2 4.8 %collective-permute-start.4 = (f32[8,4096]{1,0:T(8,128)S(1)}, f32[8,4096]{1,0:T(8,128)S(1)}, u32[]{:S(2)}, u32[]{:S(2)}) collective-permute-start(f32[8,4096]{1,0:T(8,128)S(1)} %get-tuple-element.40), channel_id=1, source_target_pairs={{0,1},{1,2},{2,3},{3,4},{4,5},{5,6},{6,7},{8,9},{9,10},{10,11},{11... | collective-permute-start | bytes 393224 | tf_op jit(solution)/shard_map/ppermute | solution.py:371
  13.1 0.0 copy-start.13
  13.1 0.0 copy-start.14
  13.1 0.0 copy-start.15
  13.1 1.4 collective-permute-start.5
  14.5 1.3 collective-permute-done.4
  15.8 4.3 %collective-permute-done.5 = f32[8,4096]{1,0:T(8,128)S(1)} collective-permute-done((f32[8,4096]{1,0:T(8,128)S(1)}, f32[8,4096]{1,0:T(8,128)S(1)}, u32[]{:S(2)}, u32[]{:S(2)}) %collective-permute-start.5) | collective-permute-done | bytes 131104 | tf_op jit(solution)/shard_map/ppermute | solution.py:372
  20.1 1.7 %pad_maximum_fusion = f32[24,4096]{1,0:T(8,128)} fusion(f32[8,4096]{1,0:T(8,128)} %own.1, f32[8,4096]{1,0:T(8,128)S(1)} %collective-permute-done.5, f32[8,4096]{1,0:T(8,128)S(1)} %collective-permute-done.4), kind=kLoop, calls=%fused_computation.6 | loop fusion | flops 196608 | bytes 786432 | tf_op jit(solution)/shard_map/concatenate | solution.py:373
  21.8 0.0 all-gather.3.cloned.1.call-update
  21.8 0.0 copy-start.2
  21.8 1.6 %copy-done.2 = f32[8,16,4096]{2,1,0:T(8,128)S(1)} copy-done((f32[8,16,4096]{2,1,0:T(8,128)S(1)}, f32[8,16,4096]{2,1,0:T(8,128)}, u32[]{:S(2)}) %copy-start.2) | copy-done | bytes 2097176
  23.4 2.6 %to_rows.1 = (f32[4,8,4096]{2,1,0:T(8,128)S(1)}, f32[4,8,4096]{2,1,0:T(8,128)}, f32[4,8,4096]{2,1,0:T(8,128)}, f32[4,8,4096]{2,1,0:T(8,128)S(1)}) custom-call(f32[128,4096]{1,0:T(8,128)S(1)} %bitcast.20), custom_call_target="tpu_custom_call" | custom-call | flops 5242880 | bytes 8388608 | tf_op jit(solution)/shard_map/to_rows/pallas_call | solution.py:256
  26.0 4.4 %collective-permute-start = (f32[4,8,4096]{2,1,0:T(8,128)}, f32[4,8,4096]{2,1,0:T(8,128)S(1)}, u32[]{:S(2)}, u32[]{:S(2)}) collective-permute-start(f32[4,8,4096]{2,1,0:T(8,128)} %get-tuple-element.21.own2), channel_id=1, source_target_pairs={{0,1},{1,2},{2,3},{3,4},{4,5},{5,6},{6,7},{8,9},{9,10},{10,11},{11... | collective-permute-start | bytes 1572872 | tf_op jit(solution)/shard_map/ppermute | solution.py:381
  30.4 1.3 collective-permute-start.3
  31.7 4.6 %collective-permute-start.1 = (f32[4,8,4096]{2,1,0:T(8,128)S(1)}, f32[4,8,4096]{2,1,0:T(8,128)S(1)}, u32[]{:S(2)}, u32[]{:S(2)}) collective-permute-start(f32[4,8,4096]{2,1,0:T(8,128)S(1)} %get-tuple-element.22.own3.refs_2_), channel_id=1, source_target_pairs={{0,1},{1,2},{2,3},{3,4},{4,5},{5,6},{6,7},{8,9},{9,10},{10,11},{11... | collective-permute-start | bytes 1572872 | tf_op jit(solution)/shard_map/ppermute | solution.py:379
  36.3 1.3 collective-permute-start.2
  37.6 0.0 copy-done.13
  37.6 0.1 compare_convert_fusion.same
  37.7 0.0 copy-done.14
  37.7 5.1 %all-gather.3.cloned.1.call-done = f32[96,4096]{1,0:T(8,128)} async-done(((f32[24,4096]{1,0:T(8,128)}), f32[96,4096]{1,0:T(8,128)}) %all-gather.3.cloned.1.call-update) | async-done | bytes 1572880 | tf_op jit(solution)/shard_map/all_gather | solution.py:374
  42.8 0.0 copy-done.15
  42.8 1.8 %slice_multiply_fusion = (f32[4,16,4096]{2,1,0:T(8,128)S(1)}, f32[4,16,1,4096]{3,1,0,2:T(8,128)S(1)}) fusion(f32[4,24,4096]{2,1,0:T(8,128)} %bitcast.24, f32[4]{0:T(128)S(1)} %copy-done.15, f32[4,16,4096]{2,1,0:T(8,128)} %param.9), kind=kLoop, calls=%fused_computation.3 | loop fusion | flops 524288 | bytes 4194320 | tf_op jit(solution)/shard_map/mul | solution.py:376
  44.6 2.1 %broadcast_in_dim.24.refs_10_.refs_13_ = f32[4,16,1,4096]{3,2,1,0:T(1,128)} reshape(f32[4,16,4096]{2,1,0:T(8,128)S(1)} %get-tuple-element.45) | data formatting | bytes 2097152 | tf_op jit(solution)/shard_map/broadcast_in_dim | solution.py:376
  46.8 0.0 copy-start.1
  46.8 1.1 copy.10.own_coef.refs_9_.refs_12_
  47.8 0.0 copy-done.1
  47.9 0.0 copy-start
  47.9 13.1 %interior.1 = (f32[4,8,4096]{2,1,0:T(8,128)S(1)}, f32[4,8,4096]{2,1,0:T(8,128)S(1)}, f32[4,8,4096]{2,1,0:T(8,128)S(1)}, f32[4,8,4096]{2,1,0:T(8,128)S(1)}, f32[4,8,4096]{2,1,0:T(8,128)S(1)}) custom-call(f32[4,8,4096]{2,1,0:T(8,128)S(1)} %get-tuple-element.23.own0.refs_1_, f32[4,8,4096]{2,1,0:T(8,128)} %get-tuple-element.24.own1, ...), custom_call_target="tpu_custom_call" | custom-call | flops 31457280 | bytes 8388608 | tf_op jit(solution)/shard_map/interior/pallas_call | solution.py:256
  61.0 0.0 copy-done
  61.0 0.0 copy-start.6
  61.0 0.8 copy-done.6
  61.8 0.0 copy-start.7
  61.8 0.8 copy-done.7
  62.6 0.0 copy-start.8
  62.6 0.8 copy-done.8
  63.4 0.8 copy-done.9
  64.2 0.8 copy-done.10
  65.0 9.0 %collective-permute-done.1.refs_0_.refs_1_ = f32[4,8,4096]{2,1,0:T(8,128)S(1)} collective-permute-done((f32[4,8,4096]{2,1,0:T(8,128)S(1)}, f32[4,8,4096]{2,1,0:T(8,128)S(1)}, u32[]{:S(2)}, u32[]{:S(2)}) %collective-permute-start.1) | collective-permute-done | bytes 524320 | tf_op jit(solution)/shard_map/ppermute | solution.py:379
  74.0 0.0 collective-permute-done.2.refs_3_.refs_2_
  74.0 0.8 copy-done.3
  74.8 18.1 %edge_first.1 = (f32[4,8,4096]{2,1,0:T(8,128)S(1)}, f32[4,8,4096]{2,1,0:T(8,128)S(1)}, f32[4,8,4096]{2,1,0:T(8,128)S(1)}, f32[4,8,4096]{2,1,0:T(8,128)S(1)}, f32...) custom-call(f32[4,8,4096]{2,1,0:T(8,128)S(1)} %collective-permute-don, ...), custom_call_target="tpu_custom_call" | custom-call | flops 41943040 | bytes 8388608 | tf_op jit(solution)/shard_map/edge_first/pallas_call | solution.py:256
  92.9 0.0 copy-start.5
  92.9 0.8 copy-done.5
  93.7 0.0 collective-permute-done.refs_0_
  93.7 0.0 collective-permute-done.3.refs_3_
  93.7 1.0 copy-done.4
  94.7 26.2 %edge_last.1 = (f32[128,4096]{1,0:T(8,128)}, f32[8,2048]{1,0:T(8,128)S(1)}) custom-call(f32[4,8,4096]{2,1,0:T(8,128)S(1)} %collective-permute-done.refs_0_, f32[4,8,4096]{2,1,0:T(8,128)S(1)} %collective-permute-done.1.refs_0_.refs_1_, f32[4,8,4096]{2,1,0:T(8,128)S(1)} %copy-done.4, f32[4,8,4096]{2,1,0:T(8,128)S(1)} %collective-permute-done.3.refs_3_, ...), custom_call_target="tpu_custom_call" | custom-call | flops 52428800 | bytes 8388608 | tf_op jit(solution)/shard_map/edge_last/pallas_call | solution.py:256
  121.0 5.8 %all_gather.11.everyone = f32[32,2048]{1,0:T(8,128)S(1)} all-gather(f32[8,2048]{1,0:T(8,128)S(1)} %get-tuple-element.39.own), channel_id=1, replica_groups=mesh['ens'=4,'slab'=8] {'ens'}, dimensions={0}, use_global_device_ids=true | all-gather | bytes 327680 | tf_op jit(solution)/shard_map/all_gather | solution.py:397
  126.7 0.0 copy-done.11
  126.8 0.0 copy-done.12
  126.8 0.6 products.1
  127.4 2.5 %collective-permute-start.6 = (f32[32,40]{1,0:T(8,128)S(1)}, f32[32,40]{1,0:T(8,128)S(1)}, u32[]{:S(2)}, u32[]{:S(2)}) collective-permute-start(f32[32,40]{1,0:T(8,128)S(1)} %products.1), channel_id=1, source_target_pairs={{0,1},{1,0},{2,3},{3,2},{4,5},{5,4},{6,7},{7,6},{8,9},{9,8},{10,11... | collective-permute-start | bytes 15368 | tf_op jit(solution)/shard_map/ppermute | solution.py:408
  129.9 0.2 convert_reduce_fusion
  130.1 1.5 %collective-permute-done.6 = f32[32,40]{1,0:T(8,128)S(1)} collective-permute-done((f32[32,40]{1,0:T(8,128)S(1)}, f32[32,40]{1,0:T(8,128)S(1)}, u32[]{:S(2)}, u32[]{:S(2)}) %collective-permute-start.6) | collective-permute-done | bytes 5152 | tf_op jit(solution)/shard_map/ppermute | solution.py:408
  131.6 3.1 %collective-permute-start.7 = (f32[32,40]{1,0:T(8,128)S(1)}, f32[32,40]{1,0:T(8,128)S(1)}, u32[]{:S(2)}, u32[]{:S(2)}) collective-permute-start(f32[32,40]{1,0:T(8,128)S(1)} %add.42), channel_id=1, source_target_pairs={{0,2},{1,3},{2,0},{3,1},{4,6},{5,7},{6,4},{7,5},{8,10},{9,11},{10,... | collective-permute-start | bytes 15368 | tf_op jit(solution)/shard_map/ppermute | solution.py:408
  134.7 0.1 constant_dynamic-slice_fusion.own_same
  134.8 0.1 copy.13.rank_col
  134.9 1.6 %collective-permute-done.7 = f32[32,40]{1,0:T(8,128)S(1)} collective-permute-done((f32[32,40]{1,0:T(8,128)S(1)}, f32[32,40]{1,0:T(8,128)S(1)}, u32[]{:S(2)}, u32[]{:S(2)}) %collective-permute-start.7) | collective-permute-done | bytes 5152 | tf_op jit(solution)/shard_map/ppermute | solution.py:408
  136.5 3.0 %collective-permute-start.8 = (f32[32,40]{1,0:T(8,128)S(1)}, f32[32,40]{1,0:T(8,128)S(1)}, u32[]{:S(2)}, u32[]{:S(2)}) collective-permute-start(f32[32,40]{1,0:T(8,128)S(1)} %add.43), channel_id=1, source_target_pairs={{0,4},{1,5},{2,6},{3,7},{4,0},{5,1},{6,2},{7,3},{8,12},{9,13},{10,... | collective-permute-start | bytes 15368 | tf_op jit(solution)/shard_map/ppermute | solution.py:408
  139.5 1.6 %fusion.1.anomalies = f32[32,4096]{1,0:T(8,128)S(1)} fusion(f32[4,24,4096]{2,1,0:T(8,128)} %bitcast.25, s32[32]{0:T(128)S(1)} %copy-done.13), kind=kOutput, calls=%fused_computation.2 | convolution fusion | flops 50725888 | bytes 1573888 | tf_op jit(solution)/shard_map/dot_general | solution.py:27
  141.1 0.1 collective-permute-done.8
  141.2 2.1 %update.1 = f32[8,4096]{1,0:T(8,128)} custom-call(f32[1,32,40]{2,1,0:T(8,128)S(1)} %add_bitcast_fusion.summands, f32[32,32]{1,0:T(8,128)S(1)} %compare_convert_fusion.same, f32[32,8]{1,0:T(8,128)S(1)} %constant_dynamic-slice_fusion.own_same, s32[1,32]{1,0:T(1,128)S(1)} %bitcast.23, s32[32,1]{1,0:T(8,128)S(1)} %copy.13.rank_col, ...), custom_call_target="tpu_custom_call" | custom-call | tf_op jit(solution)/shard_map/update/pallas_call | solution.py:410
  (10 shorter events, 0.0 us)
Async XLA Ops:
  7.2 35.7 %all-gather.3.cloned.1.call-start = ((), (), s32[]{:S(2)}) async-start(), calls=%async_computation | async-start | bytes 1966080 | tf_op jit(solution)/shard_map/all_gather | solution.py:374
  8.2 7.6 %collective-permute-start.4 = (f32[8,4096]{1,0:T(8,128)S(1)}, f32[8,4096]{1,0:T(8,128)S(1)}, u32[]{:S(2)}, u32[]{:S(2)}) collective-permute-start(f32[8,4096]{1,0:T(8,128)S(1)} %get-tuple-element.40), channel_id=1, source_target_pairs={{0,1},{1,2},{2,3},{3,4},{4,5},{5,6},{6,7},{8,9},{9,10},{10,11},{11... | collective-permute-start | bytes 393224 | tf_op jit(solution)/shard_map/ppermute | solution.py:371
  13.1 24.5 %copy-start.13 = (s32[32]{0:T(128)S(1)}, s32[32]{0:T(128)}, u32[]{:S(2)}) copy-start(s32[32]{0:T(128)} %param.14) | copy-start | bytes 388
  13.1 24.6 %copy-start.14 = (s32[2048]{0:T(1024)S(1)}, s32[2048]{0:T(1024)}, u32[]{:S(2)}) copy-start(s32[2048]{0:T(1024)} %param.11) | copy-start | bytes 24580
  13.1 29.7 %copy-start.15 = (f32[4]{0:T(128)S(1)}, f32[4]{0:T(128)}, u32[]{:S(2)}) copy-start(f32[4]{0:T(128)} %constant.64.clone) | copy-start | bytes 52
  13.1 7.0 %collective-permute-start.5 = (f32[8,4096]{1,0:T(8,128)S(1)}, f32[8,4096]{1,0:T(8,128)S(1)}, u32[]{:S(2)}, u32[]{:S(2)}) collective-permute-start(f32[8,4096]{1,0:T(8,128)S(1)} %get-tuple-element.41), channel_id=1, source_target_pairs={{1,0},{2,1},{3,2},{4,3},{5,4},{6,5},{7,6},{9,8},{10,9},{11,10},{12... | collective-permute-start | bytes 393224 | tf_op jit(solution)/shard_map/ppermute | solution.py:372
  21.8 1.6 %copy-start.2 = (f32[8,16,4096]{2,1,0:T(8,128)S(1)}, f32[8,16,4096]{2,1,0:T(8,128)}, u32[]{:S(2)}) copy-start(f32[8,16,4096]{2,1,0:T(8,128)} %param.8) | copy-start | bytes 6291460
  26.0 67.7 %collective-permute-start = (f32[4,8,4096]{2,1,0:T(8,128)}, f32[4,8,4096]{2,1,0:T(8,128)S(1)}, u32[]{:S(2)}, u32[]{:S(2)}) collective-permute-start(f32[4,8,4096]{2,1,0:T(8,128)} %get-tuple-element.21.own2), channel_id=1, source_target_pairs={{0,1},{1,2},{2,3},{3,4},{4,5},{5,6},{6,7},{8,9},{9,10},{10,11},{11... | collective-permute-start | bytes 1572872 | tf_op jit(solution)/shard_map/ppermute | solution.py:381
  30.4 63.3 %collective-permute-start.3 = (f32[4,8,4096]{2,1,0:T(8,128)}, f32[4,8,4096]{2,1,0:T(8,128)S(1)}, u32[]{:S(2)}, u32[]{:S(2)}) collective-permute-start(f32[4,8,4096]{2,1,0:T(8,128)} %get-tuple-element.24.own1), channel_id=1, source_target_pairs={{1,0},{2,1},{3,2},{4,3},{5,4},{6,5},{7,6},{9,8},{10,9},{11,10},{12... | collective-permute-start | bytes 1572872 | tf_op jit(solution)/shard_map/ppermute | solution.py:382
  31.7 42.3 %collective-permute-start.1 = (f32[4,8,4096]{2,1,0:T(8,128)S(1)}, f32[4,8,4096]{2,1,0:T(8,128)S(1)}, u32[]{:S(2)}, u32[]{:S(2)}) collective-permute-start(f32[4,8,4096]{2,1,0:T(8,128)S(1)} %get-tuple-element.22.own3.refs_2_), channel_id=1, source_target_pairs={{0,1},{1,2},{2,3},{3,4},{4,5},{5,6},{6,7},{8,9},{9,10},{10,11},{11... | collective-permute-start | bytes 1572872 | tf_op jit(solution)/shard_map/ppermute | solution.py:379
  36.3 37.7 %collective-permute-start.2 = (f32[4,8,4096]{2,1,0:T(8,128)S(1)}, f32[4,8,4096]{2,1,0:T(8,128)S(1)}, u32[]{:S(2)}, u32[]{:S(2)}) collective-permute-start(f32[4,8,4096]{2,1,0:T(8,128)S(1)} %get-tuple-element.23.own0.refs_1_), channel_id=1, source_target_pairs={{1,0},{2,1},{3,2},{4,3},{5,4},{6,5},{7,6},{9,8},{10,9},{11,10},{12... | collective-permute-start | bytes 1572872 | tf_op jit(solution)/shard_map/ppermute | solution.py:380
  46.8 1.1 copy-start.1
  47.9 13.1 %copy-start = (f32[4,16,1,4096]{3,2,1,0:T(1,128)}, f32[4,16,1,4096]{3,2,1,0:T(1,128)S(1)}, u32[]{:S(2)}) copy-start(f32[4,16,1,4096]{3,2,1,0:T(1,128)S(1)} %copy.10.own_coef.refs_9_.refs_12_) | copy-start | bytes 3145732
  61.0 0.8 copy-start.6
  61.8 0.8 copy-start.7
  62.6 0.8 copy-start.8
  63.4 0.8 copy-start.9
  64.2 0.8 copy-start.10
  74.0 0.8 copy-start.3
  92.9 0.8 copy-start.5
  93.7 1.0 copy-start.4
  94.7 32.0 %copy-start.11 = (f32[8,2048]{1,0:T(8,128)S(1)}, f32[8,2048]{1,0:T(8,128)}, u32[]{:S(2)}) copy-start(f32[8,2048]{1,0:T(8,128)} %values.1) | copy-start | bytes 196612
  94.7 32.0 %copy-start.12 = (f32[2048]{0:T(1024)S(1)}, f32[2048]{0:T(1024)}, u32[]{:S(2)}) copy-start(f32[2048]{0:T(1024)} %param.13) | copy-start | bytes 24580
  127.4 4.2 %collective-permute-start.6 = (f32[32,40]{1,0:T(8,128)S(1)}, f32[32,40]{1,0:T(8,128)S(1)}, u32[]{:S(2)}, u32[]{:S(2)}) collective-permute-start(f32[32,40]{1,0:T(8,128)S(1)} %products.1), channel_id=1, source_target_pairs={{0,1},{1,0},{2,3},{3,2},{4,5},{5,4},{6,7},{7,6},{8,9},{9,8},{10,11... | collective-permute-start | bytes 15368 | tf_op jit(solution)/shard_map/ppermute | solution.py:408
  131.6 4.8 %collective-permute-start.7 = (f32[32,40]{1,0:T(8,128)S(1)}, f32[32,40]{1,0:T(8,128)S(1)}, u32[]{:S(2)}, u32[]{:S(2)}) collective-permute-start(f32[32,40]{1,0:T(8,128)S(1)} %add.42), channel_id=1, source_target_pairs={{0,2},{1,3},{2,0},{3,1},{4,6},{5,7},{6,4},{7,5},{8,10},{9,11},{10,... | collective-permute-start | bytes 15368 | tf_op jit(solution)/shard_map/ppermute | solution.py:408
  136.5 4.8 %collective-permute-start.8 = (f32[32,40]{1,0:T(8,128)S(1)}, f32[32,40]{1,0:T(8,128)S(1)}, u32[]{:S(2)}, u32[]{:S(2)}) collective-permute-start(f32[32,40]{1,0:T(8,128)S(1)} %add.43), channel_id=1, source_target_pairs={{0,4},{1,5},{2,6},{3,7},{4,0},{5,1},{6,2},{7,3},{8,12},{9,13},{10,... | collective-permute-start | bytes 15368 | tf_op jit(solution)/shard_map/ppermute | solution.py:408
Sparse Core Ops, SparseCore 0:
  21.9 20.8 all-gather.2

commit v2 on v1

v2 whole, which is shorter than its diff:
```python
import functools
import math

import jax
import jax.numpy as jnp
from jax import lax
from jax.experimental import pallas as pl
from jax.experimental.pallas import tpu as pltpu
from jax.sharding import PartitionSpec as P

STEPS = 4
GROUPS = 8
HALO = 2 * STEPS
LANES = 128
SUBLANES = 8
ROWS = 16
GROUP = 4
LAG = 3
WIDE = 8
TOGETHER = 2
VMEM_LIMIT = 30 * 1024 * 1024
TALL_LIMIT = 60 * 1024 * 1024
ANYWHERE = pl.BlockSpec(memory_space=pl.ANY)
IN_VMEM = pl.BlockSpec(memory_space=pltpu.VMEM)
IN_SMEM = pl.BlockSpec(memory_space=pltpu.SMEM)


def hdot(left, right):
    return jnp.dot(left, right, precision=lax.Precision.HIGHEST, preferred_element_type=jnp.float32)


def limited(left, right):
    return jnp.minimum(jnp.maximum(left, jnp.minimum(right, 0.0)), jnp.maximum(right, 0.0))


def block_at(block):
    return pl.ds(pl.multiple_of(block * LANES, LANES), LANES)


def wide(row):
    return jnp.broadcast_to(row, (SUBLANES, LANES))


def columns_pass(source, first_row, count, target, target_row, coef, params, blocks):
    lane = lax.broadcasted_iota(jnp.int32, (SUBLANES, LANES), 1)
    first, last = lane == 0, lane == LANES - 1
    c, c_rolled, d, d_rolled, slope, twice, left, right, laplace = ({} for _ in range(9))
    for tick in range(blocks + 2 * LAG + 4):
        for i in range(count):
            row = first_row + i
            b = tick - 1
            if b <= blocks:
                c[i, b] = source[row, :, block_at(b % blocks)]
                c_rolled[i, b] = pltpu.roll(c[i, b], LANES - 1, 1)
            b = tick - 2
            if -1 <= b <= blocks:
                c_next = c_rolled[i, b]
                if b < blocks:
                    c_next = jnp.where(last, c_rolled[i, b + 1], c_next)
                d[i, b] = c_next - c[i, b]
                d_rolled[i, b] = pltpu.roll(d[i, b], 1, 1)
            b = tick - 2 - LAG
            if -1 <= b <= blocks:
                d_back = d_rolled[i, b]
                if b >= 0:
                    d_back = jnp.where(first, d_rolled[i, b - 1], d_back)
                slope[i, b] = limited(d_back, d[i, b])
                twice[i, b] = d[i, b] + d[i, b]
                laplace[i, b] = d[i, b] - d_back
                left[i, b] = pltpu.roll(twice[i, b] - slope[i, b], 1, 1)
                right[i, b] = pltpu.roll(slope[i, b], LANES - 1, 1)
            b = tick - 3 - 2 * LAG
            if 0 <= b < blocks:
                at = block_at(b)
                speed = wide(coef[1, row, :, at])
                forward = jnp.where(first, left[i, b - 1], left[i, b])
                backward = twice[i, b] - jnp.where(last, right[i, b + 1], right[i, b])
                change = jnp.where(speed > 0.0, forward, backward) + slope[i, b]
                value = c[i, b] - (0.5 * speed) * change
                value = value + wide(coef[2, row, :, at]) * laplace[i, b]
                value = value + params[:, at] * wide(coef[3, row, :, at])
                target[target_row + i, :, at] = value


def rows_pass(source, row, partial, target, coef, at):
    c = [source[row - 2 + i, :, at] for i in range(GROUP + 4)]
    d = [c[i + 1] - c[i] for i in range(GROUP + 3)]
    slope = [None] + [limited(d[i - 1], d[i]) for i in range(1, GROUP + 3)]
    twice = [None] + [d[i] + d[i] for i in range(1, GROUP + 2)]
    for i in range(2, GROUP + 2):
        here = row - 2 + i
        speed = wide(coef[0, here, :, at])
        forward = twice[i - 1] - slope[i - 1]
        backward = twice[i] - slope[i + 1]
        change = wide(coef[2, here, :, at]) * (d[i] - d[i - 1])
        change = change - (0.5 * speed) * (jnp.where(speed > 0.0, forward, backward) + slope[i])
        target[here, :, at] = partial[i - 2, :, at] + change


def advance_group(source, target, row, partial, coef, params, blocks):
    @pl.loop(0, GROUP // TOGETHER)
    def _(i):
        columns_pass(
            source, row + i * TOGETHER, TOGETHER, partial, i * TOGETHER, coef, params, blocks
        )

    @pl.loop(0, blocks // WIDE)
    def _(wide_block):
        for i in range(WIDE):
            rows_pass(source, row, partial, target, coef, block_at(wide_block * WIDE + i))


class Copies:
    def __init__(self, sems):
        self.sems, self.used = sems, 0

    def start(self, source, target):
        copy = pltpu.make_async_copy(source, target, self.sems.at[self.used])
        self.used += 1
        copy.start()
        return copy


def place(row):
    return pl.ds(row + HALO, GROUP)


def to_rows_kernel(blocks, tracer, *rest):
    outs, (staged, sems) = rest[: ROWS // GROUP], rest[ROWS // GROUP :]

    def copy(block):
        return pltpu.make_async_copy(tracer.at[:, block_at(block)], staged.at[block], sems.at[block])

    @pl.loop(0, blocks)
    def _(block):
        copy(block).start()

    @pl.loop(0, blocks)
    def _(block):
        copy(block).wait()
        for row in range(ROWS):
            outs[row // GROUP][row % GROUP, :, block_at(block)] = staged[
                block, pl.ds(row, SUBLANES, stride=ROWS), :
            ]


def interior_kernel(blocks, own0, own1, own2, own3, own_coef, params, *rest):
    outs, (*levels, partial, coef, sems) = rest[:5], rest[5:]
    copies = Copies(sems)
    waits = [
        copies.start(own, levels[0].at[place(GROUP * i)])
        for i, own in enumerate((own0, own1, own2, own3))
    ]
    waits.append(copies.start(own_coef, coef.at[:, HALO : HALO + ROWS, 0]))
    for copy in waits:
        copy.wait()
    for level, start, count in ((0, 2, 3), (1, 4, 2), (2, 6, 1)):
        @pl.loop(0, count)
        def _(i):
            row = start + HALO + GROUP * i
            advance_group(levels[level], levels[level + 1], row, partial, coef, params, blocks)

    waits = [
        copies.start(levels[level].at[place(row)], out)
        for out, (level, row) in zip(outs, ((1, 2), (1, 10), (2, 4), (2, 8), (3, 6)))
    ]
    for copy in waits:
        copy.wait()


def edge_steps(outer, blocks, waits, levels, partial, coef, params, ready):
    for level in range(STEPS):
        for copy in waits[level]:
            copy.wait()
        low, high = 2 * level - outer, ROWS + outer - GROUP - 2 * level

        @pl.loop(0, 2)
        def _(side):
            row = low + HALO + side * (high - low)
            advance_group(levels[level], levels[level + 1], row, partial, coef, params, blocks)

        ready(level, low, high)


def load_coef(copies, own_coef, gathered, coef):
    return [
        copies.start(own_coef, coef.at[:, HALO : HALO + ROWS, 0]),
        copies.start(gathered.at[:, 0:HALO], coef.at[:, 0:HALO, 0]),
        copies.start(gathered.at[:, HALO : 2 * HALO], coef.at[:, HALO + ROWS :, 0]),
    ]


def middle_kernel(blocks, *refs):
    sources, refs = refs[:9], refs[9:]
    own_coef, gathered, params = refs[:3]
    outs, (*levels, partial, coef, sems) = refs[3:11], refs[11:]
    copies = Copies(sems)
    places = ((0, -4), (0, 0), (0, 12), (0, 16), (1, 2), (1, 10), (2, 4), (2, 8), (3, 6))
    waits = [[] for _ in range(STEPS)]
    for source, (level, row) in zip(sources, places):
        waits[level].append(copies.start(source, levels[level].at[place(row)]))
    waits[0] += load_coef(copies, own_coef, gathered, coef)
    sends = []

    def ready(level, low, high):
        for row, out in ((low, outs[2 * level]), (high, outs[2 * level + 1])):
            sends.append(copies.start(levels[level + 1].at[place(row)], out))

    edge_steps(2, blocks, waits, levels, partial, coef, params, ready)
    for copy in sends:
        copy.wait()


def last_kernel(blocks, *refs):
    sources, refs = refs[:12], refs[12:]
    own_coef, gathered, params, row_of, offset_of, shift_of = refs[:6]
    out, predicted, *levels, partial, coef, staged, sems, out_sems = refs[6:]
    copies = Copies(sems)
    places = (
        (0, -8), (0, -4), (0, 16), (0, 20),
        (1, -2), (1, 14), (2, 0), (2, 12), (3, 2), (3, 10), (4, 4), (4, 8),
    )
    waits = [[] for _ in range(STEPS + 1)]
    for source, (level, row) in zip(sources, places):
        waits[level].append(copies.start(source, levels[level].at[place(row)]))
    waits[0] += load_coef(copies, own_coef, gathered, coef)
    edge_steps(6, blocks, waits, levels, partial, coef, params, lambda *_: None)
    for copy in waits[STEPS]:
        copy.wait()

    def out_copy(block):
        return pltpu.make_async_copy(staged.at[block], out.at[:, block_at(block)], out_sems.at[block])

    @pl.loop(0, blocks)
    def _(block):
        for row in range(ROWS):
            staged[block, pl.ds(row, SUBLANES, stride=ROWS), :] = levels[STEPS][
                HALO + row, :, block_at(block)
            ]
        out_copy(block).start()

    lane = lax.broadcasted_iota(jnp.int32, (SUBLANES, LANES), 1)

    @pl.loop(0, predicted.shape[1] // LANES)
    def _(block):
        base = block * LANES
        found = jnp.zeros((SUBLANES, LANES), jnp.float32)
        for i in range(LANES):
            at = pl.ds(pl.multiple_of(offset_of[base + i], LANES), LANES)
            value = levels[STEPS][row_of[base + i], :, at]
            found = jnp.where(lane == i, pltpu.roll(value, shift_of[base + i], 1), found)
        predicted[:, block_at(block)] = found

    @pl.loop(0, blocks)
    def _(block):
        out_copy(block).wait()


def scratch(columns, *more):
    return (
        [pltpu.VMEM((ROWS + 2 * HALO, SUBLANES, columns), jnp.float32)] * (STEPS + 1)
        + [
            pltpu.VMEM((GROUP, SUBLANES, columns), jnp.float32),
            pltpu.VMEM((4, ROWS + 2 * HALO, 1, columns), jnp.float32),
        ]
        + list(more)
    )


def kernel_call(body, name, outs, specs, out_specs, scratches, cost, operands, limit=VMEM_LIMIT):
    return pl.pallas_call(
        body,
        out_shape=tuple(jax.ShapeDtypeStruct(shape, jnp.float32) for shape in outs),
        in_specs=specs,
        out_specs=out_specs,
        scratch_shapes=scratches,
        compiler_params=pltpu.CompilerParams(vmem_limit_bytes=limit),
        cost_estimate=pl.CostEstimate(flops=0, bytes_accessed=cost * 3600000, transcendentals=0),
        name=name,
    )(*operands)


def row_groups(tracer):
    members, rows, columns = tracer.shape
    if members != SUBLANES or rows != ROWS:
        raise ValueError("block shape")
    blocks = columns // LANES
    return kernel_call(
        functools.partial(to_rows_kernel, blocks), "to_rows",
        [(GROUP, members, columns)] * 4, [ANYWHERE], (IN_VMEM,) * 4,
        [
            pltpu.VMEM((blocks, members * rows, LANES), jnp.float32),
            pltpu.SemaphoreType.DMA((blocks,)),
        ],
        3, [tracer.reshape(members * rows, columns)], TALL_LIMIT,
    )


def transport(shape, own, own_coef, halo_coef, params, obs_index, halos):
    members, rows, columns = shape
    blocks = columns // LANES
    group = (GROUP, members, columns)
    flat = (members * rows, columns)
    dma = pltpu.SemaphoreType.DMA
    staged = pltpu.VMEM((blocks, members * rows, LANES), jnp.float32)
    low0, high0 = halos(own[3], own[0])
    inner = kernel_call(
        functools.partial(interior_kernel, blocks), "interior",
        [group] * 5, [ANYWHERE] * 5 + [IN_VMEM], (ANYWHERE,) * 5,
        scratch(columns, dma((10,))), 8, [*own, own_coef, params],
    )
    upper, lower, low0, high0, *_ = lax.optimization_barrier(
        (own[2], own[1], low0, high0, inner[0])
    )
    low1, high1 = halos(upper, lower)
    first = kernel_call(
        functools.partial(middle_kernel, blocks), "edge_first",
        [group] * 8, [ANYWHERE] * 11 + [IN_VMEM], (ANYWHERE,) * 8,
        scratch(columns, dma((20,))), 10,
        [low0, own[0], own[3], high0, *inner, own_coef, halo_coef, params],
    )
    row_of = obs_index // columns + HALO
    lane_of = obs_index % LANES
    offset_of = obs_index % columns - lane_of
    shift_of = (jnp.arange(obs_index.shape[0], dtype=jnp.int32) - lane_of) % LANES
    field, predicted = kernel_call(
        functools.partial(last_kernel, blocks), "edge_last",
        [flat, (members, obs_index.shape[0])],
        [ANYWHERE] * 14 + [IN_VMEM] + [IN_SMEM] * 3, (ANYWHERE, IN_VMEM),
        scratch(columns, staged, dma((15,)), dma((blocks,))), 15,
        [low1, low0, high0, high1, *first, own_coef, halo_coef, params, row_of, offset_of, shift_of],
    )
    return field.reshape(shape), predicted


def products_kernel(total_obs, per_group, spread, everyone, own, values, variance, same, out):
    weight = 1.0 / (variance[...] * total_obs)
    innovation = (values[...] - own[...]) * weight
    predicted = everyone[...]
    anomalies = (predicted - hdot(same[...], predicted) / per_group) * spread
    right = jnp.concatenate([anomalies * weight, innovation], axis=0)
    out[...] = lax.dot_general(
        anomalies,
        right,
        (((1,), (1,)), ((), ())),
        precision=lax.Precision.HIGHEST,
        preferred_element_type=jnp.float32,
    )


def update_kernel(per_group, summands, same, own_same, rank_row, rank_col, anomalies, own, out):
    members = same.shape[0]
    total = summands[0]
    for index in range(1, summands.shape[0]):
        total = total + summands[index]
    together = same[...]
    row = lax.broadcasted_iota(jnp.int32, (members, members), 0)
    col = lax.broadcasted_iota(jnp.int32, (members, members), 1)
    system = jnp.where(row == col, 1.0, 0.0) + together * total[:, 0:members]
    right = own_same[...] * total[:, members:]
    for pivot in range(per_group):
        pick = jnp.where(rank_row[...] == pivot, together, 0.0)
        pivot_system = hdot(pick, system)
        pivot_right = hdot(pick, right)
        pivot_value = jnp.sum(pick * pivot_system, axis=1, keepdims=True)
        factor = jnp.sum(pick * system, axis=1, keepdims=True)
        is_pivot = rank_col[...] == pivot
        scale = 1.0 / pivot_value
        scaled_system, scaled_right = pivot_system * scale, pivot_right * scale
        system = jnp.where(is_pivot, scaled_system, system - factor * scaled_system)
        right = jnp.where(is_pivot, scaled_right, right - factor * scaled_right)
    change = lax.dot_general(
        right,
        anomalies[...],
        (((0,), (0,)), ((), ())),
        precision=lax.Precision.HIGHEST,
        preferred_element_type=jnp.float32,
    )
    out[...] = own[...] + change


def local(tracer, coefficients, parameters, obs_index, obs_values, obs_variance, member_group):
    local_members, rows, columns = tracer.shape
    ens_pos = lax.axis_index("ens")
    ens_count = lax.axis_size("ens")
    slab_count = lax.axis_size("slab")
    if ens_count != coefficients.shape[0] or slab_count & (slab_count - 1):
        raise ValueError("mesh shape")
    forward = [(i, i + 1) for i in range(slab_count - 1)]
    backward = [(target, source) for source, target in forward]

    own_array = lax.dynamic_slice_in_dim(coefficients, ens_pos, 1, 0)[0]
    coef_low = lax.ppermute(own_array[rows - HALO :], "slab", forward)
    coef_high = lax.ppermute(own_array[:HALO], "slab", backward)
    own = row_groups(tracer)
    coef_low, coef_high, _ = lax.optimization_barrier((coef_low, coef_high, own[0]))
    shared = jnp.concatenate([coef_low, coef_high, parameters], axis=0)
    gathered = lax.all_gather(shared, "ens", axis=0, tiled=False)

    def halos(upper, lower):
        return lax.ppermute(upper, "slab", forward), lax.ppermute(lower, "slab", backward)

    members = member_group.shape[0]
    per_group = members // GROUPS
    spread = 1.0 / math.sqrt(per_group - 1)
    same_bool = member_group[:, None] == member_group[None, :]
    same = same_bool.astype(jnp.float32)
    earlier = jnp.arange(members)[None, :] < jnp.arange(members)[:, None]
    rank = jnp.sum((same_bool & earlier).astype(jnp.int32), axis=1)
    own_same = lax.dynamic_slice_in_dim(same, ens_pos * local_members, local_members, 1)
    all_params = gathered[:, 2 * HALO :, :].reshape(members, columns)
    param_anomalies = (all_params - hdot(same, all_params) / per_group) * spread

    field, predicted = transport(
        tracer.shape, own, coefficients, gathered, parameters, obs_index, halos
    )
    everyone = lax.all_gather(predicted, "ens", axis=0, tiled=True)
    total_obs = obs_variance.shape[0] * slab_count
    products = pl.pallas_call(
        functools.partial(products_kernel, float(total_obs), per_group, spread),
        out_shape=jax.ShapeDtypeStruct((members, members + local_members), jnp.float32),
        compiler_params=pltpu.CompilerParams(vmem_limit_bytes=VMEM_LIMIT),
        name="products",
    )(everyone, predicted, obs_values, obs_variance[None, :], same)
    distance = 1
    while distance < slab_count:
        pairs = [(i, i ^ distance) for i in range(slab_count)]
        products = products + lax.ppermute(products, "slab", pairs)
        distance *= 2
    updated = pl.pallas_call(
        functools.partial(update_kernel, per_group),
        out_shape=jax.ShapeDtypeStruct(parameters.shape, jnp.float32),
        compiler_params=pltpu.CompilerParams(vmem_limit_bytes=VMEM_LIMIT),
        name="update",
    )(products[None], same, own_same, rank[None, :], rank[:, None], param_anomalies, parameters)
    return (field, updated)


def solution(mesh):
    in_specs = (
        P("ens", "slab", None),
        P(None, "slab", None),
        P("ens", None),
        P("slab"),
        P("ens", "slab"),
        P("slab"),
        P(),
    )
    out_specs = (P("ens", "slab", None), P("ens", None))
    return jax.shard_map(local, mesh=mesh, in_specs=in_specs, out_specs=out_specs, check_vma=False)
```

time: 151 us -> 132 us (0.87)
  waiting for transfers between devices: 22.9 us -> 9.52 us
  Pallas kernels: 62.7 us -> 55 us
  local copies, waits for them, and re-layouts: 12.6 us -> 18.6 us
  other arithmetic: 3.77 us -> 1.07 us
    unnamed x32 -> x56, local copies, waits for them, and re-layouts: 8.27 us -> 17.5 us
    pallas_call x4, Pallas kernels: 60 us -> 52.2 us  [kernel_call(): pl.pallas_call(body, out_shape=tuple((jax.ShapeDtypeStruct(shape, jnp.flo...]
    ppermute x4, waiting for transfers between devices: 8.99 us -> 2.97 us  [the longest x2 2.97 us: halos(): lax.ppermute(upper, 'slab', forward)]
    all_gather x1, waiting for transfers between devices: 5.14 us -> 0.02 us  [local(): gathered = lax.all_gather(shared, 'ens', axis=0, tiled=False)]
    broadcast_in_dim x2 -> x0, local copies, waits for them, and re-layouts: 3.21 us -> none  [the longest x1 2.13 us: local(): halo_coef = (gathered[:, :2 * HALO] * halving)[:, :, None, :]]
    ppermute x1, waiting for transfers between devices: 4.3 us -> 2.14 us  [local(): coef_high = lax.ppermute(own_array[:HALO], 'slab', backward)]
    mul x1 -> x0, other arithmetic: 1.8 us -> none  [local(): halo_coef = (gathered[:, :2 * HALO] * halving)[:, :, None, :]]
  transfers between devices with their start and end apart: 10 -> 10, of which waited for: 7 -> 5; matrix products, arithmetic and copies ran while one was open for 5% -> 1% of each run, Pallas kernels for 22% -> 22%
where the time goes in v2:
time: 132 us
  Pallas kernels  55 us (42%)
  starting transfers between devices  26.9 us (20%)
  local copies, waits for them, and re-layouts  18.6 us (14%)
  between operations  14.3 us (11%)
  waiting for transfers between devices  9.52 us (7%)
  blocking collectives  5.79 us (4%)
    pallas_call x4, Pallas kernels, kernel_call(): pl.pallas_call(body, out_shape=tuple((jax.ShapeDtypeStruct(shape, jnp.flo...  52.2 us
    unnamed x56, local copies, waits for them, and re-layouts  17.5 us
    ppermute x2, starting transfers between devices, halos(): lax.ppermute(upper, 'slab', forward)  9.45 us
    ppermute x3, starting transfers between devices, local(): products = products + lax.ppermute(products, 'slab', pairs)  8.48 us
    all_gather x1, blocking collectives, local(): everyone = lax.all_gather(predicted, 'ens', axis=0, tiled=True)  5.79 us
    ppermute x1, starting transfers between devices, local(): coef_low = lax.ppermute(own_array[rows - HALO:], 'slab', forward)  4.85 us
    ppermute x3, waiting for transfers between devices, local(): products = products + lax.ppermute(products, 'slab', pairs)  4.37 us
    ppermute x2, waiting for transfers between devices, halos(): lax.ppermute(upper, 'slab', forward)  2.97 us
  transfers between devices with their start and end apart: 10, of which 5 were waited for; matrix products, arithmetic and copies ran while one was open for 1% of the time, Pallas kernels for 22%

profile of v2, /device:TPU:0, one launch (start us, length us, event | category | flops | bytes accessed | tf_op | source)
XLA Modules:
  0.0 131.6 jit_solution(6822807989321520757)
XLA Ops:
  7.2 0.0 all-gather.3.cloned.1.call-start
  7.2 1.0 dynamic-slice_bitcast_fusion
  8.2 4.8 %collective-permute-start.4 = (f32[8,4096]{1,0:T(8,128)S(1)}, f32[8,4096]{1,0:T(8,128)S(1)}, u32[]{:S(2)}, u32[]{:S(2)}) collective-permute-start(f32[8,4096]{1,0:T(8,128)S(1)} %get-tuple-element.53), channel_id=1, source_target_pairs={{0,1},{1,2},{2,3},{3,4},{4,5},{5,6},{6,7},{8,9},{9,10},{10,11},{11... | collective-permute-start | bytes 393224 | tf_op jit(solution)/shard_map/ppermute | solution.py:393
  13.1 1.3 collective-permute-start.5
  14.4 0.0 copy-start
  14.4 3.4 %to_rows.1 = (f32[4,8,4096]{2,1,0:T(8,128)}, f32[4,8,4096]{2,1,0:T(8,128)}, f32[4,8,4096]{2,1,0:T(8,128)}, f32[4,8,4096]{2,1,0:T(8,128)}) custom-call(f32[128,4096]{1,0:T(8,128)} %bitcast.24), custom_call_target="tpu_custom_call" | custom-call | bytes 10800000 | tf_op jit(solution)/shard_map/to_rows/pallas_call | solution.py:271
  17.8 0.0 collective-permute-done.4
  17.8 2.1 %collective-permute-done.5 = f32[8,4096]{1,0:T(8,128)S(1)} collective-permute-done((f32[8,4096]{1,0:T(8,128)S(1)}, f32[8,4096]{1,0:T(8,128)S(1)}, u32[]{:S(2)}, u32[]{:S(2)}) %collective-permute-start.5) | collective-permute-done | bytes 131104 | tf_op jit(solution)/shard_map/ppermute | solution.py:394
  19.9 0.8 pad_maximum_fusion
  20.7 0.0 all-gather.3.cloned.1.call-update
  20.8 4.4 %collective-permute-start = (f32[4,8,4096]{2,1,0:T(8,128)}, f32[4,8,4096]{2,1,0:T(8,128)S(1)}, u32[]{:S(2)}, u32[]{:S(2)}) collective-permute-start(f32[4,8,4096]{2,1,0:T(8,128)} %get-tuple-element.29.own3.refs_2_), channel_id=1, source_target_pairs={{0,1},{1,2},{2,3},{3,4},{4,5},{5,6},{6,7},{8,9},{9,10},{10,11},{11... | collective-permute-start | bytes 1572872 | tf_op jit(solution)/shard_map/ppermute | solution.py:401
  25.1 1.3 collective-permute-start.1
  26.4 0.0 copy-start.4
  26.5 1.0 copy-done.4
  27.5 1.1 copy-done.6
  28.6 10.8 %interior.1 = (f32[4,8,4096]{2,1,0:T(8,128)S(1)}, f32[4,8,4096]{2,1,0:T(8,128)S(1)}, f32[4,8,4096]{2,1,0:T(8,128)S(1)}, f32[4,8,4096]{2,1,0:T(8,128)S(1)}, f32[4,8,4096]{2,1,0:T(8,128)S(1)}) custom-call(f32[4,8,4096]{2,1,0:T(8,128)S(1)} %copy-done.4, f32[4,8,4096]{2,1,0:T(8,128)} %get-tuple-element.35.own1, f32[4,8,4096]{2,1,0:T(8,128)} %get-tuple-element.32.own2, ...), custom_call_target="tpu_custom_call" | custom-call | bytes 28800000 | tf_op jit(solution)/shard_map/interior/pallas_call | solution.py:271
  39.4 0.0 copy-start.14
  39.4 0.8 copy-done.14
  40.2 0.8 copy-done.16
  41.0 0.8 copy-done.18
  41.8 0.8 copy-done.20
  42.6 0.8 copy-done.22
  43.4 3.0 %collective-permute-done.refs_0_.refs_1_ = f32[4,8,4096]{2,1,0:T(8,128)S(1)} collective-permute-done((f32[4,8,4096]{2,1,0:T(8,128)}, f32[4,8,4096]{2,1,0:T(8,128)S(1)}, u32[]{:S(2)}, u32[]{:S(2)}) %collective-permute-start) | collective-permute-done | bytes 524320 | tf_op jit(solution)/shard_map/ppermute | solution.py:401
  46.4 0.8 copy-done.8
  47.2 0.0 collective-permute-done.1.refs_3_.refs_2_
  47.2 0.8 copy-done.11
  48.0 5.1 %collective-permute-start.2 = (f32[4,8,4096]{2,1,0:T(8,128)}, f32[4,8,4096]{2,1,0:T(8,128)}, u32[]{:S(2)}, u32[]{:S(2)}) collective-permute-start(f32[4,8,4096]{2,1,0:T(8,128)} %get-tuple-element.32.own2), channel_id=1, source_target_pairs={{0,1},{1,2},{2,3},{3,4},{4,5},{5,6},{6,7},{8,9},{9,10},{10,11},{11... | collective-permute-start | bytes 1572872 | tf_op jit(solution)/shard_map/ppermute | solution.py:401
  53.1 1.5 %collective-permute-start.3 = (f32[4,8,4096]{2,1,0:T(8,128)}, f32[4,8,4096]{2,1,0:T(8,128)}, u32[]{:S(2)}, u32[]{:S(2)}) collective-permute-start(f32[4,8,4096]{2,1,0:T(8,128)} %get-tuple-element.35.own1), channel_id=1, source_target_pairs={{1,0},{2,1},{3,2},{4,3},{5,4},{6,5},{7,6},{9,8},{10,9},{11,10},{12... | collective-permute-start | bytes 1572872 | tf_op jit(solution)/shard_map/ppermute | solution.py:401
  54.5 0.1 compare_convert_fusion.same
  54.6 0.0 all-gather.3.cloned.1.call-done
  54.7 0.0 copy-done.5
  54.7 0.0 copy-start.1
  54.7 1.4 %copy-done.1 = f32[96,4096]{1,0:T(8,128)S(1)} copy-done((f32[96,4096]{1,0:T(8,128)S(1)}, f32[96,4096]{1,0:T(8,128)}, u32[]{:S(2)}) %copy-start.1) | copy-done | bytes 1572888
  56.1 1.0 copy-done.7
  57.1 1.0 copy-done.9
  58.2 1.0 copy-done.12
  59.2 1.0 copy-done.15
  60.3 1.0 copy-done.17
  61.3 1.0 copy-done.19
  62.3 1.0 copy-done.21
  63.4 1.0 copy-done.23
  64.4 14.6 %edge_first.1 = (f32[4,8,4096]{2,1,0:T(8,128)S(1)}, f32[4,8,4096]{2,1,0:T(8,128)S(1)}, f32[4,8,4096]{2,1,0:T(8,128)S(1)}, f32[4,8,4096]{2,1,0:T(8,128)S(1)}, f32...) custom-call(f32[4,8,4096]{2,1,0:T(8,128)S(1)} %copy-done.9, ...), custom_call_target="tpu_custom_call" | custom-call | bytes 36000000 | tf_op jit(solution)/shard_map/edge_first/pallas_call | solution.py:271
  79.1 0.0 collective-permute-done.2.refs_0_
  79.1 0.0 collective-permute-done.3.refs_3_
  79.1 0.0 copy-done.2
  79.1 0.0 copy-done.10
  79.1 0.0 copy-done.13
  79.1 0.0 copy-start.24
  79.1 0.0 copy-start.25
  79.2 23.4 %edge_last.1 = (f32[128,4096]{1,0:T(8,128)}, f32[8,2048]{1,0:T(8,128)S(1)}) custom-call(f32[4,8,4096]{2,1,0:T(8,128)} %collective-permute-done.2.refs_0_, f32[4,8,4096]{2,1,0:T(8,128)S(1)} %copy-done.10, f32[4,8,4096]{2,1,0:T(8,128)S(1)} %copy-done.13, f32[4,8,4096]{2,1,0:T(8,128)} %collective-permute-done.3.refs_3_, ...), custom_call_target="tpu_custom_call" | custom-call | bytes 54000000 | tf_op jit(solution)/shard_map/edge_last/pallas_call | solution.py:271
  102.5 5.8 %all_gather.11.everyone = f32[32,2048]{1,0:T(8,128)S(1)} all-gather(f32[8,2048]{1,0:T(8,128)S(1)} %get-tuple-element.51.own), channel_id=1, replica_groups=mesh['ens'=4,'slab'=8] {'ens'}, dimensions={0}, use_global_device_ids=true | all-gather | bytes 327680 | tf_op jit(solution)/shard_map/all_gather | solution.py:417
  108.3 0.0 copy-done.24
  108.3 0.6 products.1
  109.0 2.7 %collective-permute-start.6 = (f32[32,40]{1,0:T(8,128)S(1)}, f32[32,40]{1,0:T(8,128)S(1)}, u32[]{:S(2)}, u32[]{:S(2)}) collective-permute-start(f32[32,40]{1,0:T(8,128)S(1)} %products.1), channel_id=1, source_target_pairs={{0,1},{1,0},{2,3},{3,2},{4,5},{5,4},{6,7},{7,6},{8,9},{9,8},{10,11... | collective-permute-start | bytes 15368 | tf_op jit(solution)/shard_map/ppermute | solution.py:428
  111.7 0.2 convert_reduce_fusion
  111.8 1.5 %collective-permute-done.6 = f32[32,40]{1,0:T(8,128)S(1)} collective-permute-done((f32[32,40]{1,0:T(8,128)S(1)}, f32[32,40]{1,0:T(8,128)S(1)}, u32[]{:S(2)}, u32[]{:S(2)}) %collective-permute-start.6) | collective-permute-done | bytes 5152 | tf_op jit(solution)/shard_map/ppermute | solution.py:428
  113.4 2.8 %collective-permute-start.7 = (f32[32,40]{1,0:T(8,128)S(1)}, f32[32,40]{1,0:T(8,128)S(1)}, u32[]{:S(2)}, u32[]{:S(2)}) collective-permute-start(f32[32,40]{1,0:T(8,128)S(1)} %add.42), channel_id=1, source_target_pairs={{0,2},{1,3},{2,0},{3,1},{4,6},{5,7},{6,4},{7,5},{8,10},{9,11},{10,... | collective-permute-start | bytes 15368 | tf_op jit(solution)/shard_map/ppermute | solution.py:428
  116.1 0.1 constant_dynamic-slice_fusion.own_same
  116.2 0.1 copy.9.rank_col
  116.3 1.6 %collective-permute-done.7 = f32[32,40]{1,0:T(8,128)S(1)} collective-permute-done((f32[32,40]{1,0:T(8,128)S(1)}, f32[32,40]{1,0:T(8,128)S(1)}, u32[]{:S(2)}, u32[]{:S(2)}) %collective-permute-start.7) | collective-permute-done | bytes 5152 | tf_op jit(solution)/shard_map/ppermute | solution.py:428
  117.8 3.0 %collective-permute-start.8 = (f32[32,40]{1,0:T(8,128)S(1)}, f32[32,40]{1,0:T(8,128)S(1)}, u32[]{:S(2)}, u32[]{:S(2)}) collective-permute-start(f32[32,40]{1,0:T(8,128)S(1)} %add.43), channel_id=1, source_target_pairs={{0,4},{1,5},{2,6},{3,7},{4,0},{5,1},{6,2},{7,3},{8,12},{9,13},{10,... | collective-permute-start | bytes 15368 | tf_op jit(solution)/shard_map/ppermute | solution.py:428
  120.9 0.4 fusion.1.anomalies
  121.3 1.3 collective-permute-done.8
  122.6 2.1 %update.1 = f32[8,4096]{1,0:T(8,128)} custom-call(f32[1,32,40]{2,1,0:T(8,128)S(1)} %add_bitcast_fusion.summands, f32[32,32]{1,0:T(8,128)S(1)} %compare_convert_fusion.same, f32[32,8]{1,0:T(8,128)S(1)} %constant_dynamic-slice_fusion.own_same, s32[1,32]{1,0:T(1,128)S(1)} %bitcast.23, s32[32,1]{1,0:T(8,128)S(1)} %copy.9.rank_col, ...), custom_call_target="tpu_custom_call" | custom-call | tf_op jit(solution)/shard_map/update/pallas_call | solution.py:430
  (31 shorter events, 0.1 us)
Async XLA Ops:
  7.2 12.8 %copy-start.3 = (f32[8,4096]{1,0:T(8,128)S(1)}, f32[8,4096]{1,0:T(8,128)}, u32[]{:S(2)}) copy-start(f32[8,4096]{1,0:T(8,128)} %own.1) | copy-start | bytes 393220
  7.2 47.5 %all-gather.3.cloned.1.call-start = ((), (), s32[]{:S(2)}) async-start(), calls=%async_computation | async-start | bytes 1966080 | tf_op jit(solution)/shard_map/all_gather | solution.py:398
  8.2 9.6 %collective-permute-start.4 = (f32[8,4096]{1,0:T(8,128)S(1)}, f32[8,4096]{1,0:T(8,128)S(1)}, u32[]{:S(2)}, u32[]{:S(2)}) collective-permute-start(f32[8,4096]{1,0:T(8,128)S(1)} %get-tuple-element.53), channel_id=1, source_target_pairs={{0,1},{1,2},{2,3},{3,4},{4,5},{5,6},{6,7},{8,9},{9,10},{10,11},{11... | collective-permute-start | bytes 393224 | tf_op jit(solution)/shard_map/ppermute | solution.py:393
  13.1 6.9 %collective-permute-start.5 = (f32[8,4096]{1,0:T(8,128)S(1)}, f32[8,4096]{1,0:T(8,128)S(1)}, u32[]{:S(2)}, u32[]{:S(2)}) collective-permute-start(f32[8,4096]{1,0:T(8,128)S(1)} %get-tuple-element.52), channel_id=1, source_target_pairs={{1,0},{2,1},{3,2},{4,3},{5,4},{6,5},{7,6},{9,8},{10,9},{11,10},{12... | collective-permute-start | bytes 393224 | tf_op jit(solution)/shard_map/ppermute | solution.py:394
  14.4 12.1 %copy-start = (f32[4,16,4096]{2,1,0:T(8,128)S(1)}, f32[4,16,4096]{2,1,0:T(8,128)}, u32[]{:S(2)}) copy-start(f32[4,16,4096]{2,1,0:T(8,128)} %refs_12_.1) | copy-start | bytes 3145732
  20.8 25.6 %collective-permute-start = (f32[4,8,4096]{2,1,0:T(8,128)}, f32[4,8,4096]{2,1,0:T(8,128)S(1)}, u32[]{:S(2)}, u32[]{:S(2)}) collective-permute-start(f32[4,8,4096]{2,1,0:T(8,128)} %get-tuple-element.29.own3.refs_2_), channel_id=1, source_target_pairs={{0,1},{1,2},{2,3},{3,4},{4,5},{5,6},{6,7},{8,9},{9,10},{10,11},{11... | collective-permute-start | bytes 1572872 | tf_op jit(solution)/shard_map/ppermute | solution.py:401
  25.1 22.1 %collective-permute-start.1 = (f32[4,8,4096]{2,1,0:T(8,128)}, f32[4,8,4096]{2,1,0:T(8,128)S(1)}, u32[]{:S(2)}, u32[]{:S(2)}) collective-permute-start(f32[4,8,4096]{2,1,0:T(8,128)} %get-tuple-element.30.own0.refs_1_), channel_id=1, source_target_pairs={{1,0},{2,1},{3,2},{4,3},{5,4},{6,5},{7,6},{9,8},{10,9},{11,10},{12... | collective-permute-start | bytes 1572872 | tf_op jit(solution)/shard_map/ppermute | solution.py:401
  26.4 1.0 copy-start.4
  27.5 1.1 copy-start.6
  28.6 26.0 %copy-start.26 = (s32[32]{0:T(128)S(1)}, s32[32]{0:T(128)}, u32[]{:S(2)}) copy-start(s32[32]{0:T(128)} %param.13) | copy-start | bytes 388
  28.6 26.1 %copy-start.27 = (s32[2048]{0:T(1024)S(1)}, s32[2048]{0:T(1024)}, u32[]{:S(2)}) copy-start(s32[2048]{0:T(1024)} %param.10) | copy-start | bytes 24580
  28.6 26.1 %copy-start.5 = (f32[4,8,4096]{2,1,0:T(8,128)S(1)}, f32[4,8,4096]{2,1,0:T(8,128)}, u32[]{:S(2)}) copy-start(f32[4,8,4096]{2,1,0:T(8,128)} %get-tuple-element.30.own0.refs_1_) | copy-start | bytes 1572868
  39.4 0.8 copy-start.14
  40.2 0.8 copy-start.16
  41.0 0.8 copy-start.18
  41.8 0.8 copy-start.20
  42.6 0.8 copy-start.22
  46.4 0.8 copy-start.8
  47.2 0.8 copy-start.11
  48.0 31.1 %collective-permute-start.2 = (f32[4,8,4096]{2,1,0:T(8,128)}, f32[4,8,4096]{2,1,0:T(8,128)}, u32[]{:S(2)}, u32[]{:S(2)}) collective-permute-start(f32[4,8,4096]{2,1,0:T(8,128)} %get-tuple-element.32.own2), channel_id=1, source_target_pairs={{0,1},{1,2},{2,3},{3,4},{4,5},{5,6},{6,7},{8,9},{9,10},{10,11},{11... | collective-permute-start | bytes 1572872 | tf_op jit(solution)/shard_map/ppermute | solution.py:401
  53.1 26.0 %collective-permute-start.3 = (f32[4,8,4096]{2,1,0:T(8,128)}, f32[4,8,4096]{2,1,0:T(8,128)}, u32[]{:S(2)}, u32[]{:S(2)}) collective-permute-start(f32[4,8,4096]{2,1,0:T(8,128)} %get-tuple-element.35.own1), channel_id=1, source_target_pairs={{1,0},{2,1},{3,2},{4,3},{5,4},{6,5},{7,6},{9,8},{10,9},{11,10},{12... | collective-permute-start | bytes 1572872 | tf_op jit(solution)/shard_map/ppermute | solution.py:401
  54.7 1.4 %copy-start.1 = (f32[96,4096]{1,0:T(8,128)S(1)}, f32[96,4096]{1,0:T(8,128)}, u32[]{:S(2)}) copy-start(f32[96,4096]{1,0:T(8,128)} %all-gather.3.cloned.1.call-done) | copy-start | bytes 4718596
  56.1 1.0 copy-start.7
  57.1 1.0 copy-start.9
  58.2 1.0 copy-start.12
  59.2 1.0 copy-start.15
  60.3 1.0 copy-start.17
  61.3 1.0 copy-start.19
  62.3 1.0 copy-start.21
  63.4 1.0 copy-start.23
  64.4 14.7 %copy-start.2 = (f32[96,4096]{1,0:T(8,128)S(1)}, f32[96,4096]{1,0:T(8,128)}, u32[]{:S(2)}) copy-start(f32[96,4096]{1,0:T(8,128)} %all-gather.3.cloned.1.call-done) | copy-start | bytes 4718596
  64.4 14.7 %copy-start.10 = (f32[4,8,4096]{2,1,0:T(8,128)S(1)}, f32[4,8,4096]{2,1,0:T(8,128)}, u32[]{:S(2)}) copy-start(f32[4,8,4096]{2,1,0:T(8,128)} %copy-done.8) | copy-start | bytes 1572868
  64.4 14.7 %copy-start.13 = (f32[4,8,4096]{2,1,0:T(8,128)S(1)}, f32[4,8,4096]{2,1,0:T(8,128)}, u32[]{:S(2)}) copy-start(f32[4,8,4096]{2,1,0:T(8,128)} %copy-done.11) | copy-start | bytes 1572868
  79.1 29.2 %copy-start.24 = (f32[8,2048]{1,0:T(8,128)S(1)}, f32[8,2048]{1,0:T(8,128)}, u32[]{:S(2)}) copy-start(f32[8,2048]{1,0:T(8,128)} %values.1) | copy-start | bytes 196612
  79.1 29.2 %copy-start.25 = (f32[2048]{0:T(1024)S(1)}, f32[2048]{0:T(1024)}, u32[]{:S(2)}) copy-start(f32[2048]{0:T(1024)} %param.12) | copy-start | bytes 24580
  109.0 4.4 %collective-permute-start.6 = (f32[32,40]{1,0:T(8,128)S(1)}, f32[32,40]{1,0:T(8,128)S(1)}, u32[]{:S(2)}, u32[]{:S(2)}) collective-permute-start(f32[32,40]{1,0:T(8,128)S(1)} %products.1), channel_id=1, source_target_pairs={{0,1},{1,0},{2,3},{3,2},{4,5},{5,4},{6,7},{7,6},{8,9},{9,8},{10,11... | collective-permute-start | bytes 15368 | tf_op jit(solution)/shard_map/ppermute | solution.py:428
  113.4 4.5 %collective-permute-start.7 = (f32[32,40]{1,0:T(8,128)S(1)}, f32[32,40]{1,0:T(8,128)S(1)}, u32[]{:S(2)}, u32[]{:S(2)}) collective-permute-start(f32[32,40]{1,0:T(8,128)S(1)} %add.42), channel_id=1, source_target_pairs={{0,2},{1,3},{2,0},{3,1},{4,6},{5,7},{6,4},{7,5},{8,10},{9,11},{10,... | collective-permute-start | bytes 15368 | tf_op jit(solution)/shard_map/ppermute | solution.py:428
  117.8 4.8 %collective-permute-start.8 = (f32[32,40]{1,0:T(8,128)S(1)}, f32[32,40]{1,0:T(8,128)S(1)}, u32[]{:S(2)}, u32[]{:S(2)}) collective-permute-start(f32[32,40]{1,0:T(8,128)S(1)} %add.43), channel_id=1, source_target_pairs={{0,4},{1,5},{2,6},{3,7},{4,0},{5,1},{6,2},{7,3},{8,12},{9,13},{10,... | collective-permute-start | bytes 15368 | tf_op jit(solution)/shard_map/ppermute | solution.py:428
Sparse Core Ops, SparseCore 0:
  20.9 20.8 all-gather.2

commit v3 on v2

--- a/solution.py
+++ b/solution.py
@@ -20,7 +20,8 @@
 TOGETHER = 2
 VMEM_LIMIT = 30 * 1024 * 1024
 TALL_LIMIT = 60 * 1024 * 1024
-ANYWHERE = pl.BlockSpec(memory_space=pl.ANY)
+COST_BYTES = 200000
+ANYWHERE = pl.BlockSpec(memory_space=pltpu.HBM)
 IN_VMEM = pl.BlockSpec(memory_space=pltpu.VMEM)
 IN_SMEM = pl.BlockSpec(memory_space=pltpu.SMEM)
 
@@ -44,6 +45,7 @@
 def columns_pass(source, first_row, count, target, target_row, coef, params, blocks):
     lane = lax.broadcasted_iota(jnp.int32, (SUBLANES, LANES), 1)
     first, last = lane == 0, lane == LANES - 1
+    places = [[coef_row(array, first_row + i) for array in range(4)] for i in range(count)]
     c, c_rolled, d, d_rolled, slope, twice, left, right, laplace = ({} for _ in range(9))
     for tick in range(blocks + 2 * LAG + 4):
         for i in range(count):
@@ -72,29 +74,34 @@
             b = tick - 3 - 2 * LAG
             if 0 <= b < blocks:
                 at = block_at(b)
-                speed = wide(coef[1, row, :, at])
+                speed = wide(coef[places[i][1], :, at])
                 forward = jnp.where(first, left[i, b - 1], left[i, b])
                 backward = twice[i, b] - jnp.where(last, right[i, b + 1], right[i, b])
                 change = jnp.where(speed > 0.0, forward, backward) + slope[i, b]
                 value = c[i, b] - (0.5 * speed) * change
-                value = value + wide(coef[2, row, :, at]) * laplace[i, b]
-                value = value + params[:, at] * wide(coef[3, row, :, at])
+                value = value + wide(coef[places[i][2], :, at]) * laplace[i, b]
+                value = value + params[:, at] * wide(coef[places[i][3], :, at])
                 target[target_row + i, :, at] = value
 
 
-def rows_pass(source, row, partial, target, coef, at):
+def rows_pass(source, row, places, partial, target, coef, block, blocks):
+    at = block_at(block)
     c = [source[row - 2 + i, :, at] for i in range(GROUP + 4)]
     d = [c[i + 1] - c[i] for i in range(GROUP + 3)]
     slope = [None] + [limited(d[i - 1], d[i]) for i in range(1, GROUP + 3)]
     twice = [None] + [d[i] + d[i] for i in range(1, GROUP + 2)]
     for i in range(2, GROUP + 2):
         here = row - 2 + i
-        speed = wide(coef[0, here, :, at])
+        speed = wide(coef[places[i - 2][0], :, at])
         forward = twice[i - 1] - slope[i - 1]
         backward = twice[i] - slope[i + 1]
-        change = wide(coef[2, here, :, at]) * (d[i] - d[i - 1])
+        change = wide(coef[places[i - 2][1], :, at]) * (d[i] - d[i - 1])
         change = change - (0.5 * speed) * (jnp.where(speed > 0.0, forward, backward) + slope[i])
-        target[here, :, at] = partial[i - 2, :, at] + change
+        value = partial[i - 2, :, at] + change
+        if target.shape[1:] == value.shape:
+            target[here * blocks + block] = value
+        else:
+            target[here, :, at] = value
 
 
 def advance_group(source, target, row, partial, coef, params, blocks):
@@ -104,10 +111,12 @@
             source, row + i * TOGETHER, TOGETHER, partial, i * TOGETHER, coef, params, blocks
         )
 
+    places = [[coef_row(array, row + i) for array in (0, 2)] for i in range(GROUP)]
+
     @pl.loop(0, blocks // WIDE)
     def _(wide_block):
         for i in range(WIDE):
-            rows_pass(source, row, partial, target, coef, block_at(wide_block * WIDE + i))
+            rows_pass(source, row, places, partial, target, coef, wide_block * WIDE + i, blocks)
 
 
 class Copies:
@@ -117,6 +126,7 @@
     def start(self, source, target):
         copy = pltpu.make_async_copy(source, target, self.sems.at[self.used])
         self.used += 1
+        assert self.used <= self.sems.shape[0]
         copy.start()
         return copy
 
@@ -125,9 +135,13 @@
     return pl.ds(row + HALO, GROUP)
 
 
-def to_rows_kernel(blocks, tracer, *rest):
-    outs, (staged, sems) = rest[: ROWS // GROUP], rest[ROWS // GROUP :]
-
+def region(levels, level, row, blocks):
+    if level == STEPS:
+        return levels[level].at[pl.ds((row + HALO) * blocks, GROUP * blocks)]
+    return levels[level].at[place(row)]
+
+
+def fill_rows(blocks, first_rows, tracer, outs, staged, sems):
     def copy(block):
         return pltpu.make_async_copy(tracer.at[:, block_at(block)], staged.at[block], sems.at[block])
 
@@ -138,20 +152,45 @@
     @pl.loop(0, blocks)
     def _(block):
         copy(block).wait()
-        for row in range(ROWS):
-            outs[row // GROUP][row % GROUP, :, block_at(block)] = staged[
-                block, pl.ds(row, SUBLANES, stride=ROWS), :
-            ]
+        for out, first_row in zip(outs, first_rows):
+            for row in range(GROUP):
+                out[row, :, block_at(block)] = staged[
+                    block, pl.ds(first_row + row, SUBLANES, stride=ROWS), :
+                ]
+
+
+def outer_rows_kernel(blocks, tracer, own_coef, place_of, up, down, staged, sems, coef_sems):
+    copies = Copies(coef_sems)
+    upper = lax.rem(place_of[0], 2) * 2
+    waits = []
+    for array in range(4):
+        at = pl.ds(2 * array, 2)
+        waits.append(copies.start(own_coef.at[array, pl.ds(ROWS - 2, 2)], up.at[GROUP, at]))
+        waits.append(copies.start(own_coef.at[array, pl.ds(0, 2)], down.at[GROUP, at]))
+    for array in range(2):
+        at = pl.ds(4 * array, 4)
+        source = own_coef.at[upper + array]
+        waits.append(copies.start(source.at[pl.ds(ROWS - 6, 4)], up.at[GROUP + 1, at]))
+        waits.append(copies.start(source.at[pl.ds(2, 4)], down.at[GROUP + 1, at]))
+    fill_rows(blocks, (0, ROWS - GROUP), tracer, (down, up), staged, sems)
+    for copy in waits:
+        copy.wait()
+
+
+def inner_rows_kernel(blocks, tracer, outer, low, high, staged, sems):
+    fill_rows(blocks, (GROUP, ROWS - 2 * GROUP), tracer, (low, high), staged, sems)
 
 
 def interior_kernel(blocks, own0, own1, own2, own3, own_coef, params, *rest):
     outs, (*levels, partial, coef, sems) = rest[:5], rest[5:]
     copies = Copies(sems)
     waits = [
-        copies.start(own, levels[0].at[place(GROUP * i)])
+        copies.start(own.at[0:GROUP], levels[0].at[place(GROUP * i)])
         for i, own in enumerate((own0, own1, own2, own3))
     ]
-    waits.append(copies.start(own_coef, coef.at[:, HALO : HALO + ROWS, 0]))
+    waits += [
+        copies.start(own_coef.at[array], coef.at[pl.ds(array * ROWS, ROWS), 0]) for array in range(4)
+    ]
     for copy in waits:
         copy.wait()
     for level, start, count in ((0, 2, 3), (1, 4, 2), (2, 6, 1)):
@@ -182,29 +221,54 @@
         ready(level, low, high)
 
 
-def load_coef(copies, own_coef, gathered, coef):
-    return [
-        copies.start(own_coef, coef.at[:, HALO : HALO + ROWS, 0]),
-        copies.start(gathered.at[:, 0:HALO], coef.at[:, 0:HALO, 0]),
-        copies.start(gathered.at[:, HALO : 2 * HALO], coef.at[:, HALO + ROWS :, 0]),
+def coef_row(array, row):
+    own = array * ROWS + row - HALO
+    near_low = 4 * ROWS + 2 * array + row - (HALO - 2)
+    near_high = 4 * ROWS + 8 + 2 * array + row - (HALO + ROWS)
+    far_low = 4 * ROWS + 16 + 4 * array + row - (HALO - 6)
+    far_high = 4 * ROWS + 32 + 4 * array + row - (HALO + ROWS + 2)
+    low = jnp.where(row < HALO - 2, far_low, near_low)
+    high = jnp.where(row < HALO + ROWS + 2, near_high, far_high)
+    return jnp.where(row < HALO, low, jnp.where(row < HALO + ROWS, own, high))
+
+
+def load_coef(copies, own_coef, low, high, coef):
+    waits = [
+        copies.start(own_coef.at[array], coef.at[pl.ds(array * ROWS, ROWS), 0]) for array in range(4)
     ]
+    for side, source in enumerate((low, high)):
+        waits.append(copies.start(source.at[GROUP], coef.at[pl.ds(4 * ROWS + 8 * side, 8), 0]))
+    return waits
+
+
+def load_outer_coef(copies, mine, theirs, place_of, coef):
+    waits = []
+    own_half = lax.rem(place_of[0], 2)
+    for source, half in ((mine, own_half), (theirs, 1 - own_half)):
+        for side in range(2):
+            first = 4 * ROWS + 16 + 16 * side + 8 * half
+            waits.append(copies.start(source.at[side], coef.at[pl.ds(first, 8), 0]))
+    return waits
 
 
 def middle_kernel(blocks, *refs):
     sources, refs = refs[:9], refs[9:]
-    own_coef, gathered, params = refs[:3]
-    outs, (*levels, partial, coef, sems) = refs[3:11], refs[11:]
+    own_coef, params = refs[:2]
+    outs, (*levels, partial, coef, sems) = refs[2:10], refs[10:]
     copies = Copies(sems)
     places = ((0, -4), (0, 0), (0, 12), (0, 16), (1, 2), (1, 10), (2, 4), (2, 8), (3, 6))
     waits = [[] for _ in range(STEPS)]
     for source, (level, row) in zip(sources, places):
-        waits[level].append(copies.start(source, levels[level].at[place(row)]))
-    waits[0] += load_coef(copies, own_coef, gathered, coef)
+        count = GROUP * blocks if level == STEPS else GROUP
+        waits[level].append(
+            copies.start(source.at[0:count], region(levels, level, row, blocks))
+        )
+    waits[0] += load_coef(copies, own_coef, sources[0], sources[3], coef)
     sends = []
 
     def ready(level, low, high):
         for row, out in ((low, outs[2 * level]), (high, outs[2 * level + 1])):
-            sends.append(copies.start(levels[level + 1].at[place(row)], out))
+            sends.append(copies.start(region(levels, level + 1, row, blocks), out))
 
     edge_steps(2, blocks, waits, levels, partial, coef, params, ready)
     for copy in sends:
@@ -213,8 +277,8 @@
 
 def last_kernel(blocks, *refs):
     sources, refs = refs[:12], refs[12:]
-    own_coef, gathered, params, row_of, offset_of, shift_of = refs[:6]
-    out, predicted, *levels, partial, coef, staged, sems, out_sems = refs[6:]
+    own_coef, mine, theirs, params, place_of, cell_of, shift_of = refs[:7]
+    out, predicted, *levels, partial, coef, staged, sems, out_sems = refs[7:]
     copies = Copies(sems)
     places = (
         (0, -8), (0, -4), (0, 16), (0, 20),
@@ -222,8 +286,12 @@
     )
     waits = [[] for _ in range(STEPS + 1)]
     for source, (level, row) in zip(sources, places):
-        waits[level].append(copies.start(source, levels[level].at[place(row)]))
-    waits[0] += load_coef(copies, own_coef, gathered, coef)
+        count = GROUP * blocks if level == STEPS else GROUP
+        waits[level].append(
+            copies.start(source.at[0:count], region(levels, level, row, blocks))
+        )
+    waits[0] += load_coef(copies, own_coef, sources[1], sources[2], coef)
+    waits[0] += load_outer_coef(copies, mine, theirs, place_of, coef)
     edge_steps(6, blocks, waits, levels, partial, coef, params, lambda *_: None)
     for copy in waits[STEPS]:
         copy.wait()
@@ -235,7 +303,7 @@
     def _(block):
         for row in range(ROWS):
             staged[block, pl.ds(row, SUBLANES, stride=ROWS), :] = levels[STEPS][
-                HALO + row, :, block_at(block)
+                (HALO + row) * blocks + block
             ]
         out_copy(block).start()
 
@@ -246,8 +314,7 @@
         base = block * LANES
         found = jnp.zeros((SUBLANES, LANES), jnp.float32)
         for i in range(LANES):
-            at = pl.ds(pl.multiple_of(offset_of[base + i], LANES), LANES)
-            value = levels[STEPS][row_of[base + i], :, at]
+            value = levels[STEPS][cell_of[base + i]]
             found = jnp.where(lane == i, pltpu.roll(value, shift_of[base + i], 1), found)
         predicted[:, block_at(block)] = found
 
@@ -258,10 +325,13 @@
 
 def scratch(columns, *more):
     return (
-        [pltpu.VMEM((ROWS + 2 * HALO, SUBLANES, columns), jnp.float32)] * (STEPS + 1)
+        [pltpu.VMEM((ROWS + 2 * HALO, SUBLANES, columns), jnp.float32)] * STEPS
         + [
+            pltpu.VMEM(
+                ((ROWS + 2 * HALO) * columns // LANES, SUBLANES, LANES), jnp.float32
+            ),
             pltpu.VMEM((GROUP, SUBLANES, columns), jnp.float32),
-            pltpu.VMEM((4, ROWS + 2 * HALO, 1, columns), jnp.float32),
+            pltpu.VMEM((4 * ROWS + 48, 1, columns), jnp.float32),
         ]
         + list(more)
     )
@@ -275,39 +345,44 @@
         out_specs=out_specs,
         scratch_shapes=scratches,
         compiler_params=pltpu.CompilerParams(vmem_limit_bytes=limit),
-        cost_estimate=pl.CostEstimate(flops=0, bytes_accessed=cost * 3600000, transcendentals=0),
+        cost_estimate=pl.CostEstimate(flops=0, bytes_accessed=cost * COST_BYTES, transcendentals=0),
         name=name,
     )(*operands)
 
 
-def row_groups(tracer):
+def row_groups(tracer, coefficients, place_of):
     members, rows, columns = tracer.shape
     if members != SUBLANES or rows != ROWS:
         raise ValueError("block shape")
     blocks = columns // LANES
-    return kernel_call(
-        functools.partial(to_rows_kernel, blocks), "to_rows",
-        [(GROUP, members, columns)] * 4, [ANYWHERE], (IN_VMEM,) * 4,
-        [
-            pltpu.VMEM((blocks, members * rows, LANES), jnp.float32),
-            pltpu.SemaphoreType.DMA((blocks,)),
-        ],
-        3, [tracer.reshape(members * rows, columns)], TALL_LIMIT,
-    )
-
-
-def transport(shape, own, own_coef, halo_coef, params, obs_index, halos):
+    flat = tracer.reshape(members * rows, columns)
+    dma = pltpu.SemaphoreType.DMA
+    scratches = [pltpu.VMEM((blocks, members * rows, LANES), jnp.float32), dma((blocks,))]
+    up, down = kernel_call(
+        functools.partial(outer_rows_kernel, blocks), "outer_rows",
+        [(GROUP + 2, members, columns)] * 2, [ANYWHERE, ANYWHERE, IN_SMEM], (IN_VMEM,) * 2,
+        scratches + [dma((12,))], 3, [flat, coefficients, place_of], TALL_LIMIT,
+    )
+    low, high = kernel_call(
+        functools.partial(inner_rows_kernel, blocks), "inner_rows",
+        [(GROUP, members, columns)] * 2, [ANYWHERE, ANYWHERE], (IN_VMEM,) * 2,
+        scratches, 3, [flat, up], TALL_LIMIT,
+    )
+    return down, low, high, up
+
+
+def transport(shape, own, low0, high0, own_coef, params, place_of, obs_index, halos, other_core):
     members, rows, columns = shape
     blocks = columns // LANES
     group = (GROUP, members, columns)
     flat = (members * rows, columns)
+    cells = (GROUP * blocks, members, LANES)
     dma = pltpu.SemaphoreType.DMA
     staged = pltpu.VMEM((blocks, members * rows, LANES), jnp.float32)
-    low0, high0 = halos(own[3], own[0])
     inner = kernel_call(
         functools.partial(interior_kernel, blocks), "interior",
         [group] * 5, [ANYWHERE] * 5 + [IN_VMEM], (ANYWHERE,) * 5,
-        scratch(columns, dma((10,))), 8, [*own, own_coef, params],
+        scratch(columns, dma((16,))), 8, [*own, own_coef, params],
     )
     upper, lower, low0, high0, *_ = lax.optimization_barrier(
         (own[2], own[1], low0, high0, inner[0])
@@ -315,20 +390,21 @@
     low1, high1 = halos(upper, lower)
     first = kernel_call(
         functools.partial(middle_kernel, blocks), "edge_first",
-        [group] * 8, [ANYWHERE] * 11 + [IN_VMEM], (ANYWHERE,) * 8,
-        scratch(columns, dma((20,))), 10,
-        [low0, own[0], own[3], high0, *inner, own_coef, halo_coef, params],
-    )
-    row_of = obs_index // columns + HALO
+        [group] * 6 + [cells] * 2, [ANYWHERE] * 10 + [IN_VMEM], (ANYWHERE,) * 8,
+        scratch(columns, dma((26,))), 10,
+        [low0, own[0], own[3], high0, *inner, own_coef, params],
+    )
+    mine, _ = lax.optimization_barrier((jnp.stack([low0[GROUP + 1], high0[GROUP + 1]]), first[0]))
+    theirs = other_core(mine)
+    cell_of = obs_index // LANES + HALO * blocks
     lane_of = obs_index % LANES
-    offset_of = obs_index % columns - lane_of
     shift_of = (jnp.arange(obs_index.shape[0], dtype=jnp.int32) - lane_of) % LANES
     field, predicted = kernel_call(
         functools.partial(last_kernel, blocks), "edge_last",
         [flat, (members, obs_index.shape[0])],
-        [ANYWHERE] * 14 + [IN_VMEM] + [IN_SMEM] * 3, (ANYWHERE, IN_VMEM),
-        scratch(columns, staged, dma((15,)), dma((blocks,))), 15,
-        [low1, low0, high0, high1, *first, own_coef, halo_coef, params, row_of, offset_of, shift_of],
+        [ANYWHERE] * 15 + [IN_VMEM] + [IN_SMEM] * 3, (ANYWHERE, IN_VMEM),
+        scratch(columns, staged, dma((29,)), dma((blocks,))), 15,
+        [low1, low0, high0, high1, *first, own_coef, mine, theirs, params, place_of, cell_of, shift_of],
     )
     return field.reshape(shape), predicted
 
@@ -384,21 +460,25 @@
     ens_pos = lax.axis_index("ens")
     ens_count = lax.axis_size("ens")
     slab_count = lax.axis_size("slab")
-    if ens_count != coefficients.shape[0] or slab_count & (slab_count - 1):
+    if ens_count != 4 or coefficients.shape[0] != 4 or slab_count & (slab_count - 1):
         raise ValueError("mesh shape")
     forward = [(i, i + 1) for i in range(slab_count - 1)]
     backward = [(target, source) for source, target in forward]
 
-    own_array = lax.dynamic_slice_in_dim(coefficients, ens_pos, 1, 0)[0]
-    coef_low = lax.ppermute(own_array[rows - HALO :], "slab", forward)
-    coef_high = lax.ppermute(own_array[:HALO], "slab", backward)
-    own = row_groups(tracer)
-    coef_low, coef_high, _ = lax.optimization_barrier((coef_low, coef_high, own[0]))
-    shared = jnp.concatenate([coef_low, coef_high, parameters], axis=0)
-    gathered = lax.all_gather(shared, "ens", axis=0, tiled=False)
-
     def halos(upper, lower):
         return lax.ppermute(upper, "slab", forward), lax.ppermute(lower, "slab", backward)
+
+    place_of = jnp.reshape(ens_pos, (1,))
+    own = row_groups(tracer, coefficients, place_of)
+    low0, high0 = halos(own[3], own[0])
+
+    later, _ = lax.optimization_barrier((parameters, own[1]))
+    pair = jnp.stack([later, lax.ppermute(later, "ens", [(i, i ^ 1) for i in range(ens_count)])])
+    other = lax.ppermute(pair, "ens", [(i, i ^ 2) for i in range(ens_count)])
+    shared = jnp.concatenate([pair, other], axis=0)
+
+    def other_core(mine):
+        return lax.ppermute(mine, "ens", [(i, i ^ 1) for i in range(ens_count)])
 
     members = member_group.shape[0]
     per_group = members // GROUPS
@@ -408,12 +488,15 @@
     earlier = jnp.arange(members)[None, :] < jnp.arange(members)[:, None]
     rank = jnp.sum((same_bool & earlier).astype(jnp.int32), axis=1)
     own_same = lax.dynamic_slice_in_dim(same, ens_pos * local_members, local_members, 1)
-    all_params = gathered[:, 2 * HALO :, :].reshape(members, columns)
+    field, predicted = transport(
+        tracer.shape, own, low0, high0,
+        coefficients, parameters, place_of, obs_index, halos, other_core,
+    )
+    all_params = jnp.concatenate(
+        [lax.dynamic_index_in_dim(shared, ens_pos ^ i, 0, False) for i in range(ens_count)], axis=0
+    )
     param_anomalies = (all_params - hdot(same, all_params) / per_group) * spread
 
-    field, predicted = transport(
-        tracer.shape, own, coefficients, gathered, parameters, obs_index, halos
-    )
     everyone = lax.all_gather(predicted, "ens", axis=0, tiled=True)
     total_obs = obs_variance.shape[0] * slab_count
     products = pl.pallas_call(

time: 132 us -> 126 us (0.955)
  between operations: 14.3 us -> 0.89 us
  waiting for transfers between devices: 9.52 us -> 20.9 us
  starting transfers between devices: 26.9 us -> 23.3 us
  local copies, waits for them, and re-layouts: 18.6 us -> 16.1 us
    ppermute x2, waiting for transfers between devices: 2.97 us -> 17.2 us  [halos(): lax.ppermute(upper, 'slab', forward)]
    ppermute x2 -> x3, starting transfers between devices: 6.14 us -> 1.59 us  [the longest x1 1.52 us: local(): other = lax.ppermute(pair, 'ens', [(i, i ^ 2) for i in range(ens_count)])]
    ppermute x2 -> x3, waiting for transfers between devices: 2.14 us -> 0.01 us  [the longest x1 0.01 us: local(): lax.ppermute(later, 'ens', [(i, i ^ 1) for i in range(ens_count)])]
    unnamed x56 -> x52, local copies, waits for them, and re-layouts: 17.5 us -> 15.9 us
    pallas_call x4 -> x5, Pallas kernels: 52.2 us -> 52.9 us  [kernel_call(): pl.pallas_call(body, out_shape=tuple((jax.ShapeDtypeStruct(shape, jnp.flo...]
  transfers between devices with their start and end apart: 10 -> 10, of which waited for: 5 -> 4; matrix products, arithmetic and copies ran while one was open for 1% -> 2% of each run, Pallas kernels for 22% -> 40%
where the time goes in v3:
time: 126 us; the launch traced here: 125 us
  Pallas kernels  55.7 us (44%)
  starting transfers between devices  23.3 us (18%)
  waiting for transfers between devices  20.9 us (17%)
  local copies, waits for them, and re-layouts  16.1 us (13%)
  blocking collectives  5.79 us (5%)
  other arithmetic  2.02 us (2%)
    pallas_call x5, Pallas kernels, kernel_call(): pl.pallas_call(body, out_shape=tuple((jax.ShapeDtypeStruct(shape, jnp.flo...  52.9 us
    ppermute x2, waiting for transfers between devices, halos(): lax.ppermute(upper, 'slab', forward)  17.2 us
    unnamed x52, local copies, waits for them, and re-layouts  15.9 us
    ppermute x2, starting transfers between devices, halos(): lax.ppermute(upper, 'slab', forward)  10.1 us
    ppermute x3, starting transfers between devices, local(): products = products + lax.ppermute(products, 'slab', pairs)  8.84 us
    all_gather x1, blocking collectives, local(): everyone = lax.all_gather(predicted, 'ens', axis=0, tiled=True)  5.79 us
    ppermute x3, waiting for transfers between devices, local(): products = products + lax.ppermute(products, 'slab', pairs)  3.68 us
    ppermute x2, starting transfers between devices, halos(): lax.ppermute(lower, 'slab', backward)  2.75 us
  transfers between devices with their start and end apart: 10, of which 4 were waited for; matrix products, arithmetic and copies ran while one was open for 2% of the time, Pallas kernels for 40%

profile of v3, /device:TPU:0, one launch (start us, length us, event | category | flops | bytes accessed | tf_op | source)
XLA Modules:
  0.0 125.1 jit_solution(10378310726208029134)
XLA Ops:
  0.6 3.4 %outer_rows.1 = (f32[6,8,4096]{2,1,0:T(8,128)}, f32[6,8,4096]{2,1,0:T(8,128)}) custom-call(f32[128,4096]{1,0:T(8,128)} %bitcast.23, f32[4,16,4096]{2,1,0:T(8,128)} %refs_12_.1, s32[1]{0:T(128)} %bitcast.1.place_of.refs_16_), custom_call_target="tpu_custom_call" | custom-call | bytes 600000 | tf_op jit(solution)/shard_map/outer_rows/pallas_call | solution.py:341
  4.0 0.0 copy-start.2
  4.0 0.0 copy-start
  4.0 0.0 copy-start.1
  4.0 5.0 %collective-permute-start = (f32[6,8,4096]{2,1,0:T(8,128)}, f32[6,8,4096]{2,1,0:T(8,128)S(1)}, u32[]{:S(2)}, u32[]{:S(2)}) collective-permute-start(f32[6,8,4096]{2,1,0:T(8,128)} %get-tuple-element.27.outer.own3.refs_2_), channel_id=1, source_target_pairs={{0,1},{1,2},{2,3},{3,4},{4,5},{5,6},{6,7},{8,9},{9,10},{10,11},{11... | collective-permute-start | bytes 2359304 | tf_op jit(solution)/shard_map/ppermute | solution.py:469
  9.1 1.3 %collective-permute-start.1 = (f32[6,8,4096]{2,1,0:T(8,128)}, f32[6,8,4096]{2,1,0:T(8,128)S(1)}, u32[]{:S(2)}, u32[]{:S(2)}) collective-permute-start(f32[6,8,4096]{2,1,0:T(8,128)} %get-tuple-element.30.own0.refs_1_), channel_id=1, source_target_pairs={{1,0},{2,1},{3,2},{4,3},{5,4},{6,5},{7,6},{9,8},{10,9},{11,10},{12... | collective-permute-start | bytes 2359304 | tf_op jit(solution)/shard_map/ppermute | solution.py:469
  10.4 0.0 copy-start.24
  10.4 2.9 %inner_rows.1 = (f32[4,8,4096]{2,1,0:T(8,128)}, f32[4,8,4096]{2,1,0:T(8,128)}) custom-call(f32[128,4096]{1,0:T(8,128)} %bitcast.24, f32[6,8,4096]{2,1,0:T(8,128)} %get-tuple-element.27.outer.own3.refs_2_), custom_call_target="tpu_custom_call" | custom-call | bytes 600000 | tf_op jit(solution)/shard_map/inner_rows/pallas_call | solution.py:341
  13.3 0.0 copy-start.25
  13.3 0.1 collective-permute-start.8
  13.4 0.0 copy-done
  13.4 0.0 copy-done.1
  13.4 0.0 copy-start.3
  13.4 1.1 copy-done.3
  14.6 11.1 %interior.1 = (f32[4,8,4096]{2,1,0:T(8,128)S(1)}, f32[4,8,4096]{2,1,0:T(8,128)S(1)}, f32[4,8,4096]{2,1,0:T(8,128)S(1)}, f32[4,8,4096]{2,1,0:T(8,128)S(1)}, f32[4,8,4096]{2,1,0:T(8,128)S(1)}) custom-call(f32[6,8,4096]{2,1,0:T(8,128)S(1)} %copy-done.3, f32[4,8,4096]{2,1,0:T(8,128)} %get-tuple-element.35.own1, f32[4,8,4096]{2,1,0:T(8,128)} %get-tuple-element.32.own2, ...), custom_call_target="tpu_custom_call" | custom-call | bytes 1600000 | tf_op jit(solution)/shard_map/interior/pallas_call | solution.py:341
  25.7 0.0 copy-done.25
  25.7 0.1 compare_convert_fusion.same
  25.8 17.2 %collective-permute-done.refs_0_.refs_1_ = f32[6,8,4096]{2,1,0:T(8,128)S(1)} collective-permute-done((f32[6,8,4096]{2,1,0:T(8,128)}, f32[6,8,4096]{2,1,0:T(8,128)S(1)}, u32[]{:S(2)}, u32[]{:S(2)}) %collective-permute-start) | collective-permute-done | bytes 786464 | tf_op jit(solution)/shard_map/ppermute | solution.py:469
  43.0 0.0 collective-permute-done.1.refs_3_.refs_2_
  43.0 5.1 %collective-permute-start.2 = (f32[4,8,4096]{2,1,0:T(8,128)}, f32[4,8,4096]{2,1,0:T(8,128)}, u32[]{:S(2)}, u32[]{:S(2)}) collective-permute-start(f32[4,8,4096]{2,1,0:T(8,128)} %get-tuple-element.32.own2), channel_id=1, source_target_pairs={{0,1},{1,2},{2,3},{3,4},{4,5},{5,6},{6,7},{8,9},{9,10},{10,11},{11... | collective-permute-start | bytes 1572872 | tf_op jit(solution)/shard_map/ppermute | solution.py:469
  48.1 1.5 %collective-permute-start.3 = (f32[4,8,4096]{2,1,0:T(8,128)}, f32[4,8,4096]{2,1,0:T(8,128)}, u32[]{:S(2)}, u32[]{:S(2)}) collective-permute-start(f32[4,8,4096]{2,1,0:T(8,128)} %get-tuple-element.35.own1), channel_id=1, source_target_pairs={{1,0},{2,1},{3,2},{4,3},{5,4},{6,5},{7,6},{9,8},{10,9},{11,10},{12... | collective-permute-start | bytes 1572872 | tf_op jit(solution)/shard_map/ppermute | solution.py:469
  49.6 14.5 %edge_first.1 = (f32[4,8,4096]{2,1,0:T(8,128)S(1)}, f32[4,8,4096]{2,1,0:T(8,128)S(1)}, f32[4,8,4096]{2,1,0:T(8,128)S(1)}, f32[4,8,4096]{2,1,0:T(8,128)S(1)}, f32...) custom-call(f32[6,8,4096]{2,1,0:T(8,128)S(1)} %collective-permute-do, ...), custom_call_target="tpu_custom_call" | custom-call | bytes 2000000 | tf_op jit(solution)/shard_map/edge_first/pallas_call | solution.py:341
  64.1 0.0 copy-start.4
  64.1 0.8 copy-done.4
  64.9 0.8 copy-done.6
  65.7 0.8 copy-done.8
  66.5 0.8 copy-done.10
  67.3 0.8 copy-done.12
  68.1 0.8 copy-done.14
  68.9 0.8 copy-done.16
  69.7 0.8 copy-done.18
  70.5 0.0 collective-permute-start.4
  70.5 0.0 collective-permute-done.8
  70.5 0.7 pad_maximum_fusion.2
  71.3 0.0 copy-done.22
  71.3 1.5 %collective-permute-start.9 = (f32[2,8,4096]{2,1,0:T(8,128)}, f32[2,8,4096]{2,1,0:T(8,128)}, u32[]{:S(2)}, u32[]{:S(2)}) collective-permute-start(f32[2,8,4096]{2,1,0:T(8,128)} %pad_maximum_fusion.2), channel_id=1, source_target_pairs={{0,16},{8,24},{16,0},{24,8},{1,17},{9,25},{17,1},{25,9},{2,18},{10... | collective-permute-start | bytes 786440 | tf_op jit(solution)/shard_map/ppermute | solution.py:477
  72.8 0.2 convert_reduce_fusion
  73.0 0.1 copy.9.rank_col
  73.1 0.1 constant_dynamic-slice_fusion.own_same
  73.1 0.0 collective-permute-done.4.refs_14_
  73.2 0.0 collective-permute-done.2.refs_0_
  73.2 0.0 collective-permute-done.3.refs_3_
  73.2 0.0 copy-start.5
  73.2 1.0 copy-done.5
  74.2 1.0 copy-done.7
  75.3 1.0 copy-done.9
  76.3 1.0 copy-done.11
  77.3 1.0 copy-done.13
  78.4 1.0 copy-done.15
  79.4 1.0 copy-done.17
  80.5 1.0 copy-done.19
  81.5 21.0 %edge_last.1 = (f32[128,4096]{1,0:T(8,128)}, f32[8,2048]{1,0:T(8,128)S(1)}) custom-call(f32[4,8,4096]{2,1,0:T(8,128)} %collective-permute-done.2.refs_0_, f32[6,8,4096]{2,1,0:T(8,128)S(1)} %collective-permute-done.refs_0_.refs_1_, f32[6,8,4096]{2,1,0:T(8,128)S(1)} %collective-permute-done.1.refs_3_.refs_2_, f32[4,8,4096]{2,1,0:T(8,128)} %collective-permute-done.3.refs_3_, ...), custom_call_target="tpu_custom_call" | custom-call | bytes 3000000 | tf_op jit(solution)/shard_map/edge_last/pallas_call | solution.py:341
  102.5 5.8 %all_gather.3.everyone = f32[32,2048]{1,0:T(8,128)S(1)} all-gather(f32[8,2048]{1,0:T(8,128)S(1)} %get-tuple-element.50.own), channel_id=1, replica_groups=mesh['ens'=4,'slab'=8] {'ens'}, dimensions={0}, use_global_device_ids=true | all-gather | bytes 327680 | tf_op jit(solution)/shard_map/all_gather | solution.py:500
  108.3 0.6 products.1
  109.0 2.7 %collective-permute-start.5 = (f32[32,40]{1,0:T(8,128)S(1)}, f32[32,40]{1,0:T(8,128)S(1)}, u32[]{:S(2)}, u32[]{:S(2)}) collective-permute-start(f32[32,40]{1,0:T(8,128)S(1)} %products.1), channel_id=1, source_target_pairs={{0,1},{1,0},{2,3},{3,2},{4,5},{5,4},{6,7},{7,6},{8,9},{9,8},{10,11... | collective-permute-start | bytes 15368 | tf_op jit(solution)/shard_map/ppermute | solution.py:511
  111.7 0.0 collective-permute-done.9
  111.7 1.0 pad_maximum_fusion
  112.7 0.7 collective-permute-done.5
  113.4 3.1 %collective-permute-start.6 = (f32[32,40]{1,0:T(8,128)S(1)}, f32[32,40]{1,0:T(8,128)S(1)}, u32[]{:S(2)}, u32[]{:S(2)}) collective-permute-start(f32[32,40]{1,0:T(8,128)S(1)} %add.46), channel_id=1, source_target_pairs={{0,2},{1,3},{2,0},{3,1},{4,6},{5,7},{6,4},{7,5},{8,10},{9,11},{10,... | collective-permute-start | bytes 15368 | tf_op jit(solution)/shard_map/ppermute | solution.py:511
  116.6 1.7 %collective-permute-done.6 = f32[32,40]{1,0:T(8,128)S(1)} collective-permute-done((f32[32,40]{1,0:T(8,128)S(1)}, f32[32,40]{1,0:T(8,128)S(1)}, u32[]{:S(2)}, u32[]{:S(2)}) %collective-permute-start.6) | collective-permute-done | bytes 5152 | tf_op jit(solution)/shard_map/ppermute | solution.py:511
  118.2 3.0 %collective-permute-start.7 = (f32[32,40]{1,0:T(8,128)S(1)}, f32[32,40]{1,0:T(8,128)S(1)}, u32[]{:S(2)}, u32[]{:S(2)}) collective-permute-start(f32[32,40]{1,0:T(8,128)S(1)} %add.47), channel_id=1, source_target_pairs={{0,4},{1,5},{2,6},{3,7},{4,0},{5,1},{6,2},{7,3},{8,12},{9,13},{10,... | collective-permute-start | bytes 15368 | tf_op jit(solution)/shard_map/ppermute | solution.py:511
  121.3 0.4 fusion.1.anomalies
  121.7 1.3 %collective-permute-done.7 = f32[32,40]{1,0:T(8,128)S(1)} collective-permute-done((f32[32,40]{1,0:T(8,128)S(1)}, f32[32,40]{1,0:T(8,128)S(1)}, u32[]{:S(2)}, u32[]{:S(2)}) %collective-permute-start.7) | collective-permute-done | bytes 5152 | tf_op jit(solution)/shard_map/ppermute | solution.py:511
  123.0 2.1 %update.1 = f32[8,4096]{1,0:T(8,128)} custom-call(f32[1,32,40]{2,1,0:T(8,128)S(1)} %add_bitcast_fusion.summands, f32[32,32]{1,0:T(8,128)S(1)} %compare_convert_fusion.same, f32[32,8]{1,0:T(8,128)S(1)} %constant_dynamic-slice_fusion.own_same, s32[1,32]{1,0:T(1,128)S(1)} %bitcast.22, s32[32,1]{1,0:T(8,128)S(1)} %copy.9.rank_col, ...), custom_call_target="tpu_custom_call" | custom-call | tf_op jit(solution)/shard_map/update/pallas_call | solution.py:513
  (31 shorter events, 0.1 us)
Async XLA Ops:
  4.0 9.3 %copy-start.2 = (f32[8,4096]{1,0:T(8,128)S(1)}, f32[8,4096]{1,0:T(8,128)}, u32[]{:S(2)}) copy-start(f32[8,4096]{1,0:T(8,128)} %own.1) | copy-start | bytes 393220
  4.0 9.4 %copy-start = (f32[4,16,4096]{2,1,0:T(8,128)S(1)}, f32[4,16,4096]{2,1,0:T(8,128)}, u32[]{:S(2)}) copy-start(f32[4,16,4096]{2,1,0:T(8,128)} %refs_12_.1) | copy-start | bytes 3145732
  4.0 9.4 %copy-start.1 = (f32[6,8,4096]{2,1,0:T(8,128)S(1)}, f32[6,8,4096]{2,1,0:T(8,128)}, u32[]{:S(2)}) copy-start(f32[6,8,4096]{2,1,0:T(8,128)} %get-tuple-element.27.outer.own3.refs_2_) | copy-start | bytes 2359300
  4.0 38.9 %collective-permute-start = (f32[6,8,4096]{2,1,0:T(8,128)}, f32[6,8,4096]{2,1,0:T(8,128)S(1)}, u32[]{:S(2)}, u32[]{:S(2)}) collective-permute-start(f32[6,8,4096]{2,1,0:T(8,128)} %get-tuple-element.27.outer.own3.refs_2_), channel_id=1, source_target_pairs={{0,1},{1,2},{2,3},{3,4},{4,5},{5,6},{6,7},{8,9},{9,10},{10,11},{11... | collective-permute-start | bytes 2359304 | tf_op jit(solution)/shard_map/ppermute | solution.py:469
  9.1 33.9 %collective-permute-start.1 = (f32[6,8,4096]{2,1,0:T(8,128)}, f32[6,8,4096]{2,1,0:T(8,128)S(1)}, u32[]{:S(2)}, u32[]{:S(2)}) collective-permute-start(f32[6,8,4096]{2,1,0:T(8,128)} %get-tuple-element.30.own0.refs_1_), channel_id=1, source_target_pairs={{1,0},{2,1},{3,2},{4,3},{5,4},{6,5},{7,6},{9,8},{10,9},{11,10},{12... | collective-permute-start | bytes 2359304 | tf_op jit(solution)/shard_map/ppermute | solution.py:469
  10.4 15.4 %copy-start.24 = (s32[2048]{0:T(1024)S(1)}, s32[2048]{0:T(1024)}, u32[]{:S(2)}) copy-start(s32[2048]{0:T(1024)} %param.10) | copy-start | bytes 24580
  13.3 12.4 %copy-start.25 = (s32[32]{0:T(128)S(1)}, s32[32]{0:T(128)}, u32[]{:S(2)}) copy-start(s32[32]{0:T(128)} %param.13) | copy-start | bytes 388
  13.3 57.2 %collective-permute-start.8 = (f32[8,4096]{1,0:T(8,128)S(1)}, f32[8,4096]{1,0:T(8,128)S(1)}, u32[]{:S(2)}, u32[]{:S(2)}) collective-permute-start(f32[8,4096]{1,0:T(8,128)S(1)} %copy-done.2), channel_id=1, source_target_pairs={{0,8},{8,0},{16,24},{24,16},{1,9},{9,1},{17,25},{25,17},{2,10},{10... | collective-permute-start | bytes 393224 | tf_op jit(solution)/shard_map/ppermute | solution.py:476
  13.4 1.1 copy-start.3
  43.0 30.2 %collective-permute-start.2 = (f32[4,8,4096]{2,1,0:T(8,128)}, f32[4,8,4096]{2,1,0:T(8,128)}, u32[]{:S(2)}, u32[]{:S(2)}) collective-permute-start(f32[4,8,4096]{2,1,0:T(8,128)} %get-tuple-element.32.own2), channel_id=1, source_target_pairs={{0,1},{1,2},{2,3},{3,4},{4,5},{5,6},{6,7},{8,9},{9,10},{10,11},{11... | collective-permute-start | bytes 1572872 | tf_op jit(solution)/shard_map/ppermute | solution.py:469
  48.1 25.1 %collective-permute-start.3 = (f32[4,8,4096]{2,1,0:T(8,128)}, f32[4,8,4096]{2,1,0:T(8,128)}, u32[]{:S(2)}, u32[]{:S(2)}) collective-permute-start(f32[4,8,4096]{2,1,0:T(8,128)} %get-tuple-element.35.own1), channel_id=1, source_target_pairs={{1,0},{2,1},{3,2},{4,3},{5,4},{6,5},{7,6},{9,8},{10,9},{11,10},{12... | collective-permute-start | bytes 1572872 | tf_op jit(solution)/shard_map/ppermute | solution.py:469
  64.1 0.8 copy-start.4
  64.9 0.8 copy-start.6
  65.7 0.8 copy-start.8
  66.5 0.8 copy-start.10
  67.3 0.8 copy-start.12
  68.1 0.8 copy-start.14
  68.9 0.8 copy-start.16
  69.7 0.8 copy-start.18
  70.5 2.6 %collective-permute-start.4 = (f32[2,8,4096]{2,1,0:T(8,128)S(1)}, f32[2,8,4096]{2,1,0:T(8,128)S(1)}, u32[]{:S(2)}, u32[]{:S(2)}) collective-permute-start(f32[2,8,4096]{2,1,0:T(8,128)S(1)} %pad_maximum_fusion.1.refs_13_), channel_id=1, source_target_pairs={{0,8},{8,0},{16,24},{24,16},{1,9},{9,1},{17,25},{25,17},{2,10},{10... | collective-permute-start | bytes 786440 | tf_op jit(solution)/shard_map/ppermute | solution.py:481
  70.5 0.7 copy-start.22
  71.3 40.4 %collective-permute-start.9 = (f32[2,8,4096]{2,1,0:T(8,128)}, f32[2,8,4096]{2,1,0:T(8,128)}, u32[]{:S(2)}, u32[]{:S(2)}) collective-permute-start(f32[2,8,4096]{2,1,0:T(8,128)} %pad_maximum_fusion.2), channel_id=1, source_target_pairs={{0,16},{8,24},{16,0},{24,8},{1,17},{9,25},{17,1},{25,9},{2,18},{10... | collective-permute-start | bytes 786440 | tf_op jit(solution)/shard_map/ppermute | solution.py:477
  73.2 1.0 copy-start.5
  74.2 1.0 copy-start.7
  75.2 1.0 copy-start.9
  76.3 1.0 copy-start.11
  77.3 1.0 copy-start.13
  78.4 1.0 copy-start.15
  79.4 1.0 copy-start.17
  80.5 1.0 copy-start.19
  81.5 26.8 %copy-start.20 = (f32[8,2048]{1,0:T(8,128)S(1)}, f32[8,2048]{1,0:T(8,128)}, u32[]{:S(2)}) copy-start(f32[8,2048]{1,0:T(8,128)} %values.1) | copy-start | bytes 196612
  81.5 26.8 %copy-start.21 = (f32[2048]{0:T(1024)S(1)}, f32[2048]{0:T(1024)}, u32[]{:S(2)}) copy-start(f32[2048]{0:T(1024)} %param.12) | copy-start | bytes 24580
  81.5 30.2 %copy-start.23 = (f32[8,4096]{1,0:T(8,128)S(1)}, f32[8,4096]{1,0:T(8,128)}, u32[]{:S(2)}) copy-start(f32[8,4096]{1,0:T(8,128)} %copy-done.22) | copy-start | bytes 393220
  109.0 4.4 %collective-permute-start.5 = (f32[32,40]{1,0:T(8,128)S(1)}, f32[32,40]{1,0:T(8,128)S(1)}, u32[]{:S(2)}, u32[]{:S(2)}) collective-permute-start(f32[32,40]{1,0:T(8,128)S(1)} %products.1), channel_id=1, source_target_pairs={{0,1},{1,0},{2,3},{3,2},{4,5},{5,4},{6,7},{7,6},{8,9},{9,8},{10,11... | collective-permute-start | bytes 15368 | tf_op jit(solution)/shard_map/ppermute | solution.py:511
  113.4 4.8 %collective-permute-start.6 = (f32[32,40]{1,0:T(8,128)S(1)}, f32[32,40]{1,0:T(8,128)S(1)}, u32[]{:S(2)}, u32[]{:S(2)}) collective-permute-start(f32[32,40]{1,0:T(8,128)S(1)} %add.46), channel_id=1, source_target_pairs={{0,2},{1,3},{2,0},{3,1},{4,6},{5,7},{6,4},{7,5},{8,10},{9,11},{10,... | collective-permute-start | bytes 15368 | tf_op jit(solution)/shard_map/ppermute | solution.py:511
  118.2 4.8 %collective-permute-start.7 = (f32[32,40]{1,0:T(8,128)S(1)}, f32[32,40]{1,0:T(8,128)S(1)}, u32[]{:S(2)}, u32[]{:S(2)}) collective-permute-start(f32[32,40]{1,0:T(8,128)S(1)} %add.47), channel_id=1, source_target_pairs={{0,4},{1,5},{2,6},{3,7},{4,0},{5,1},{6,2},{7,3},{8,12},{9,13},{10,... | collective-permute-start | bytes 15368 | tf_op jit(solution)/shard_map/ppermute | solution.py:511

commit v4 on v3

--- a/solution.py
+++ b/solution.py
@@ -18,8 +18,8 @@
 LAG = 3
 WIDE = 8
 TOGETHER = 2
-VMEM_LIMIT = 30 * 1024 * 1024
-TALL_LIMIT = 60 * 1024 * 1024
+VMEM_LIMIT = 16 * 1024 * 1024
+TALL_LIMIT = 58 * 1024 * 1024
 COST_BYTES = 200000
 ANYWHERE = pl.BlockSpec(memory_space=pltpu.HBM)
 IN_VMEM = pl.BlockSpec(memory_space=pltpu.VMEM)
@@ -159,19 +159,15 @@
                 ]
 
 
-def outer_rows_kernel(blocks, tracer, own_coef, place_of, up, down, staged, sems, coef_sems):
+def outer_rows_kernel(
+    blocks, tracer, own_coef, place_of, up, down, up_coef, down_coef, staged, sems, coef_sems
+):
     copies = Copies(coef_sems)
-    upper = lax.rem(place_of[0], 2) * 2
-    waits = []
-    for array in range(4):
-        at = pl.ds(2 * array, 2)
-        waits.append(copies.start(own_coef.at[array, pl.ds(ROWS - 2, 2)], up.at[GROUP, at]))
-        waits.append(copies.start(own_coef.at[array, pl.ds(0, 2)], down.at[GROUP, at]))
-    for array in range(2):
-        at = pl.ds(4 * array, 4)
-        source = own_coef.at[upper + array]
-        waits.append(copies.start(source.at[pl.ds(ROWS - 6, 4)], up.at[GROUP + 1, at]))
-        waits.append(copies.start(source.at[pl.ds(2, 4)], down.at[GROUP + 1, at]))
+    source = own_coef.at[place_of[0]]
+    waits = [
+        copies.start(source.at[pl.ds(ROWS - HALO, HALO)], up_coef),
+        copies.start(source.at[pl.ds(0, HALO)], down_coef),
+    ]
     fill_rows(blocks, (0, ROWS - GROUP), tracer, (down, up), staged, sems)
     for copy in waits:
         copy.wait()
@@ -223,38 +219,27 @@
 
 def coef_row(array, row):
     own = array * ROWS + row - HALO
-    near_low = 4 * ROWS + 2 * array + row - (HALO - 2)
-    near_high = 4 * ROWS + 8 + 2 * array + row - (HALO + ROWS)
-    far_low = 4 * ROWS + 16 + 4 * array + row - (HALO - 6)
-    far_high = 4 * ROWS + 32 + 4 * array + row - (HALO + ROWS + 2)
-    low = jnp.where(row < HALO - 2, far_low, near_low)
-    high = jnp.where(row < HALO + ROWS + 2, near_high, far_high)
+    low = 4 * ROWS + 2 * HALO * array + row
+    high = 4 * ROWS + 2 * HALO * array + row - ROWS
     return jnp.where(row < HALO, low, jnp.where(row < HALO + ROWS, own, high))
 
 
-def load_coef(copies, own_coef, low, high, coef):
+def load_coef(copies, own_coef, pair, other, place_of, coef):
     waits = [
         copies.start(own_coef.at[array], coef.at[pl.ds(array * ROWS, ROWS), 0]) for array in range(4)
     ]
-    for side, source in enumerate((low, high)):
-        waits.append(copies.start(source.at[GROUP], coef.at[pl.ds(4 * ROWS + 8 * side, 8), 0]))
-    return waits
-
-
-def load_outer_coef(copies, mine, theirs, place_of, coef):
-    waits = []
-    own_half = lax.rem(place_of[0], 2)
-    for source, half in ((mine, own_half), (theirs, 1 - own_half)):
+    for number, source in enumerate((pair.at[0], pair.at[1], other.at[0], other.at[1])):
+        array = jnp.bitwise_xor(place_of[0], number)
         for side in range(2):
-            first = 4 * ROWS + 16 + 16 * side + 8 * half
-            waits.append(copies.start(source.at[side], coef.at[pl.ds(first, 8), 0]))
+            first = 4 * ROWS + 2 * HALO * array + HALO * side
+            waits.append(copies.start(source.at[side], coef.at[pl.ds(first, HALO), 0]))
     return waits
 
 
 def middle_kernel(blocks, *refs):
     sources, refs = refs[:9], refs[9:]
-    own_coef, params = refs[:2]
-    outs, (*levels, partial, coef, sems) = refs[2:10], refs[10:]
+    own_coef, pair, other, params, place_of = refs[:5]
+    outs, (*levels, partial, coef, sems) = refs[5:13], refs[13:]
     copies = Copies(sems)
     places = ((0, -4), (0, 0), (0, 12), (0, 16), (1, 2), (1, 10), (2, 4), (2, 8), (3, 6))
     waits = [[] for _ in range(STEPS)]
@@ -263,7 +248,7 @@
         waits[level].append(
             copies.start(source.at[0:count], region(levels, level, row, blocks))
         )
-    waits[0] += load_coef(copies, own_coef, sources[0], sources[3], coef)
+    waits[0] += load_coef(copies, own_coef, pair, other, place_of, coef)
     sends = []
 
     def ready(level, low, high):
@@ -277,7 +262,7 @@
 
 def last_kernel(blocks, *refs):
     sources, refs = refs[:12], refs[12:]
-    own_coef, mine, theirs, params, place_of, cell_of, shift_of = refs[:7]
+    own_coef, pair, other, params, place_of, cell_of, shift_of = refs[:7]
     out, predicted, *levels, partial, coef, staged, sems, out_sems = refs[7:]
     copies = Copies(sems)
     places = (
@@ -290,8 +275,7 @@
         waits[level].append(
             copies.start(source.at[0:count], region(levels, level, row, blocks))
         )
-    waits[0] += load_coef(copies, own_coef, sources[1], sources[2], coef)
-    waits[0] += load_outer_coef(copies, mine, theirs, place_of, coef)
+    waits[0] += load_coef(copies, own_coef, pair, other, place_of, coef)
     edge_steps(6, blocks, waits, levels, partial, coef, params, lambda *_: None)
     for copy in waits[STEPS]:
         copy.wait()
@@ -331,20 +315,20 @@
                 ((ROWS + 2 * HALO) * columns // LANES, SUBLANES, LANES), jnp.float32
             ),
             pltpu.VMEM((GROUP, SUBLANES, columns), jnp.float32),
-            pltpu.VMEM((4 * ROWS + 48, 1, columns), jnp.float32),
+            pltpu.VMEM((4 * (ROWS + 2 * HALO), 1, columns), jnp.float32),
         ]
         + list(more)
     )
 
 
-def kernel_call(body, name, outs, specs, out_specs, scratches, cost, operands, limit=VMEM_LIMIT):
+def kernel_call(body, name, outs, specs, out_specs, scratches, cost, operands):
     return pl.pallas_call(
         body,
         out_shape=tuple(jax.ShapeDtypeStruct(shape, jnp.float32) for shape in outs),
         in_specs=specs,
         out_specs=out_specs,
         scratch_shapes=scratches,
-        compiler_params=pltpu.CompilerParams(vmem_limit_bytes=limit),
+        compiler_params=pltpu.CompilerParams(vmem_limit_bytes=TALL_LIMIT),
         cost_estimate=pl.CostEstimate(flops=0, bytes_accessed=cost * COST_BYTES, transcendentals=0),
         name=name,
     )(*operands)
@@ -358,20 +342,22 @@
     flat = tracer.reshape(members * rows, columns)
     dma = pltpu.SemaphoreType.DMA
     scratches = [pltpu.VMEM((blocks, members * rows, LANES), jnp.float32), dma((blocks,))]
-    up, down = kernel_call(
+    group, edge = (GROUP, members, columns), (HALO, columns)
+    up, down, up_coef, down_coef = kernel_call(
         functools.partial(outer_rows_kernel, blocks), "outer_rows",
-        [(GROUP + 2, members, columns)] * 2, [ANYWHERE, ANYWHERE, IN_SMEM], (IN_VMEM,) * 2,
-        scratches + [dma((12,))], 3, [flat, coefficients, place_of], TALL_LIMIT,
+        [group, group, edge, edge], [ANYWHERE, ANYWHERE, IN_SMEM],
+        (IN_VMEM, IN_VMEM, ANYWHERE, ANYWHERE),
+        scratches + [dma((2,))], 3, [flat, coefficients, place_of],
     )
     low, high = kernel_call(
         functools.partial(inner_rows_kernel, blocks), "inner_rows",
-        [(GROUP, members, columns)] * 2, [ANYWHERE, ANYWHERE], (IN_VMEM,) * 2,
-        scratches, 3, [flat, up], TALL_LIMIT,
-    )
-    return down, low, high, up
-
-
-def transport(shape, own, low0, high0, own_coef, params, place_of, obs_index, halos, other_core):
+        [group] * 2, [ANYWHERE, ANYWHERE], (IN_VMEM,) * 2,
+        scratches, 3, [flat, up],
+    )
+    return (down, low, high, up), (up_coef, down_coef)
+
+
+def transport(shape, own, low0, high0, own_coef, pair, other, params, place_of, obs_index, halos):
     members, rows, columns = shape
     blocks = columns // LANES
     group = (GROUP, members, columns)
@@ -390,12 +376,10 @@
     low1, high1 = halos(upper, lower)
     first = kernel_call(
         functools.partial(middle_kernel, blocks), "edge_first",
-        [group] * 6 + [cells] * 2, [ANYWHERE] * 10 + [IN_VMEM], (ANYWHERE,) * 8,
-        scratch(columns, dma((26,))), 10,
-        [low0, own[0], own[3], high0, *inner, own_coef, params],
-    )
-    mine, _ = lax.optimization_barrier((jnp.stack([low0[GROUP + 1], high0[GROUP + 1]]), first[0]))
-    theirs = other_core(mine)
+        [group] * 6 + [cells] * 2, [ANYWHERE] * 12 + [IN_VMEM, IN_SMEM], (ANYWHERE,) * 8,
+        scratch(columns, dma((29,))), 10,
+        [low0, own[0], own[3], high0, *inner, own_coef, pair, other, params, place_of],
+    )
     cell_of = obs_index // LANES + HALO * blocks
     lane_of = obs_index % LANES
     shift_of = (jnp.arange(obs_index.shape[0], dtype=jnp.int32) - lane_of) % LANES
@@ -404,9 +388,9 @@
         [flat, (members, obs_index.shape[0])],
         [ANYWHERE] * 15 + [IN_VMEM] + [IN_SMEM] * 3, (ANYWHERE, IN_VMEM),
         scratch(columns, staged, dma((29,)), dma((blocks,))), 15,
-        [low1, low0, high0, high1, *first, own_coef, mine, theirs, params, place_of, cell_of, shift_of],
-    )
-    return field.reshape(shape), predicted
+        [low1, low0, high0, high1, *first, own_coef, pair, other, params, place_of, cell_of, shift_of],
+    )
+    return field.reshape(shape), predicted, inner[0]
 
 
 def products_kernel(total_obs, per_group, spread, everyone, own, values, variance, same, out):
@@ -465,20 +449,19 @@
     forward = [(i, i + 1) for i in range(slab_count - 1)]
     backward = [(target, source) for source, target in forward]
 
+    def over_ens(mine):
+        pair = jnp.stack([mine, lax.ppermute(mine, "ens", [(i, i ^ 1) for i in range(ens_count)])])
+        return pair, lax.ppermute(pair, "ens", [(i, i ^ 2) for i in range(ens_count)])
+
     def halos(upper, lower):
         return lax.ppermute(upper, "slab", forward), lax.ppermute(lower, "slab", backward)
 
     place_of = jnp.reshape(ens_pos, (1,))
-    own = row_groups(tracer, coefficients, place_of)
+    own, coef_edges = row_groups(tracer, coefficients, place_of)
     low0, high0 = halos(own[3], own[0])
 
-    later, _ = lax.optimization_barrier((parameters, own[1]))
-    pair = jnp.stack([later, lax.ppermute(later, "ens", [(i, i ^ 1) for i in range(ens_count)])])
-    other = lax.ppermute(pair, "ens", [(i, i ^ 2) for i in range(ens_count)])
-    shared = jnp.concatenate([pair, other], axis=0)
-
-    def other_core(mine):
-        return lax.ppermute(mine, "ens", [(i, i ^ 1) for i in range(ens_count)])
+    edge_low, edge_high = halos(*coef_edges)
+    pair, other = over_ens(jnp.stack([edge_low, edge_high]))
 
     members = member_group.shape[0]
     per_group = members // GROUPS
@@ -488,15 +471,17 @@
     earlier = jnp.arange(members)[None, :] < jnp.arange(members)[:, None]
     rank = jnp.sum((same_bool & earlier).astype(jnp.int32), axis=1)
     own_same = lax.dynamic_slice_in_dim(same, ens_pos * local_members, local_members, 1)
-    field, predicted = transport(
+    field, predicted, first_done = transport(
         tracer.shape, own, low0, high0,
-        coefficients, parameters, place_of, obs_index, halos, other_core,
-    )
+        coefficients, pair, other, parameters, place_of, obs_index, halos,
+    )
+
+    later, _ = lax.optimization_barrier((parameters, first_done))
+    shared = jnp.concatenate(over_ens(later), axis=0)
     all_params = jnp.concatenate(
         [lax.dynamic_index_in_dim(shared, ens_pos ^ i, 0, False) for i in range(ens_count)], axis=0
     )
     param_anomalies = (all_params - hdot(same, all_params) / per_group) * spread
-
     everyone = lax.all_gather(predicted, "ens", axis=0, tiled=True)
     total_obs = obs_variance.shape[0] * slab_count
     products = pl.pallas_call(

time: 126 us -> 123 us (0.976)
  Pallas kernels: 55.7 us -> 71 us
  local copies, waits for them, and re-layouts: 16.1 us -> 1.89 us
  waiting for transfers between devices: 20.9 us -> 8.37 us
  starting transfers between devices: 23.3 us -> 30.8 us
    ppermute x2 -> x3, waiting for transfers between devices: 17.2 us -> 0.8 us  [halos(): lax.ppermute(upper, 'slab', forward)]
    pallas_call x5, Pallas kernels: 52.9 us -> 68.3 us  [kernel_call(): pl.pallas_call(body, out_shape=tuple((jax.ShapeDtypeStruct(shape, jnp.flo...]
    unnamed x52 -> x26, local copies, waits for them, and re-layouts: 15.9 us -> 1.7 us
    ppermute x2 -> x3, starting transfers between devices: 10.1 us -> 15.4 us  [halos(): lax.ppermute(upper, 'slab', forward)]
    ppermute x3 -> x4, waiting for transfers between devices: 0.01 us -> 3.88 us  [the longest x2 3.4 us: over_ens(): lax.ppermute(pair, 'ens', [(i, i ^ 2) for i in range(ens_count)])]
    ppermute x3 -> x4, starting transfers between devices: 1.59 us -> 3.73 us  [the longest x2 3.12 us: over_ens(): lax.ppermute(pair, 'ens', [(i, i ^ 2) for i in range(ens_count)])]
    ppermute x2 -> x3, starting transfers between devices: 2.75 us -> 3.86 us  [halos(): lax.ppermute(lower, 'slab', backward)]
  transfers between devices with their start and end apart: 10 -> 13, of which waited for: 4 -> 6; matrix products, arithmetic and copies ran while one was open for 2% -> 3% of each run, Pallas kernels for 40% -> 48%
where the time goes in v4:
time: 123 us; the launch traced here: 122 us
  Pallas kernels  71 us (58%)
  starting transfers between devices  30.8 us (25%)
  waiting for transfers between devices  8.37 us (7%)
  blocking collectives  6 us (5%)
  other arithmetic  2.67 us (2%)
  local copies, waits for them, and re-layouts  1.89 us (2%)
    pallas_call x5, Pallas kernels, kernel_call(): pl.pallas_call(body, out_shape=tuple((jax.ShapeDtypeStruct(shape, jnp.flo...  68.3 us
    ppermute x3, starting transfers between devices, halos(): lax.ppermute(upper, 'slab', forward)  15.4 us
    ppermute x3, starting transfers between devices, local(): products = products + lax.ppermute(products, 'slab', pairs)  7.8 us
    all_gather x1, blocking collectives, local(): everyone = lax.all_gather(predicted, 'ens', axis=0, tiled=True)  6 us
    ppermute x3, starting transfers between devices, halos(): lax.ppermute(lower, 'slab', backward)  3.86 us
    ppermute x3, waiting for transfers between devices, local(): products = products + lax.ppermute(products, 'slab', pairs)  3.68 us
    ppermute x2, waiting for transfers between devices, over_ens(): lax.ppermute(pair, 'ens', [(i, i ^ 2) for i in range(ens_count)])  3.4 us
    ppermute x2, starting transfers between devices, over_ens(): lax.ppermute(pair, 'ens', [(i, i ^ 2) for i in range(ens_count)])  3.12 us
  transfers between devices with their start and end apart: 13, of which 6 were waited for; matrix products, arithmetic and copies ran while one was open for 3% of the time, Pallas kernels for 48%

profile of v4, /device:TPU:0, one launch (start us, length us, event | category | flops | bytes accessed | tf_op | source)
XLA Modules:
  0.0 122.1 jit_solution(8424802425066168422)
XLA Ops:
  0.6 10.3 %outer_rows.1 = (f32[4,8,4096]{2,1,0:T(8,128)}, f32[4,8,4096]{2,1,0:T(8,128)}, f32[8,4096]{1,0:T(8,128)}, f32[8,4096]{1,0:T(8,128)}) custom-call(f32[128,4096]{1,0:T(8,128)} %bitcast.28, f32[4,16,4096]{2,1,0:T(8,128)} %refs_12_.3, s32[1]{0:T(128)} %bitcast.1.place_of.refs_13_.refs_16_), custom_call_target="tpu_custom_call" | custom-call | bytes 600000 | tf_op jit(solution)/shard_map/outer_rows/pallas_call | solution.py:325
  11.0 1.3 %collective-permute-start.5 = (f32[8,4096]{1,0:T(8,128)}, f32[8,4096]{1,0:T(8,128)S(1)}, u32[]{:S(2)}, u32[]{:S(2)}) collective-permute-start(f32[8,4096]{1,0:T(8,128)} %get-tuple-element.42), channel_id=1, source_target_pairs={{1,0},{2,1},{3,2},{4,3},{5,4},{6,5},{7,6},{9,8},{10,9},{11,10},{12... | collective-permute-start | bytes 393224 | tf_op jit(solution)/shard_map/ppermute | solution.py:457
  12.3 5.5 %collective-permute-start.4 = (f32[8,4096]{1,0:T(8,128)}, f32[8,4096]{1,0:T(8,128)S(1)}, u32[]{:S(2)}, u32[]{:S(2)}) collective-permute-start(f32[8,4096]{1,0:T(8,128)} %get-tuple-element.41), channel_id=1, source_target_pairs={{0,1},{1,2},{2,3},{3,4},{4,5},{5,6},{6,7},{8,9},{9,10},{10,11},{11... | collective-permute-start | bytes 393224 | tf_op jit(solution)/shard_map/ppermute | solution.py:457
  17.8 4.8 %collective-permute-start = (f32[4,8,4096]{2,1,0:T(8,128)}, f32[4,8,4096]{2,1,0:T(8,128)S(1)}, u32[]{:S(2)}, u32[]{:S(2)}) collective-permute-start(f32[4,8,4096]{2,1,0:T(8,128)} %get-tuple-element.28.outer.own3.refs_2_), channel_id=1, source_target_pairs={{0,1},{1,2},{2,3},{3,4},{4,5},{5,6},{6,7},{8,9},{9,10},{10,11},{11... | collective-permute-start | bytes 1572872 | tf_op jit(solution)/shard_map/ppermute | solution.py:457
  22.6 1.3 %collective-permute-start.1 = (f32[4,8,4096]{2,1,0:T(8,128)}, f32[4,8,4096]{2,1,0:T(8,128)S(1)}, u32[]{:S(2)}, u32[]{:S(2)}) collective-permute-start(f32[4,8,4096]{2,1,0:T(8,128)} %get-tuple-element.31.own0.refs_1_), channel_id=1, source_target_pairs={{1,0},{2,1},{3,2},{4,3},{5,4},{6,5},{7,6},{9,8},{10,9},{11,10},{12... | collective-permute-start | bytes 1572872 | tf_op jit(solution)/shard_map/ppermute | solution.py:457
  23.9 2.9 %inner_rows.1 = (f32[4,8,4096]{2,1,0:T(8,128)}, f32[4,8,4096]{2,1,0:T(8,128)}) custom-call(f32[128,4096]{1,0:T(8,128)} %bitcast.29, f32[4,8,4096]{2,1,0:T(8,128)} %get-tuple-element.28.outer.own3.refs_2_), custom_call_target="tpu_custom_call" | custom-call | bytes 600000 | tf_op jit(solution)/shard_map/inner_rows/pallas_call | solution.py:325
  26.9 0.0 copy-start
  26.9 0.0 copy-start.11
  26.9 0.0 copy-start.12
  26.9 0.0 copy-start.10
  26.9 0.0 copy-start.9
  26.9 13.8 %interior.1 = (f32[4,8,4096]{2,1,0:T(8,128)}, f32[4,8,4096]{2,1,0:T(8,128)}, f32[4,8,4096]{2,1,0:T(8,128)}, f32[4,8,4096]{2,1,0:T(8,128)}, f32[4,8,4096]{2,1,0:T(8,128)}) custom-call(f32[4,8,4096]{2,1,0:T(8,128)} %get-tuple-element.31.own0.refs_1_, f32[4,8,4096]{2,1,0:T(8,128)} %get-tuple-element.36.own1, f32[4,8,4096]{2,1,0:T(8,128)} %get-tuple-element.33.own2, ...), custom_call_target="tpu_custom_call" | custom-call | bytes 1600000 | tf_op jit(solution)/shard_map/interior/pallas_call | solution.py:325
  40.7 0.0 copy-done
  40.8 0.1 collective-permute-start.11
  40.8 0.0 collective-permute-done.5
  40.8 0.0 collective-permute-done.4
  40.9 0.5 collective-permute-start.6
  41.4 0.0 copy-done.11
  41.4 0.6 add_select_fusion
  42.1 0.0 copy-done.12
  42.1 0.1 compare_convert_fusion.same
  42.1 0.5 collective-permute-done.6
  42.6 0.0 copy-start.5
  42.7 1.6 %collective-permute-start.7 = (f32[2,2,8,4096]{3,2,1,0:T(8,128)S(1)}, f32[2,2,8,4096]{3,2,1,0:T(8,128)S(1)}, u32[]{:S(2)}, u32[]{:S(2)}) collective-permute-start(f32[2,2,8,4096]{3,2,1,0:T(8,128)S(1)} %pad_maximum_fusion.refs_10_.refs_13_), channel_id=1, source_target_pairs={{0,16},{8,24},{16,0},{24,8},{1,17},{9,25},{17,1},{25,9},{2,18},{10... | collective-permute-start | bytes 1572872 | tf_op jit(solution)/shard_map/ppermute | solution.py:454
  44.3 0.8 collective-permute-done.refs_0_.refs_1_
  45.1 0.0 collective-permute-done.1.refs_3_.refs_2_
  45.1 0.0 copy-done.10
  45.1 5.1 %collective-permute-start.2 = (f32[4,8,4096]{2,1,0:T(8,128)S(1)}, f32[4,8,4096]{2,1,0:T(8,128)}, u32[]{:S(2)}, u32[]{:S(2)}) collective-permute-start(f32[4,8,4096]{2,1,0:T(8,128)S(1)} %copy-done.10), channel_id=1, source_target_pairs={{0,1},{1,2},{2,3},{3,4},{4,5},{5,6},{6,7},{8,9},{9,10},{10,11},{11... | collective-permute-start | bytes 1572872 | tf_op jit(solution)/shard_map/ppermute | solution.py:457
  50.2 0.0 copy-done.9
  50.2 1.3 %collective-permute-start.3 = (f32[4,8,4096]{2,1,0:T(8,128)S(1)}, f32[4,8,4096]{2,1,0:T(8,128)}, u32[]{:S(2)}, u32[]{:S(2)}) collective-permute-start(f32[4,8,4096]{2,1,0:T(8,128)S(1)} %copy-done.9), channel_id=1, source_target_pairs={{1,0},{2,1},{3,2},{4,3},{5,4},{6,5},{7,6},{9,8},{10,9},{11,10},{12... | collective-permute-start | bytes 1572872 | tf_op jit(solution)/shard_map/ppermute | solution.py:457
  51.5 0.0 collective-permute-done.11
  51.5 0.7 pad_maximum_fusion.3
  52.2 1.5 %collective-permute-start.12 = (f32[2,8,4096]{2,1,0:T(8,128)}, f32[2,8,4096]{2,1,0:T(8,128)}, u32[]{:S(2)}, u32[]{:S(2)}) collective-permute-start(f32[2,8,4096]{2,1,0:T(8,128)} %pad_maximum_fusion.3), channel_id=1, source_target_pairs={{0,16},{8,24},{16,0},{24,8},{1,17},{9,25},{17,1},{25,9},{2,18},{10... | collective-permute-start | bytes 786440 | tf_op jit(solution)/shard_map/ppermute | solution.py:454
  53.7 0.2 convert_reduce_fusion
  53.9 0.1 copy.9.rank_col
  54.0 0.1 constant_dynamic-slice_fusion.own_same
  54.1 3.4 %collective-permute-done.7.refs_11_.refs_14_ = f32[2,2,8,4096]{3,2,1,0:T(8,128)S(1)} collective-permute-done((f32[2,2,8,4096]{3,2,1,0:T(8,128)S(1)}, f32[2,2,8,4096]{3,2,1,0:T(8,128)S(1)}, u32[]{:S(2)}, u32[]{:S(2)}) %collective-permute-start.7) | collective-permute-done | bytes 524320 | tf_op jit(solution)/shard_map/ppermute | solution.py:454
  57.5 0.0 copy-done.5
  57.5 0.0 copy-done.6
  57.5 0.0 copy-done.7
  57.5 0.8 copy-done.8
  58.3 17.7 %edge_first.1 = (f32[4,8,4096]{2,1,0:T(8,128)}, f32[4,8,4096]{2,1,0:T(8,128)}, f32[4,8,4096]{2,1,0:T(8,128)}, f32[4,8,4096]{2,1,0:T(8,128)}, f32[4,8,4096]{2,1,0...) custom-call(f32[4,8,4096]{2,1,0:T(8,128)} %copy-done.6, ...), custom_call_target="tpu_custom_call" | custom-call | bytes 2000000 | tf_op jit(solution)/shard_map/edge_first/pallas_call | solution.py:325
  76.0 0.0 collective-permute-done.2.refs_0_
  76.0 0.0 collective-permute-done.3.refs_3_
  76.0 0.0 copy-start.3
  76.0 0.0 copy-start.4
  76.0 0.0 copy-start.1
  76.0 23.5 %edge_last.1 = (f32[128,4096]{1,0:T(8,128)}, f32[8,2048]{1,0:T(8,128)}) custom-call(f32[4,8,4096]{2,1,0:T(8,128)} %collective-permute-done.2.refs_0_, f32[4,8,4096]{2,1,0:T(8,128)} %copy-done.6, f32[4,8,4096]{2,1,0:T(8,128)} %copy-done.7, f32[4,8,4096]{2,1,0:T(8,128)} %collective-permute-done.3.refs_3_, f32[4,8,4096]{2,1,0:T(8,128)} %get-tuple-element.43.refs_4_, ...), custom_call_target="tpu_custom_call" | custom-call | bytes 3000000 | tf_op jit(solution)/shard_map/edge_last/pallas_call | solution.py:325
  99.6 6.0 %all_gather.3.everyone = f32[32,2048]{1,0:T(8,128)S(1)} all-gather(f32[8,2048]{1,0:T(8,128)} %get-tuple-element.52.own), channel_id=1, replica_groups=mesh['ens'=4,'slab'=8] {'ens'}, dimensions={0}, use_global_device_ids=true | all-gather | bytes 327680 | tf_op jit(solution)/shard_map/all_gather | solution.py:485
  105.6 0.0 copy-done.3
  105.6 0.0 copy-done.4
  105.6 0.8 copy-done.2
  106.4 0.6 products.1
  107.0 2.7 %collective-permute-start.8 = (f32[32,40]{1,0:T(8,128)S(1)}, f32[32,40]{1,0:T(8,128)S(1)}, u32[]{:S(2)}, u32[]{:S(2)}) collective-permute-start(f32[32,40]{1,0:T(8,128)S(1)} %products.1), channel_id=1, source_target_pairs={{0,1},{1,0},{2,3},{3,2},{4,5},{5,4},{6,7},{7,6},{8,9},{9,8},{10,11... | collective-permute-start | bytes 15368 | tf_op jit(solution)/shard_map/ppermute | solution.py:496
  109.7 0.0 collective-permute-done.12
  109.7 0.0 copy-done.1
  109.7 1.0 pad_maximum_fusion.1
  110.7 0.7 collective-permute-done.8
  111.5 2.1 %collective-permute-start.9 = (f32[32,40]{1,0:T(8,128)S(1)}, f32[32,40]{1,0:T(8,128)S(1)}, u32[]{:S(2)}, u32[]{:S(2)}) collective-permute-start(f32[32,40]{1,0:T(8,128)S(1)} %add.46), channel_id=1, source_target_pairs={{0,2},{1,3},{2,0},{3,1},{4,6},{5,7},{6,4},{7,5},{8,10},{9,11},{10,... | collective-permute-start | bytes 15368 | tf_op jit(solution)/shard_map/ppermute | solution.py:496
  113.6 1.7 %collective-permute-done.9 = f32[32,40]{1,0:T(8,128)S(1)} collective-permute-done((f32[32,40]{1,0:T(8,128)S(1)}, f32[32,40]{1,0:T(8,128)S(1)}, u32[]{:S(2)}, u32[]{:S(2)}) %collective-permute-start.9) | collective-permute-done | bytes 5152 | tf_op jit(solution)/shard_map/ppermute | solution.py:496
  115.3 3.0 %collective-permute-start.10 = (f32[32,40]{1,0:T(8,128)S(1)}, f32[32,40]{1,0:T(8,128)S(1)}, u32[]{:S(2)}, u32[]{:S(2)}) collective-permute-start(f32[32,40]{1,0:T(8,128)S(1)} %add.47), channel_id=1, source_target_pairs={{0,4},{1,5},{2,6},{3,7},{4,0},{5,1},{6,2},{7,3},{8,12},{9,13},{10,... | collective-permute-start | bytes 15368 | tf_op jit(solution)/shard_map/ppermute | solution.py:496
  118.3 0.4 fusion.1.anomalies
  118.7 1.3 %collective-permute-done.10 = f32[32,40]{1,0:T(8,128)S(1)} collective-permute-done((f32[32,40]{1,0:T(8,128)S(1)}, f32[32,40]{1,0:T(8,128)S(1)}, u32[]{:S(2)}, u32[]{:S(2)}) %collective-permute-start.10) | collective-permute-done | bytes 5152 | tf_op jit(solution)/shard_map/ppermute | solution.py:496
  120.0 2.1 %update.1 = f32[8,4096]{1,0:T(8,128)} custom-call(f32[1,32,40]{2,1,0:T(8,128)S(1)} %add_bitcast_fusion.summands, f32[32,32]{1,0:T(8,128)S(1)} %compare_convert_fusion.same, f32[32,8]{1,0:T(8,128)S(1)} %constant_dynamic-slice_fusion.own_same, s32[1,32]{1,0:T(1,128)S(1)} %bitcast.27, s32[32,1]{1,0:T(8,128)S(1)} %copy.9.rank_col, ...), custom_call_target="tpu_custom_call" | custom-call | tf_op jit(solution)/shard_map/update/pallas_call | solution.py:498
  (10 shorter events, 0.1 us)
Async XLA Ops:
  11.0 29.9 %collective-permute-start.5 = (f32[8,4096]{1,0:T(8,128)}, f32[8,4096]{1,0:T(8,128)S(1)}, u32[]{:S(2)}, u32[]{:S(2)}) collective-permute-start(f32[8,4096]{1,0:T(8,128)} %get-tuple-element.42), channel_id=1, source_target_pairs={{1,0},{2,1},{3,2},{4,3},{5,4},{6,5},{7,6},{9,8},{10,9},{11,10},{12... | collective-permute-start | bytes 393224 | tf_op jit(solution)/shard_map/ppermute | solution.py:457
  12.3 28.6 %collective-permute-start.4 = (f32[8,4096]{1,0:T(8,128)}, f32[8,4096]{1,0:T(8,128)S(1)}, u32[]{:S(2)}, u32[]{:S(2)}) collective-permute-start(f32[8,4096]{1,0:T(8,128)} %get-tuple-element.41), channel_id=1, source_target_pairs={{0,1},{1,2},{2,3},{3,4},{4,5},{5,6},{6,7},{8,9},{9,10},{10,11},{11... | collective-permute-start | bytes 393224 | tf_op jit(solution)/shard_map/ppermute | solution.py:457
  17.8 27.3 %collective-permute-start = (f32[4,8,4096]{2,1,0:T(8,128)}, f32[4,8,4096]{2,1,0:T(8,128)S(1)}, u32[]{:S(2)}, u32[]{:S(2)}) collective-permute-start(f32[4,8,4096]{2,1,0:T(8,128)} %get-tuple-element.28.outer.own3.refs_2_), channel_id=1, source_target_pairs={{0,1},{1,2},{2,3},{3,4},{4,5},{5,6},{6,7},{8,9},{9,10},{10,11},{11... | collective-permute-start | bytes 1572872 | tf_op jit(solution)/shard_map/ppermute | solution.py:457
  22.6 22.4 %collective-permute-start.1 = (f32[4,8,4096]{2,1,0:T(8,128)}, f32[4,8,4096]{2,1,0:T(8,128)S(1)}, u32[]{:S(2)}, u32[]{:S(2)}) collective-permute-start(f32[4,8,4096]{2,1,0:T(8,128)} %get-tuple-element.31.own0.refs_1_), channel_id=1, source_target_pairs={{1,0},{2,1},{3,2},{4,3},{5,4},{6,5},{7,6},{9,8},{10,9},{11,10},{12... | collective-permute-start | bytes 1572872 | tf_op jit(solution)/shard_map/ppermute | solution.py:457
  26.9 13.9 %copy-start = (f32[8,4096]{1,0:T(8,128)S(1)}, f32[8,4096]{1,0:T(8,128)}, u32[]{:S(2)}) copy-start(f32[8,4096]{1,0:T(8,128)} %own.1) | copy-start | bytes 393220
  26.9 14.6 %copy-start.11 = (s32[2048]{0:T(1024)S(1)}, s32[2048]{0:T(1024)}, u32[]{:S(2)}) copy-start(s32[2048]{0:T(1024)} %param.10) | copy-start | bytes 24580
  26.9 15.2 %copy-start.12 = (s32[32]{0:T(128)S(1)}, s32[32]{0:T(128)}, u32[]{:S(2)}) copy-start(s32[32]{0:T(128)} %param.13) | copy-start | bytes 388
  26.9 18.2 %copy-start.10 = (f32[4,8,4096]{2,1,0:T(8,128)S(1)}, f32[4,8,4096]{2,1,0:T(8,128)}, u32[]{:S(2)}) copy-start(f32[4,8,4096]{2,1,0:T(8,128)} %get-tuple-element.33.own2) | copy-start | bytes 1572868
  26.9 23.3 %copy-start.9 = (f32[4,8,4096]{2,1,0:T(8,128)S(1)}, f32[4,8,4096]{2,1,0:T(8,128)}, u32[]{:S(2)}) copy-start(f32[4,8,4096]{2,1,0:T(8,128)} %get-tuple-element.36.own1) | copy-start | bytes 1572868
  40.8 10.7 %collective-permute-start.11 = (f32[8,4096]{1,0:T(8,128)S(1)}, f32[8,4096]{1,0:T(8,128)S(1)}, u32[]{:S(2)}, u32[]{:S(2)}) collective-permute-start(f32[8,4096]{1,0:T(8,128)S(1)} %copy-done), channel_id=1, source_target_pairs={{0,8},{8,0},{16,24},{24,16},{1,9},{9,1},{17,25},{25,17},{2,10},{10... | collective-permute-start | bytes 393224 | tf_op jit(solution)/shard_map/ppermute | solution.py:453
  40.9 1.7 %collective-permute-start.6 = (f32[2,8,4096]{2,1,0:T(8,128)S(1)}, f32[2,8,4096]{2,1,0:T(8,128)S(1)}, u32[]{:S(2)}, u32[]{:S(2)}) collective-permute-start(f32[2,8,4096]{2,1,0:T(8,128)S(1)} %get-tuple-element.59), channel_id=1, source_target_pairs={{0,8},{8,0},{16,24},{24,16},{1,9},{9,1},{17,25},{25,17},{2,10},{10... | collective-permute-start | bytes 786440 | tf_op jit(solution)/shard_map/ppermute | solution.py:453
  42.6 14.8 %copy-start.5 = (f32[2,2,8,4096]{3,2,1,0:T(8,128)}, f32[2,2,8,4096]{3,2,1,0:T(8,128)S(1)}, u32[]{:S(2)}) copy-start(f32[2,2,8,4096]{3,2,1,0:T(8,128)S(1)} %pad_maximum_fusion.refs_10_.refs_13_) | copy-start | bytes 1572868
  42.7 14.8 %collective-permute-start.7 = (f32[2,2,8,4096]{3,2,1,0:T(8,128)S(1)}, f32[2,2,8,4096]{3,2,1,0:T(8,128)S(1)}, u32[]{:S(2)}, u32[]{:S(2)}) collective-permute-start(f32[2,2,8,4096]{3,2,1,0:T(8,128)S(1)} %pad_maximum_fusion.refs_10_.refs_13_), channel_id=1, source_target_pairs={{0,16},{8,24},{16,0},{24,8},{1,17},{9,25},{17,1},{25,9},{2,18},{10... | collective-permute-start | bytes 1572872 | tf_op jit(solution)/shard_map/ppermute | solution.py:454
  45.1 12.4 %copy-start.6 = (f32[4,8,4096]{2,1,0:T(8,128)}, f32[4,8,4096]{2,1,0:T(8,128)S(1)}, u32[]{:S(2)}) copy-start(f32[4,8,4096]{2,1,0:T(8,128)S(1)} %collective-permute-done.refs_0_.refs_1_) | copy-start | bytes 1572868
  45.1 12.4 %copy-start.7 = (f32[4,8,4096]{2,1,0:T(8,128)}, f32[4,8,4096]{2,1,0:T(8,128)S(1)}, u32[]{:S(2)}) copy-start(f32[4,8,4096]{2,1,0:T(8,128)S(1)} %collective-permute-done.1.refs_3_.refs_2_) | copy-start | bytes 1572868
  45.1 30.9 %collective-permute-start.2 = (f32[4,8,4096]{2,1,0:T(8,128)S(1)}, f32[4,8,4096]{2,1,0:T(8,128)}, u32[]{:S(2)}, u32[]{:S(2)}) collective-permute-start(f32[4,8,4096]{2,1,0:T(8,128)S(1)} %copy-done.10), channel_id=1, source_target_pairs={{0,1},{1,2},{2,3},{3,4},{4,5},{5,6},{6,7},{8,9},{9,10},{10,11},{11... | collective-permute-start | bytes 1572872 | tf_op jit(solution)/shard_map/ppermute | solution.py:457
  50.2 25.8 %collective-permute-start.3 = (f32[4,8,4096]{2,1,0:T(8,128)S(1)}, f32[4,8,4096]{2,1,0:T(8,128)}, u32[]{:S(2)}, u32[]{:S(2)}) collective-permute-start(f32[4,8,4096]{2,1,0:T(8,128)S(1)} %copy-done.9), channel_id=1, source_target_pairs={{1,0},{2,1},{3,2},{4,3},{5,4},{6,5},{7,6},{9,8},{10,9},{11,10},{12... | collective-permute-start | bytes 1572872 | tf_op jit(solution)/shard_map/ppermute | solution.py:457
  52.2 57.5 %collective-permute-start.12 = (f32[2,8,4096]{2,1,0:T(8,128)}, f32[2,8,4096]{2,1,0:T(8,128)}, u32[]{:S(2)}, u32[]{:S(2)}) collective-permute-start(f32[2,8,4096]{2,1,0:T(8,128)} %pad_maximum_fusion.3), channel_id=1, source_target_pairs={{0,16},{8,24},{16,0},{24,8},{1,17},{9,25},{17,1},{25,9},{2,18},{10... | collective-permute-start | bytes 786440 | tf_op jit(solution)/shard_map/ppermute | solution.py:454
  57.5 0.8 copy-start.8
  76.0 29.6 %copy-start.3 = (f32[8,2048]{1,0:T(8,128)S(1)}, f32[8,2048]{1,0:T(8,128)}, u32[]{:S(2)}) copy-start(f32[8,2048]{1,0:T(8,128)} %values.1) | copy-start | bytes 196612
  76.0 29.6 %copy-start.4 = (f32[2048]{0:T(1024)S(1)}, f32[2048]{0:T(1024)}, u32[]{:S(2)}) copy-start(f32[2048]{0:T(1024)} %param.12) | copy-start | bytes 24580
  76.0 33.7 %copy-start.1 = (f32[8,4096]{1,0:T(8,128)S(1)}, f32[8,4096]{1,0:T(8,128)}, u32[]{:S(2)}) copy-start(f32[8,4096]{1,0:T(8,128)} %own.1) | copy-start | bytes 393220
  105.6 0.8 copy-start.2
  107.0 4.4 %collective-permute-start.8 = (f32[32,40]{1,0:T(8,128)S(1)}, f32[32,40]{1,0:T(8,128)S(1)}, u32[]{:S(2)}, u32[]{:S(2)}) collective-permute-start(f32[32,40]{1,0:T(8,128)S(1)} %products.1), channel_id=1, source_target_pairs={{0,1},{1,0},{2,3},{3,2},{4,5},{5,4},{6,7},{7,6},{8,9},{9,8},{10,11... | collective-permute-start | bytes 15368 | tf_op jit(solution)/shard_map/ppermute | solution.py:496
  111.5 3.8 %collective-permute-start.9 = (f32[32,40]{1,0:T(8,128)S(1)}, f32[32,40]{1,0:T(8,128)S(1)}, u32[]{:S(2)}, u32[]{:S(2)}) collective-permute-start(f32[32,40]{1,0:T(8,128)S(1)} %add.46), channel_id=1, source_target_pairs={{0,2},{1,3},{2,0},{3,1},{4,6},{5,7},{6,4},{7,5},{8,10},{9,11},{10,... | collective-permute-start | bytes 15368 | tf_op jit(solution)/shard_map/ppermute | solution.py:496
  115.3 4.8 %collective-permute-start.10 = (f32[32,40]{1,0:T(8,128)S(1)}, f32[32,40]{1,0:T(8,128)S(1)}, u32[]{:S(2)}, u32[]{:S(2)}) collective-permute-start(f32[32,40]{1,0:T(8,128)S(1)} %add.47), channel_id=1, source_target_pairs={{0,4},{1,5},{2,6},{3,7},{4,0},{5,1},{6,2},{7,3},{8,12},{9,13},{10,... | collective-permute-start | bytes 15368 | tf_op jit(solution)/shard_map/ppermute | solution.py:496

commit v5 on v4

--- a/solution.py
+++ b/solution.py
@@ -16,8 +16,6 @@
 ROWS = 16
 GROUP = 4
 LAG = 3
-WIDE = 8
-TOGETHER = 2
 VMEM_LIMIT = 16 * 1024 * 1024
 TALL_LIMIT = 58 * 1024 * 1024
 COST_BYTES = 200000
@@ -42,46 +40,44 @@
     return jnp.broadcast_to(row, (SUBLANES, LANES))
 
 
-def columns_pass(source, first_row, count, target, target_row, coef, params, blocks):
+def columns_pass(source, row, target, target_row, coef, params, blocks):
     lane = lax.broadcasted_iota(jnp.int32, (SUBLANES, LANES), 1)
     first, last = lane == 0, lane == LANES - 1
-    places = [[coef_row(array, first_row + i) for array in range(4)] for i in range(count)]
+    places = [coef_row(array, row) for array in range(4)]
     c, c_rolled, d, d_rolled, slope, twice, left, right, laplace = ({} for _ in range(9))
     for tick in range(blocks + 2 * LAG + 4):
-        for i in range(count):
-            row = first_row + i
-            b = tick - 1
-            if b <= blocks:
-                c[i, b] = source[row, :, block_at(b % blocks)]
-                c_rolled[i, b] = pltpu.roll(c[i, b], LANES - 1, 1)
-            b = tick - 2
-            if -1 <= b <= blocks:
-                c_next = c_rolled[i, b]
-                if b < blocks:
-                    c_next = jnp.where(last, c_rolled[i, b + 1], c_next)
-                d[i, b] = c_next - c[i, b]
-                d_rolled[i, b] = pltpu.roll(d[i, b], 1, 1)
-            b = tick - 2 - LAG
-            if -1 <= b <= blocks:
-                d_back = d_rolled[i, b]
-                if b >= 0:
-                    d_back = jnp.where(first, d_rolled[i, b - 1], d_back)
-                slope[i, b] = limited(d_back, d[i, b])
-                twice[i, b] = d[i, b] + d[i, b]
-                laplace[i, b] = d[i, b] - d_back
-                left[i, b] = pltpu.roll(twice[i, b] - slope[i, b], 1, 1)
-                right[i, b] = pltpu.roll(slope[i, b], LANES - 1, 1)
-            b = tick - 3 - 2 * LAG
-            if 0 <= b < blocks:
-                at = block_at(b)
-                speed = wide(coef[places[i][1], :, at])
-                forward = jnp.where(first, left[i, b - 1], left[i, b])
-                backward = twice[i, b] - jnp.where(last, right[i, b + 1], right[i, b])
-                change = jnp.where(speed > 0.0, forward, backward) + slope[i, b]
-                value = c[i, b] - (0.5 * speed) * change
-                value = value + wide(coef[places[i][2], :, at]) * laplace[i, b]
-                value = value + params[:, at] * wide(coef[places[i][3], :, at])
-                target[target_row + i, :, at] = value
+        b = tick - 1
+        if b <= blocks:
+            c[b] = source[row, :, block_at(b % blocks)]
+            c_rolled[b] = pltpu.roll(c[b], LANES - 1, 1)
+        b = tick - 2
+        if -1 <= b <= blocks:
+            c_next = c_rolled[b]
+            if b < blocks:
+                c_next = jnp.where(last, c_rolled[b + 1], c_next)
+            d[b] = c_next - c[b]
+            d_rolled[b] = pltpu.roll(d[b], 1, 1)
+        b = tick - 2 - LAG
+        if -1 <= b <= blocks:
+            d_back = d_rolled[b]
+            if b >= 0:
+                d_back = jnp.where(first, d_rolled[b - 1], d_back)
+            slope[b] = limited(d_back, d[b])
+            twice[b] = d[b] + d[b]
+            laplace[b] = d[b] - d_back
+            left[b] = pltpu.roll(twice[b] - slope[b], 1, 1)
+            right[b] = pltpu.roll(slope[b], LANES - 1, 1)
+        b = tick - 3 - 2 * LAG
+        if 0 <= b < blocks:
+            at = block_at(b)
+            speed = wide(coef[places[1], :, at])
+            forward = jnp.where(first, left[b - 1], left[b])
+            backward = twice[b] - jnp.where(last, right[b + 1], right[b])
+            change = jnp.where(speed > 0.0, forward, backward) + slope[b]
+            value = c[b] - (0.5 * speed) * change
+            value = value + wide(coef[places[2], :, at]) * laplace[b]
+            value = value + params[:, at] * wide(coef[places[3], :, at])
+            target[target_row, :, at] = value
 
 
 def rows_pass(source, row, places, partial, target, coef, block, blocks):
@@ -105,18 +101,11 @@
 
 
 def advance_group(source, target, row, partial, coef, params, blocks):
-    @pl.loop(0, GROUP // TOGETHER)
-    def _(i):
-        columns_pass(
-            source, row + i * TOGETHER, TOGETHER, partial, i * TOGETHER, coef, params, blocks
-        )
-
+    for i in range(GROUP):
+        columns_pass(source, row + i, partial, i, coef, params, blocks)
     places = [[coef_row(array, row + i) for array in (0, 2)] for i in range(GROUP)]
-
-    @pl.loop(0, blocks // WIDE)
-    def _(wide_block):
-        for i in range(WIDE):
-            rows_pass(source, row, places, partial, target, coef, wide_block * WIDE + i, blocks)
+    for block in range(blocks):
+        rows_pass(source, row, places, partial, target, coef, block, blocks)
 
 
 class Copies:
@@ -263,7 +252,7 @@
 def last_kernel(blocks, *refs):
     sources, refs = refs[:12], refs[12:]
     own_coef, pair, other, params, place_of, cell_of, shift_of = refs[:7]
-    out, predicted, *levels, partial, coef, staged, sems, out_sems = refs[7:]
+    low_out, high_out, predicted, *levels, partial, coef, sems = refs[7:]
     copies = Copies(sems)
     places = (
         (0, -8), (0, -4), (0, 16), (0, 20),
@@ -280,17 +269,10 @@
     for copy in waits[STEPS]:
         copy.wait()
 
-    def out_copy(block):
-        return pltpu.make_async_copy(staged.at[block], out.at[:, block_at(block)], out_sems.at[block])
-
-    @pl.loop(0, blocks)
-    def _(block):
-        for row in range(ROWS):
-            staged[block, pl.ds(row, SUBLANES, stride=ROWS), :] = levels[STEPS][
-                (HALO + row) * blocks + block
-            ]
-        out_copy(block).start()
-
+    sends = [
+        copies.start(region(levels, STEPS, row, blocks), out)
+        for row, out in ((0, low_out), (ROWS - GROUP, high_out))
+    ]
     lane = lax.broadcasted_iota(jnp.int32, (SUBLANES, LANES), 1)
 
     @pl.loop(0, predicted.shape[1] // LANES)
@@ -301,6 +283,29 @@
             value = levels[STEPS][cell_of[base + i]]
             found = jnp.where(lane == i, pltpu.roll(value, shift_of[base + i], 1), found)
         predicted[:, block_at(block)] = found
+
+    for copy in sends:
+        copy.wait()
+
+
+def field_kernel(blocks, *refs):
+    parts, (out, cells, staged, sems, out_sems) = refs[: ROWS // GROUP], refs[ROWS // GROUP :]
+    copies = Copies(sems)
+    size = GROUP * blocks
+    waits = [
+        copies.start(part, cells.at[pl.ds(i * size, size)]) for i, part in enumerate(parts)
+    ]
+    for copy in waits:
+        copy.wait()
+
+    def out_copy(block):
+        return pltpu.make_async_copy(staged.at[block], out.at[:, block_at(block)], out_sems.at[block])
+
+    @pl.loop(0, blocks)
+    def _(block):
+        for row in range(ROWS):
+            staged[block, pl.ds(row, SUBLANES, stride=ROWS), :] = cells[row * blocks + block]
+        out_copy(block).start()
 
     @pl.loop(0, blocks)
     def _(block):
@@ -346,7 +351,7 @@
     up, down, up_coef, down_coef = kernel_call(
         functools.partial(outer_rows_kernel, blocks), "outer_rows",
         [group, group, edge, edge], [ANYWHERE, ANYWHERE, IN_SMEM],
-        (IN_VMEM, IN_VMEM, ANYWHERE, ANYWHERE),
+        (IN_VMEM,) * 4,
         scratches + [dma((2,))], 3, [flat, coefficients, place_of],
     )
     low, high = kernel_call(
@@ -365,10 +370,11 @@
     cells = (GROUP * blocks, members, LANES)
     dma = pltpu.SemaphoreType.DMA
     staged = pltpu.VMEM((blocks, members * rows, LANES), jnp.float32)
+    gated, pair = lax.optimization_barrier((params, pair))
     inner = kernel_call(
         functools.partial(interior_kernel, blocks), "interior",
         [group] * 5, [ANYWHERE] * 5 + [IN_VMEM], (ANYWHERE,) * 5,
-        scratch(columns, dma((16,))), 8, [*own, own_coef, params],
+        scratch(columns, dma((16,))), 8, [*own, own_coef, gated],
     )
     upper, lower, low0, high0, *_ = lax.optimization_barrier(
         (own[2], own[1], low0, high0, inner[0])
@@ -383,12 +389,18 @@
     cell_of = obs_index // LANES + HALO * blocks
     lane_of = obs_index % LANES
     shift_of = (jnp.arange(obs_index.shape[0], dtype=jnp.int32) - lane_of) % LANES
-    field, predicted = kernel_call(
+    low4, high4, predicted = kernel_call(
         functools.partial(last_kernel, blocks), "edge_last",
-        [flat, (members, obs_index.shape[0])],
-        [ANYWHERE] * 15 + [IN_VMEM] + [IN_SMEM] * 3, (ANYWHERE, IN_VMEM),
-        scratch(columns, staged, dma((29,)), dma((blocks,))), 15,
+        [cells, cells, (members, obs_index.shape[0])],
+        [ANYWHERE] * 15 + [IN_VMEM] + [IN_SMEM] * 3, (ANYWHERE, ANYWHERE, IN_VMEM),
+        scratch(columns, dma((31,))), 15,
         [low1, low0, high0, high1, *first, own_coef, pair, other, params, place_of, cell_of, shift_of],
+    )
+    (field,) = kernel_call(
+        functools.partial(field_kernel, blocks), "field",
+        [flat], [ANYWHERE] * 4, (ANYWHERE,),
+        [pltpu.VMEM((rows * blocks, members, LANES), jnp.float32), staged, dma((4,)), dma((blocks,))],
+        4, [low4, first[6], first[7], high4],
     )
     return field.reshape(shape), predicted, inner[0]
 

time: 123 us -> 158 us (1.28)
  Pallas kernels: 71 us -> 103 us
  waiting for transfers between devices: 8.37 us -> 12.2 us
    pallas_call x5 -> x6, Pallas kernels: 68.3 us -> 100 us  [kernel_call(): pl.pallas_call(body, out_shape=tuple((jax.ShapeDtypeStruct(shape, jnp.flo...]
    ppermute x3, waiting for transfers between devices: 0.8 us -> 3.07 us  [halos(): lax.ppermute(upper, 'slab', forward)]
    ppermute x3, waiting for transfers between devices: 0.01 us -> 1.77 us  [halos(): lax.ppermute(lower, 'slab', backward)]
  transfers between devices with their start and end apart: 13 -> 13, of which waited for: 6 -> 5; matrix products, arithmetic and copies ran while one was open for 3% -> 2% of each run, Pallas kernels for 48% -> 62%
where the time goes in v5:
time: 158 us; the launch traced here: 157 us
  Pallas kernels  103 us (65%)
  starting transfers between devices  30.1 us (19%)
  waiting for transfers between devices  12.2 us (8%)
  blocking collectives  6 us (4%)
  other arithmetic  2.66 us (2%)
  local copies, waits for them, and re-layouts  1.9 us (1%)
    pallas_call x6, Pallas kernels, kernel_call(): pl.pallas_call(body, out_shape=tuple((jax.ShapeDtypeStruct(shape, jnp.flo...  100 us
    ppermute x3, starting transfers between devices, halos(): lax.ppermute(upper, 'slab', forward)  15 us
    ppermute x3, starting transfers between devices, local(): products = products + lax.ppermute(products, 'slab', pairs)  8.71 us
    all_gather x1, blocking collectives, local(): everyone = lax.all_gather(predicted, 'ens', axis=0, tiled=True)  6 us
    ppermute x2, waiting for transfers between devices, over_ens(): lax.ppermute(pair, 'ens', [(i, i ^ 2) for i in range(ens_count)])  4.96 us
    ppermute x3, starting transfers between devices, halos(): lax.ppermute(lower, 'slab', backward)  4.05 us
  transfers between devices with their start and end apart: 13, of which 5 were waited for; matrix products, arithmetic and copies ran while one was open for 2% of the time, Pallas kernels for 62%

profile of v5, /device:TPU:0, one launch (start us, length us, event | category | flops | bytes accessed | tf_op | source)
XLA Modules:
  0.0 157.4 jit_solution(6766551136091397127)
XLA Ops:
  0.6 3.1 %outer_rows.1 = (f32[4,8,4096]{2,1,0:T(8,128)}, f32[4,8,4096]{2,1,0:T(8,128)}, f32[8,4096]{1,0:T(8,128)}, f32[8,4096]{1,0:T(8,128)}) custom-call(f32[128,4096]{1,0:T(8,128)} %bitcast.28, f32[4,16,4096]{2,1,0:T(8,128)} %refs_12_.3, s32[1]{0:T(128)} %bitcast.1.place_of.refs_13_.refs_16_), custom_call_target="tpu_custom_call" | custom-call | bytes 600000 | tf_op jit(solution)/shard_map/outer_rows/pallas_call | solution.py:330
  3.7 0.0 copy-start.11
  3.7 1.3 collective-permute-start.3
  5.0 5.5 %collective-permute-start.2 = (f32[8,4096]{1,0:T(8,128)}, f32[8,4096]{1,0:T(8,128)S(1)}, u32[]{:S(2)}, u32[]{:S(2)}) collective-permute-start(f32[8,4096]{1,0:T(8,128)} %get-tuple-element.35), channel_id=1, source_target_pairs={{0,1},{1,2},{2,3},{3,4},{4,5},{5,6},{6,7},{8,9},{9,10},{10,11},{11... | collective-permute-start | bytes 393224 | tf_op jit(solution)/shard_map/ppermute | solution.py:469
  10.5 1.8 %collective-permute-done.3 = f32[8,4096]{1,0:T(8,128)S(1)} collective-permute-done((f32[8,4096]{1,0:T(8,128)}, f32[8,4096]{1,0:T(8,128)S(1)}, u32[]{:S(2)}, u32[]{:S(2)}) %collective-permute-start.3) | collective-permute-done | bytes 131104 | tf_op jit(solution)/shard_map/ppermute | solution.py:469
  12.3 3.1 %collective-permute-done.2 = f32[8,4096]{1,0:T(8,128)S(1)} collective-permute-done((f32[8,4096]{1,0:T(8,128)}, f32[8,4096]{1,0:T(8,128)S(1)}, u32[]{:S(2)}, u32[]{:S(2)}) %collective-permute-start.2) | collective-permute-done | bytes 131104 | tf_op jit(solution)/shard_map/ppermute | solution.py:469
  15.4 0.1 collective-permute-start.4
  15.5 4.3 %collective-permute-start = (f32[4,8,4096]{2,1,0:T(8,128)}, f32[4,8,4096]{2,1,0:T(8,128)S(1)}, u32[]{:S(2)}, u32[]{:S(2)}) collective-permute-start(f32[4,8,4096]{2,1,0:T(8,128)} %get-tuple-element.31.outer.own3.refs_2_), channel_id=1, source_target_pairs={{0,1},{1,2},{2,3},{3,4},{4,5},{5,6},{6,7},{8,9},{9,10},{10,11},{11... | collective-permute-start | bytes 1572872 | tf_op jit(solution)/shard_map/ppermute | solution.py:469
  19.8 1.3 collective-permute-start.1
  21.1 2.9 %inner_rows.1 = (f32[4,8,4096]{2,1,0:T(8,128)}, f32[4,8,4096]{2,1,0:T(8,128)}) custom-call(f32[128,4096]{1,0:T(8,128)} %bitcast.29, f32[4,8,4096]{2,1,0:T(8,128)} %get-tuple-element.31.outer.own3.refs_2_), custom_call_target="tpu_custom_call" | custom-call | bytes 600000 | tf_op jit(solution)/shard_map/inner_rows/pallas_call | solution.py:330
  24.0 0.0 copy-done.11
  24.0 0.6 add_select_fusion
  24.6 0.0 collective-permute-done.4
  24.6 0.0 copy-start.10
  24.6 0.0 copy-start.9
  24.7 0.0 copy-start.5
  24.7 24.2 %interior.1 = (f32[4,8,4096]{2,1,0:T(8,128)}, f32[4,8,4096]{2,1,0:T(8,128)}, f32[4,8,4096]{2,1,0:T(8,128)}, f32[4,8,4096]{2,1,0:T(8,128)}, f32[4,8,4096]{2,1,0:T(8,128)}) custom-call(f32[4,8,4096]{2,1,0:T(8,128)} %get-tuple-element.34.own0.refs_1_, f32[4,8,4096]{2,1,0:T(8,128)} %get-tuple-element.42.own1, f32[4,8,4096]{2,1,0:T(8,128)} %get-tuple-element.39.own2, ...), custom_call_target="tpu_custom_call" | custom-call | bytes 1600000 | tf_op jit(solution)/shard_map/interior/pallas_call | solution.py:330
  48.9 0.0 copy-done
  48.9 0.3 collective-permute-start.11
  49.2 0.0 copy-done.12
  49.2 0.1 compare_convert_fusion.same
  49.3 1.5 collective-permute-start.7
  50.8 0.0 collective-permute-done.refs_0_.refs_1_
  50.8 0.0 collective-permute-done.1.refs_3_.refs_2_
  50.8 0.0 copy-done.10
  50.8 0.0 copy-start.7
  50.8 5.2 %collective-permute-start.5 = (f32[4,8,4096]{2,1,0:T(8,128)S(1)}, f32[4,8,4096]{2,1,0:T(8,128)}, u32[]{:S(2)}, u32[]{:S(2)}) collective-permute-start(f32[4,8,4096]{2,1,0:T(8,128)S(1)} %copy-done.10), channel_id=1, source_target_pairs={{0,1},{1,2},{2,3},{3,4},{4,5},{5,6},{6,7},{8,9},{9,10},{10,11},{11... | collective-permute-start | bytes 1572872 | tf_op jit(solution)/shard_map/ppermute | solution.py:469
  56.0 0.0 copy-done.9
  56.0 1.5 collective-permute-start.6
  57.5 0.0 collective-permute-done.11
  57.5 0.7 pad_maximum_fusion.3
  58.2 0.5 collective-permute-start.12
  58.7 0.2 convert_reduce_fusion
  58.9 0.1 copy.9.rank_col
  59.0 0.1 constant_dynamic-slice_fusion.own_same
  59.1 5.0 %collective-permute-done.7.refs_11_.refs_14_ = f32[2,2,8,4096]{3,2,1,0:T(8,128)S(1)} collective-permute-done((f32[2,2,8,4096]{3,2,1,0:T(8,128)S(1)}, f32[2,2,8,4096]{3,2,1,0:T(8,128)S(1)}, u32[]{:S(2)}, u32[]{:S(2)}) %collective-permute-start.7) | collective-permute-done | bytes 524320 | tf_op jit(solution)/shard_map/ppermute | solution.py:466
  64.0 0.0 copy-done.5
  64.0 0.0 copy-done.6
  64.0 0.0 copy-done.7
  64.0 0.8 copy-done.8
  64.8 31.2 %edge_first.1 = (f32[4,8,4096]{2,1,0:T(8,128)}, f32[4,8,4096]{2,1,0:T(8,128)}, f32[4,8,4096]{2,1,0:T(8,128)}, f32[4,8,4096]{2,1,0:T(8,128)}, f32[4,8,4096]{2,1,0...) custom-call(f32[4,8,4096]{2,1,0:T(8,128)} %copy-done.6, ...), custom_call_target="tpu_custom_call" | custom-call | bytes 2000000 | tf_op jit(solution)/shard_map/edge_first/pallas_call | solution.py:330
  96.0 0.0 collective-permute-done.5.refs_0_
  96.1 0.0 collective-permute-done.6.refs_3_
  96.1 0.0 copy-start.3
  96.1 0.0 copy-start.4
  96.1 0.0 copy-start.1
  96.1 35.8 %edge_last.1 = (f32[128,8,128]{2,1,0:T(8,128)}, f32[128,8,128]{2,1,0:T(8,128)}, f32[8,2048]{1,0:T(8,128)}) custom-call(f32[4,8,4096]{2,1,0:T(8,128)} %collective-permute-done.5.refs_0_, f32[4,8,4096]{2,1,0:T(8,128)} %copy-done.6, f32[4,8,4096]{2,1,0:T(8,128)} %copy-done.7, f32[4,8,4096]{2,1,0:T(8,128)} %collective-permute-done.6.refs_3_, ...), custom_call_target="tpu_custom_call" | custom-call | bytes 3000000 | tf_op jit(solution)/shard_map/edge_last/pallas_call | solution.py:330
  131.9 6.0 %all_gather.3.everyone = f32[32,2048]{1,0:T(8,128)S(1)} all-gather(f32[8,2048]{1,0:T(8,128)} %get-tuple-element.58.own), channel_id=1, replica_groups=mesh['ens'=4,'slab'=8] {'ens'}, dimensions={0}, use_global_device_ids=true | all-gather | bytes 327680 | tf_op jit(solution)/shard_map/all_gather | solution.py:497
  137.9 0.0 copy-done.3
  137.9 0.0 copy-done.4
  137.9 0.8 copy-done.2
  138.8 0.6 products.1
  139.4 2.5 %collective-permute-start.8 = (f32[32,40]{1,0:T(8,128)S(1)}, f32[32,40]{1,0:T(8,128)S(1)}, u32[]{:S(2)}, u32[]{:S(2)}) collective-permute-start(f32[32,40]{1,0:T(8,128)S(1)} %products.1), channel_id=1, source_target_pairs={{0,1},{1,0},{2,3},{3,2},{4,5},{5,4},{6,7},{7,6},{8,9},{9,8},{10,11... | collective-permute-start | bytes 15368 | tf_op jit(solution)/shard_map/ppermute | solution.py:508
  141.9 0.0 collective-permute-done.12
  141.9 0.0 copy-done.1
  141.9 1.0 pad_maximum_fusion.1
  142.9 0.7 collective-permute-done.8
  143.6 3.2 %collective-permute-start.9 = (f32[32,40]{1,0:T(8,128)S(1)}, f32[32,40]{1,0:T(8,128)S(1)}, u32[]{:S(2)}, u32[]{:S(2)}) collective-permute-start(f32[32,40]{1,0:T(8,128)S(1)} %add.46), channel_id=1, source_target_pairs={{0,2},{1,3},{2,0},{3,1},{4,6},{5,7},{6,4},{7,5},{8,10},{9,11},{10,... | collective-permute-start | bytes 15368 | tf_op jit(solution)/shard_map/ppermute | solution.py:508
  146.8 1.7 %collective-permute-done.9 = f32[32,40]{1,0:T(8,128)S(1)} collective-permute-done((f32[32,40]{1,0:T(8,128)S(1)}, f32[32,40]{1,0:T(8,128)S(1)}, u32[]{:S(2)}, u32[]{:S(2)}) %collective-permute-start.9) | collective-permute-done | bytes 5152 | tf_op jit(solution)/shard_map/ppermute | solution.py:508
  148.5 3.0 %collective-permute-start.10 = (f32[32,40]{1,0:T(8,128)S(1)}, f32[32,40]{1,0:T(8,128)S(1)}, u32[]{:S(2)}, u32[]{:S(2)}) collective-permute-start(f32[32,40]{1,0:T(8,128)S(1)} %add.47), channel_id=1, source_target_pairs={{0,4},{1,5},{2,6},{3,7},{4,0},{5,1},{6,2},{7,3},{8,12},{9,13},{10,... | collective-permute-start | bytes 15368 | tf_op jit(solution)/shard_map/ppermute | solution.py:508
  151.5 0.4 fusion.1.anomalies
  152.0 3.3 %field.1 = f32[128,4096]{1,0:T(8,128)} custom-call(f32[128,8,128]{2,1,0:T(8,128)} %get-tuple-element.56.refs_0_, f32[128,8,128]{2,1,0:T(8,128)} %get-tuple-element.54.refs_10_.refs_1_, f32[128,8,128]{2,1,0:T(8,128)} %get-tuple-element.55.refs_11_.refs_2_, f32[128,8,128]{2,1,0:T(8,128)} %get-tuple-element.57.refs_3_), custom_call_target="tpu_custom_call" | custom-call | bytes 800000 | tf_op jit(solution)/shard_map/field/pallas_call | solution.py:330
  155.3 0.0 collective-permute-done.10
  155.3 2.1 %update.1 = f32[8,4096]{1,0:T(8,128)} custom-call(f32[1,32,40]{2,1,0:T(8,128)S(1)} %add_bitcast_fusion.summands, f32[32,32]{1,0:T(8,128)S(1)} %compare_convert_fusion.same, f32[32,8]{1,0:T(8,128)S(1)} %constant_dynamic-slice_fusion.own_same, s32[1,32]{1,0:T(1,128)S(1)} %bitcast.27, s32[32,1]{1,0:T(8,128)S(1)} %copy.9.rank_col, ...), custom_call_target="tpu_custom_call" | custom-call | tf_op jit(solution)/shard_map/update/pallas_call | solution.py:510
  (11 shorter events, 0.1 us)
Async XLA Ops:
  3.7 20.3 %copy-start.11 = (s32[2048]{0:T(1024)S(1)}, s32[2048]{0:T(1024)}, u32[]{:S(2)}) copy-start(s32[2048]{0:T(1024)} %param.10) | copy-start | bytes 24580
  3.7 8.5 %collective-permute-start.3 = (f32[8,4096]{1,0:T(8,128)}, f32[8,4096]{1,0:T(8,128)S(1)}, u32[]{:S(2)}, u32[]{:S(2)}) collective-permute-start(f32[8,4096]{1,0:T(8,128)} %get-tuple-element.36), channel_id=1, source_target_pairs={{1,0},{2,1},{3,2},{4,3},{5,4},{6,5},{7,6},{9,8},{10,9},{11,10},{12... | collective-permute-start | bytes 393224 | tf_op jit(solution)/shard_map/ppermute | solution.py:469
  5.0 10.3 %collective-permute-start.2 = (f32[8,4096]{1,0:T(8,128)}, f32[8,4096]{1,0:T(8,128)S(1)}, u32[]{:S(2)}, u32[]{:S(2)}) collective-permute-start(f32[8,4096]{1,0:T(8,128)} %get-tuple-element.35), channel_id=1, source_target_pairs={{0,1},{1,2},{2,3},{3,4},{4,5},{5,6},{6,7},{8,9},{9,10},{10,11},{11... | collective-permute-start | bytes 393224 | tf_op jit(solution)/shard_map/ppermute | solution.py:469
  15.4 9.2 %collective-permute-start.4 = (f32[2,8,4096]{2,1,0:T(8,128)S(1)}, f32[2,8,4096]{2,1,0:T(8,128)S(1)}, u32[]{:S(2)}, u32[]{:S(2)}) collective-permute-start(f32[2,8,4096]{2,1,0:T(8,128)S(1)} %get-tuple-element.65), channel_id=1, source_target_pairs={{0,8},{8,0},{16,24},{24,16},{1,9},{9,1},{17,25},{25,17},{2,10},{10... | collective-permute-start | bytes 786440 | tf_op jit(solution)/shard_map/ppermute | solution.py:465
  15.5 35.3 %collective-permute-start = (f32[4,8,4096]{2,1,0:T(8,128)}, f32[4,8,4096]{2,1,0:T(8,128)S(1)}, u32[]{:S(2)}, u32[]{:S(2)}) collective-permute-start(f32[4,8,4096]{2,1,0:T(8,128)} %get-tuple-element.31.outer.own3.refs_2_), channel_id=1, source_target_pairs={{0,1},{1,2},{2,3},{3,4},{4,5},{5,6},{6,7},{8,9},{9,10},{10,11},{11... | collective-permute-start | bytes 1572872 | tf_op jit(solution)/shard_map/ppermute | solution.py:469
  19.8 31.0 %collective-permute-start.1 = (f32[4,8,4096]{2,1,0:T(8,128)}, f32[4,8,4096]{2,1,0:T(8,128)S(1)}, u32[]{:S(2)}, u32[]{:S(2)}) collective-permute-start(f32[4,8,4096]{2,1,0:T(8,128)} %get-tuple-element.34.own0.refs_1_), channel_id=1, source_target_pairs={{1,0},{2,1},{3,2},{4,3},{5,4},{6,5},{7,6},{9,8},{10,9},{11,10},{12... | collective-permute-start | bytes 1572872 | tf_op jit(solution)/shard_map/ppermute | solution.py:469
  24.6 24.3 %copy-start = (f32[8,4096]{1,0:T(8,128)S(1)}, f32[8,4096]{1,0:T(8,128)}, u32[]{:S(2)}) copy-start(f32[8,4096]{1,0:T(8,128)} %own.1) | copy-start | bytes 393220
  24.6 24.6 %copy-start.12 = (s32[32]{0:T(128)S(1)}, s32[32]{0:T(128)}, u32[]{:S(2)}) copy-start(s32[32]{0:T(128)} %param.13) | copy-start | bytes 388
  24.6 26.2 %copy-start.10 = (f32[4,8,4096]{2,1,0:T(8,128)S(1)}, f32[4,8,4096]{2,1,0:T(8,128)}, u32[]{:S(2)}) copy-start(f32[4,8,4096]{2,1,0:T(8,128)} %get-tuple-element.39.own2) | copy-start | bytes 1572868
  24.6 31.4 %copy-start.9 = (f32[4,8,4096]{2,1,0:T(8,128)S(1)}, f32[4,8,4096]{2,1,0:T(8,128)}, u32[]{:S(2)}) copy-start(f32[4,8,4096]{2,1,0:T(8,128)} %get-tuple-element.42.own1) | copy-start | bytes 1572868
  24.7 39.4 %copy-start.5 = (f32[2,2,8,4096]{3,2,1,0:T(8,128)}, f32[2,2,8,4096]{3,2,1,0:T(8,128)S(1)}, u32[]{:S(2)}) copy-start(f32[2,2,8,4096]{3,2,1,0:T(8,128)S(1)} %pad_maximum_fusion.refs_10_.refs_13_) | copy-start | bytes 1572868
  48.9 8.5 %collective-permute-start.11 = (f32[8,4096]{1,0:T(8,128)S(1)}, f32[8,4096]{1,0:T(8,128)S(1)}, u32[]{:S(2)}, u32[]{:S(2)}) collective-permute-start(f32[8,4096]{1,0:T(8,128)S(1)} %copy-done), channel_id=1, source_target_pairs={{0,8},{8,0},{16,24},{24,16},{1,9},{9,1},{17,25},{25,17},{2,10},{10... | collective-permute-start | bytes 393224 | tf_op jit(solution)/shard_map/ppermute | solution.py:465
  49.3 14.8 %collective-permute-start.7 = (f32[2,2,8,4096]{3,2,1,0:T(8,128)S(1)}, f32[2,2,8,4096]{3,2,1,0:T(8,128)S(1)}, u32[]{:S(2)}, u32[]{:S(2)}) collective-permute-start(f32[2,2,8,4096]{3,2,1,0:T(8,128)S(1)} %pad_maximum_fusion.refs_10_.refs_13_), channel_id=1, source_target_pairs={{0,16},{8,24},{16,0},{24,8},{1,17},{9,25},{17,1},{25,9},{2,18},{10... | collective-permute-start | bytes 1572872 | tf_op jit(solution)/shard_map/ppermute | solution.py:466
  50.8 13.2 %copy-start.6 = (f32[4,8,4096]{2,1,0:T(8,128)}, f32[4,8,4096]{2,1,0:T(8,128)S(1)}, u32[]{:S(2)}) copy-start(f32[4,8,4096]{2,1,0:T(8,128)S(1)} %collective-permute-done.refs_0_.refs_1_) | copy-start | bytes 1572868
  50.8 13.2 %copy-start.7 = (f32[4,8,4096]{2,1,0:T(8,128)}, f32[4,8,4096]{2,1,0:T(8,128)S(1)}, u32[]{:S(2)}) copy-start(f32[4,8,4096]{2,1,0:T(8,128)S(1)} %collective-permute-done.1.refs_3_.refs_2_) | copy-start | bytes 1572868
  50.8 45.2 %collective-permute-start.5 = (f32[4,8,4096]{2,1,0:T(8,128)S(1)}, f32[4,8,4096]{2,1,0:T(8,128)}, u32[]{:S(2)}, u32[]{:S(2)}) collective-permute-start(f32[4,8,4096]{2,1,0:T(8,128)S(1)} %copy-done.10), channel_id=1, source_target_pairs={{0,1},{1,2},{2,3},{3,4},{4,5},{5,6},{6,7},{8,9},{9,10},{10,11},{11... | collective-permute-start | bytes 1572872 | tf_op jit(solution)/shard_map/ppermute | solution.py:469
  56.0 40.1 %collective-permute-start.6 = (f32[4,8,4096]{2,1,0:T(8,128)S(1)}, f32[4,8,4096]{2,1,0:T(8,128)}, u32[]{:S(2)}, u32[]{:S(2)}) collective-permute-start(f32[4,8,4096]{2,1,0:T(8,128)S(1)} %copy-done.9), channel_id=1, source_target_pairs={{1,0},{2,1},{3,2},{4,3},{5,4},{6,5},{7,6},{9,8},{10,9},{11,10},{12... | collective-permute-start | bytes 1572872 | tf_op jit(solution)/shard_map/ppermute | solution.py:469
  58.2 83.7 %collective-permute-start.12 = (f32[2,8,4096]{2,1,0:T(8,128)}, f32[2,8,4096]{2,1,0:T(8,128)}, u32[]{:S(2)}, u32[]{:S(2)}) collective-permute-start(f32[2,8,4096]{2,1,0:T(8,128)} %pad_maximum_fusion.3), channel_id=1, source_target_pairs={{0,16},{8,24},{16,0},{24,8},{1,17},{9,25},{17,1},{25,9},{2,18},{10... | collective-permute-start | bytes 786440 | tf_op jit(solution)/shard_map/ppermute | solution.py:466
  64.0 0.8 copy-start.8
  96.1 41.8 %copy-start.3 = (f32[8,2048]{1,0:T(8,128)S(1)}, f32[8,2048]{1,0:T(8,128)}, u32[]{:S(2)}) copy-start(f32[8,2048]{1,0:T(8,128)} %values.1) | copy-start | bytes 196612
  96.1 41.8 %copy-start.4 = (f32[2048]{0:T(1024)S(1)}, f32[2048]{0:T(1024)}, u32[]{:S(2)}) copy-start(f32[2048]{0:T(1024)} %param.12) | copy-start | bytes 24580
  96.1 45.8 %copy-start.1 = (f32[8,4096]{1,0:T(8,128)S(1)}, f32[8,4096]{1,0:T(8,128)}, u32[]{:S(2)}) copy-start(f32[8,4096]{1,0:T(8,128)} %own.1) | copy-start | bytes 393220
  137.9 0.8 copy-start.2
  139.4 4.2 %collective-permute-start.8 = (f32[32,40]{1,0:T(8,128)S(1)}, f32[32,40]{1,0:T(8,128)S(1)}, u32[]{:S(2)}, u32[]{:S(2)}) collective-permute-start(f32[32,40]{1,0:T(8,128)S(1)} %products.1), channel_id=1, source_target_pairs={{0,1},{1,0},{2,3},{3,2},{4,5},{5,4},{6,7},{7,6},{8,9},{9,8},{10,11... | collective-permute-start | bytes 15368 | tf_op jit(solution)/shard_map/ppermute | solution.py:508
  143.6 4.9 %collective-permute-start.9 = (f32[32,40]{1,0:T(8,128)S(1)}, f32[32,40]{1,0:T(8,128)S(1)}, u32[]{:S(2)}, u32[]{:S(2)}) collective-permute-start(f32[32,40]{1,0:T(8,128)S(1)} %add.46), channel_id=1, source_target_pairs={{0,2},{1,3},{2,0},{3,1},{4,6},{5,7},{6,4},{7,5},{8,10},{9,11},{10,... | collective-permute-start | bytes 15368 | tf_op jit(solution)/shard_map/ppermute | solution.py:508
  148.5 6.8 %collective-permute-start.10 = (f32[32,40]{1,0:T(8,128)S(1)}, f32[32,40]{1,0:T(8,128)S(1)}, u32[]{:S(2)}, u32[]{:S(2)}) collective-permute-start(f32[32,40]{1,0:T(8,128)S(1)} %add.47), channel_id=1, source_target_pairs={{0,4},{1,5},{2,6},{3,7},{4,0},{5,1},{6,2},{7,3},{8,12},{9,13},{10,... | collective-permute-start | bytes 15368 | tf_op jit(solution)/shard_map/ppermute | solution.py:508

commit v6 on v4

--- a/solution.py
+++ b/solution.py
@@ -16,8 +16,11 @@
 ROWS = 16
 GROUP = 4
 LAG = 3
+TOGETHER = 2
 WIDE = 8
-TOGETHER = 2
+MOVED = 16
+PICKED = 32
+ALL_ROWS = ROWS + 2 * HALO
 VMEM_LIMIT = 16 * 1024 * 1024
 TALL_LIMIT = 58 * 1024 * 1024
 COST_BYTES = 200000
@@ -42,17 +45,16 @@
     return jnp.broadcast_to(row, (SUBLANES, LANES))
 
 
-def columns_pass(source, first_row, count, target, target_row, coef, params, blocks):
+def columns_pass(levels, cell, row, count, partial, first_cell, coef, params, blocks):
     lane = lax.broadcasted_iota(jnp.int32, (SUBLANES, LANES), 1)
     first, last = lane == 0, lane == LANES - 1
-    places = [[coef_row(array, first_row + i) for array in range(4)] for i in range(count)]
+    places = [[coef_row(array, row + i) for array in range(4)] for i in range(count)]
     c, c_rolled, d, d_rolled, slope, twice, left, right, laplace = ({} for _ in range(9))
     for tick in range(blocks + 2 * LAG + 4):
         for i in range(count):
-            row = first_row + i
             b = tick - 1
             if b <= blocks:
-                c[i, b] = source[row, :, block_at(b % blocks)]
+                c[i, b] = levels[cell + i * blocks + b % blocks]
                 c_rolled[i, b] = pltpu.roll(c[i, b], LANES - 1, 1)
             b = tick - 2
             if -1 <= b <= blocks:
@@ -81,34 +83,33 @@
                 value = c[i, b] - (0.5 * speed) * change
                 value = value + wide(coef[places[i][2], :, at]) * laplace[i, b]
                 value = value + params[:, at] * wide(coef[places[i][3], :, at])
-                target[target_row + i, :, at] = value
-
-
-def rows_pass(source, row, places, partial, target, coef, block, blocks):
+                partial[first_cell + i * blocks + b] = value
+
+
+def rows_pass(levels, cell, places, partial, result, coef, block, blocks):
     at = block_at(block)
-    c = [source[row - 2 + i, :, at] for i in range(GROUP + 4)]
+    c = [levels[cell + (i - 2) * blocks + block] for i in range(GROUP + 4)]
     d = [c[i + 1] - c[i] for i in range(GROUP + 3)]
     slope = [None] + [limited(d[i - 1], d[i]) for i in range(1, GROUP + 3)]
     twice = [None] + [d[i] + d[i] for i in range(1, GROUP + 2)]
     for i in range(2, GROUP + 2):
-        here = row - 2 + i
         speed = wide(coef[places[i - 2][0], :, at])
         forward = twice[i - 1] - slope[i - 1]
         backward = twice[i] - slope[i + 1]
         change = wide(coef[places[i - 2][1], :, at]) * (d[i] - d[i - 1])
         change = change - (0.5 * speed) * (jnp.where(speed > 0.0, forward, backward) + slope[i])
-        value = partial[i - 2, :, at] + change
-        if target.shape[1:] == value.shape:
-            target[here * blocks + block] = value
-        else:
-            target[here, :, at] = value
-
-
-def advance_group(source, target, row, partial, coef, params, blocks):
+        here = (i - 2) * blocks + block
+        result[here] = partial[here] + change
+
+
+def advance_group(level, row, levels, partial, result, coef, params, blocks):
+    cell = (level * ALL_ROWS + row) * blocks
+
     @pl.loop(0, GROUP // TOGETHER)
     def _(i):
+        done = i * (TOGETHER * blocks)
         columns_pass(
-            source, row + i * TOGETHER, TOGETHER, partial, i * TOGETHER, coef, params, blocks
+            levels, cell + done, row + i * TOGETHER, TOGETHER, partial, done, coef, params, blocks
         )
 
     places = [[coef_row(array, row + i) for array in (0, 2)] for i in range(GROUP)]
@@ -116,29 +117,34 @@
     @pl.loop(0, blocks // WIDE)
     def _(wide_block):
         for i in range(WIDE):
-            rows_pass(source, row, places, partial, target, coef, wide_block * WIDE + i, blocks)
+            rows_pass(levels, cell, places, partial, result, coef, wide_block * WIDE + i, blocks)
+
+    @pl.loop(0, GROUP * blocks // MOVED)
+    def _(i):
+        first = i * MOVED
+        moved = [result[first + k] for k in range(MOVED)]
+        for k in range(MOVED):
+            levels[cell + ALL_ROWS * blocks + first + k] = moved[k]
 
 
 class Copies:
     def __init__(self, sems):
         self.sems, self.used = sems, 0
 
-    def start(self, source, target):
+    def make(self, source, target):
         copy = pltpu.make_async_copy(source, target, self.sems.at[self.used])
         self.used += 1
         assert self.used <= self.sems.shape[0]
+        return copy
+
+    def start(self, source, target):
+        copy = self.make(source, target)
         copy.start()
         return copy
 
 
-def place(row):
-    return pl.ds(row + HALO, GROUP)
-
-
 def region(levels, level, row, blocks):
-    if level == STEPS:
-        return levels[level].at[pl.ds((row + HALO) * blocks, GROUP * blocks)]
-    return levels[level].at[place(row)]
+    return levels.at[pl.ds((level * ALL_ROWS + HALO + row) * blocks, GROUP * blocks)]
 
 
 def fill_rows(blocks, first_rows, tracer, outs, staged, sems):
@@ -154,7 +160,7 @@
         copy(block).wait()
         for out, first_row in zip(outs, first_rows):
             for row in range(GROUP):
-                out[row, :, block_at(block)] = staged[
+                out[row * blocks + block] = staged[
                     block, pl.ds(first_row + row, SUBLANES, stride=ROWS), :
                 ]
 
@@ -178,10 +184,10 @@
 
 
 def interior_kernel(blocks, own0, own1, own2, own3, own_coef, params, *rest):
-    outs, (*levels, partial, coef, sems) = rest[:5], rest[5:]
+    outs, (levels, partial, result, coef, sems) = rest[:5], rest[5:]
     copies = Copies(sems)
     waits = [
-        copies.start(own.at[0:GROUP], levels[0].at[place(GROUP * i)])
+        copies.start(own, region(levels, 0, GROUP * i, blocks))
         for i, own in enumerate((own0, own1, own2, own3))
     ]
     waits += [
@@ -189,32 +195,37 @@
     ]
     for copy in waits:
         copy.wait()
-    for level, start, count in ((0, 2, 3), (1, 4, 2), (2, 6, 1)):
-        @pl.loop(0, count)
-        def _(i):
-            row = start + HALO + GROUP * i
-            advance_group(levels[level], levels[level + 1], row, partial, coef, params, blocks)
+
+    @pl.loop(0, 6)
+    def _(i):
+        level = jnp.where(i < 3, 0, jnp.where(i < 5, 1, 2))
+        row = jnp.where(i < 3, 2 + 4 * i, jnp.where(i < 5, 4 * i - 8, 6))
+        advance_group(level, row + HALO, levels, partial, result, coef, params, blocks)
 
     waits = [
-        copies.start(levels[level].at[place(row)], out)
+        copies.start(region(levels, level, row, blocks), out)
         for out, (level, row) in zip(outs, ((1, 2), (1, 10), (2, 4), (2, 8), (3, 6)))
     ]
     for copy in waits:
         copy.wait()
 
 
-def edge_steps(outer, blocks, waits, levels, partial, coef, params, ready):
-    for level in range(STEPS):
-        for copy in waits[level]:
-            copy.wait()
-        low, high = 2 * level - outer, ROWS + outer - GROUP - 2 * level
-
-        @pl.loop(0, 2)
-        def _(side):
-            row = low + HALO + side * (high - low)
-            advance_group(levels[level], levels[level + 1], row, partial, coef, params, blocks)
-
-        ready(level, low, high)
+def edge_steps(outer, blocks, waits, sends, levels, partial, result, coef, params):
+    @pl.loop(0, 2 * STEPS)
+    def _(step):
+        level, side = lax.div(step, 2), lax.rem(step, 2)
+        for k in range(STEPS):
+            @pl.when(step == 2 * k)
+            def _():
+                for copy in waits[k]:
+                    copy.wait()
+
+        low = 2 * level - outer
+        high = ROWS + outer - GROUP - 2 * level
+        row = jnp.where(side == 0, low, high) + HALO
+        advance_group(level, row, levels, partial, result, coef, params, blocks)
+        for k, copy in enumerate(sends):
+            pl.when(step == k)(copy.start)
 
 
 def coef_row(array, row):
@@ -239,23 +250,19 @@
 def middle_kernel(blocks, *refs):
     sources, refs = refs[:9], refs[9:]
     own_coef, pair, other, params, place_of = refs[:5]
-    outs, (*levels, partial, coef, sems) = refs[5:13], refs[13:]
+    outs, (levels, partial, result, coef, sems) = refs[5:13], refs[13:]
     copies = Copies(sems)
     places = ((0, -4), (0, 0), (0, 12), (0, 16), (1, 2), (1, 10), (2, 4), (2, 8), (3, 6))
     waits = [[] for _ in range(STEPS)]
     for source, (level, row) in zip(sources, places):
-        count = GROUP * blocks if level == STEPS else GROUP
-        waits[level].append(
-            copies.start(source.at[0:count], region(levels, level, row, blocks))
-        )
+        waits[level].append(copies.start(source, region(levels, level, row, blocks)))
     waits[0] += load_coef(copies, own_coef, pair, other, place_of, coef)
-    sends = []
-
-    def ready(level, low, high):
-        for row, out in ((low, outs[2 * level]), (high, outs[2 * level + 1])):
-            sends.append(copies.start(region(levels, level + 1, row, blocks), out))
-
-    edge_steps(2, blocks, waits, levels, partial, coef, params, ready)
+    places = [(k + 1, row) for k in range(STEPS) for row in (2 * k - 2, ROWS + 2 - GROUP - 2 * k)]
+    sends = [
+        copies.make(region(levels, level, row, blocks), out)
+        for out, (level, row) in zip(outs, places)
+    ]
+    edge_steps(2, blocks, waits, sends, levels, partial, result, coef, params)
     for copy in sends:
         copy.wait()
 
@@ -263,7 +270,7 @@
 def last_kernel(blocks, *refs):
     sources, refs = refs[:12], refs[12:]
     own_coef, pair, other, params, place_of, cell_of, shift_of = refs[:7]
-    out, predicted, *levels, partial, coef, staged, sems, out_sems = refs[7:]
+    low_out, high_out, predicted, levels, partial, result, coef, sems = refs[7:]
     copies = Copies(sems)
     places = (
         (0, -8), (0, -4), (0, 16), (0, 20),
@@ -271,13 +278,43 @@
     )
     waits = [[] for _ in range(STEPS + 1)]
     for source, (level, row) in zip(sources, places):
-        count = GROUP * blocks if level == STEPS else GROUP
-        waits[level].append(
-            copies.start(source.at[0:count], region(levels, level, row, blocks))
-        )
+        waits[level].append(copies.start(source, region(levels, level, row, blocks)))
     waits[0] += load_coef(copies, own_coef, pair, other, place_of, coef)
-    edge_steps(6, blocks, waits, levels, partial, coef, params, lambda *_: None)
+    edge_steps(6, blocks, waits, (), levels, partial, result, coef, params)
     for copy in waits[STEPS]:
+        copy.wait()
+    sends = [
+        copies.start(region(levels, STEPS, row, blocks), out)
+        for row, out in ((0, low_out), (ROWS - GROUP, high_out))
+    ]
+    lane = lax.broadcasted_iota(jnp.int32, (SUBLANES, LANES), 1)
+
+    @pl.loop(0, predicted.shape[1] // LANES)
+    def _(block):
+        base = block * LANES
+
+        def some(part, found):
+            for i in range(PICKED):
+                o = part * PICKED + i
+                value = pltpu.roll(levels[cell_of[base + o]], shift_of[base + o], 1)
+                found = jnp.where(lane == o, value, found)
+            return found
+
+        empty = jnp.zeros((SUBLANES, LANES), jnp.float32)
+        predicted[:, block_at(block)] = lax.fori_loop(0, LANES // PICKED, some, empty)
+
+    for copy in sends:
+        copy.wait()
+
+
+def field_kernel(blocks, *refs):
+    parts, (out, cells, staged, sems, out_sems) = refs[: ROWS // GROUP], refs[ROWS // GROUP :]
+    copies = Copies(sems)
+    size = GROUP * blocks
+    waits = [
+        copies.start(part, cells.at[pl.ds(i * size, size)]) for i, part in enumerate(parts)
+    ]
+    for copy in waits:
         copy.wait()
 
     def out_copy(block):
@@ -286,21 +323,8 @@
     @pl.loop(0, blocks)
     def _(block):
         for row in range(ROWS):
-            staged[block, pl.ds(row, SUBLANES, stride=ROWS), :] = levels[STEPS][
-                (HALO + row) * blocks + block
-            ]
+            staged[block, pl.ds(row, SUBLANES, stride=ROWS), :] = cells[row * blocks + block]
         out_copy(block).start()
-
-    lane = lax.broadcasted_iota(jnp.int32, (SUBLANES, LANES), 1)
-
-    @pl.loop(0, predicted.shape[1] // LANES)
-    def _(block):
-        base = block * LANES
-        found = jnp.zeros((SUBLANES, LANES), jnp.float32)
-        for i in range(LANES):
-            value = levels[STEPS][cell_of[base + i]]
-            found = jnp.where(lane == i, pltpu.roll(value, shift_of[base + i], 1), found)
-        predicted[:, block_at(block)] = found
 
     @pl.loop(0, blocks)
     def _(block):
@@ -308,17 +332,15 @@
 
 
 def scratch(columns, *more):
-    return (
-        [pltpu.VMEM((ROWS + 2 * HALO, SUBLANES, columns), jnp.float32)] * STEPS
-        + [
-            pltpu.VMEM(
-                ((ROWS + 2 * HALO) * columns // LANES, SUBLANES, LANES), jnp.float32
-            ),
-            pltpu.VMEM((GROUP, SUBLANES, columns), jnp.float32),
-            pltpu.VMEM((4 * (ROWS + 2 * HALO), 1, columns), jnp.float32),
-        ]
-        + list(more)
-    )
+    blocks = columns // LANES
+    group = pltpu.VMEM((GROUP * blocks, SUBLANES, LANES), jnp.float32)
+    return [
+        pltpu.VMEM(((STEPS + 1) * ALL_ROWS * blocks, SUBLANES, LANES), jnp.float32),
+        group,
+        group,
+        pltpu.VMEM((4 * ALL_ROWS, 1, columns), jnp.float32),
+        *more,
+    ]
 
 
 def kernel_call(body, name, outs, specs, out_specs, scratches, cost, operands):
@@ -342,11 +364,11 @@
     flat = tracer.reshape(members * rows, columns)
     dma = pltpu.SemaphoreType.DMA
     scratches = [pltpu.VMEM((blocks, members * rows, LANES), jnp.float32), dma((blocks,))]
-    group, edge = (GROUP, members, columns), (HALO, columns)
+    group, edge = (GROUP * blocks, members, LANES), (HALO, columns)
     up, down, up_coef, down_coef = kernel_call(
         functools.partial(outer_rows_kernel, blocks), "outer_rows",
         [group, group, edge, edge], [ANYWHERE, ANYWHERE, IN_SMEM],
-        (IN_VMEM, IN_VMEM, ANYWHERE, ANYWHERE),
+        (IN_VMEM,) * 4,
         scratches + [dma((2,))], 3, [flat, coefficients, place_of],
     )
     low, high = kernel_call(
@@ -360,15 +382,15 @@
 def transport(shape, own, low0, high0, own_coef, pair, other, params, place_of, obs_index, halos):
     members, rows, columns = shape
     blocks = columns // LANES
-    group = (GROUP, members, columns)
+    group = (GROUP * blocks, members, LANES)
     flat = (members * rows, columns)
-    cells = (GROUP * blocks, members, LANES)
     dma = pltpu.SemaphoreType.DMA
     staged = pltpu.VMEM((blocks, members * rows, LANES), jnp.float32)
+    gated, pair = lax.optimization_barrier((params, pair))
     inner = kernel_call(
         functools.partial(interior_kernel, blocks), "interior",
         [group] * 5, [ANYWHERE] * 5 + [IN_VMEM], (ANYWHERE,) * 5,
-        scratch(columns, dma((16,))), 8, [*own, own_coef, params],
+        scratch(columns, dma((16,))), 8, [*own, own_coef, gated],
     )
     upper, lower, low0, high0, *_ = lax.optimization_barrier(
         (own[2], own[1], low0, high0, inner[0])
@@ -376,19 +398,25 @@
     low1, high1 = halos(upper, lower)
     first = kernel_call(
         functools.partial(middle_kernel, blocks), "edge_first",
-        [group] * 6 + [cells] * 2, [ANYWHERE] * 12 + [IN_VMEM, IN_SMEM], (ANYWHERE,) * 8,
+        [group] * 8, [ANYWHERE] * 12 + [IN_VMEM, IN_SMEM], (ANYWHERE,) * 8,
         scratch(columns, dma((29,))), 10,
         [low0, own[0], own[3], high0, *inner, own_coef, pair, other, params, place_of],
     )
-    cell_of = obs_index // LANES + HALO * blocks
+    cell_of = obs_index // LANES + (STEPS * ALL_ROWS + HALO) * blocks
     lane_of = obs_index % LANES
     shift_of = (jnp.arange(obs_index.shape[0], dtype=jnp.int32) - lane_of) % LANES
-    field, predicted = kernel_call(
+    low4, high4, predicted = kernel_call(
         functools.partial(last_kernel, blocks), "edge_last",
-        [flat, (members, obs_index.shape[0])],
-        [ANYWHERE] * 15 + [IN_VMEM] + [IN_SMEM] * 3, (ANYWHERE, IN_VMEM),
-        scratch(columns, staged, dma((29,)), dma((blocks,))), 15,
+        [group, group, (members, obs_index.shape[0])],
+        [ANYWHERE] * 15 + [IN_VMEM] + [IN_SMEM] * 3, (ANYWHERE, ANYWHERE, IN_VMEM),
+        scratch(columns, dma((31,))), 15,
         [low1, low0, high0, high1, *first, own_coef, pair, other, params, place_of, cell_of, shift_of],
+    )
+    (field,) = kernel_call(
+        functools.partial(field_kernel, blocks), "field",
+        [flat], [ANYWHERE] * 4, (ANYWHERE,),
+        [pltpu.VMEM((rows * blocks, members, LANES), jnp.float32), staged, dma((4,)), dma((blocks,))],
+        4, [low4, first[6], first[7], high4],
     )
     return field.reshape(shape), predicted, inner[0]
 

time: 123 us -> 126 us (1.024)
  waiting for transfers between devices: 8.37 us -> 11.5 us
    ppermute x3, waiting for transfers between devices: 0.8 us -> 5.18 us  [halos(): lax.ppermute(upper, 'slab', forward)]
    ppermute x3, waiting for transfers between devices: 0.01 us -> 1.77 us  [halos(): lax.ppermute(lower, 'slab', backward)]
    ppermute x2, waiting for transfers between devices: 3.4 us -> 2.11 us  [over_ens(): lax.ppermute(pair, 'ens', [(i, i ^ 2) for i in range(ens_count)])]
    ppermute x3, waiting for transfers between devices: 3.68 us -> 2.4 us  [local(): products = products + lax.ppermute(products, 'slab', pairs)]
    pallas_call x5 -> x6, Pallas kernels: 68.3 us -> 68.2 us  [kernel_call(): pl.pallas_call(body, out_shape=tuple((jax.ShapeDtypeStruct(shape, jnp.flo...]
  transfers between devices with their start and end apart: 13 -> 13, of which waited for: 6 -> 6; matrix products, arithmetic and copies ran while one was open for 3% -> 3% of each run, Pallas kernels for 48% -> 53%
where the time goes in v6:
time: 126 us; the launch traced here: 125 us
  Pallas kernels  70.9 us (56%)
  starting transfers between devices  30.8 us (24%)
  waiting for transfers between devices  11.5 us (9%)
  blocking collectives  6 us (5%)
  other arithmetic  2.66 us (2%)
  local copies, waits for them, and re-layouts  1.89 us (2%)
    pallas_call x6, Pallas kernels, kernel_call(): pl.pallas_call(body, out_shape=tuple((jax.ShapeDtypeStruct(shape, jnp.flo...  68.2 us
    ppermute x3, starting transfers between devices, halos(): lax.ppermute(upper, 'slab', forward)  14.9 us
    ppermute x3, starting transfers between devices, local(): products = products + lax.ppermute(products, 'slab', pairs)  8.71 us
    all_gather x1, blocking collectives, local(): everyone = lax.all_gather(predicted, 'ens', axis=0, tiled=True)  6 us
    ppermute x3, waiting for transfers between devices, halos(): lax.ppermute(upper, 'slab', forward)  5.18 us
    ppermute x3, starting transfers between devices, halos(): lax.ppermute(lower, 'slab', backward)  3.86 us
    ppermute x2, starting transfers between devices, over_ens(): lax.ppermute(pair, 'ens', [(i, i ^ 2) for i in range(ens_count)])  3.04 us
  transfers between devices with their start and end apart: 13, of which 6 were waited for; matrix products, arithmetic and copies ran while one was open for 3% of the time, Pallas kernels for 53%

profile of v6, /device:TPU:0, one launch (start us, length us, event | category | flops | bytes accessed | tf_op | source)
XLA Modules:
  0.0 125.1 jit_solution(4659533514091078652)
XLA Ops:
  0.6 3.1 %outer_rows.1 = (f32[128,8,128]{2,1,0:T(8,128)}, f32[128,8,128]{2,1,0:T(8,128)}, f32[8,4096]{1,0:T(8,128)}, f32[8,4096]{1,0:T(8,128)}) custom-call(f32[128,4096]{1,0:T(8,128)} %bitcast.28, f32[4,16,4096]{2,1,0:T(8,128)} %refs_12_.3, s32[1]{0:T(128)} %bitcast.1.place_of.refs_13_.refs_16_), custom_call_target="tpu_custom_call" | custom-call | bytes 600000 | tf_op jit(solution)/shard_map/outer_rows/pallas_call | solution.py:347
  3.7 0.0 copy-start.11
  3.7 1.3 %collective-permute-start.3 = (f32[8,4096]{1,0:T(8,128)}, f32[8,4096]{1,0:T(8,128)S(1)}, u32[]{:S(2)}, u32[]{:S(2)}) collective-permute-start(f32[8,4096]{1,0:T(8,128)} %get-tuple-element.36), channel_id=1, source_target_pairs={{1,0},{2,1},{3,2},{4,3},{5,4},{6,5},{7,6},{9,8},{10,9},{11,10},{12... | collective-permute-start | bytes 393224 | tf_op jit(solution)/shard_map/ppermute | solution.py:485
  5.0 5.5 %collective-permute-start.2 = (f32[8,4096]{1,0:T(8,128)}, f32[8,4096]{1,0:T(8,128)S(1)}, u32[]{:S(2)}, u32[]{:S(2)}) collective-permute-start(f32[8,4096]{1,0:T(8,128)} %get-tuple-element.35), channel_id=1, source_target_pairs={{0,1},{1,2},{2,3},{3,4},{4,5},{5,6},{6,7},{8,9},{9,10},{10,11},{11... | collective-permute-start | bytes 393224 | tf_op jit(solution)/shard_map/ppermute | solution.py:485
  10.5 1.8 %collective-permute-done.3 = f32[8,4096]{1,0:T(8,128)S(1)} collective-permute-done((f32[8,4096]{1,0:T(8,128)}, f32[8,4096]{1,0:T(8,128)S(1)}, u32[]{:S(2)}, u32[]{:S(2)}) %collective-permute-start.3) | collective-permute-done | bytes 131104 | tf_op jit(solution)/shard_map/ppermute | solution.py:485
  12.3 3.1 %collective-permute-done.2 = f32[8,4096]{1,0:T(8,128)S(1)} collective-permute-done((f32[8,4096]{1,0:T(8,128)}, f32[8,4096]{1,0:T(8,128)S(1)}, u32[]{:S(2)}, u32[]{:S(2)}) %collective-permute-start.2) | collective-permute-done | bytes 131104 | tf_op jit(solution)/shard_map/ppermute | solution.py:485
  15.4 0.1 collective-permute-start.4
  15.5 4.3 %collective-permute-start = (f32[128,8,128]{2,1,0:T(8,128)}, f32[128,8,128]{2,1,0:T(8,128)S(1)}, u32[]{:S(2)}, u32[]{:S(2)}) collective-permute-start(f32[128,8,128]{2,1,0:T(8,128)} %get-tuple-element.31.outer.own3.refs_2_), channel_id=1, source_target_pairs={{0,1},{1,2},{2,3},{3,4},{4,5},{5,6},{6,7},{8,9},{9,10},{10,11},{11... | collective-permute-start | bytes 1572872 | tf_op jit(solution)/shard_map/ppermute | solution.py:485
  19.8 1.3 %collective-permute-start.1 = (f32[128,8,128]{2,1,0:T(8,128)}, f32[128,8,128]{2,1,0:T(8,128)S(1)}, u32[]{:S(2)}, u32[]{:S(2)}) collective-permute-start(f32[128,8,128]{2,1,0:T(8,128)} %get-tuple-element.34.own0.refs_1_), channel_id=1, source_target_pairs={{1,0},{2,1},{3,2},{4,3},{5,4},{6,5},{7,6},{9,8},{10,9},{11,10},{12... | collective-permute-start | bytes 1572872 | tf_op jit(solution)/shard_map/ppermute | solution.py:485
  21.1 2.9 %inner_rows.1 = (f32[128,8,128]{2,1,0:T(8,128)}, f32[128,8,128]{2,1,0:T(8,128)}) custom-call(f32[128,4096]{1,0:T(8,128)} %bitcast.29, f32[128,8,128]{2,1,0:T(8,128)} %get-tuple-element.31.outer.own3.refs_2_), custom_call_target="tpu_custom_call" | custom-call | bytes 600000 | tf_op jit(solution)/shard_map/inner_rows/pallas_call | solution.py:347
  24.0 0.0 copy-done.11
  24.0 0.6 add_select_fusion
  24.6 0.0 collective-permute-done.4
  24.6 0.0 copy-start
  24.6 0.0 copy-start.10
  24.6 0.0 copy-start.9
  24.7 0.0 copy-start.5
  24.7 14.4 %interior.1 = (f32[128,8,128]{2,1,0:T(8,128)}, f32[128,8,128]{2,1,0:T(8,128)}, f32[128,8,128]{2,1,0:T(8,128)}, f32[128,8,128]{2,1,0:T(8,128)}, f32[128,8,128]{2,1,0:T(8,128)}) custom-call(f32[128,8,128]{2,1,0:T(8,128)} %get-tuple-element.34.own0.refs_1_, f32[128,8,128]{2,1,0:T(8,128)} %get-tuple-element.42.own1, f32[128,8,128]{2,1,0:T(8,128)} %get-tuple-element.39.own2, ...), custom_call_target="tpu_custom_call" | custom-call | bytes 1600000 | tf_op jit(solution)/shard_map/interior/pallas_call | solution.py:347
  39.1 0.0 copy-done
  39.1 0.3 collective-permute-start.11
  39.4 0.0 copy-done.12
  39.4 0.1 compare_convert_fusion.same
  39.5 1.5 %collective-permute-start.7 = (f32[2,2,8,4096]{3,2,1,0:T(8,128)S(1)}, f32[2,2,8,4096]{3,2,1,0:T(8,128)S(1)}, u32[]{:S(2)}, u32[]{:S(2)}) collective-permute-start(f32[2,2,8,4096]{3,2,1,0:T(8,128)S(1)} %pad_maximum_fusion.refs_10_.refs_13_), channel_id=1, source_target_pairs={{0,16},{8,24},{16,0},{24,8},{1,17},{9,25},{17,1},{25,9},{2,18},{10... | collective-permute-start | bytes 1572872 | tf_op jit(solution)/shard_map/ppermute | solution.py:482
  41.0 2.1 %collective-permute-done.refs_0_.refs_1_ = f32[128,8,128]{2,1,0:T(8,128)S(1)} collective-permute-done((f32[128,8,128]{2,1,0:T(8,128)}, f32[128,8,128]{2,1,0:T(8,128)S(1)}, u32[]{:S(2)}, u32[]{:S(2)}) %collective-permute-start) | collective-permute-done | bytes 524320 | tf_op jit(solution)/shard_map/ppermute | solution.py:485
  43.1 0.0 collective-permute-done.1.refs_3_.refs_2_
  43.1 0.0 copy-done.10
  43.1 5.1 %collective-permute-start.5 = (f32[128,8,128]{2,1,0:T(8,128)S(1)}, f32[128,8,128]{2,1,0:T(8,128)}, u32[]{:S(2)}, u32[]{:S(2)}) collective-permute-start(f32[128,8,128]{2,1,0:T(8,128)S(1)} %copy-done.10), channel_id=1, source_target_pairs={{0,1},{1,2},{2,3},{3,4},{4,5},{5,6},{6,7},{8,9},{9,10},{10,11},{11... | collective-permute-start | bytes 1572872 | tf_op jit(solution)/shard_map/ppermute | solution.py:485
  48.2 0.0 copy-done.9
  48.2 1.3 %collective-permute-start.6 = (f32[128,8,128]{2,1,0:T(8,128)S(1)}, f32[128,8,128]{2,1,0:T(8,128)}, u32[]{:S(2)}, u32[]{:S(2)}) collective-permute-start(f32[128,8,128]{2,1,0:T(8,128)S(1)} %copy-done.9), channel_id=1, source_target_pairs={{1,0},{2,1},{3,2},{4,3},{5,4},{6,5},{7,6},{9,8},{10,9},{11,10},{12... | collective-permute-start | bytes 1572872 | tf_op jit(solution)/shard_map/ppermute | solution.py:485
  49.5 0.0 collective-permute-done.11
  49.5 0.7 pad_maximum_fusion.3
  50.2 1.5 %collective-permute-start.12 = (f32[2,8,4096]{2,1,0:T(8,128)}, f32[2,8,4096]{2,1,0:T(8,128)}, u32[]{:S(2)}, u32[]{:S(2)}) collective-permute-start(f32[2,8,4096]{2,1,0:T(8,128)} %pad_maximum_fusion.3), channel_id=1, source_target_pairs={{0,16},{8,24},{16,0},{24,8},{1,17},{9,25},{17,1},{25,9},{2,18},{10... | collective-permute-start | bytes 786440 | tf_op jit(solution)/shard_map/ppermute | solution.py:482
  51.8 0.2 convert_reduce_fusion
  52.0 0.1 copy.9.rank_col
  52.0 0.1 constant_dynamic-slice_fusion.own_same
  52.1 2.1 %collective-permute-done.7.refs_11_.refs_14_ = f32[2,2,8,4096]{3,2,1,0:T(8,128)S(1)} collective-permute-done((f32[2,2,8,4096]{3,2,1,0:T(8,128)S(1)}, f32[2,2,8,4096]{3,2,1,0:T(8,128)S(1)}, u32[]{:S(2)}, u32[]{:S(2)}) %collective-permute-start.7) | collective-permute-done | bytes 524320 | tf_op jit(solution)/shard_map/ppermute | solution.py:482
  54.2 0.0 copy-done.5
  54.2 0.0 copy-done.6
  54.2 0.0 copy-done.7
  54.2 0.8 copy-done.8
  55.0 18.0 %edge_first.1 = (f32[128,8,128]{2,1,0:T(8,128)}, f32[128,8,128]{2,1,0:T(8,128)}, f32[128,8,128]{2,1,0:T(8,128)}, f32[128,8,128]{2,1,0:T(8,128)}, f32[128,8,128]{...) custom-call(f32[128,8,128]{2,1,0:T(8,128)} %copy-done.6, ...), custom_call_target="tpu_custom_call" | custom-call | bytes 2000000 | tf_op jit(solution)/shard_map/edge_first/pallas_call | solution.py:347
  73.1 0.0 collective-permute-done.5.refs_0_
  73.1 0.0 collective-permute-done.6.refs_3_
  73.1 0.0 copy-start.3
  73.1 0.0 copy-start.4
  73.1 0.0 copy-start.1
  73.1 26.5 %edge_last.1 = (f32[128,8,128]{2,1,0:T(8,128)}, f32[128,8,128]{2,1,0:T(8,128)}, f32[8,2048]{1,0:T(8,128)}) custom-call(f32[128,8,128]{2,1,0:T(8,128)} %collective-permute-done.5.refs_0_, f32[128,8,128]{2,1,0:T(8,128)} %copy-done.6, f32[128,8,128]{2,1,0:T(8,128)} %copy-done.7, f32[128,8,128]{2,1,0:T(8,128)} %collective-permute-done.6.refs_3_, ...), custom_call_target="tpu_custom_call" | custom-call | bytes 3000000 | tf_op jit(solution)/shard_map/edge_last/pallas_call | solution.py:347
  99.6 6.0 %all_gather.3.everyone = f32[32,2048]{1,0:T(8,128)S(1)} all-gather(f32[8,2048]{1,0:T(8,128)} %get-tuple-element.58.own), channel_id=1, replica_groups=mesh['ens'=4,'slab'=8] {'ens'}, dimensions={0}, use_global_device_ids=true | all-gather | bytes 327680 | tf_op jit(solution)/shard_map/all_gather | solution.py:513
  105.6 0.0 copy-done.3
  105.6 0.0 copy-done.4
  105.6 0.8 copy-done.2
  106.5 0.6 products.1
  107.1 2.5 %collective-permute-start.8 = (f32[32,40]{1,0:T(8,128)S(1)}, f32[32,40]{1,0:T(8,128)S(1)}, u32[]{:S(2)}, u32[]{:S(2)}) collective-permute-start(f32[32,40]{1,0:T(8,128)S(1)} %products.1), channel_id=1, source_target_pairs={{0,1},{1,0},{2,3},{3,2},{4,5},{5,4},{6,7},{7,6},{8,9},{9,8},{10,11... | collective-permute-start | bytes 15368 | tf_op jit(solution)/shard_map/ppermute | solution.py:524
  109.6 0.0 collective-permute-done.12
  109.6 0.0 copy-done.1
  109.6 1.0 pad_maximum_fusion.1
  110.6 0.7 collective-permute-done.8
  111.3 3.2 %collective-permute-start.9 = (f32[32,40]{1,0:T(8,128)S(1)}, f32[32,40]{1,0:T(8,128)S(1)}, u32[]{:S(2)}, u32[]{:S(2)}) collective-permute-start(f32[32,40]{1,0:T(8,128)S(1)} %add.46), channel_id=1, source_target_pairs={{0,2},{1,3},{2,0},{3,1},{4,6},{5,7},{6,4},{7,5},{8,10},{9,11},{10,... | collective-permute-start | bytes 15368 | tf_op jit(solution)/shard_map/ppermute | solution.py:524
  114.5 1.7 %collective-permute-done.9 = f32[32,40]{1,0:T(8,128)S(1)} collective-permute-done((f32[32,40]{1,0:T(8,128)S(1)}, f32[32,40]{1,0:T(8,128)S(1)}, u32[]{:S(2)}, u32[]{:S(2)}) %collective-permute-start.9) | collective-permute-done | bytes 5152 | tf_op jit(solution)/shard_map/ppermute | solution.py:524
  116.2 3.0 %collective-permute-start.10 = (f32[32,40]{1,0:T(8,128)S(1)}, f32[32,40]{1,0:T(8,128)S(1)}, u32[]{:S(2)}, u32[]{:S(2)}) collective-permute-start(f32[32,40]{1,0:T(8,128)S(1)} %add.47), channel_id=1, source_target_pairs={{0,4},{1,5},{2,6},{3,7},{4,0},{5,1},{6,2},{7,3},{8,12},{9,13},{10,... | collective-permute-start | bytes 15368 | tf_op jit(solution)/shard_map/ppermute | solution.py:524
  119.2 0.4 fusion.1.anomalies
  119.7 3.3 %field.1 = f32[128,4096]{1,0:T(8,128)} custom-call(f32[128,8,128]{2,1,0:T(8,128)} %get-tuple-element.56.refs_0_, f32[128,8,128]{2,1,0:T(8,128)} %get-tuple-element.54.refs_10_.refs_1_, f32[128,8,128]{2,1,0:T(8,128)} %get-tuple-element.55.refs_11_.refs_2_, f32[128,8,128]{2,1,0:T(8,128)} %get-tuple-element.57.refs_3_), custom_call_target="tpu_custom_call" | custom-call | bytes 800000 | tf_op jit(solution)/shard_map/field/pallas_call | solution.py:347
  123.0 0.0 collective-permute-done.10
  123.0 2.1 %update.1 = f32[8,4096]{1,0:T(8,128)} custom-call(f32[1,32,40]{2,1,0:T(8,128)S(1)} %add_bitcast_fusion.summands, f32[32,32]{1,0:T(8,128)S(1)} %compare_convert_fusion.same, f32[32,8]{1,0:T(8,128)S(1)} %constant_dynamic-slice_fusion.own_same, s32[1,32]{1,0:T(1,128)S(1)} %bitcast.27, s32[32,1]{1,0:T(8,128)S(1)} %copy.9.rank_col, ...), custom_call_target="tpu_custom_call" | custom-call | tf_op jit(solution)/shard_map/update/pallas_call | solution.py:526
  (11 shorter events, 0.1 us)
Async XLA Ops:
  3.7 20.3 %copy-start.11 = (s32[2048]{0:T(1024)S(1)}, s32[2048]{0:T(1024)}, u32[]{:S(2)}) copy-start(s32[2048]{0:T(1024)} %param.10) | copy-start | bytes 24580
  3.7 8.5 %collective-permute-start.3 = (f32[8,4096]{1,0:T(8,128)}, f32[8,4096]{1,0:T(8,128)S(1)}, u32[]{:S(2)}, u32[]{:S(2)}) collective-permute-start(f32[8,4096]{1,0:T(8,128)} %get-tuple-element.36), channel_id=1, source_target_pairs={{1,0},{2,1},{3,2},{4,3},{5,4},{6,5},{7,6},{9,8},{10,9},{11,10},{12... | collective-permute-start | bytes 393224 | tf_op jit(solution)/shard_map/ppermute | solution.py:485
  5.0 10.3 %collective-permute-start.2 = (f32[8,4096]{1,0:T(8,128)}, f32[8,4096]{1,0:T(8,128)S(1)}, u32[]{:S(2)}, u32[]{:S(2)}) collective-permute-start(f32[8,4096]{1,0:T(8,128)} %get-tuple-element.35), channel_id=1, source_target_pairs={{0,1},{1,2},{2,3},{3,4},{4,5},{5,6},{6,7},{8,9},{9,10},{10,11},{11... | collective-permute-start | bytes 393224 | tf_op jit(solution)/shard_map/ppermute | solution.py:485
  15.4 9.2 %collective-permute-start.4 = (f32[2,8,4096]{2,1,0:T(8,128)S(1)}, f32[2,8,4096]{2,1,0:T(8,128)S(1)}, u32[]{:S(2)}, u32[]{:S(2)}) collective-permute-start(f32[2,8,4096]{2,1,0:T(8,128)S(1)} %get-tuple-element.65), channel_id=1, source_target_pairs={{0,8},{8,0},{16,24},{24,16},{1,9},{9,1},{17,25},{25,17},{2,10},{10... | collective-permute-start | bytes 786440 | tf_op jit(solution)/shard_map/ppermute | solution.py:481
  15.5 27.6 %collective-permute-start = (f32[128,8,128]{2,1,0:T(8,128)}, f32[128,8,128]{2,1,0:T(8,128)S(1)}, u32[]{:S(2)}, u32[]{:S(2)}) collective-permute-start(f32[128,8,128]{2,1,0:T(8,128)} %get-tuple-element.31.outer.own3.refs_2_), channel_id=1, source_target_pairs={{0,1},{1,2},{2,3},{3,4},{4,5},{5,6},{6,7},{8,9},{9,10},{10,11},{11... | collective-permute-start | bytes 1572872 | tf_op jit(solution)/shard_map/ppermute | solution.py:485
  19.8 23.3 %collective-permute-start.1 = (f32[128,8,128]{2,1,0:T(8,128)}, f32[128,8,128]{2,1,0:T(8,128)S(1)}, u32[]{:S(2)}, u32[]{:S(2)}) collective-permute-start(f32[128,8,128]{2,1,0:T(8,128)} %get-tuple-element.34.own0.refs_1_), channel_id=1, source_target_pairs={{1,0},{2,1},{3,2},{4,3},{5,4},{6,5},{7,6},{9,8},{10,9},{11,10},{12... | collective-permute-start | bytes 1572872 | tf_op jit(solution)/shard_map/ppermute | solution.py:485
  24.6 14.5 %copy-start = (f32[8,4096]{1,0:T(8,128)S(1)}, f32[8,4096]{1,0:T(8,128)}, u32[]{:S(2)}) copy-start(f32[8,4096]{1,0:T(8,128)} %own.1) | copy-start | bytes 393220
  24.6 14.8 %copy-start.12 = (s32[32]{0:T(128)S(1)}, s32[32]{0:T(128)}, u32[]{:S(2)}) copy-start(s32[32]{0:T(128)} %param.13) | copy-start | bytes 388
  24.6 18.5 %copy-start.10 = (f32[128,8,128]{2,1,0:T(8,128)S(1)}, f32[128,8,128]{2,1,0:T(8,128)}, u32[]{:S(2)}) copy-start(f32[128,8,128]{2,1,0:T(8,128)} %get-tuple-element.39.own2) | copy-start | bytes 1572868
  24.6 23.6 %copy-start.9 = (f32[128,8,128]{2,1,0:T(8,128)S(1)}, f32[128,8,128]{2,1,0:T(8,128)}, u32[]{:S(2)}) copy-start(f32[128,8,128]{2,1,0:T(8,128)} %get-tuple-element.42.own1) | copy-start | bytes 1572868
  24.7 29.6 %copy-start.5 = (f32[2,2,8,4096]{3,2,1,0:T(8,128)}, f32[2,2,8,4096]{3,2,1,0:T(8,128)S(1)}, u32[]{:S(2)}) copy-start(f32[2,2,8,4096]{3,2,1,0:T(8,128)S(1)} %pad_maximum_fusion.refs_10_.refs_13_) | copy-start | bytes 1572868
  39.1 10.4 %collective-permute-start.11 = (f32[8,4096]{1,0:T(8,128)S(1)}, f32[8,4096]{1,0:T(8,128)S(1)}, u32[]{:S(2)}, u32[]{:S(2)}) collective-permute-start(f32[8,4096]{1,0:T(8,128)S(1)} %copy-done), channel_id=1, source_target_pairs={{0,8},{8,0},{16,24},{24,16},{1,9},{9,1},{17,25},{25,17},{2,10},{10... | collective-permute-start | bytes 393224 | tf_op jit(solution)/shard_map/ppermute | solution.py:481
  39.5 14.8 %collective-permute-start.7 = (f32[2,2,8,4096]{3,2,1,0:T(8,128)S(1)}, f32[2,2,8,4096]{3,2,1,0:T(8,128)S(1)}, u32[]{:S(2)}, u32[]{:S(2)}) collective-permute-start(f32[2,2,8,4096]{3,2,1,0:T(8,128)S(1)} %pad_maximum_fusion.refs_10_.refs_13_), channel_id=1, source_target_pairs={{0,16},{8,24},{16,0},{24,8},{1,17},{9,25},{17,1},{25,9},{2,18},{10... | collective-permute-start | bytes 1572872 | tf_op jit(solution)/shard_map/ppermute | solution.py:482
  43.1 11.1 %copy-start.6 = (f32[128,8,128]{2,1,0:T(8,128)}, f32[128,8,128]{2,1,0:T(8,128)S(1)}, u32[]{:S(2)}) copy-start(f32[128,8,128]{2,1,0:T(8,128)S(1)} %collective-permute-done.refs_0_.refs_1_) | copy-start | bytes 1572868
  43.1 11.1 %copy-start.7 = (f32[128,8,128]{2,1,0:T(8,128)}, f32[128,8,128]{2,1,0:T(8,128)S(1)}, u32[]{:S(2)}) copy-start(f32[128,8,128]{2,1,0:T(8,128)S(1)} %collective-permute-done.1.refs_3_.refs_2_) | copy-start | bytes 1572868
  43.1 30.0 %collective-permute-start.5 = (f32[128,8,128]{2,1,0:T(8,128)S(1)}, f32[128,8,128]{2,1,0:T(8,128)}, u32[]{:S(2)}, u32[]{:S(2)}) collective-permute-start(f32[128,8,128]{2,1,0:T(8,128)S(1)} %copy-done.10), channel_id=1, source_target_pairs={{0,1},{1,2},{2,3},{3,4},{4,5},{5,6},{6,7},{8,9},{9,10},{10,11},{11... | collective-permute-start | bytes 1572872 | tf_op jit(solution)/shard_map/ppermute | solution.py:485
  48.2 24.9 %collective-permute-start.6 = (f32[128,8,128]{2,1,0:T(8,128)S(1)}, f32[128,8,128]{2,1,0:T(8,128)}, u32[]{:S(2)}, u32[]{:S(2)}) collective-permute-start(f32[128,8,128]{2,1,0:T(8,128)S(1)} %copy-done.9), channel_id=1, source_target_pairs={{1,0},{2,1},{3,2},{4,3},{5,4},{6,5},{7,6},{9,8},{10,9},{11,10},{12... | collective-permute-start | bytes 1572872 | tf_op jit(solution)/shard_map/ppermute | solution.py:485
  50.2 59.3 %collective-permute-start.12 = (f32[2,8,4096]{2,1,0:T(8,128)}, f32[2,8,4096]{2,1,0:T(8,128)}, u32[]{:S(2)}, u32[]{:S(2)}) collective-permute-start(f32[2,8,4096]{2,1,0:T(8,128)} %pad_maximum_fusion.3), channel_id=1, source_target_pairs={{0,16},{8,24},{16,0},{24,8},{1,17},{9,25},{17,1},{25,9},{2,18},{10... | collective-permute-start | bytes 786440 | tf_op jit(solution)/shard_map/ppermute | solution.py:482
  54.2 0.8 copy-start.8
  73.1 32.5 %copy-start.3 = (f32[8,2048]{1,0:T(8,128)S(1)}, f32[8,2048]{1,0:T(8,128)}, u32[]{:S(2)}) copy-start(f32[8,2048]{1,0:T(8,128)} %values.1) | copy-start | bytes 196612
  73.1 32.5 %copy-start.4 = (f32[2048]{0:T(1024)S(1)}, f32[2048]{0:T(1024)}, u32[]{:S(2)}) copy-start(f32[2048]{0:T(1024)} %param.12) | copy-start | bytes 24580
  73.1 36.5 %copy-start.1 = (f32[8,4096]{1,0:T(8,128)S(1)}, f32[8,4096]{1,0:T(8,128)}, u32[]{:S(2)}) copy-start(f32[8,4096]{1,0:T(8,128)} %own.1) | copy-start | bytes 393220
  105.6 0.8 copy-start.2
  107.1 4.2 %collective-permute-start.8 = (f32[32,40]{1,0:T(8,128)S(1)}, f32[32,40]{1,0:T(8,128)S(1)}, u32[]{:S(2)}, u32[]{:S(2)}) collective-permute-start(f32[32,40]{1,0:T(8,128)S(1)} %products.1), channel_id=1, source_target_pairs={{0,1},{1,0},{2,3},{3,2},{4,5},{5,4},{6,7},{7,6},{8,9},{9,8},{10,11... | collective-permute-start | bytes 15368 | tf_op jit(solution)/shard_map/ppermute | solution.py:524
  111.3 4.9 %collective-permute-start.9 = (f32[32,40]{1,0:T(8,128)S(1)}, f32[32,40]{1,0:T(8,128)S(1)}, u32[]{:S(2)}, u32[]{:S(2)}) collective-permute-start(f32[32,40]{1,0:T(8,128)S(1)} %add.46), channel_id=1, source_target_pairs={{0,2},{1,3},{2,0},{3,1},{4,6},{5,7},{6,4},{7,5},{8,10},{9,11},{10,... | collective-permute-start | bytes 15368 | tf_op jit(solution)/shard_map/ppermute | solution.py:524
  116.2 6.7 %collective-permute-start.10 = (f32[32,40]{1,0:T(8,128)S(1)}, f32[32,40]{1,0:T(8,128)S(1)}, u32[]{:S(2)}, u32[]{:S(2)}) collective-permute-start(f32[32,40]{1,0:T(8,128)S(1)} %add.47), channel_id=1, source_target_pairs={{0,4},{1,5},{2,6},{3,7},{4,0},{5,1},{6,2},{7,3},{8,12},{9,13},{10,... | collective-permute-start | bytes 15368 | tf_op jit(solution)/shard_map/ppermute | solution.py:524

commit v7 on v6

--- a/solution.py
+++ b/solution.py
@@ -15,11 +15,10 @@
 SUBLANES = 8
 ROWS = 16
 GROUP = 4
-LAG = 3
+WIDE = 4
 TOGETHER = 2
-WIDE = 8
 MOVED = 16
-PICKED = 32
+PICKED = 128
 ALL_ROWS = ROWS + 2 * HALO
 VMEM_LIMIT = 16 * 1024 * 1024
 TALL_LIMIT = 58 * 1024 * 1024
@@ -45,45 +44,62 @@
     return jnp.broadcast_to(row, (SUBLANES, LANES))
 
 
-def columns_pass(levels, cell, row, count, partial, first_cell, coef, params, blocks):
+def edge_lanes():
     lane = lax.broadcasted_iota(jnp.int32, (SUBLANES, LANES), 1)
-    first, last = lane == 0, lane == LANES - 1
-    places = [[coef_row(array, row + i) for array in range(4)] for i in range(count)]
-    c, c_rolled, d, d_rolled, slope, twice, left, right, laplace = ({} for _ in range(9))
-    for tick in range(blocks + 2 * LAG + 4):
-        for i in range(count):
-            b = tick - 1
-            if b <= blocks:
-                c[i, b] = levels[cell + i * blocks + b % blocks]
-                c_rolled[i, b] = pltpu.roll(c[i, b], LANES - 1, 1)
-            b = tick - 2
-            if -1 <= b <= blocks:
-                c_next = c_rolled[i, b]
-                if b < blocks:
-                    c_next = jnp.where(last, c_rolled[i, b + 1], c_next)
-                d[i, b] = c_next - c[i, b]
-                d_rolled[i, b] = pltpu.roll(d[i, b], 1, 1)
-            b = tick - 2 - LAG
-            if -1 <= b <= blocks:
-                d_back = d_rolled[i, b]
-                if b >= 0:
-                    d_back = jnp.where(first, d_rolled[i, b - 1], d_back)
-                slope[i, b] = limited(d_back, d[i, b])
-                twice[i, b] = d[i, b] + d[i, b]
-                laplace[i, b] = d[i, b] - d_back
-                left[i, b] = pltpu.roll(twice[i, b] - slope[i, b], 1, 1)
-                right[i, b] = pltpu.roll(slope[i, b], LANES - 1, 1)
-            b = tick - 3 - 2 * LAG
-            if 0 <= b < blocks:
-                at = block_at(b)
-                speed = wide(coef[places[i][1], :, at])
-                forward = jnp.where(first, left[i, b - 1], left[i, b])
-                backward = twice[i, b] - jnp.where(last, right[i, b + 1], right[i, b])
-                change = jnp.where(speed > 0.0, forward, backward) + slope[i, b]
-                value = c[i, b] - (0.5 * speed) * change
-                value = value + wide(coef[places[i][2], :, at]) * laplace[i, b]
-                value = value + params[:, at] * wide(coef[places[i][3], :, at])
-                partial[first_cell + i * blocks + b] = value
+    return lane == 0, lane == LANES - 1
+
+
+def to_left(value):
+    return pltpu.roll(value, LANES - 1, 1)
+
+
+def to_right(value):
+    return pltpu.roll(value, 1, 1)
+
+
+def difference_pass(levels, cell, first_cell, diff, blocks):
+    _, last = edge_lanes()
+    centre = levels[cell]
+    rolled = to_left(centre)
+    for b in range(blocks):
+        following = levels[cell + (b + 1) % blocks]
+        rolled_following = to_left(following)
+        diff[first_cell + b] = jnp.where(last, rolled_following, rolled) - centre
+        centre, rolled = following, rolled_following
+
+
+def slope_pass(levels, cell, places, first_cell, diff, slopes, linear, coef, params, blocks):
+    first, _ = edge_lanes()
+    rolled = to_right(diff[first_cell + blocks - 1])
+    for b in range(blocks):
+        at = block_at(b)
+        d = diff[first_cell + b]
+        here = to_right(d)
+        d_back = jnp.where(first, rolled, here)
+        rolled = here
+        slopes[first_cell + b] = limited(d_back, d)
+        value = levels[cell + b] + wide(coef[places[2], :, at]) * (d - d_back)
+        linear[first_cell + b] = value + params[:, at] * wide(coef[places[3], :, at])
+
+
+def flux_pass(places, first_cell, diff, slopes, linear, partial, coef, blocks):
+    first, last = edge_lanes()
+
+    def parts(b):
+        d, slope = diff[first_cell + b], slopes[first_cell + b]
+        twice = d + d
+        return slope, twice, to_right(twice - slope), to_left(slope)
+
+    before = parts(blocks - 1)
+    here = parts(0)
+    for b in range(blocks):
+        after = parts((b + 1) % blocks)
+        speed = wide(coef[places[1], :, block_at(b)])
+        forward = jnp.where(first, before[2], here[2])
+        backward = here[1] - jnp.where(last, after[3], here[3])
+        change = jnp.where(speed > 0.0, forward, backward) + here[0]
+        partial[first_cell + b] = linear[first_cell + b] - (0.5 * speed) * change
+        before, here = here, after
 
 
 def rows_pass(levels, cell, places, partial, result, coef, block, blocks):
@@ -96,23 +112,33 @@
         speed = wide(coef[places[i - 2][0], :, at])
         forward = twice[i - 1] - slope[i - 1]
         backward = twice[i] - slope[i + 1]
-        change = wide(coef[places[i - 2][1], :, at]) * (d[i] - d[i - 1])
+        change = wide(coef[places[i - 2][2], :, at]) * (d[i] - d[i - 1])
         change = change - (0.5 * speed) * (jnp.where(speed > 0.0, forward, backward) + slope[i])
         here = (i - 2) * blocks + block
         result[here] = partial[here] + change
 
 
-def advance_group(level, row, levels, partial, result, coef, params, blocks):
+def advance_group(level, row, levels, work, result, coef, params, blocks):
+    diff, slopes, linear, partial = work
     cell = (level * ALL_ROWS + row) * blocks
-
-    @pl.loop(0, GROUP // TOGETHER)
-    def _(i):
-        done = i * (TOGETHER * blocks)
-        columns_pass(
-            levels, cell + done, row + i * TOGETHER, TOGETHER, partial, done, coef, params, blocks
+    places = [[coef_row(array, row + i) for array in range(4)] for i in range(GROUP)]
+
+    def over_rows(one_row):
+        @pl.loop(0, GROUP // TOGETHER)
+        def _(pair):
+            for k in range(TOGETHER):
+                i = pair * TOGETHER + k
+                one_row([coef_row(array, row + i) for array in range(4)], i * blocks)
+
+    over_rows(lambda _, at: difference_pass(levels, cell + at, at, diff, blocks))
+    over_rows(
+        lambda where, at: slope_pass(
+            levels, cell + at, where, at, diff, slopes, linear, coef, params, blocks
         )
-
-    places = [[coef_row(array, row + i) for array in (0, 2)] for i in range(GROUP)]
+    )
+    over_rows(
+        lambda where, at: flux_pass(where, at, diff, slopes, linear, partial, coef, blocks)
+    )
 
     @pl.loop(0, blocks // WIDE)
     def _(wide_block):
@@ -184,7 +210,7 @@
 
 
 def interior_kernel(blocks, own0, own1, own2, own3, own_coef, params, *rest):
-    outs, (levels, partial, result, coef, sems) = rest[:5], rest[5:]
+    outs, (levels, *work, result, coef, sems) = rest[:5], rest[5:]
     copies = Copies(sems)
     waits = [
         copies.start(own, region(levels, 0, GROUP * i, blocks))
@@ -200,7 +226,7 @@
     def _(i):
         level = jnp.where(i < 3, 0, jnp.where(i < 5, 1, 2))
         row = jnp.where(i < 3, 2 + 4 * i, jnp.where(i < 5, 4 * i - 8, 6))
-        advance_group(level, row + HALO, levels, partial, result, coef, params, blocks)
+        advance_group(level, row + HALO, levels, work, result, coef, params, blocks)
 
     waits = [
         copies.start(region(levels, level, row, blocks), out)
@@ -210,7 +236,7 @@
         copy.wait()
 
 
-def edge_steps(outer, blocks, waits, sends, levels, partial, result, coef, params):
+def edge_steps(outer, blocks, waits, sends, levels, work, result, coef, params):
     @pl.loop(0, 2 * STEPS)
     def _(step):
         level, side = lax.div(step, 2), lax.rem(step, 2)
@@ -223,7 +249,7 @@
         low = 2 * level - outer
         high = ROWS + outer - GROUP - 2 * level
         row = jnp.where(side == 0, low, high) + HALO
-        advance_group(level, row, levels, partial, result, coef, params, blocks)
+        advance_group(level, row, levels, work, result, coef, params, blocks)
         for k, copy in enumerate(sends):
             pl.when(step == k)(copy.start)
 
@@ -250,7 +276,7 @@
 def middle_kernel(blocks, *refs):
     sources, refs = refs[:9], refs[9:]
     own_coef, pair, other, params, place_of = refs[:5]
-    outs, (levels, partial, result, coef, sems) = refs[5:13], refs[13:]
+    outs, (levels, *work, result, coef, sems) = refs[5:13], refs[13:]
     copies = Copies(sems)
     places = ((0, -4), (0, 0), (0, 12), (0, 16), (1, 2), (1, 10), (2, 4), (2, 8), (3, 6))
     waits = [[] for _ in range(STEPS)]
@@ -262,7 +288,7 @@
         copies.make(region(levels, level, row, blocks), out)
         for out, (level, row) in zip(outs, places)
     ]
-    edge_steps(2, blocks, waits, sends, levels, partial, result, coef, params)
+    edge_steps(2, blocks, waits, sends, levels, work, result, coef, params)
     for copy in sends:
         copy.wait()
 
@@ -270,7 +296,7 @@
 def last_kernel(blocks, *refs):
     sources, refs = refs[:12], refs[12:]
     own_coef, pair, other, params, place_of, cell_of, shift_of = refs[:7]
-    low_out, high_out, predicted, levels, partial, result, coef, sems = refs[7:]
+    low_out, high_out, predicted, levels, *work, result, coef, sems = refs[7:]
     copies = Copies(sems)
     places = (
         (0, -8), (0, -4), (0, 16), (0, 20),
@@ -280,7 +306,7 @@
     for source, (level, row) in zip(sources, places):
         waits[level].append(copies.start(source, region(levels, level, row, blocks)))
     waits[0] += load_coef(copies, own_coef, pair, other, place_of, coef)
-    edge_steps(6, blocks, waits, (), levels, partial, result, coef, params)
+    edge_steps(6, blocks, waits, (), levels, work, result, coef, params)
     for copy in waits[STEPS]:
         copy.wait()
     sends = [
@@ -336,8 +362,7 @@
     group = pltpu.VMEM((GROUP * blocks, SUBLANES, LANES), jnp.float32)
     return [
         pltpu.VMEM(((STEPS + 1) * ALL_ROWS * blocks, SUBLANES, LANES), jnp.float32),
-        group,
-        group,
+        *[group] * 5,
         pltpu.VMEM((4 * ALL_ROWS, 1, columns), jnp.float32),
         *more,
     ]

time: 126 us -> 119 us (0.944)
  Pallas kernels: 70.9 us -> 64.8 us
    pallas_call x6, Pallas kernels: 68.2 us -> 62 us  [kernel_call(): pl.pallas_call(body, out_shape=tuple((jax.ShapeDtypeStruct(shape, jnp.flo...]
  transfers between devices with their start and end apart: 13 -> 13, of which waited for: 6 -> 6; matrix products, arithmetic and copies ran while one was open for 3% -> 3% of each run, Pallas kernels for 53% -> 50%
where the time goes in v7:
time: 119 us
  Pallas kernels  64.8 us (54%)
  starting transfers between devices  30.9 us (26%)
  waiting for transfers between devices  11.3 us (9%)
  blocking collectives  6 us (5%)
  other arithmetic  2.66 us (2%)
  local copies, waits for them, and re-layouts  1.89 us (2%)
    pallas_call x6, Pallas kernels, kernel_call(): pl.pallas_call(body, out_shape=tuple((jax.ShapeDtypeStruct(shape, jnp.flo...  62 us
    ppermute x3, starting transfers between devices, halos(): lax.ppermute(upper, 'slab', forward)  14.9 us
    ppermute x3, starting transfers between devices, local(): products = products + lax.ppermute(products, 'slab', pairs)  8.73 us
    all_gather x1, blocking collectives, local(): everyone = lax.all_gather(predicted, 'ens', axis=0, tiled=True)  6 us
    ppermute x3, waiting for transfers between devices, halos(): lax.ppermute(upper, 'slab', forward)  5.81 us
    ppermute x3, starting transfers between devices, halos(): lax.ppermute(lower, 'slab', backward)  3.86 us
    ppermute x2, starting transfers between devices, over_ens(): lax.ppermute(pair, 'ens', [(i, i ^ 2) for i in range(ens_count)])  3.04 us
    ppermute x3, waiting for transfers between devices, local(): products = products + lax.ppermute(products, 'slab', pairs)  2.4 us
  transfers between devices with their start and end apart: 13, of which 6 were waited for; matrix products, arithmetic and copies ran while one was open for 3% of the time, Pallas kernels for 50%

profile of v7, /device:TPU:0, one launch (start us, length us, event | category | flops | bytes accessed | tf_op | source)
XLA Modules:
  0.0 118.8 jit_solution(18165825620004117777)
XLA Ops:
  0.6 3.1 %outer_rows.1 = (f32[128,8,128]{2,1,0:T(8,128)}, f32[128,8,128]{2,1,0:T(8,128)}, f32[8,4096]{1,0:T(8,128)}, f32[8,4096]{1,0:T(8,128)}) custom-call(f32[128,4096]{1,0:T(8,128)} %bitcast.28, f32[4,16,4096]{2,1,0:T(8,128)} %refs_12_.3, s32[1]{0:T(128)} %bitcast.1.place_of.refs_13_.refs_16_), custom_call_target="tpu_custom_call" | custom-call | bytes 600000 | tf_op jit(solution)/shard_map/outer_rows/pallas_call | solution.py:372
  3.7 0.0 copy-start.11
  3.7 1.3 %collective-permute-start.3 = (f32[8,4096]{1,0:T(8,128)}, f32[8,4096]{1,0:T(8,128)S(1)}, u32[]{:S(2)}, u32[]{:S(2)}) collective-permute-start(f32[8,4096]{1,0:T(8,128)} %get-tuple-element.36), channel_id=1, source_target_pairs={{1,0},{2,1},{3,2},{4,3},{5,4},{6,5},{7,6},{9,8},{10,9},{11,10},{12... | collective-permute-start | bytes 393224 | tf_op jit(solution)/shard_map/ppermute | solution.py:510
  5.0 5.5 %collective-permute-start.2 = (f32[8,4096]{1,0:T(8,128)}, f32[8,4096]{1,0:T(8,128)S(1)}, u32[]{:S(2)}, u32[]{:S(2)}) collective-permute-start(f32[8,4096]{1,0:T(8,128)} %get-tuple-element.35), channel_id=1, source_target_pairs={{0,1},{1,2},{2,3},{3,4},{4,5},{5,6},{6,7},{8,9},{9,10},{10,11},{11... | collective-permute-start | bytes 393224 | tf_op jit(solution)/shard_map/ppermute | solution.py:510
  10.5 1.8 %collective-permute-done.3 = f32[8,4096]{1,0:T(8,128)S(1)} collective-permute-done((f32[8,4096]{1,0:T(8,128)}, f32[8,4096]{1,0:T(8,128)S(1)}, u32[]{:S(2)}, u32[]{:S(2)}) %collective-permute-start.3) | collective-permute-done | bytes 131104 | tf_op jit(solution)/shard_map/ppermute | solution.py:510
  12.3 3.1 %collective-permute-done.2 = f32[8,4096]{1,0:T(8,128)S(1)} collective-permute-done((f32[8,4096]{1,0:T(8,128)}, f32[8,4096]{1,0:T(8,128)S(1)}, u32[]{:S(2)}, u32[]{:S(2)}) %collective-permute-start.2) | collective-permute-done | bytes 131104 | tf_op jit(solution)/shard_map/ppermute | solution.py:510
  15.4 0.1 collective-permute-start.4
  15.5 4.3 %collective-permute-start = (f32[128,8,128]{2,1,0:T(8,128)}, f32[128,8,128]{2,1,0:T(8,128)S(1)}, u32[]{:S(2)}, u32[]{:S(2)}) collective-permute-start(f32[128,8,128]{2,1,0:T(8,128)} %get-tuple-element.31.outer.own3.refs_2_), channel_id=1, source_target_pairs={{0,1},{1,2},{2,3},{3,4},{4,5},{5,6},{6,7},{8,9},{9,10},{10,11},{11... | collective-permute-start | bytes 1572872 | tf_op jit(solution)/shard_map/ppermute | solution.py:510
  19.8 1.3 %collective-permute-start.1 = (f32[128,8,128]{2,1,0:T(8,128)}, f32[128,8,128]{2,1,0:T(8,128)S(1)}, u32[]{:S(2)}, u32[]{:S(2)}) collective-permute-start(f32[128,8,128]{2,1,0:T(8,128)} %get-tuple-element.34.own0.refs_1_), channel_id=1, source_target_pairs={{1,0},{2,1},{3,2},{4,3},{5,4},{6,5},{7,6},{9,8},{10,9},{11,10},{12... | collective-permute-start | bytes 1572872 | tf_op jit(solution)/shard_map/ppermute | solution.py:510
  21.1 2.9 %inner_rows.1 = (f32[128,8,128]{2,1,0:T(8,128)}, f32[128,8,128]{2,1,0:T(8,128)}) custom-call(f32[128,4096]{1,0:T(8,128)} %bitcast.29, f32[128,8,128]{2,1,0:T(8,128)} %get-tuple-element.31.outer.own3.refs_2_), custom_call_target="tpu_custom_call" | custom-call | bytes 600000 | tf_op jit(solution)/shard_map/inner_rows/pallas_call | solution.py:372
  24.0 0.0 copy-done.11
  24.0 0.6 add_select_fusion
  24.6 0.0 collective-permute-done.4
  24.6 0.0 copy-start
  24.6 0.0 copy-start.10
  24.6 0.0 copy-start.9
  24.7 0.0 copy-start.5
  24.7 13.8 %interior.1 = (f32[128,8,128]{2,1,0:T(8,128)}, f32[128,8,128]{2,1,0:T(8,128)}, f32[128,8,128]{2,1,0:T(8,128)}, f32[128,8,128]{2,1,0:T(8,128)}, f32[128,8,128]{2,1,0:T(8,128)}) custom-call(f32[128,8,128]{2,1,0:T(8,128)} %get-tuple-element.34.own0.refs_1_, f32[128,8,128]{2,1,0:T(8,128)} %get-tuple-element.42.own1, f32[128,8,128]{2,1,0:T(8,128)} %get-tuple-element.39.own2, ...), custom_call_target="tpu_custom_call" | custom-call | bytes 1600000 | tf_op jit(solution)/shard_map/interior/pallas_call | solution.py:372
  38.5 0.0 copy-done
  38.5 0.3 collective-permute-start.11
  38.8 0.0 copy-done.12
  38.8 0.1 compare_convert_fusion.same
  38.8 1.5 %collective-permute-start.7 = (f32[2,2,8,4096]{3,2,1,0:T(8,128)S(1)}, f32[2,2,8,4096]{3,2,1,0:T(8,128)S(1)}, u32[]{:S(2)}, u32[]{:S(2)}) collective-permute-start(f32[2,2,8,4096]{3,2,1,0:T(8,128)S(1)} %pad_maximum_fusion.refs_10_.refs_13_), channel_id=1, source_target_pairs={{0,16},{8,24},{16,0},{24,8},{1,17},{9,25},{17,1},{25,9},{2,18},{10... | collective-permute-start | bytes 1572872 | tf_op jit(solution)/shard_map/ppermute | solution.py:507
  40.4 2.7 %collective-permute-done.refs_0_.refs_1_ = f32[128,8,128]{2,1,0:T(8,128)S(1)} collective-permute-done((f32[128,8,128]{2,1,0:T(8,128)}, f32[128,8,128]{2,1,0:T(8,128)S(1)}, u32[]{:S(2)}, u32[]{:S(2)}) %collective-permute-start) | collective-permute-done | bytes 524320 | tf_op jit(solution)/shard_map/ppermute | solution.py:510
  43.1 0.0 collective-permute-done.1.refs_3_.refs_2_
  43.1 0.0 copy-done.10
  43.1 5.1 %collective-permute-start.5 = (f32[128,8,128]{2,1,0:T(8,128)S(1)}, f32[128,8,128]{2,1,0:T(8,128)}, u32[]{:S(2)}, u32[]{:S(2)}) collective-permute-start(f32[128,8,128]{2,1,0:T(8,128)S(1)} %copy-done.10), channel_id=1, source_target_pairs={{0,1},{1,2},{2,3},{3,4},{4,5},{5,6},{6,7},{8,9},{9,10},{10,11},{11... | collective-permute-start | bytes 1572872 | tf_op jit(solution)/shard_map/ppermute | solution.py:510
  48.2 0.0 copy-done.9
  48.2 1.3 %collective-permute-start.6 = (f32[128,8,128]{2,1,0:T(8,128)S(1)}, f32[128,8,128]{2,1,0:T(8,128)}, u32[]{:S(2)}, u32[]{:S(2)}) collective-permute-start(f32[128,8,128]{2,1,0:T(8,128)S(1)} %copy-done.9), channel_id=1, source_target_pairs={{1,0},{2,1},{3,2},{4,3},{5,4},{6,5},{7,6},{9,8},{10,9},{11,10},{12... | collective-permute-start | bytes 1572872 | tf_op jit(solution)/shard_map/ppermute | solution.py:510
  49.5 0.0 collective-permute-done.11
  49.5 0.7 pad_maximum_fusion.3
  50.2 1.5 %collective-permute-start.12 = (f32[2,8,4096]{2,1,0:T(8,128)}, f32[2,8,4096]{2,1,0:T(8,128)}, u32[]{:S(2)}, u32[]{:S(2)}) collective-permute-start(f32[2,8,4096]{2,1,0:T(8,128)} %pad_maximum_fusion.3), channel_id=1, source_target_pairs={{0,16},{8,24},{16,0},{24,8},{1,17},{9,25},{17,1},{25,9},{2,18},{10... | collective-permute-start | bytes 786440 | tf_op jit(solution)/shard_map/ppermute | solution.py:507
  51.8 0.2 convert_reduce_fusion
  52.0 0.1 copy.9.rank_col
  52.0 0.1 constant_dynamic-slice_fusion.own_same
  52.1 1.3 %collective-permute-done.7.refs_11_.refs_14_ = f32[2,2,8,4096]{3,2,1,0:T(8,128)S(1)} collective-permute-done((f32[2,2,8,4096]{3,2,1,0:T(8,128)S(1)}, f32[2,2,8,4096]{3,2,1,0:T(8,128)S(1)}, u32[]{:S(2)}, u32[]{:S(2)}) %collective-permute-start.7) | collective-permute-done | bytes 524320 | tf_op jit(solution)/shard_map/ppermute | solution.py:507
  53.4 0.0 copy-done.5
  53.4 0.0 copy-done.6
  53.4 0.0 copy-done.7
  53.4 0.8 copy-done.8
  54.2 17.2 %edge_first.1 = (f32[128,8,128]{2,1,0:T(8,128)}, f32[128,8,128]{2,1,0:T(8,128)}, f32[128,8,128]{2,1,0:T(8,128)}, f32[128,8,128]{2,1,0:T(8,128)}, f32[128,8,128]{...) custom-call(f32[128,8,128]{2,1,0:T(8,128)} %copy-done.6, ...), custom_call_target="tpu_custom_call" | custom-call | bytes 2000000 | tf_op jit(solution)/shard_map/edge_first/pallas_call | solution.py:372
  71.4 0.0 collective-permute-done.5.refs_0_
  71.4 0.0 collective-permute-done.6.refs_3_
  71.4 0.0 copy-start.3
  71.4 0.0 copy-start.4
  71.4 0.0 copy-start.1
  71.5 21.9 %edge_last.1 = (f32[128,8,128]{2,1,0:T(8,128)}, f32[128,8,128]{2,1,0:T(8,128)}, f32[8,2048]{1,0:T(8,128)}) custom-call(f32[128,8,128]{2,1,0:T(8,128)} %collective-permute-done.5.refs_0_, f32[128,8,128]{2,1,0:T(8,128)} %copy-done.6, f32[128,8,128]{2,1,0:T(8,128)} %copy-done.7, f32[128,8,128]{2,1,0:T(8,128)} %collective-permute-done.6.refs_3_, ...), custom_call_target="tpu_custom_call" | custom-call | bytes 3000000 | tf_op jit(solution)/shard_map/edge_last/pallas_call | solution.py:372
  93.3 6.0 %all_gather.3.everyone = f32[32,2048]{1,0:T(8,128)S(1)} all-gather(f32[8,2048]{1,0:T(8,128)} %get-tuple-element.58.own), channel_id=1, replica_groups=mesh['ens'=4,'slab'=8] {'ens'}, dimensions={0}, use_global_device_ids=true | all-gather | bytes 327680 | tf_op jit(solution)/shard_map/all_gather | solution.py:538
  99.3 0.0 copy-done.3
  99.3 0.0 copy-done.4
  99.3 0.8 copy-done.2
  100.2 0.6 products.1
  100.8 2.5 %collective-permute-start.8 = (f32[32,40]{1,0:T(8,128)S(1)}, f32[32,40]{1,0:T(8,128)S(1)}, u32[]{:S(2)}, u32[]{:S(2)}) collective-permute-start(f32[32,40]{1,0:T(8,128)S(1)} %products.1), channel_id=1, source_target_pairs={{0,1},{1,0},{2,3},{3,2},{4,5},{5,4},{6,7},{7,6},{8,9},{9,8},{10,11... | collective-permute-start | bytes 15368 | tf_op jit(solution)/shard_map/ppermute | solution.py:549
  103.3 0.0 collective-permute-done.12
  103.3 0.0 copy-done.1
  103.3 1.0 pad_maximum_fusion.1
  104.3 0.7 collective-permute-done.8
  105.0 3.2 %collective-permute-start.9 = (f32[32,40]{1,0:T(8,128)S(1)}, f32[32,40]{1,0:T(8,128)S(1)}, u32[]{:S(2)}, u32[]{:S(2)}) collective-permute-start(f32[32,40]{1,0:T(8,128)S(1)} %add.46), channel_id=1, source_target_pairs={{0,2},{1,3},{2,0},{3,1},{4,6},{5,7},{6,4},{7,5},{8,10},{9,11},{10,... | collective-permute-start | bytes 15368 | tf_op jit(solution)/shard_map/ppermute | solution.py:549
  108.3 1.7 %collective-permute-done.9 = f32[32,40]{1,0:T(8,128)S(1)} collective-permute-done((f32[32,40]{1,0:T(8,128)S(1)}, f32[32,40]{1,0:T(8,128)S(1)}, u32[]{:S(2)}, u32[]{:S(2)}) %collective-permute-start.9) | collective-permute-done | bytes 5152 | tf_op jit(solution)/shard_map/ppermute | solution.py:549
  109.9 3.0 %collective-permute-start.10 = (f32[32,40]{1,0:T(8,128)S(1)}, f32[32,40]{1,0:T(8,128)S(1)}, u32[]{:S(2)}, u32[]{:S(2)}) collective-permute-start(f32[32,40]{1,0:T(8,128)S(1)} %add.47), channel_id=1, source_target_pairs={{0,4},{1,5},{2,6},{3,7},{4,0},{5,1},{6,2},{7,3},{8,12},{9,13},{10,... | collective-permute-start | bytes 15368 | tf_op jit(solution)/shard_map/ppermute | solution.py:549
  113.0 0.4 fusion.1.anomalies
  113.4 3.3 %field.1 = f32[128,4096]{1,0:T(8,128)} custom-call(f32[128,8,128]{2,1,0:T(8,128)} %get-tuple-element.56.refs_0_, f32[128,8,128]{2,1,0:T(8,128)} %get-tuple-element.54.refs_10_.refs_1_, f32[128,8,128]{2,1,0:T(8,128)} %get-tuple-element.55.refs_11_.refs_2_, f32[128,8,128]{2,1,0:T(8,128)} %get-tuple-element.57.refs_3_), custom_call_target="tpu_custom_call" | custom-call | bytes 800000 | tf_op jit(solution)/shard_map/field/pallas_call | solution.py:372
  116.7 0.0 collective-permute-done.10
  116.7 2.1 %update.1 = f32[8,4096]{1,0:T(8,128)} custom-call(f32[1,32,40]{2,1,0:T(8,128)S(1)} %add_bitcast_fusion.summands, f32[32,32]{1,0:T(8,128)S(1)} %compare_convert_fusion.same, f32[32,8]{1,0:T(8,128)S(1)} %constant_dynamic-slice_fusion.own_same, s32[1,32]{1,0:T(1,128)S(1)} %bitcast.27, s32[32,1]{1,0:T(8,128)S(1)} %copy.9.rank_col, ...), custom_call_target="tpu_custom_call" | custom-call | tf_op jit(solution)/shard_map/update/pallas_call | solution.py:551
  (11 shorter events, 0.1 us)
Async XLA Ops:
  3.7 20.3 %copy-start.11 = (s32[2048]{0:T(1024)S(1)}, s32[2048]{0:T(1024)}, u32[]{:S(2)}) copy-start(s32[2048]{0:T(1024)} %param.10) | copy-start | bytes 24580
  3.7 8.5 %collective-permute-start.3 = (f32[8,4096]{1,0:T(8,128)}, f32[8,4096]{1,0:T(8,128)S(1)}, u32[]{:S(2)}, u32[]{:S(2)}) collective-permute-start(f32[8,4096]{1,0:T(8,128)} %get-tuple-element.36), channel_id=1, source_target_pairs={{1,0},{2,1},{3,2},{4,3},{5,4},{6,5},{7,6},{9,8},{10,9},{11,10},{12... | collective-permute-start | bytes 393224 | tf_op jit(solution)/shard_map/ppermute | solution.py:510
  5.0 10.3 %collective-permute-start.2 = (f32[8,4096]{1,0:T(8,128)}, f32[8,4096]{1,0:T(8,128)S(1)}, u32[]{:S(2)}, u32[]{:S(2)}) collective-permute-start(f32[8,4096]{1,0:T(8,128)} %get-tuple-element.35), channel_id=1, source_target_pairs={{0,1},{1,2},{2,3},{3,4},{4,5},{5,6},{6,7},{8,9},{9,10},{10,11},{11... | collective-permute-start | bytes 393224 | tf_op jit(solution)/shard_map/ppermute | solution.py:510
  15.4 9.2 %collective-permute-start.4 = (f32[2,8,4096]{2,1,0:T(8,128)S(1)}, f32[2,8,4096]{2,1,0:T(8,128)S(1)}, u32[]{:S(2)}, u32[]{:S(2)}) collective-permute-start(f32[2,8,4096]{2,1,0:T(8,128)S(1)} %get-tuple-element.65), channel_id=1, source_target_pairs={{0,8},{8,0},{16,24},{24,16},{1,9},{9,1},{17,25},{25,17},{2,10},{10... | collective-permute-start | bytes 786440 | tf_op jit(solution)/shard_map/ppermute | solution.py:506
  15.5 27.6 %collective-permute-start = (f32[128,8,128]{2,1,0:T(8,128)}, f32[128,8,128]{2,1,0:T(8,128)S(1)}, u32[]{:S(2)}, u32[]{:S(2)}) collective-permute-start(f32[128,8,128]{2,1,0:T(8,128)} %get-tuple-element.31.outer.own3.refs_2_), channel_id=1, source_target_pairs={{0,1},{1,2},{2,3},{3,4},{4,5},{5,6},{6,7},{8,9},{9,10},{10,11},{11... | collective-permute-start | bytes 1572872 | tf_op jit(solution)/shard_map/ppermute | solution.py:510
  19.8 23.3 %collective-permute-start.1 = (f32[128,8,128]{2,1,0:T(8,128)}, f32[128,8,128]{2,1,0:T(8,128)S(1)}, u32[]{:S(2)}, u32[]{:S(2)}) collective-permute-start(f32[128,8,128]{2,1,0:T(8,128)} %get-tuple-element.34.own0.refs_1_), channel_id=1, source_target_pairs={{1,0},{2,1},{3,2},{4,3},{5,4},{6,5},{7,6},{9,8},{10,9},{11,10},{12... | collective-permute-start | bytes 1572872 | tf_op jit(solution)/shard_map/ppermute | solution.py:510
  24.6 13.9 %copy-start = (f32[8,4096]{1,0:T(8,128)S(1)}, f32[8,4096]{1,0:T(8,128)}, u32[]{:S(2)}) copy-start(f32[8,4096]{1,0:T(8,128)} %own.1) | copy-start | bytes 393220
  24.6 14.2 %copy-start.12 = (s32[32]{0:T(128)S(1)}, s32[32]{0:T(128)}, u32[]{:S(2)}) copy-start(s32[32]{0:T(128)} %param.13) | copy-start | bytes 388
  24.6 18.5 %copy-start.10 = (f32[128,8,128]{2,1,0:T(8,128)S(1)}, f32[128,8,128]{2,1,0:T(8,128)}, u32[]{:S(2)}) copy-start(f32[128,8,128]{2,1,0:T(8,128)} %get-tuple-element.39.own2) | copy-start | bytes 1572868
  24.6 23.6 %copy-start.9 = (f32[128,8,128]{2,1,0:T(8,128)S(1)}, f32[128,8,128]{2,1,0:T(8,128)}, u32[]{:S(2)}) copy-start(f32[128,8,128]{2,1,0:T(8,128)} %get-tuple-element.42.own1) | copy-start | bytes 1572868
  24.7 28.7 %copy-start.5 = (f32[2,2,8,4096]{3,2,1,0:T(8,128)}, f32[2,2,8,4096]{3,2,1,0:T(8,128)S(1)}, u32[]{:S(2)}) copy-start(f32[2,2,8,4096]{3,2,1,0:T(8,128)S(1)} %pad_maximum_fusion.refs_10_.refs_13_) | copy-start | bytes 1572868
  38.5 11.0 %collective-permute-start.11 = (f32[8,4096]{1,0:T(8,128)S(1)}, f32[8,4096]{1,0:T(8,128)S(1)}, u32[]{:S(2)}, u32[]{:S(2)}) collective-permute-start(f32[8,4096]{1,0:T(8,128)S(1)} %copy-done), channel_id=1, source_target_pairs={{0,8},{8,0},{16,24},{24,16},{1,9},{9,1},{17,25},{25,17},{2,10},{10... | collective-permute-start | bytes 393224 | tf_op jit(solution)/shard_map/ppermute | solution.py:506
  38.8 14.6 %collective-permute-start.7 = (f32[2,2,8,4096]{3,2,1,0:T(8,128)S(1)}, f32[2,2,8,4096]{3,2,1,0:T(8,128)S(1)}, u32[]{:S(2)}, u32[]{:S(2)}) collective-permute-start(f32[2,2,8,4096]{3,2,1,0:T(8,128)S(1)} %pad_maximum_fusion.refs_10_.refs_13_), channel_id=1, source_target_pairs={{0,16},{8,24},{16,0},{24,8},{1,17},{9,25},{17,1},{25,9},{2,18},{10... | collective-permute-start | bytes 1572872 | tf_op jit(solution)/shard_map/ppermute | solution.py:507
  43.1 10.3 %copy-start.6 = (f32[128,8,128]{2,1,0:T(8,128)}, f32[128,8,128]{2,1,0:T(8,128)S(1)}, u32[]{:S(2)}) copy-start(f32[128,8,128]{2,1,0:T(8,128)S(1)} %collective-permute-done.refs_0_.refs_1_) | copy-start | bytes 1572868
  43.1 10.3 %copy-start.7 = (f32[128,8,128]{2,1,0:T(8,128)}, f32[128,8,128]{2,1,0:T(8,128)S(1)}, u32[]{:S(2)}) copy-start(f32[128,8,128]{2,1,0:T(8,128)S(1)} %collective-permute-done.1.refs_3_.refs_2_) | copy-start | bytes 1572868
  43.1 28.3 %collective-permute-start.5 = (f32[128,8,128]{2,1,0:T(8,128)S(1)}, f32[128,8,128]{2,1,0:T(8,128)}, u32[]{:S(2)}, u32[]{:S(2)}) collective-permute-start(f32[128,8,128]{2,1,0:T(8,128)S(1)} %copy-done.10), channel_id=1, source_target_pairs={{0,1},{1,2},{2,3},{3,4},{4,5},{5,6},{6,7},{8,9},{9,10},{10,11},{11... | collective-permute-start | bytes 1572872 | tf_op jit(solution)/shard_map/ppermute | solution.py:510
  48.2 23.2 %collective-permute-start.6 = (f32[128,8,128]{2,1,0:T(8,128)S(1)}, f32[128,8,128]{2,1,0:T(8,128)}, u32[]{:S(2)}, u32[]{:S(2)}) collective-permute-start(f32[128,8,128]{2,1,0:T(8,128)S(1)} %copy-done.9), channel_id=1, source_target_pairs={{1,0},{2,1},{3,2},{4,3},{5,4},{6,5},{7,6},{9,8},{10,9},{11,10},{12... | collective-permute-start | bytes 1572872 | tf_op jit(solution)/shard_map/ppermute | solution.py:510
  50.2 53.1 %collective-permute-start.12 = (f32[2,8,4096]{2,1,0:T(8,128)}, f32[2,8,4096]{2,1,0:T(8,128)}, u32[]{:S(2)}, u32[]{:S(2)}) collective-permute-start(f32[2,8,4096]{2,1,0:T(8,128)} %pad_maximum_fusion.3), channel_id=1, source_target_pairs={{0,16},{8,24},{16,0},{24,8},{1,17},{9,25},{17,1},{25,9},{2,18},{10... | collective-permute-start | bytes 786440 | tf_op jit(solution)/shard_map/ppermute | solution.py:507
  53.4 0.8 copy-start.8
  71.4 27.9 %copy-start.3 = (f32[8,2048]{1,0:T(8,128)S(1)}, f32[8,2048]{1,0:T(8,128)}, u32[]{:S(2)}) copy-start(f32[8,2048]{1,0:T(8,128)} %values.1) | copy-start | bytes 196612
  71.4 27.9 %copy-start.4 = (f32[2048]{0:T(1024)S(1)}, f32[2048]{0:T(1024)}, u32[]{:S(2)}) copy-start(f32[2048]{0:T(1024)} %param.12) | copy-start | bytes 24580
  71.4 31.9 %copy-start.1 = (f32[8,4096]{1,0:T(8,128)S(1)}, f32[8,4096]{1,0:T(8,128)}, u32[]{:S(2)}) copy-start(f32[8,4096]{1,0:T(8,128)} %own.1) | copy-start | bytes 393220
  99.3 0.8 copy-start.2
  100.8 4.2 %collective-permute-start.8 = (f32[32,40]{1,0:T(8,128)S(1)}, f32[32,40]{1,0:T(8,128)S(1)}, u32[]{:S(2)}, u32[]{:S(2)}) collective-permute-start(f32[32,40]{1,0:T(8,128)S(1)} %products.1), channel_id=1, source_target_pairs={{0,1},{1,0},{2,3},{3,2},{4,5},{5,4},{6,7},{7,6},{8,9},{9,8},{10,11... | collective-permute-start | bytes 15368 | tf_op jit(solution)/shard_map/ppermute | solution.py:549
  105.0 4.9 %collective-permute-start.9 = (f32[32,40]{1,0:T(8,128)S(1)}, f32[32,40]{1,0:T(8,128)S(1)}, u32[]{:S(2)}, u32[]{:S(2)}) collective-permute-start(f32[32,40]{1,0:T(8,128)S(1)} %add.46), channel_id=1, source_target_pairs={{0,2},{1,3},{2,0},{3,1},{4,6},{5,7},{6,4},{7,5},{8,10},{9,11},{10,... | collective-permute-start | bytes 15368 | tf_op jit(solution)/shard_map/ppermute | solution.py:549
  109.9 6.7 %collective-permute-start.10 = (f32[32,40]{1,0:T(8,128)S(1)}, f32[32,40]{1,0:T(8,128)S(1)}, u32[]{:S(2)}, u32[]{:S(2)}) collective-permute-start(f32[32,40]{1,0:T(8,128)S(1)} %add.47), channel_id=1, source_target_pairs={{0,4},{1,5},{2,6},{3,7},{4,0},{5,1},{6,2},{7,3},{8,12},{9,13},{10,... | collective-permute-start | bytes 15368 | tf_op jit(solution)/shard_map/ppermute | solution.py:549

commit v8 on v7

--- a/solution.py
+++ b/solution.py
@@ -40,8 +40,8 @@
     return pl.ds(pl.multiple_of(block * LANES, LANES), LANES)
 
 
-def wide(row):
-    return jnp.broadcast_to(row, (SUBLANES, LANES))
+def everywhere(coef, block, place):
+    return coef[block, pl.ds(place, SUBLANES, stride=0), :]
 
 
 def edge_lanes():
@@ -78,8 +78,8 @@
         d_back = jnp.where(first, rolled, here)
         rolled = here
         slopes[first_cell + b] = limited(d_back, d)
-        value = levels[cell + b] + wide(coef[places[2], :, at]) * (d - d_back)
-        linear[first_cell + b] = value + params[:, at] * wide(coef[places[3], :, at])
+        value = levels[cell + b] + everywhere(coef, b, places[2]) * (d - d_back)
+        linear[first_cell + b] = value + params[:, at] * everywhere(coef, b, places[3])
 
 
 def flux_pass(places, first_cell, diff, slopes, linear, partial, coef, blocks):
@@ -94,7 +94,7 @@
     here = parts(0)
     for b in range(blocks):
         after = parts((b + 1) % blocks)
-        speed = wide(coef[places[1], :, block_at(b)])
+        speed = everywhere(coef, b, places[1])
         forward = jnp.where(first, before[2], here[2])
         backward = here[1] - jnp.where(last, after[3], here[3])
         change = jnp.where(speed > 0.0, forward, backward) + here[0]
@@ -103,16 +103,15 @@
 
 
 def rows_pass(levels, cell, places, partial, result, coef, block, blocks):
-    at = block_at(block)
     c = [levels[cell + (i - 2) * blocks + block] for i in range(GROUP + 4)]
     d = [c[i + 1] - c[i] for i in range(GROUP + 3)]
     slope = [None] + [limited(d[i - 1], d[i]) for i in range(1, GROUP + 3)]
     twice = [None] + [d[i] + d[i] for i in range(1, GROUP + 2)]
     for i in range(2, GROUP + 2):
-        speed = wide(coef[places[i - 2][0], :, at])
+        speed = everywhere(coef, block, places[i - 2][0])
         forward = twice[i - 1] - slope[i - 1]
         backward = twice[i] - slope[i + 1]
-        change = wide(coef[places[i - 2][2], :, at]) * (d[i] - d[i - 1])
+        change = everywhere(coef, block, places[i - 2][2]) * (d[i] - d[i - 1])
         change = change - (0.5 * speed) * (jnp.where(speed > 0.0, forward, backward) + slope[i])
         here = (i - 2) * blocks + block
         result[here] = partial[here] + change
@@ -192,21 +191,30 @@
 
 
 def outer_rows_kernel(
-    blocks, tracer, own_coef, place_of, up, down, up_coef, down_coef, staged, sems, coef_sems
+    blocks, tracer, own_coef, place_of, up, down, up_coef, down_coef, edge, edge_sem, staged, sems
 ):
-    copies = Copies(coef_sems)
-    source = own_coef.at[place_of[0]]
-    waits = [
-        copies.start(source.at[pl.ds(ROWS - HALO, HALO)], up_coef),
-        copies.start(source.at[pl.ds(0, HALO)], down_coef),
-    ]
+    copy = pltpu.make_async_copy(own_coef.at[place_of[0]], edge, edge_sem)
+    copy.start()
     fill_rows(blocks, (0, ROWS - GROUP), tracer, (down, up), staged, sems)
-    for copy in waits:
-        copy.wait()
-
-
-def inner_rows_kernel(blocks, tracer, outer, low, high, staged, sems):
+    copy.wait()
+    for block in range(blocks):
+        at = block_at(block)
+        up_coef[block] = edge[ROWS - HALO :, at]
+        down_coef[block] = edge[0:HALO, at]
+
+
+def inner_rows_kernel(
+    blocks, tracer, own_coef, outer, low, high, by_block, whole, coef_sem, staged, sems
+):
+    copy = pltpu.make_async_copy(own_coef, whole, coef_sem)
+    copy.start()
     fill_rows(blocks, (GROUP, ROWS - 2 * GROUP), tracer, (low, high), staged, sems)
+    copy.wait()
+
+    @pl.loop(0, blocks)
+    def _(block):
+        for array in range(4):
+            by_block[block, array * ROWS : (array + 1) * ROWS, :] = whole[array, :, block_at(block)]
 
 
 def interior_kernel(blocks, own0, own1, own2, own3, own_coef, params, *rest):
@@ -216,9 +224,7 @@
         copies.start(own, region(levels, 0, GROUP * i, blocks))
         for i, own in enumerate((own0, own1, own2, own3))
     ]
-    waits += [
-        copies.start(own_coef.at[array], coef.at[pl.ds(array * ROWS, ROWS), 0]) for array in range(4)
-    ]
+    waits.append(copies.start(own_coef, coef.at[:, 0 : 4 * ROWS]))
     for copy in waits:
         copy.wait()
 
@@ -262,14 +268,12 @@
 
 
 def load_coef(copies, own_coef, pair, other, place_of, coef):
-    waits = [
-        copies.start(own_coef.at[array], coef.at[pl.ds(array * ROWS, ROWS), 0]) for array in range(4)
-    ]
+    waits = [copies.start(own_coef, coef.at[:, 0 : 4 * ROWS])]
     for number, source in enumerate((pair.at[0], pair.at[1], other.at[0], other.at[1])):
         array = jnp.bitwise_xor(place_of[0], number)
         for side in range(2):
             first = 4 * ROWS + 2 * HALO * array + HALO * side
-            waits.append(copies.start(source.at[side], coef.at[pl.ds(first, HALO), 0]))
+            waits.append(copies.start(source.at[side], coef.at[:, pl.ds(first, HALO)]))
     return waits
 
 
@@ -363,7 +367,7 @@
     return [
         pltpu.VMEM(((STEPS + 1) * ALL_ROWS * blocks, SUBLANES, LANES), jnp.float32),
         *[group] * 5,
-        pltpu.VMEM((4 * ALL_ROWS, 1, columns), jnp.float32),
+        pltpu.VMEM((blocks, 4 * ALL_ROWS, LANES), jnp.float32),
         *more,
     ]
 
@@ -389,19 +393,20 @@
     flat = tracer.reshape(members * rows, columns)
     dma = pltpu.SemaphoreType.DMA
     scratches = [pltpu.VMEM((blocks, members * rows, LANES), jnp.float32), dma((blocks,))]
-    group, edge = (GROUP * blocks, members, LANES), (HALO, columns)
+    group, edge = (GROUP * blocks, members, LANES), (blocks, HALO, LANES)
     up, down, up_coef, down_coef = kernel_call(
         functools.partial(outer_rows_kernel, blocks), "outer_rows",
-        [group, group, edge, edge], [ANYWHERE, ANYWHERE, IN_SMEM],
-        (IN_VMEM,) * 4,
-        scratches + [dma((2,))], 3, [flat, coefficients, place_of],
-    )
-    low, high = kernel_call(
+        [group, group, edge, edge], [ANYWHERE, ANYWHERE, IN_SMEM], (IN_VMEM,) * 4,
+        [pltpu.VMEM((rows, columns), jnp.float32), dma] + scratches, 3,
+        [flat, coefficients, place_of],
+    )
+    low, high, by_block = kernel_call(
         functools.partial(inner_rows_kernel, blocks), "inner_rows",
-        [group] * 2, [ANYWHERE, ANYWHERE], (IN_VMEM,) * 2,
-        scratches, 3, [flat, up],
-    )
-    return (down, low, high, up), (up_coef, down_coef)
+        [group, group, (blocks, 4 * rows, LANES)], [ANYWHERE] * 3, (IN_VMEM,) * 3,
+        [pltpu.VMEM((4, rows, columns), jnp.float32), dma] + scratches, 3,
+        [flat, coefficients, up],
+    )
+    return (down, low, high, up), (up_coef, down_coef), by_block
 
 
 def transport(shape, own, low0, high0, own_coef, pair, other, params, place_of, obs_index, halos):
@@ -510,7 +515,7 @@
         return lax.ppermute(upper, "slab", forward), lax.ppermute(lower, "slab", backward)
 
     place_of = jnp.reshape(ens_pos, (1,))
-    own, coef_edges = row_groups(tracer, coefficients, place_of)
+    own, coef_edges, own_coef = row_groups(tracer, coefficients, place_of)
     low0, high0 = halos(own[3], own[0])
 
     edge_low, edge_high = halos(*coef_edges)
@@ -526,7 +531,7 @@
     own_same = lax.dynamic_slice_in_dim(same, ens_pos * local_members, local_members, 1)
     field, predicted, first_done = transport(
         tracer.shape, own, low0, high0,
-        coefficients, pair, other, parameters, place_of, obs_index, halos,
+        own_coef, pair, other, parameters, place_of, obs_index, halos,
     )
 
     later, _ = lax.optimization_barrier((parameters, first_done))

time: 119 us -> 121 us (1.017)
  Pallas kernels: 64.8 us -> 66.3 us
    pallas_call x6, Pallas kernels: 62 us -> 63.5 us  [kernel_call(): pl.pallas_call(body, out_shape=tuple((jax.ShapeDtypeStruct(shape, jnp.flo...]
  transfers between devices with their start and end apart: 13 -> 13, of which waited for: 6 -> 6; matrix products, arithmetic and copies ran while one was open for 3% -> 3% of each run, Pallas kernels for 50% -> 51%
where the time goes in v8:
time: 121 us; the launch traced here: 120 us
  Pallas kernels  66.3 us (55%)
  starting transfers between devices  30.9 us (26%)
  waiting for transfers between devices  11.5 us (10%)
  blocking collectives  6 us (5%)
  other arithmetic  2.65 us (2%)
  local copies, waits for them, and re-layouts  1.88 us (2%)
    pallas_call x6, Pallas kernels, kernel_call(): pl.pallas_call(body, out_shape=tuple((jax.ShapeDtypeStruct(shape, jnp.flo...  63.5 us
    ppermute x3, starting transfers between devices, halos(): lax.ppermute(upper, 'slab', forward)  14.9 us
    ppermute x3, starting transfers between devices, local(): products = products + lax.ppermute(products, 'slab', pairs)  8.71 us
    all_gather x1, blocking collectives, local(): everyone = lax.all_gather(predicted, 'ens', axis=0, tiled=True)  6 us
    ppermute x3, waiting for transfers between devices, halos(): lax.ppermute(upper, 'slab', forward)  4.79 us
    ppermute x3, starting transfers between devices, halos(): lax.ppermute(lower, 'slab', backward)  3.86 us
    ppermute x2, starting transfers between devices, over_ens(): lax.ppermute(pair, 'ens', [(i, i ^ 2) for i in range(ens_count)])  3.04 us
    ppermute x2, waiting for transfers between devices, over_ens(): lax.ppermute(pair, 'ens', [(i, i ^ 2) for i in range(ens_count)])  2.49 us
  transfers between devices with their start and end apart: 13, of which 6 were waited for; matrix products, arithmetic and copies ran while one was open for 3% of the time, Pallas kernels for 51%

profile of v8, /device:TPU:0, one launch (start us, length us, event | category | flops | bytes accessed | tf_op | source)
XLA Modules:
  0.0 120.5 jit_solution(6744468525335704209)
XLA Ops:
  0.6 3.0 %outer_rows.1 = (f32[128,8,128]{2,1,0:T(8,128)}, f32[128,8,128]{2,1,0:T(8,128)}, f32[32,8,128]{2,1,0:T(8,128)}, f32[32,8,128]{2,1,0:T(8,128)}) custom-call(f32[128,4096]{1,0:T(8,128)} %bitcast.28, f32[4,16,4096]{2,1,0:T(8,128)} %own_coef.3, s32[1]{0:T(128)} %bitcast.1.place_of.refs_13_.refs_16_), custom_call_target="tpu_custom_call" | custom-call | bytes 600000 | tf_op jit(solution)/shard_map/outer_rows/pallas_call | solution.py:376
  3.7 1.3 %collective-permute-start.3 = (f32[32,8,128]{2,1,0:T(8,128)}, f32[32,8,128]{2,1,0:T(8,128)S(1)}, u32[]{:S(2)}, u32[]{:S(2)}) collective-permute-start(f32[32,8,128]{2,1,0:T(8,128)} %get-tuple-element.38), channel_id=1, source_target_pairs={{1,0},{2,1},{3,2},{4,3},{5,4},{6,5},{7,6},{9,8},{10,9},{11,10},{12... | collective-permute-start | bytes 393224 | tf_op jit(solution)/shard_map/ppermute | solution.py:515
  5.0 5.5 %collective-permute-start.2 = (f32[32,8,128]{2,1,0:T(8,128)}, f32[32,8,128]{2,1,0:T(8,128)S(1)}, u32[]{:S(2)}, u32[]{:S(2)}) collective-permute-start(f32[32,8,128]{2,1,0:T(8,128)} %get-tuple-element.37), channel_id=1, source_target_pairs={{0,1},{1,2},{2,3},{3,4},{4,5},{5,6},{6,7},{8,9},{9,10},{10,11},{11... | collective-permute-start | bytes 393224 | tf_op jit(solution)/shard_map/ppermute | solution.py:515
  10.4 1.8 %collective-permute-done.3 = f32[32,8,128]{2,1,0:T(8,128)S(1)} collective-permute-done((f32[32,8,128]{2,1,0:T(8,128)}, f32[32,8,128]{2,1,0:T(8,128)S(1)}, u32[]{:S(2)}, u32[]{:S(2)}) %collective-permute-start.3) | collective-permute-done | bytes 131104 | tf_op jit(solution)/shard_map/ppermute | solution.py:515
  12.2 3.1 %collective-permute-done.2 = f32[32,8,128]{2,1,0:T(8,128)S(1)} collective-permute-done((f32[32,8,128]{2,1,0:T(8,128)}, f32[32,8,128]{2,1,0:T(8,128)S(1)}, u32[]{:S(2)}, u32[]{:S(2)}) %collective-permute-start.2) | collective-permute-done | bytes 131104 | tf_op jit(solution)/shard_map/ppermute | solution.py:515
  15.3 0.0 copy-start.11
  15.3 0.1 collective-permute-start.4
  15.4 4.3 %collective-permute-start = (f32[128,8,128]{2,1,0:T(8,128)}, f32[128,8,128]{2,1,0:T(8,128)S(1)}, u32[]{:S(2)}, u32[]{:S(2)}) collective-permute-start(f32[128,8,128]{2,1,0:T(8,128)} %get-tuple-element.32.outer.own3.refs_2_), channel_id=1, source_target_pairs={{0,1},{1,2},{2,3},{3,4},{4,5},{5,6},{6,7},{8,9},{9,10},{10,11},{11... | collective-permute-start | bytes 1572872 | tf_op jit(solution)/shard_map/ppermute | solution.py:515
  19.7 1.3 %collective-permute-start.1 = (f32[128,8,128]{2,1,0:T(8,128)}, f32[128,8,128]{2,1,0:T(8,128)S(1)}, u32[]{:S(2)}, u32[]{:S(2)}) collective-permute-start(f32[128,8,128]{2,1,0:T(8,128)} %get-tuple-element.35.own0.refs_1_), channel_id=1, source_target_pairs={{1,0},{2,1},{3,2},{4,3},{5,4},{6,5},{7,6},{9,8},{10,9},{11,10},{12... | collective-permute-start | bytes 1572872 | tf_op jit(solution)/shard_map/ppermute | solution.py:515
  21.0 3.7 %inner_rows.1 = (f32[128,8,128]{2,1,0:T(8,128)}, f32[128,8,128]{2,1,0:T(8,128)}, f32[32,64,128]{2,1,0:T(8,128)}) custom-call(f32[128,4096]{1,0:T(8,128)} %bitcast.29, f32[4,16,4096]{2,1,0:T(8,128)} %own_coef.3, f32[128,8,128]{2,1,0:T(8,128)} %get-tuple-element.32.outer.own3.refs_2_), custom_call_target="tpu_custom_call" | custom-call | bytes 600000 | tf_op jit(solution)/shard_map/inner_rows/pallas_call | solution.py:376
  24.7 0.0 copy-done.11
  24.7 0.6 add_select_fusion
  25.3 0.0 collective-permute-done.4
  25.3 0.0 copy-start
  25.3 0.0 copy-start.10
  25.4 0.0 copy-start.9
  25.4 0.0 copy-start.5
  25.4 14.0 %interior.1 = (f32[128,8,128]{2,1,0:T(8,128)}, f32[128,8,128]{2,1,0:T(8,128)}, f32[128,8,128]{2,1,0:T(8,128)}, f32[128,8,128]{2,1,0:T(8,128)}, f32[128,8,128]{2,1,0:T(8,128)}) custom-call(f32[128,8,128]{2,1,0:T(8,128)} %get-tuple-element.35.own0.refs_1_, f32[128,8,128]{2,1,0:T(8,128)} %get-tuple-element.44.own1, f32[128,8,128]{2,1,0:T(8,128)} %get-tuple-element.41.own2, ...), custom_call_target="tpu_custom_call" | custom-call | bytes 1600000 | tf_op jit(solution)/shard_map/interior/pallas_call | solution.py:376
  39.4 0.0 copy-done
  39.5 0.3 collective-permute-start.11
  39.7 0.0 copy-done.12
  39.7 0.1 compare_convert_fusion.same
  39.8 1.5 %collective-permute-start.7 = (f32[2,2,32,8,128]{4,3,2,1,0:T(8,128)S(1)}, f32[2,2,32,8,128]{4,3,2,1,0:T(8,128)S(1)}, u32[]{:S(2)}, u32[]{:S(2)}) collective-permute-start(f32[2,2,32,8,128]{4,3,2,1,0:T(8,128)S(1)} %pad_maximum_fusion.refs_10_.refs_13_), channel_id=1, source_target_pairs={{0,16},{8,24},{16,0},{24,8},{1,17},{9,25},{17,1},{25,9},{2,18},{10... | collective-permute-start | bytes 1572872 | tf_op jit(solution)/shard_map/ppermute | solution.py:512
  41.3 1.7 %collective-permute-done.refs_0_.refs_1_ = f32[128,8,128]{2,1,0:T(8,128)S(1)} collective-permute-done((f32[128,8,128]{2,1,0:T(8,128)}, f32[128,8,128]{2,1,0:T(8,128)S(1)}, u32[]{:S(2)}, u32[]{:S(2)}) %collective-permute-start) | collective-permute-done | bytes 524320 | tf_op jit(solution)/shard_map/ppermute | solution.py:515
  43.0 0.0 collective-permute-done.1.refs_3_.refs_2_
  43.0 0.0 copy-done.10
  43.1 5.1 %collective-permute-start.5 = (f32[128,8,128]{2,1,0:T(8,128)S(1)}, f32[128,8,128]{2,1,0:T(8,128)}, u32[]{:S(2)}, u32[]{:S(2)}) collective-permute-start(f32[128,8,128]{2,1,0:T(8,128)S(1)} %copy-done.10), channel_id=1, source_target_pairs={{0,1},{1,2},{2,3},{3,4},{4,5},{5,6},{6,7},{8,9},{9,10},{10,11},{11... | collective-permute-start | bytes 1572872 | tf_op jit(solution)/shard_map/ppermute | solution.py:515
  48.2 0.0 copy-done.9
  48.2 1.3 %collective-permute-start.6 = (f32[128,8,128]{2,1,0:T(8,128)S(1)}, f32[128,8,128]{2,1,0:T(8,128)}, u32[]{:S(2)}, u32[]{:S(2)}) collective-permute-start(f32[128,8,128]{2,1,0:T(8,128)S(1)} %copy-done.9), channel_id=1, source_target_pairs={{1,0},{2,1},{3,2},{4,3},{5,4},{6,5},{7,6},{9,8},{10,9},{11,10},{12... | collective-permute-start | bytes 1572872 | tf_op jit(solution)/shard_map/ppermute | solution.py:515
  49.5 0.0 collective-permute-done.11
  49.5 0.7 pad_maximum_fusion.3
  50.2 1.5 %collective-permute-start.12 = (f32[2,8,4096]{2,1,0:T(8,128)}, f32[2,8,4096]{2,1,0:T(8,128)}, u32[]{:S(2)}, u32[]{:S(2)}) collective-permute-start(f32[2,8,4096]{2,1,0:T(8,128)} %pad_maximum_fusion.3), channel_id=1, source_target_pairs={{0,16},{8,24},{16,0},{24,8},{1,17},{9,25},{17,1},{25,9},{2,18},{10... | collective-permute-start | bytes 786440 | tf_op jit(solution)/shard_map/ppermute | solution.py:512
  51.7 0.2 convert_reduce_fusion
  51.9 0.1 copy.9.rank_col
  52.0 0.1 constant_dynamic-slice_fusion.own_same
  52.1 2.5 %collective-permute-done.7.refs_11_.refs_14_ = f32[2,2,32,8,128]{4,3,2,1,0:T(8,128)S(1)} collective-permute-done((f32[2,2,32,8,128]{4,3,2,1,0:T(8,128)S(1)}, f32[2,2,32,8,128]{4,3,2,1,0:T(8,128)S(1)}, u32[]{:S(2)}, u32[]{:S(2)}) %collective-permute-start.7) | collective-permute-done | bytes 524320 | tf_op jit(solution)/shard_map/ppermute | solution.py:512
  54.5 0.0 copy-done.5
  54.6 0.0 copy-done.6
  54.6 0.0 copy-done.7
  54.6 0.8 copy-done.8
  55.4 17.5 %edge_first.1 = (f32[128,8,128]{2,1,0:T(8,128)}, f32[128,8,128]{2,1,0:T(8,128)}, f32[128,8,128]{2,1,0:T(8,128)}, f32[128,8,128]{2,1,0:T(8,128)}, f32[128,8,128]{...) custom-call(f32[128,8,128]{2,1,0:T(8,128)} %copy-done.6, ...), custom_call_target="tpu_custom_call" | custom-call | bytes 2000000 | tf_op jit(solution)/shard_map/edge_first/pallas_call | solution.py:376
  72.8 0.0 collective-permute-done.5.refs_0_
  72.8 0.0 collective-permute-done.6.refs_3_
  72.8 0.0 copy-start.3
  72.9 0.0 copy-start.4
  72.9 0.0 copy-start.1
  72.9 22.1 %edge_last.1 = (f32[128,8,128]{2,1,0:T(8,128)}, f32[128,8,128]{2,1,0:T(8,128)}, f32[8,2048]{1,0:T(8,128)}) custom-call(f32[128,8,128]{2,1,0:T(8,128)} %collective-permute-done.5.refs_0_, f32[128,8,128]{2,1,0:T(8,128)} %copy-done.6, f32[128,8,128]{2,1,0:T(8,128)} %copy-done.7, f32[128,8,128]{2,1,0:T(8,128)} %collective-permute-done.6.refs_3_, ...), custom_call_target="tpu_custom_call" | custom-call | bytes 3000000 | tf_op jit(solution)/shard_map/edge_last/pallas_call | solution.py:376
  95.0 6.0 %all_gather.3.everyone = f32[32,2048]{1,0:T(8,128)S(1)} all-gather(f32[8,2048]{1,0:T(8,128)} %get-tuple-element.60.own), channel_id=1, replica_groups=mesh['ens'=4,'slab'=8] {'ens'}, dimensions={0}, use_global_device_ids=true | all-gather | bytes 327680 | tf_op jit(solution)/shard_map/all_gather | solution.py:543
  101.0 0.0 copy-done.3
  101.0 0.0 copy-done.4
  101.0 0.8 copy-done.2
  101.8 0.6 products.1
  102.5 2.5 %collective-permute-start.8 = (f32[32,40]{1,0:T(8,128)S(1)}, f32[32,40]{1,0:T(8,128)S(1)}, u32[]{:S(2)}, u32[]{:S(2)}) collective-permute-start(f32[32,40]{1,0:T(8,128)S(1)} %products.1), channel_id=1, source_target_pairs={{0,1},{1,0},{2,3},{3,2},{4,5},{5,4},{6,7},{7,6},{8,9},{9,8},{10,11... | collective-permute-start | bytes 15368 | tf_op jit(solution)/shard_map/ppermute | solution.py:554
  105.0 0.0 collective-permute-done.12
  105.0 0.0 copy-done.1
  105.0 1.0 pad_maximum_fusion.1
  105.9 0.7 collective-permute-done.8
  106.7 3.2 %collective-permute-start.9 = (f32[32,40]{1,0:T(8,128)S(1)}, f32[32,40]{1,0:T(8,128)S(1)}, u32[]{:S(2)}, u32[]{:S(2)}) collective-permute-start(f32[32,40]{1,0:T(8,128)S(1)} %add.46), channel_id=1, source_target_pairs={{0,2},{1,3},{2,0},{3,1},{4,6},{5,7},{6,4},{7,5},{8,10},{9,11},{10,... | collective-permute-start | bytes 15368 | tf_op jit(solution)/shard_map/ppermute | solution.py:554
  109.9 1.7 %collective-permute-done.9 = f32[32,40]{1,0:T(8,128)S(1)} collective-permute-done((f32[32,40]{1,0:T(8,128)S(1)}, f32[32,40]{1,0:T(8,128)S(1)}, u32[]{:S(2)}, u32[]{:S(2)}) %collective-permute-start.9) | collective-permute-done | bytes 5152 | tf_op jit(solution)/shard_map/ppermute | solution.py:554
  111.6 3.0 %collective-permute-start.10 = (f32[32,40]{1,0:T(8,128)S(1)}, f32[32,40]{1,0:T(8,128)S(1)}, u32[]{:S(2)}, u32[]{:S(2)}) collective-permute-start(f32[32,40]{1,0:T(8,128)S(1)} %add.47), channel_id=1, source_target_pairs={{0,4},{1,5},{2,6},{3,7},{4,0},{5,1},{6,2},{7,3},{8,12},{9,13},{10,... | collective-permute-start | bytes 15368 | tf_op jit(solution)/shard_map/ppermute | solution.py:554
  114.6 0.4 fusion.1.anomalies
  115.1 3.3 %field.1 = f32[128,4096]{1,0:T(8,128)} custom-call(f32[128,8,128]{2,1,0:T(8,128)} %get-tuple-element.58.refs_0_, f32[128,8,128]{2,1,0:T(8,128)} %get-tuple-element.56.refs_10_.refs_1_, f32[128,8,128]{2,1,0:T(8,128)} %get-tuple-element.57.refs_11_.refs_2_, f32[128,8,128]{2,1,0:T(8,128)} %get-tuple-element.59.refs_3_), custom_call_target="tpu_custom_call" | custom-call | bytes 800000 | tf_op jit(solution)/shard_map/field/pallas_call | solution.py:376
  118.3 0.0 collective-permute-done.10
  118.4 2.1 %update.1 = f32[8,4096]{1,0:T(8,128)} custom-call(f32[1,32,40]{2,1,0:T(8,128)S(1)} %add_bitcast_fusion.summands, f32[32,32]{1,0:T(8,128)S(1)} %compare_convert_fusion.same, f32[32,8]{1,0:T(8,128)S(1)} %constant_dynamic-slice_fusion.own_same, s32[1,32]{1,0:T(1,128)S(1)} %bitcast.27, s32[32,1]{1,0:T(8,128)S(1)} %copy.9.rank_col, ...), custom_call_target="tpu_custom_call" | custom-call | tf_op jit(solution)/shard_map/update/pallas_call | solution.py:556
  (11 shorter events, 0.1 us)
Async XLA Ops:
  3.7 8.5 %collective-permute-start.3 = (f32[32,8,128]{2,1,0:T(8,128)}, f32[32,8,128]{2,1,0:T(8,128)S(1)}, u32[]{:S(2)}, u32[]{:S(2)}) collective-permute-start(f32[32,8,128]{2,1,0:T(8,128)} %get-tuple-element.38), channel_id=1, source_target_pairs={{1,0},{2,1},{3,2},{4,3},{5,4},{6,5},{7,6},{9,8},{10,9},{11,10},{12... | collective-permute-start | bytes 393224 | tf_op jit(solution)/shard_map/ppermute | solution.py:515
  5.0 10.3 %collective-permute-start.2 = (f32[32,8,128]{2,1,0:T(8,128)}, f32[32,8,128]{2,1,0:T(8,128)S(1)}, u32[]{:S(2)}, u32[]{:S(2)}) collective-permute-start(f32[32,8,128]{2,1,0:T(8,128)} %get-tuple-element.37), channel_id=1, source_target_pairs={{0,1},{1,2},{2,3},{3,4},{4,5},{5,6},{6,7},{8,9},{9,10},{10,11},{11... | collective-permute-start | bytes 393224 | tf_op jit(solution)/shard_map/ppermute | solution.py:515
  15.3 9.4 %copy-start.11 = (s32[2048]{0:T(1024)S(1)}, s32[2048]{0:T(1024)}, u32[]{:S(2)}) copy-start(s32[2048]{0:T(1024)} %param.10) | copy-start | bytes 24580
  15.3 10.0 %collective-permute-start.4 = (f32[2,32,8,128]{3,2,1,0:T(8,128)S(1)}, f32[2,32,8,128]{3,2,1,0:T(8,128)S(1)}, u32[]{:S(2)}, u32[]{:S(2)}) collective-permute-start(f32[2,32,8,128]{3,2,1,0:T(8,128)S(1)} %get-tuple-element.67), channel_id=1, source_target_pairs={{0,8},{8,0},{16,24},{24,16},{1,9},{9,1},{17,25},{25,17},{2,10},{10... | collective-permute-start | bytes 786440 | tf_op jit(solution)/shard_map/ppermute | solution.py:511
  15.4 27.6 %collective-permute-start = (f32[128,8,128]{2,1,0:T(8,128)}, f32[128,8,128]{2,1,0:T(8,128)S(1)}, u32[]{:S(2)}, u32[]{:S(2)}) collective-permute-start(f32[128,8,128]{2,1,0:T(8,128)} %get-tuple-element.32.outer.own3.refs_2_), channel_id=1, source_target_pairs={{0,1},{1,2},{2,3},{3,4},{4,5},{5,6},{6,7},{8,9},{9,10},{10,11},{11... | collective-permute-start | bytes 1572872 | tf_op jit(solution)/shard_map/ppermute | solution.py:515
  19.7 23.3 %collective-permute-start.1 = (f32[128,8,128]{2,1,0:T(8,128)}, f32[128,8,128]{2,1,0:T(8,128)S(1)}, u32[]{:S(2)}, u32[]{:S(2)}) collective-permute-start(f32[128,8,128]{2,1,0:T(8,128)} %get-tuple-element.35.own0.refs_1_), channel_id=1, source_target_pairs={{1,0},{2,1},{3,2},{4,3},{5,4},{6,5},{7,6},{9,8},{10,9},{11,10},{12... | collective-permute-start | bytes 1572872 | tf_op jit(solution)/shard_map/ppermute | solution.py:515
  25.3 14.1 %copy-start = (f32[8,4096]{1,0:T(8,128)S(1)}, f32[8,4096]{1,0:T(8,128)}, u32[]{:S(2)}) copy-start(f32[8,4096]{1,0:T(8,128)} %own.1) | copy-start | bytes 393220
  25.3 14.4 %copy-start.12 = (s32[32]{0:T(128)S(1)}, s32[32]{0:T(128)}, u32[]{:S(2)}) copy-start(s32[32]{0:T(128)} %param.13) | copy-start | bytes 388
  25.3 17.7 %copy-start.10 = (f32[128,8,128]{2,1,0:T(8,128)S(1)}, f32[128,8,128]{2,1,0:T(8,128)}, u32[]{:S(2)}) copy-start(f32[128,8,128]{2,1,0:T(8,128)} %get-tuple-element.41.own2) | copy-start | bytes 1572868
  25.4 22.8 %copy-start.9 = (f32[128,8,128]{2,1,0:T(8,128)S(1)}, f32[128,8,128]{2,1,0:T(8,128)}, u32[]{:S(2)}) copy-start(f32[128,8,128]{2,1,0:T(8,128)} %get-tuple-element.44.own1) | copy-start | bytes 1572868
  25.4 29.1 %copy-start.5 = (f32[2,2,32,8,128]{4,3,2,1,0:T(8,128)}, f32[2,2,32,8,128]{4,3,2,1,0:T(8,128)S(1)}, u32[]{:S(2)}) copy-start(f32[2,2,32,8,128]{4,3,2,1,0:T(8,128)S(1)} %pad_maximum_fusion.refs_10_.refs_13_) | copy-start | bytes 1572868
  39.5 10.0 %collective-permute-start.11 = (f32[8,4096]{1,0:T(8,128)S(1)}, f32[8,4096]{1,0:T(8,128)S(1)}, u32[]{:S(2)}, u32[]{:S(2)}) collective-permute-start(f32[8,4096]{1,0:T(8,128)S(1)} %copy-done), channel_id=1, source_target_pairs={{0,8},{8,0},{16,24},{24,16},{1,9},{9,1},{17,25},{25,17},{2,10},{10... | collective-permute-start | bytes 393224 | tf_op jit(solution)/shard_map/ppermute | solution.py:511
  39.8 14.8 %collective-permute-start.7 = (f32[2,2,32,8,128]{4,3,2,1,0:T(8,128)S(1)}, f32[2,2,32,8,128]{4,3,2,1,0:T(8,128)S(1)}, u32[]{:S(2)}, u32[]{:S(2)}) collective-permute-start(f32[2,2,32,8,128]{4,3,2,1,0:T(8,128)S(1)} %pad_maximum_fusion.refs_10_.refs_13_), channel_id=1, source_target_pairs={{0,16},{8,24},{16,0},{24,8},{1,17},{9,25},{17,1},{25,9},{2,18},{10... | collective-permute-start | bytes 1572872 | tf_op jit(solution)/shard_map/ppermute | solution.py:512
  43.0 11.5 %copy-start.6 = (f32[128,8,128]{2,1,0:T(8,128)}, f32[128,8,128]{2,1,0:T(8,128)S(1)}, u32[]{:S(2)}) copy-start(f32[128,8,128]{2,1,0:T(8,128)S(1)} %collective-permute-done.refs_0_.refs_1_) | copy-start | bytes 1572868
  43.1 11.5 %copy-start.7 = (f32[128,8,128]{2,1,0:T(8,128)}, f32[128,8,128]{2,1,0:T(8,128)S(1)}, u32[]{:S(2)}) copy-start(f32[128,8,128]{2,1,0:T(8,128)S(1)} %collective-permute-done.1.refs_3_.refs_2_) | copy-start | bytes 1572868
  43.1 29.8 %collective-permute-start.5 = (f32[128,8,128]{2,1,0:T(8,128)S(1)}, f32[128,8,128]{2,1,0:T(8,128)}, u32[]{:S(2)}, u32[]{:S(2)}) collective-permute-start(f32[128,8,128]{2,1,0:T(8,128)S(1)} %copy-done.10), channel_id=1, source_target_pairs={{0,1},{1,2},{2,3},{3,4},{4,5},{5,6},{6,7},{8,9},{9,10},{10,11},{11... | collective-permute-start | bytes 1572872 | tf_op jit(solution)/shard_map/ppermute | solution.py:515
  48.2 24.7 %collective-permute-start.6 = (f32[128,8,128]{2,1,0:T(8,128)S(1)}, f32[128,8,128]{2,1,0:T(8,128)}, u32[]{:S(2)}, u32[]{:S(2)}) collective-permute-start(f32[128,8,128]{2,1,0:T(8,128)S(1)} %copy-done.9), channel_id=1, source_target_pairs={{1,0},{2,1},{3,2},{4,3},{5,4},{6,5},{7,6},{9,8},{10,9},{11,10},{12... | collective-permute-start | bytes 1572872 | tf_op jit(solution)/shard_map/ppermute | solution.py:515
  50.2 54.8 %collective-permute-start.12 = (f32[2,8,4096]{2,1,0:T(8,128)}, f32[2,8,4096]{2,1,0:T(8,128)}, u32[]{:S(2)}, u32[]{:S(2)}) collective-permute-start(f32[2,8,4096]{2,1,0:T(8,128)} %pad_maximum_fusion.3), channel_id=1, source_target_pairs={{0,16},{8,24},{16,0},{24,8},{1,17},{9,25},{17,1},{25,9},{2,18},{10... | collective-permute-start | bytes 786440 | tf_op jit(solution)/shard_map/ppermute | solution.py:512
  54.5 0.8 copy-start.8
  72.8 28.1 %copy-start.3 = (f32[8,2048]{1,0:T(8,128)S(1)}, f32[8,2048]{1,0:T(8,128)}, u32[]{:S(2)}) copy-start(f32[8,2048]{1,0:T(8,128)} %values.1) | copy-start | bytes 196612
  72.9 28.1 %copy-start.4 = (f32[2048]{0:T(1024)S(1)}, f32[2048]{0:T(1024)}, u32[]{:S(2)}) copy-start(f32[2048]{0:T(1024)} %param.12) | copy-start | bytes 24580
  72.9 32.1 %copy-start.1 = (f32[8,4096]{1,0:T(8,128)S(1)}, f32[8,4096]{1,0:T(8,128)}, u32[]{:S(2)}) copy-start(f32[8,4096]{1,0:T(8,128)} %own.1) | copy-start | bytes 393220
  101.0 0.8 copy-start.2
  102.5 4.2 %collective-permute-start.8 = (f32[32,40]{1,0:T(8,128)S(1)}, f32[32,40]{1,0:T(8,128)S(1)}, u32[]{:S(2)}, u32[]{:S(2)}) collective-permute-start(f32[32,40]{1,0:T(8,128)S(1)} %products.1), channel_id=1, source_target_pairs={{0,1},{1,0},{2,3},{3,2},{4,5},{5,4},{6,7},{7,6},{8,9},{9,8},{10,11... | collective-permute-start | bytes 15368 | tf_op jit(solution)/shard_map/ppermute | solution.py:554
  106.7 4.9 %collective-permute-start.9 = (f32[32,40]{1,0:T(8,128)S(1)}, f32[32,40]{1,0:T(8,128)S(1)}, u32[]{:S(2)}, u32[]{:S(2)}) collective-permute-start(f32[32,40]{1,0:T(8,128)S(1)} %add.46), channel_id=1, source_target_pairs={{0,2},{1,3},{2,0},{3,1},{4,6},{5,7},{6,4},{7,5},{8,10},{9,11},{10,... | collective-permute-start | bytes 15368 | tf_op jit(solution)/shard_map/ppermute | solution.py:554
  111.6 6.7 %collective-permute-start.10 = (f32[32,40]{1,0:T(8,128)S(1)}, f32[32,40]{1,0:T(8,128)S(1)}, u32[]{:S(2)}, u32[]{:S(2)}) collective-permute-start(f32[32,40]{1,0:T(8,128)S(1)} %add.47), channel_id=1, source_target_pairs={{0,4},{1,5},{2,6},{3,7},{4,0},{5,1},{6,2},{7,3},{8,12},{9,13},{10,... | collective-permute-start | bytes 15368 | tf_op jit(solution)/shard_map/ppermute | solution.py:554

commit v9 on v8

--- a/solution.py
+++ b/solution.py
@@ -18,6 +18,7 @@
 WIDE = 4
 TOGETHER = 2
 MOVED = 16
+FOLD = 4
 PICKED = 128
 ALL_ROWS = ROWS + 2 * HALO
 VMEM_LIMIT = 16 * 1024 * 1024
@@ -49,57 +50,75 @@
     return lane == 0, lane == LANES - 1
 
 
-def to_left(value):
-    return pltpu.roll(value, LANES - 1, 1)
-
-
-def to_right(value):
-    return pltpu.roll(value, 1, 1)
+def dealt(values, back=False):
+    shape = (FOLD * LANES, FOLD * LANES)
+    natural = lax.broadcasted_iota(jnp.int32, shape, 1 if back else 0)
+    place = lax.broadcasted_iota(jnp.int32, shape, 0 if back else 1)
+    moves = natural == FOLD * lax.rem(place, LANES) + lax.div(place, LANES)
+    moves = jnp.where(moves, 1.0, 0.0).astype(jnp.bfloat16)
+    products = []
+    for _ in range(3):
+        piece = values.astype(jnp.bfloat16)
+        products.append(jnp.dot(piece, moves, preferred_element_type=jnp.float32))
+        values = values - piece.astype(jnp.float32)
+    return products[0] + (products[1] + products[2])
+
+
+class Neighbours:
+    def __init__(self, get, blocks):
+        self.get, self.blocks, self.rolled = get, blocks, {}
+        self.first, self.last = edge_lanes()
+
+    def turned(self, b, shift):
+        b %= self.blocks
+        if (b, shift) not in self.rolled:
+            self.rolled[b, shift] = pltpu.roll(self.get(b), shift, 1)
+        return self.rolled[b, shift]
+
+    def following(self, b):
+        if b % FOLD < FOLD - 1:
+            return self.get(b + 1)
+        start = b - (FOLD - 1)
+        return jnp.where(
+            self.last, self.turned(start + FOLD, LANES - 1), self.turned(start, LANES - 1)
+        )
+
+    def preceding(self, b):
+        if b % FOLD > 0:
+            return self.get(b - 1)
+        end = b + FOLD - 1
+        return jnp.where(self.first, self.turned(end - FOLD, 1), self.turned(end, 1))
 
 
 def difference_pass(levels, cell, first_cell, diff, blocks):
-    _, last = edge_lanes()
-    centre = levels[cell]
-    rolled = to_left(centre)
+    centre = Neighbours(lambda b: levels[cell + b], blocks)
     for b in range(blocks):
-        following = levels[cell + (b + 1) % blocks]
-        rolled_following = to_left(following)
-        diff[first_cell + b] = jnp.where(last, rolled_following, rolled) - centre
-        centre, rolled = following, rolled_following
+        diff[first_cell + b] = centre.following(b) - centre.get(b)
 
 
 def slope_pass(levels, cell, places, first_cell, diff, slopes, linear, coef, params, blocks):
-    first, _ = edge_lanes()
-    rolled = to_right(diff[first_cell + blocks - 1])
+    differences = Neighbours(lambda b: diff[first_cell + b], blocks)
     for b in range(blocks):
         at = block_at(b)
-        d = diff[first_cell + b]
-        here = to_right(d)
-        d_back = jnp.where(first, rolled, here)
-        rolled = here
+        d, d_back = differences.get(b), differences.preceding(b)
         slopes[first_cell + b] = limited(d_back, d)
         value = levels[cell + b] + everywhere(coef, b, places[2]) * (d - d_back)
         linear[first_cell + b] = value + params[:, at] * everywhere(coef, b, places[3])
 
 
 def flux_pass(places, first_cell, diff, slopes, linear, partial, coef, blocks):
-    first, last = edge_lanes()
-
-    def parts(b):
-        d, slope = diff[first_cell + b], slopes[first_cell + b]
-        twice = d + d
-        return slope, twice, to_right(twice - slope), to_left(slope)
-
-    before = parts(blocks - 1)
-    here = parts(0)
+    def left_part(b):
+        d = diff[first_cell + b]
+        return d + d - slopes[first_cell + b]
+
+    left = Neighbours(left_part, blocks)
+    slope = Neighbours(lambda b: slopes[first_cell + b], blocks)
     for b in range(blocks):
-        after = parts((b + 1) % blocks)
         speed = everywhere(coef, b, places[1])
-        forward = jnp.where(first, before[2], here[2])
-        backward = here[1] - jnp.where(last, after[3], here[3])
-        change = jnp.where(speed > 0.0, forward, backward) + here[0]
+        d = diff[first_cell + b]
+        backward = d + d - slope.following(b)
+        change = jnp.where(speed > 0.0, left.preceding(b), backward) + slope.get(b)
         partial[first_cell + b] = linear[first_cell + b] - (0.5 * speed) * change
-        before, here = here, after
 
 
 def rows_pass(levels, cell, places, partial, result, coef, block, blocks):
@@ -172,7 +191,7 @@
     return levels.at[pl.ds((level * ALL_ROWS + HALO + row) * blocks, GROUP * blocks)]
 
 
-def fill_rows(blocks, first_rows, tracer, outs, staged, sems):
+def fill_rows(blocks, first_rows, tracer, mixed, staged, sems):
     def copy(block):
         return pltpu.make_async_copy(tracer.at[:, block_at(block)], staged.at[block], sems.at[block])
 
@@ -180,41 +199,87 @@
     def _(block):
         copy(block).start()
 
-    @pl.loop(0, blocks)
-    def _(block):
-        copy(block).wait()
-        for out, first_row in zip(outs, first_rows):
+    lines = len(first_rows) * GROUP * SUBLANES
+
+    @pl.loop(0, blocks // FOLD)
+    def _(part):
+        for q in range(FOLD):
+            block = part * FOLD + q
+            copy(block).wait()
+            for k, first_row in enumerate(first_rows):
+                for row in range(GROUP):
+                    line = part * lines + (k * GROUP + row) * SUBLANES
+                    mixed[pl.ds(pl.multiple_of(line, SUBLANES), SUBLANES), block_at(q)] = staged[
+                        block, pl.ds(first_row + row, SUBLANES, stride=ROWS), :
+                    ]
+
+
+def take_rows(blocks, mixed, outs):
+    lines = len(outs) * GROUP * SUBLANES
+
+    @pl.loop(0, blocks // FOLD)
+    def _(part):
+        for k, out in enumerate(outs):
             for row in range(GROUP):
-                out[row * blocks + block] = staged[
-                    block, pl.ds(first_row + row, SUBLANES, stride=ROWS), :
-                ]
+                line = part * lines + (k * GROUP + row) * SUBLANES
+                for p in range(FOLD):
+                    out[row * blocks + part * FOLD + p] = mixed[
+                        pl.ds(pl.multiple_of(line, SUBLANES), SUBLANES), block_at(p)
+                    ]
 
 
 def outer_rows_kernel(
-    blocks, tracer, own_coef, place_of, up, down, up_coef, down_coef, edge, edge_sem, staged, sems
+    blocks, tracer, own_coef, place_of, up, down, up_coef, down_coef, edge, edge_sem, mixed, staged, sems
 ):
     copy = pltpu.make_async_copy(own_coef.at[place_of[0]], edge, edge_sem)
     copy.start()
-    fill_rows(blocks, (0, ROWS - GROUP), tracer, (down, up), staged, sems)
+    fill_rows(blocks, (0, ROWS - GROUP), tracer, mixed, staged, sems)
     copy.wait()
-    for block in range(blocks):
-        at = block_at(block)
-        up_coef[block] = edge[ROWS - HALO :, at]
-        down_coef[block] = edge[0:HALO, at]
+    parts = blocks // FOLD
+    field_lines = parts * 2 * GROUP * SUBLANES
+    width = FOLD * LANES
+    for part in range(parts):
+        mixed[field_lines + part * ROWS : field_lines + (part + 1) * ROWS, :] = edge[
+            :, part * width : (part + 1) * width
+        ]
+    mixed[...] = dealt(mixed[...])
+    take_rows(blocks, mixed, (down, up))
+    for part in range(parts):
+        line = field_lines + part * ROWS
+        for p in range(FOLD):
+            down_coef[part * FOLD + p] = mixed[line : line + HALO, block_at(p)]
+            up_coef[part * FOLD + p] = mixed[line + ROWS - HALO : line + ROWS, block_at(p)]
 
 
 def inner_rows_kernel(
-    blocks, tracer, own_coef, outer, low, high, by_block, whole, coef_sem, staged, sems
+    blocks, tracer, own_coef, params, outer, low, high, by_block, dealt_params, whole, coef_sem, mixed,
+    staged, sems,
 ):
     copy = pltpu.make_async_copy(own_coef, whole, coef_sem)
     copy.start()
-    fill_rows(blocks, (GROUP, ROWS - 2 * GROUP), tracer, (low, high), staged, sems)
+    fill_rows(blocks, (GROUP, ROWS - 2 * GROUP), tracer, mixed, staged, sems)
     copy.wait()
-
-    @pl.loop(0, blocks)
-    def _(block):
+    parts = blocks // FOLD
+    coef_lines = parts * 2 * GROUP * SUBLANES
+    param_lines = coef_lines + parts * 4 * ROWS
+    width = FOLD * LANES
+    for part in range(parts):
+        at = slice(part * width, (part + 1) * width)
         for array in range(4):
-            by_block[block, array * ROWS : (array + 1) * ROWS, :] = whole[array, :, block_at(block)]
+            line = coef_lines + (part * 4 + array) * ROWS
+            mixed[line : line + ROWS, :] = whole[array, :, at]
+        line = param_lines + part * SUBLANES
+        mixed[line : line + SUBLANES, :] = params[:, at]
+    mixed[...] = dealt(mixed[...])
+    take_rows(blocks, mixed, (low, high))
+    for part in range(parts):
+        line = coef_lines + part * 4 * ROWS
+        for p in range(FOLD):
+            block = part * FOLD + p
+            by_block[block] = mixed[line : line + 4 * ROWS, block_at(p)]
+            dealt_params[:, block_at(block)] = mixed[
+                param_lines + part * SUBLANES : param_lines + (part + 1) * SUBLANES, block_at(p)
+            ]
 
 
 def interior_kernel(blocks, own0, own1, own2, own3, own_coef, params, *rest):
@@ -338,7 +403,7 @@
 
 
 def field_kernel(blocks, *refs):
-    parts, (out, cells, staged, sems, out_sems) = refs[: ROWS // GROUP], refs[ROWS // GROUP :]
+    parts, (out, cells, mixed, staged, sems, out_sems) = refs[: ROWS // GROUP], refs[ROWS // GROUP :]
     copies = Copies(sems)
     size = GROUP * blocks
     waits = [
@@ -346,15 +411,31 @@
     ]
     for copy in waits:
         copy.wait()
+    lines = ROWS * SUBLANES
+
+    def line_at(part, row):
+        return pl.ds(pl.multiple_of(part * lines + row * SUBLANES, SUBLANES), SUBLANES)
+
+    @pl.loop(0, blocks // FOLD)
+    def _(part):
+        for row in range(ROWS):
+            for p in range(FOLD):
+                mixed[line_at(part, row), block_at(p)] = cells[row * blocks + part * FOLD + p]
+
+    mixed[...] = dealt(mixed[...], back=True)
 
     def out_copy(block):
         return pltpu.make_async_copy(staged.at[block], out.at[:, block_at(block)], out_sems.at[block])
 
-    @pl.loop(0, blocks)
-    def _(block):
-        for row in range(ROWS):
-            staged[block, pl.ds(row, SUBLANES, stride=ROWS), :] = cells[row * blocks + block]
-        out_copy(block).start()
+    @pl.loop(0, blocks // FOLD)
+    def _(part):
+        for q in range(FOLD):
+            block = part * FOLD + q
+            for row in range(ROWS):
+                staged[block, pl.ds(row, SUBLANES, stride=ROWS), :] = mixed[
+                    line_at(part, row), block_at(q)
+                ]
+            out_copy(block).start()
 
     @pl.loop(0, blocks)
     def _(block):
@@ -385,28 +466,37 @@
     )(*operands)
 
 
-def row_groups(tracer, coefficients, place_of):
+def row_groups(tracer, coefficients, params, place_of):
     members, rows, columns = tracer.shape
-    if members != SUBLANES or rows != ROWS:
+    if members != SUBLANES or rows != ROWS or columns % (FOLD * LANES):
         raise ValueError("block shape")
     blocks = columns // LANES
+    parts = blocks // FOLD
     flat = tracer.reshape(members * rows, columns)
     dma = pltpu.SemaphoreType.DMA
-    scratches = [pltpu.VMEM((blocks, members * rows, LANES), jnp.float32), dma((blocks,))]
+    staged = [pltpu.VMEM((blocks, members * rows, LANES), jnp.float32), dma((blocks,))]
+
+    def mixed(lines):
+        return pltpu.VMEM((parts * lines, FOLD * LANES), jnp.float32)
+
     group, edge = (GROUP * blocks, members, LANES), (blocks, HALO, LANES)
     up, down, up_coef, down_coef = kernel_call(
         functools.partial(outer_rows_kernel, blocks), "outer_rows",
         [group, group, edge, edge], [ANYWHERE, ANYWHERE, IN_SMEM], (IN_VMEM,) * 4,
-        [pltpu.VMEM((rows, columns), jnp.float32), dma] + scratches, 3,
+        [pltpu.VMEM((rows, columns), jnp.float32), dma, mixed(2 * GROUP * members + rows)] + staged, 3,
         [flat, coefficients, place_of],
     )
-    low, high, by_block = kernel_call(
+    low, high, by_block, dealt_params = kernel_call(
         functools.partial(inner_rows_kernel, blocks), "inner_rows",
-        [group, group, (blocks, 4 * rows, LANES)], [ANYWHERE] * 3, (IN_VMEM,) * 3,
-        [pltpu.VMEM((4, rows, columns), jnp.float32), dma] + scratches, 3,
-        [flat, coefficients, up],
-    )
-    return (down, low, high, up), (up_coef, down_coef), by_block
+        [group, group, (blocks, 4 * rows, LANES), params.shape],
+        [ANYWHERE, ANYWHERE, IN_VMEM, ANYWHERE], (IN_VMEM,) * 4,
+        [
+            pltpu.VMEM((4, rows, columns), jnp.float32), dma,
+            mixed(2 * GROUP * members + 4 * rows + members),
+        ] + staged, 3,
+        [flat, coefficients, params, up],
+    )
+    return (down, low, high, up), (up_coef, down_coef), by_block, dealt_params
 
 
 def transport(shape, own, low0, high0, own_coef, pair, other, params, place_of, obs_index, halos):
@@ -432,8 +522,11 @@
         scratch(columns, dma((29,))), 10,
         [low0, own[0], own[3], high0, *inner, own_coef, pair, other, params, place_of],
     )
-    cell_of = obs_index // LANES + (STEPS * ALL_ROWS + HALO) * blocks
-    lane_of = obs_index % LANES
+    obs_row, obs_col = obs_index // columns, obs_index % columns
+    width = FOLD * LANES
+    obs_block = obs_col // width * FOLD + obs_col % FOLD
+    cell_of = (STEPS * ALL_ROWS + HALO + obs_row) * blocks + obs_block
+    lane_of = obs_col % width // FOLD
     shift_of = (jnp.arange(obs_index.shape[0], dtype=jnp.int32) - lane_of) % LANES
     low4, high4, predicted = kernel_call(
         functools.partial(last_kernel, blocks), "edge_last",
@@ -445,7 +538,11 @@
     (field,) = kernel_call(
         functools.partial(field_kernel, blocks), "field",
         [flat], [ANYWHERE] * 4, (ANYWHERE,),
-        [pltpu.VMEM((rows * blocks, members, LANES), jnp.float32), staged, dma((4,)), dma((blocks,))],
+        [
+            pltpu.VMEM((rows * blocks, members, LANES), jnp.float32),
+            pltpu.VMEM((members * rows * blocks // FOLD, FOLD * LANES), jnp.float32),
+            staged, dma((4,)), dma((blocks,)),
+        ],
         4, [low4, first[6], first[7], high4],
     )
     return field.reshape(shape), predicted, inner[0]
@@ -515,7 +612,9 @@
         return lax.ppermute(upper, "slab", forward), lax.ppermute(lower, "slab", backward)
 
     place_of = jnp.reshape(ens_pos, (1,))
-    own, coef_edges, own_coef = row_groups(tracer, coefficients, place_of)
+    own, coef_edges, own_coef, dealt_params = row_groups(
+        tracer, coefficients, parameters, place_of
+    )
     low0, high0 = halos(own[3], own[0])
 
     edge_low, edge_high = halos(*coef_edges)
@@ -531,7 +630,7 @@
     own_same = lax.dynamic_slice_in_dim(same, ens_pos * local_members, local_members, 1)
     field, predicted, first_done = transport(
         tracer.shape, own, low0, high0,
-        own_coef, pair, other, parameters, place_of, obs_index, halos,
+        own_coef, pair, other, dealt_params, place_of, obs_index, halos,
     )
 
     later, _ = lax.optimization_barrier((parameters, first_done))

time: 121 us -> 120 us (level)
  Pallas kernels: 66.3 us -> 64.2 us
    pallas_call x6, Pallas kernels: 63.5 us -> 61.5 us  [kernel_call(): pl.pallas_call(body, out_shape=tuple((jax.ShapeDtypeStruct(shape, jnp.flo...]
  transfers between devices with their start and end apart: 13 -> 13, of which waited for: 6 -> 6; matrix products, arithmetic and copies ran while one was open for 3% -> 3% of each run, Pallas kernels for 51% -> 49%
where the time goes in v9:
time: 120 us; the launch traced here: 119 us
  Pallas kernels  64.2 us (54%)
  starting transfers between devices  31.4 us (26%)
  waiting for transfers between devices  11.4 us (10%)
  blocking collectives  6 us (5%)
  other arithmetic  2.72 us (2%)
  local copies, waits for them, and re-layouts  1.89 us (2%)
    pallas_call x6, Pallas kernels, kernel_call(): pl.pallas_call(body, out_shape=tuple((jax.ShapeDtypeStruct(shape, jnp.flo...  61.5 us
    ppermute x3, starting transfers between devices, halos(): lax.ppermute(upper, 'slab', forward)  14.9 us
    ppermute x3, starting transfers between devices, local(): products = products + lax.ppermute(products, 'slab', pairs)  9.29 us
    all_gather x1, blocking collectives, local(): everyone = lax.all_gather(predicted, 'ens', axis=0, tiled=True)  6 us
    ppermute x3, waiting for transfers between devices, halos(): lax.ppermute(upper, 'slab', forward)  4.26 us
    ppermute x3, starting transfers between devices, halos(): lax.ppermute(lower, 'slab', backward)  3.86 us
    ppermute x2, starting transfers between devices, over_ens(): lax.ppermute(pair, 'ens', [(i, i ^ 2) for i in range(ens_count)])  3.03 us
    ppermute x2, waiting for transfers between devices, over_ens(): lax.ppermute(pair, 'ens', [(i, i ^ 2) for i in range(ens_count)])  3.01 us
  transfers between devices with their start and end apart: 13, of which 6 were waited for; matrix products, arithmetic and copies ran while one was open for 3% of the time, Pallas kernels for 49%

profile of v9, /device:TPU:0, one launch (start us, length us, event | category | flops | bytes accessed | tf_op | source)
XLA Modules:
  0.0 119.0 jit_solution(7927482784226302635)
XLA Ops:
  0.6 4.3 %outer_rows.1 = (f32[128,8,128]{2,1,0:T(8,128)}, f32[128,8,128]{2,1,0:T(8,128)}, f32[32,8,128]{2,1,0:T(8,128)}, f32[32,8,128]{2,1,0:T(8,128)}) custom-call(f32[128,4096]{1,0:T(8,128)} %bitcast.28, f32[4,16,4096]{2,1,0:T(8,128)} %own_coef.3, s32[1]{0:T(128)} %bitcast.1.place_of.refs_13_.refs_16_), custom_call_target="tpu_custom_call" | custom-call | bytes 600000 | tf_op jit(solution)/shard_map/outer_rows/pallas_call | solution.py:457
  5.0 1.3 %collective-permute-start.3 = (f32[32,8,128]{2,1,0:T(8,128)}, f32[32,8,128]{2,1,0:T(8,128)S(1)}, u32[]{:S(2)}, u32[]{:S(2)}) collective-permute-start(f32[32,8,128]{2,1,0:T(8,128)} %get-tuple-element.40), channel_id=1, source_target_pairs={{1,0},{2,1},{3,2},{4,3},{5,4},{6,5},{7,6},{9,8},{10,9},{11,10},{12... | collective-permute-start | bytes 393224 | tf_op jit(solution)/shard_map/ppermute | solution.py:612
  6.3 5.5 %collective-permute-start.2 = (f32[32,8,128]{2,1,0:T(8,128)}, f32[32,8,128]{2,1,0:T(8,128)S(1)}, u32[]{:S(2)}, u32[]{:S(2)}) collective-permute-start(f32[32,8,128]{2,1,0:T(8,128)} %get-tuple-element.39), channel_id=1, source_target_pairs={{0,1},{1,2},{2,3},{3,4},{4,5},{5,6},{6,7},{8,9},{9,10},{10,11},{11... | collective-permute-start | bytes 393224 | tf_op jit(solution)/shard_map/ppermute | solution.py:612
  11.8 1.8 %collective-permute-done.3 = f32[32,8,128]{2,1,0:T(8,128)S(1)} collective-permute-done((f32[32,8,128]{2,1,0:T(8,128)}, f32[32,8,128]{2,1,0:T(8,128)S(1)}, u32[]{:S(2)}, u32[]{:S(2)}) %collective-permute-start.3) | collective-permute-done | bytes 131104 | tf_op jit(solution)/shard_map/ppermute | solution.py:612
  13.5 3.1 %collective-permute-done.2 = f32[32,8,128]{2,1,0:T(8,128)S(1)} collective-permute-done((f32[32,8,128]{2,1,0:T(8,128)}, f32[32,8,128]{2,1,0:T(8,128)S(1)}, u32[]{:S(2)}, u32[]{:S(2)}) %collective-permute-start.2) | collective-permute-done | bytes 131104 | tf_op jit(solution)/shard_map/ppermute | solution.py:612
  16.6 0.0 copy-start.10
  16.6 0.1 collective-permute-start.4
  16.7 4.3 %collective-permute-start = (f32[128,8,128]{2,1,0:T(8,128)}, f32[128,8,128]{2,1,0:T(8,128)S(1)}, u32[]{:S(2)}, u32[]{:S(2)}) collective-permute-start(f32[128,8,128]{2,1,0:T(8,128)} %get-tuple-element.33.outer.own3.refs_2_), channel_id=1, source_target_pairs={{0,1},{1,2},{2,3},{3,4},{4,5},{5,6},{6,7},{8,9},{9,10},{10,11},{11... | collective-permute-start | bytes 1572872 | tf_op jit(solution)/shard_map/ppermute | solution.py:612
  21.0 1.3 %collective-permute-start.1 = (f32[128,8,128]{2,1,0:T(8,128)}, f32[128,8,128]{2,1,0:T(8,128)S(1)}, u32[]{:S(2)}, u32[]{:S(2)}) collective-permute-start(f32[128,8,128]{2,1,0:T(8,128)} %get-tuple-element.36.own0.refs_1_), channel_id=1, source_target_pairs={{1,0},{2,1},{3,2},{4,3},{5,4},{6,5},{7,6},{9,8},{10,9},{11,10},{12... | collective-permute-start | bytes 1572872 | tf_op jit(solution)/shard_map/ppermute | solution.py:612
  22.3 6.4 %inner_rows.1 = (f32[128,8,128]{2,1,0:T(8,128)}, f32[128,8,128]{2,1,0:T(8,128)}, f32[32,64,128]{2,1,0:T(8,128)}, f32[8,4096]{1,0:T(8,128)}) custom-call(f32[128,4096]{1,0:T(8,128)} %bitcast.29, f32[4,16,4096]{2,1,0:T(8,128)} %own_coef.3, f32[8,4096]{1,0:T(8,128)} %own.1, f32[128,8,128]{2,1,0:T(8,128)} %get-tuple-element.33.outer.own3.refs_2_), custom_call_target="tpu_custom_call" | custom-call | bytes 600000 | tf_op jit(solution)/shard_map/inner_rows/pallas_call | solution.py:457
  28.8 0.0 copy-done.10
  28.8 0.6 add_select_fusion
  29.4 0.0 collective-permute-done.4
  29.4 0.0 copy-start
  29.4 0.0 copy-start.11
  29.4 0.0 copy-start.9
  29.4 0.0 copy-start.8
  29.4 0.1 pad_maximum_fusion.refs_10_.refs_13_
  29.5 0.0 copy-start.4
  29.5 11.8 %interior.1 = (f32[128,8,128]{2,1,0:T(8,128)}, f32[128,8,128]{2,1,0:T(8,128)}, f32[128,8,128]{2,1,0:T(8,128)}, f32[128,8,128]{2,1,0:T(8,128)}, f32[128,8,128]{2,1,0:T(8,128)}) custom-call(f32[128,8,128]{2,1,0:T(8,128)} %get-tuple-element.36.own0.refs_1_, f32[128,8,128]{2,1,0:T(8,128)} %get-tuple-element.46.own1, f32[128,8,128]{2,1,0:T(8,128)} %get-tuple-element.43.own2, ...), custom_call_target="tpu_custom_call" | custom-call | bytes 1600000 | tf_op jit(solution)/shard_map/interior/pallas_call | solution.py:457
  41.3 0.0 copy-done
  41.3 0.3 collective-permute-start.11
  41.6 0.0 copy-done.11
  41.6 0.1 compare_convert_fusion.same
  41.7 1.5 %collective-permute-start.7 = (f32[2,2,32,8,128]{4,3,2,1,0:T(8,128)S(1)}, f32[2,2,32,8,128]{4,3,2,1,0:T(8,128)S(1)}, u32[]{:S(2)}, u32[]{:S(2)}) collective-permute-start(f32[2,2,32,8,128]{4,3,2,1,0:T(8,128)S(1)} %pad_maximum_fusion.refs_10_.refs_13_), channel_id=1, source_target_pairs={{0,16},{8,24},{16,0},{24,8},{1,17},{9,25},{17,1},{25,9},{2,18},{10... | collective-permute-start | bytes 1572872 | tf_op jit(solution)/shard_map/ppermute | solution.py:609
  43.2 1.2 %collective-permute-done.refs_0_.refs_1_ = f32[128,8,128]{2,1,0:T(8,128)S(1)} collective-permute-done((f32[128,8,128]{2,1,0:T(8,128)}, f32[128,8,128]{2,1,0:T(8,128)S(1)}, u32[]{:S(2)}, u32[]{:S(2)}) %collective-permute-start) | collective-permute-done | bytes 524320 | tf_op jit(solution)/shard_map/ppermute | solution.py:612
  44.4 0.0 collective-permute-done.1.refs_3_.refs_2_
  44.4 0.0 copy-done.9
  44.4 5.1 %collective-permute-start.5 = (f32[128,8,128]{2,1,0:T(8,128)S(1)}, f32[128,8,128]{2,1,0:T(8,128)}, u32[]{:S(2)}, u32[]{:S(2)}) collective-permute-start(f32[128,8,128]{2,1,0:T(8,128)S(1)} %copy-done.9), channel_id=1, source_target_pairs={{0,1},{1,2},{2,3},{3,4},{4,5},{5,6},{6,7},{8,9},{9,10},{10,11},{11... | collective-permute-start | bytes 1572872 | tf_op jit(solution)/shard_map/ppermute | solution.py:612
  49.5 0.0 copy-done.8
  49.5 1.3 %collective-permute-start.6 = (f32[128,8,128]{2,1,0:T(8,128)S(1)}, f32[128,8,128]{2,1,0:T(8,128)}, u32[]{:S(2)}, u32[]{:S(2)}) collective-permute-start(f32[128,8,128]{2,1,0:T(8,128)S(1)} %copy-done.8), channel_id=1, source_target_pairs={{1,0},{2,1},{3,2},{4,3},{5,4},{6,5},{7,6},{9,8},{10,9},{11,10},{12... | collective-permute-start | bytes 1572872 | tf_op jit(solution)/shard_map/ppermute | solution.py:612
  50.8 0.0 collective-permute-done.11
  50.8 0.7 pad_maximum_fusion.3
  51.5 1.5 %collective-permute-start.12 = (f32[2,8,4096]{2,1,0:T(8,128)}, f32[2,8,4096]{2,1,0:T(8,128)}, u32[]{:S(2)}, u32[]{:S(2)}) collective-permute-start(f32[2,8,4096]{2,1,0:T(8,128)} %pad_maximum_fusion.3), channel_id=1, source_target_pairs={{0,16},{8,24},{16,0},{24,8},{1,17},{9,25},{17,1},{25,9},{2,18},{10... | collective-permute-start | bytes 786440 | tf_op jit(solution)/shard_map/ppermute | solution.py:609
  53.1 0.2 convert_reduce_fusion
  53.2 0.1 copy.9.rank_col
  53.3 0.1 constant_dynamic-slice_fusion.own_same
  53.4 3.0 %collective-permute-done.7.refs_11_.refs_14_ = f32[2,2,32,8,128]{4,3,2,1,0:T(8,128)S(1)} collective-permute-done((f32[2,2,32,8,128]{4,3,2,1,0:T(8,128)S(1)}, f32[2,2,32,8,128]{4,3,2,1,0:T(8,128)S(1)}, u32[]{:S(2)}, u32[]{:S(2)}) %collective-permute-start.7) | collective-permute-done | bytes 524320 | tf_op jit(solution)/shard_map/ppermute | solution.py:609
  56.4 0.0 copy-done.4
  56.4 0.0 copy-done.5
  56.4 0.0 copy-done.6
  56.4 0.8 copy-done.7
  57.2 14.5 %edge_first.1 = (f32[128,8,128]{2,1,0:T(8,128)}, f32[128,8,128]{2,1,0:T(8,128)}, f32[128,8,128]{2,1,0:T(8,128)}, f32[128,8,128]{2,1,0:T(8,128)}, f32[128,8,128]{...) custom-call(f32[128,8,128]{2,1,0:T(8,128)} %copy-done.5, ...), custom_call_target="tpu_custom_call" | custom-call | bytes 2000000 | tf_op jit(solution)/shard_map/edge_first/pallas_call | solution.py:457
  71.7 0.0 collective-permute-done.5.refs_0_
  71.7 0.0 collective-permute-done.6.refs_3_
  71.7 0.0 copy-start.2
  71.7 0.0 copy-start.3
  71.8 19.2 %edge_last.1 = (f32[128,8,128]{2,1,0:T(8,128)}, f32[128,8,128]{2,1,0:T(8,128)}, f32[8,2048]{1,0:T(8,128)}) custom-call(f32[128,8,128]{2,1,0:T(8,128)} %collective-permute-done.5.refs_0_, f32[128,8,128]{2,1,0:T(8,128)} %copy-done.5, f32[128,8,128]{2,1,0:T(8,128)} %copy-done.6, f32[128,8,128]{2,1,0:T(8,128)} %collective-permute-done.6.refs_3_, ...), custom_call_target="tpu_custom_call" | custom-call | bytes 3000000 | tf_op jit(solution)/shard_map/edge_last/pallas_call | solution.py:457
  90.9 6.0 %all_gather.3.everyone = f32[32,2048]{1,0:T(8,128)S(1)} all-gather(f32[8,2048]{1,0:T(8,128)} %get-tuple-element.62.own), channel_id=1, replica_groups=mesh['ens'=4,'slab'=8] {'ens'}, dimensions={0}, use_global_device_ids=true | all-gather | bytes 327680 | tf_op jit(solution)/shard_map/all_gather | solution.py:642
  96.9 0.0 copy-done.2
  96.9 0.0 copy-done.3
  96.9 0.8 copy-done.1
  97.8 0.6 products.1
  98.4 2.5 %collective-permute-start.8 = (f32[32,40]{1,0:T(8,128)S(1)}, f32[32,40]{1,0:T(8,128)S(1)}, u32[]{:S(2)}, u32[]{:S(2)}) collective-permute-start(f32[32,40]{1,0:T(8,128)S(1)} %products.1), channel_id=1, source_target_pairs={{0,1},{1,0},{2,3},{3,2},{4,5},{5,4},{6,7},{7,6},{8,9},{9,8},{10,11... | collective-permute-start | bytes 15368 | tf_op jit(solution)/shard_map/ppermute | solution.py:653
  100.9 0.0 collective-permute-done.12
  100.9 1.0 pad_maximum_fusion.1
  101.9 0.7 collective-permute-done.8
  102.6 3.8 %collective-permute-start.9 = (f32[32,40]{1,0:T(8,128)S(1)}, f32[32,40]{1,0:T(8,128)S(1)}, u32[]{:S(2)}, u32[]{:S(2)}) collective-permute-start(f32[32,40]{1,0:T(8,128)S(1)} %add.66), channel_id=1, source_target_pairs={{0,2},{1,3},{2,0},{3,1},{4,6},{5,7},{6,4},{7,5},{8,10},{9,11},{10,... | collective-permute-start | bytes 15368 | tf_op jit(solution)/shard_map/ppermute | solution.py:653
  106.4 1.7 %collective-permute-done.9 = f32[32,40]{1,0:T(8,128)S(1)} collective-permute-done((f32[32,40]{1,0:T(8,128)S(1)}, f32[32,40]{1,0:T(8,128)S(1)}, u32[]{:S(2)}, u32[]{:S(2)}) %collective-permute-start.9) | collective-permute-done | bytes 5152 | tf_op jit(solution)/shard_map/ppermute | solution.py:653
  108.1 3.0 %collective-permute-start.10 = (f32[32,40]{1,0:T(8,128)S(1)}, f32[32,40]{1,0:T(8,128)S(1)}, u32[]{:S(2)}, u32[]{:S(2)}) collective-permute-start(f32[32,40]{1,0:T(8,128)S(1)} %add.67), channel_id=1, source_target_pairs={{0,4},{1,5},{2,6},{3,7},{4,0},{5,1},{6,2},{7,3},{8,12},{9,13},{10,... | collective-permute-start | bytes 15368 | tf_op jit(solution)/shard_map/ppermute | solution.py:653
  111.1 0.4 fusion.1.anomalies
  111.6 5.3 %field.1 = f32[128,4096]{1,0:T(8,128)} custom-call(f32[128,8,128]{2,1,0:T(8,128)} %get-tuple-element.60.refs_0_, f32[128,8,128]{2,1,0:T(8,128)} %get-tuple-element.58.refs_10_.refs_1_, f32[128,8,128]{2,1,0:T(8,128)} %get-tuple-element.59.refs_11_.refs_2_, f32[128,8,128]{2,1,0:T(8,128)} %get-tuple-element.61.refs_3_), custom_call_target="tpu_custom_call" | custom-call | bytes 800000 | tf_op jit(solution)/shard_map/field/pallas_call | solution.py:457
  116.9 0.0 collective-permute-done.10
  116.9 2.1 %update.1 = f32[8,4096]{1,0:T(8,128)} custom-call(f32[1,32,40]{2,1,0:T(8,128)S(1)} %add_bitcast_fusion.summands, f32[32,32]{1,0:T(8,128)S(1)} %compare_convert_fusion.same, f32[32,8]{1,0:T(8,128)S(1)} %constant_dynamic-slice_fusion.own_same, s32[1,32]{1,0:T(1,128)S(1)} %bitcast.27, s32[32,1]{1,0:T(8,128)S(1)} %copy.9.rank_col, ...), custom_call_target="tpu_custom_call" | custom-call | tf_op jit(solution)/shard_map/update/pallas_call | solution.py:655
  (9 shorter events, 0.1 us)
Async XLA Ops:
  5.0 8.5 %collective-permute-start.3 = (f32[32,8,128]{2,1,0:T(8,128)}, f32[32,8,128]{2,1,0:T(8,128)S(1)}, u32[]{:S(2)}, u32[]{:S(2)}) collective-permute-start(f32[32,8,128]{2,1,0:T(8,128)} %get-tuple-element.40), channel_id=1, source_target_pairs={{1,0},{2,1},{3,2},{4,3},{5,4},{6,5},{7,6},{9,8},{10,9},{11,10},{12... | collective-permute-start | bytes 393224 | tf_op jit(solution)/shard_map/ppermute | solution.py:612
  6.3 10.3 %collective-permute-start.2 = (f32[32,8,128]{2,1,0:T(8,128)}, f32[32,8,128]{2,1,0:T(8,128)S(1)}, u32[]{:S(2)}, u32[]{:S(2)}) collective-permute-start(f32[32,8,128]{2,1,0:T(8,128)} %get-tuple-element.39), channel_id=1, source_target_pairs={{0,1},{1,2},{2,3},{3,4},{4,5},{5,6},{6,7},{8,9},{9,10},{10,11},{11... | collective-permute-start | bytes 393224 | tf_op jit(solution)/shard_map/ppermute | solution.py:612
  16.6 12.1 %copy-start.10 = (s32[2048]{0:T(1024)S(1)}, s32[2048]{0:T(1024)}, u32[]{:S(2)}) copy-start(s32[2048]{0:T(1024)} %param.10) | copy-start | bytes 24580
  16.6 12.8 %collective-permute-start.4 = (f32[2,32,8,128]{3,2,1,0:T(8,128)S(1)}, f32[2,32,8,128]{3,2,1,0:T(8,128)S(1)}, u32[]{:S(2)}, u32[]{:S(2)}) collective-permute-start(f32[2,32,8,128]{3,2,1,0:T(8,128)S(1)} %get-tuple-element.69), channel_id=1, source_target_pairs={{0,8},{8,0},{16,24},{24,16},{1,9},{9,1},{17,25},{25,17},{2,10},{10... | collective-permute-start | bytes 786440 | tf_op jit(solution)/shard_map/ppermute | solution.py:608
  16.7 27.6 %collective-permute-start = (f32[128,8,128]{2,1,0:T(8,128)}, f32[128,8,128]{2,1,0:T(8,128)S(1)}, u32[]{:S(2)}, u32[]{:S(2)}) collective-permute-start(f32[128,8,128]{2,1,0:T(8,128)} %get-tuple-element.33.outer.own3.refs_2_), channel_id=1, source_target_pairs={{0,1},{1,2},{2,3},{3,4},{4,5},{5,6},{6,7},{8,9},{9,10},{10,11},{11... | collective-permute-start | bytes 1572872 | tf_op jit(solution)/shard_map/ppermute | solution.py:612
  21.0 23.3 %collective-permute-start.1 = (f32[128,8,128]{2,1,0:T(8,128)}, f32[128,8,128]{2,1,0:T(8,128)S(1)}, u32[]{:S(2)}, u32[]{:S(2)}) collective-permute-start(f32[128,8,128]{2,1,0:T(8,128)} %get-tuple-element.36.own0.refs_1_), channel_id=1, source_target_pairs={{1,0},{2,1},{3,2},{4,3},{5,4},{6,5},{7,6},{9,8},{10,9},{11,10},{12... | collective-permute-start | bytes 1572872 | tf_op jit(solution)/shard_map/ppermute | solution.py:612
  29.4 11.9 %copy-start = (f32[8,4096]{1,0:T(8,128)S(1)}, f32[8,4096]{1,0:T(8,128)}, u32[]{:S(2)}) copy-start(f32[8,4096]{1,0:T(8,128)} %own.1) | copy-start | bytes 393220
  29.4 12.2 %copy-start.11 = (s32[32]{0:T(128)S(1)}, s32[32]{0:T(128)}, u32[]{:S(2)}) copy-start(s32[32]{0:T(128)} %param.13) | copy-start | bytes 388
  29.4 15.0 %copy-start.9 = (f32[128,8,128]{2,1,0:T(8,128)S(1)}, f32[128,8,128]{2,1,0:T(8,128)}, u32[]{:S(2)}) copy-start(f32[128,8,128]{2,1,0:T(8,128)} %get-tuple-element.43.own2) | copy-start | bytes 1572868
  29.4 20.1 %copy-start.8 = (f32[128,8,128]{2,1,0:T(8,128)S(1)}, f32[128,8,128]{2,1,0:T(8,128)}, u32[]{:S(2)}) copy-start(f32[128,8,128]{2,1,0:T(8,128)} %get-tuple-element.46.own1) | copy-start | bytes 1572868
  29.5 26.9 %copy-start.4 = (f32[2,2,32,8,128]{4,3,2,1,0:T(8,128)}, f32[2,2,32,8,128]{4,3,2,1,0:T(8,128)S(1)}, u32[]{:S(2)}) copy-start(f32[2,2,32,8,128]{4,3,2,1,0:T(8,128)S(1)} %pad_maximum_fusion.refs_10_.refs_13_) | copy-start | bytes 1572868
  41.3 9.5 %collective-permute-start.11 = (f32[8,4096]{1,0:T(8,128)S(1)}, f32[8,4096]{1,0:T(8,128)S(1)}, u32[]{:S(2)}, u32[]{:S(2)}) collective-permute-start(f32[8,4096]{1,0:T(8,128)S(1)} %copy-done), channel_id=1, source_target_pairs={{0,8},{8,0},{16,24},{24,16},{1,9},{9,1},{17,25},{25,17},{2,10},{10... | collective-permute-start | bytes 393224 | tf_op jit(solution)/shard_map/ppermute | solution.py:608
  41.7 14.8 %collective-permute-start.7 = (f32[2,2,32,8,128]{4,3,2,1,0:T(8,128)S(1)}, f32[2,2,32,8,128]{4,3,2,1,0:T(8,128)S(1)}, u32[]{:S(2)}, u32[]{:S(2)}) collective-permute-start(f32[2,2,32,8,128]{4,3,2,1,0:T(8,128)S(1)} %pad_maximum_fusion.refs_10_.refs_13_), channel_id=1, source_target_pairs={{0,16},{8,24},{16,0},{24,8},{1,17},{9,25},{17,1},{25,9},{2,18},{10... | collective-permute-start | bytes 1572872 | tf_op jit(solution)/shard_map/ppermute | solution.py:609
  44.4 12.0 %copy-start.5 = (f32[128,8,128]{2,1,0:T(8,128)}, f32[128,8,128]{2,1,0:T(8,128)S(1)}, u32[]{:S(2)}) copy-start(f32[128,8,128]{2,1,0:T(8,128)S(1)} %collective-permute-done.refs_0_.refs_1_) | copy-start | bytes 1572868
  44.4 12.0 %copy-start.6 = (f32[128,8,128]{2,1,0:T(8,128)}, f32[128,8,128]{2,1,0:T(8,128)S(1)}, u32[]{:S(2)}) copy-start(f32[128,8,128]{2,1,0:T(8,128)S(1)} %collective-permute-done.1.refs_3_.refs_2_) | copy-start | bytes 1572868
  44.4 27.3 %collective-permute-start.5 = (f32[128,8,128]{2,1,0:T(8,128)S(1)}, f32[128,8,128]{2,1,0:T(8,128)}, u32[]{:S(2)}, u32[]{:S(2)}) collective-permute-start(f32[128,8,128]{2,1,0:T(8,128)S(1)} %copy-done.9), channel_id=1, source_target_pairs={{0,1},{1,2},{2,3},{3,4},{4,5},{5,6},{6,7},{8,9},{9,10},{10,11},{11... | collective-permute-start | bytes 1572872 | tf_op jit(solution)/shard_map/ppermute | solution.py:612
  49.5 22.2 %collective-permute-start.6 = (f32[128,8,128]{2,1,0:T(8,128)S(1)}, f32[128,8,128]{2,1,0:T(8,128)}, u32[]{:S(2)}, u32[]{:S(2)}) collective-permute-start(f32[128,8,128]{2,1,0:T(8,128)S(1)} %copy-done.8), channel_id=1, source_target_pairs={{1,0},{2,1},{3,2},{4,3},{5,4},{6,5},{7,6},{9,8},{10,9},{11,10},{12... | collective-permute-start | bytes 1572872 | tf_op jit(solution)/shard_map/ppermute | solution.py:612
  51.5 49.4 %collective-permute-start.12 = (f32[2,8,4096]{2,1,0:T(8,128)}, f32[2,8,4096]{2,1,0:T(8,128)}, u32[]{:S(2)}, u32[]{:S(2)}) collective-permute-start(f32[2,8,4096]{2,1,0:T(8,128)} %pad_maximum_fusion.3), channel_id=1, source_target_pairs={{0,16},{8,24},{16,0},{24,8},{1,17},{9,25},{17,1},{25,9},{2,18},{10... | collective-permute-start | bytes 786440 | tf_op jit(solution)/shard_map/ppermute | solution.py:609
  56.4 0.8 copy-start.7
  71.7 25.2 %copy-start.2 = (f32[8,2048]{1,0:T(8,128)S(1)}, f32[8,2048]{1,0:T(8,128)}, u32[]{:S(2)}) copy-start(f32[8,2048]{1,0:T(8,128)} %values.1) | copy-start | bytes 196612
  71.7 25.2 %copy-start.3 = (f32[2048]{0:T(1024)S(1)}, f32[2048]{0:T(1024)}, u32[]{:S(2)}) copy-start(f32[2048]{0:T(1024)} %param.12) | copy-start | bytes 24580
  96.9 0.8 copy-start.1
  98.4 4.2 %collective-permute-start.8 = (f32[32,40]{1,0:T(8,128)S(1)}, f32[32,40]{1,0:T(8,128)S(1)}, u32[]{:S(2)}, u32[]{:S(2)}) collective-permute-start(f32[32,40]{1,0:T(8,128)S(1)} %products.1), channel_id=1, source_target_pairs={{0,1},{1,0},{2,3},{3,2},{4,5},{5,4},{6,7},{7,6},{8,9},{9,8},{10,11... | collective-permute-start | bytes 15368 | tf_op jit(solution)/shard_map/ppermute | solution.py:653
  102.6 5.5 %collective-permute-start.9 = (f32[32,40]{1,0:T(8,128)S(1)}, f32[32,40]{1,0:T(8,128)S(1)}, u32[]{:S(2)}, u32[]{:S(2)}) collective-permute-start(f32[32,40]{1,0:T(8,128)S(1)} %add.66), channel_id=1, source_target_pairs={{0,2},{1,3},{2,0},{3,1},{4,6},{5,7},{6,4},{7,5},{8,10},{9,11},{10,... | collective-permute-start | bytes 15368 | tf_op jit(solution)/shard_map/ppermute | solution.py:653
  108.1 8.8 %collective-permute-start.10 = (f32[32,40]{1,0:T(8,128)S(1)}, f32[32,40]{1,0:T(8,128)S(1)}, u32[]{:S(2)}, u32[]{:S(2)}) collective-permute-start(f32[32,40]{1,0:T(8,128)S(1)} %add.67), channel_id=1, source_target_pairs={{0,4},{1,5},{2,6},{3,7},{4,0},{5,1},{6,2},{7,3},{8,12},{9,13},{10,... | collective-permute-start | bytes 15368 | tf_op jit(solution)/shard_map/ppermute | solution.py:653

commit v10 on v9

--- a/solution.py
+++ b/solution.py
@@ -15,9 +15,6 @@
 SUBLANES = 8
 ROWS = 16
 GROUP = 4
-WIDE = 4
-TOGETHER = 2
-MOVED = 16
 FOLD = 4
 PICKED = 128
 ALL_ROWS = ROWS + 2 * HALO
@@ -64,111 +61,73 @@
     return products[0] + (products[1] + products[2])
 
 
-class Neighbours:
-    def __init__(self, get, blocks):
-        self.get, self.blocks, self.rolled = get, blocks, {}
-        self.first, self.last = edge_lanes()
-
-    def turned(self, b, shift):
-        b %= self.blocks
-        if (b, shift) not in self.rolled:
-            self.rolled[b, shift] = pltpu.roll(self.get(b), shift, 1)
-        return self.rolled[b, shift]
-
-    def following(self, b):
-        if b % FOLD < FOLD - 1:
-            return self.get(b + 1)
-        start = b - (FOLD - 1)
-        return jnp.where(
-            self.last, self.turned(start + FOLD, LANES - 1), self.turned(start, LANES - 1)
-        )
-
-    def preceding(self, b):
-        if b % FOLD > 0:
-            return self.get(b - 1)
-        end = b + FOLD - 1
-        return jnp.where(self.first, self.turned(end - FOLD, 1), self.turned(end, 1))
-
-
-def difference_pass(levels, cell, first_cell, diff, blocks):
-    centre = Neighbours(lambda b: levels[cell + b], blocks)
-    for b in range(blocks):
-        diff[first_cell + b] = centre.following(b) - centre.get(b)
-
-
-def slope_pass(levels, cell, places, first_cell, diff, slopes, linear, coef, params, blocks):
-    differences = Neighbours(lambda b: diff[first_cell + b], blocks)
-    for b in range(blocks):
-        at = block_at(b)
-        d, d_back = differences.get(b), differences.preceding(b)
-        slopes[first_cell + b] = limited(d_back, d)
-        value = levels[cell + b] + everywhere(coef, b, places[2]) * (d - d_back)
-        linear[first_cell + b] = value + params[:, at] * everywhere(coef, b, places[3])
-
-
-def flux_pass(places, first_cell, diff, slopes, linear, partial, coef, blocks):
-    def left_part(b):
-        d = diff[first_cell + b]
-        return d + d - slopes[first_cell + b]
-
-    left = Neighbours(left_part, blocks)
-    slope = Neighbours(lambda b: slopes[first_cell + b], blocks)
-    for b in range(blocks):
-        speed = everywhere(coef, b, places[1])
-        d = diff[first_cell + b]
-        backward = d + d - slope.following(b)
-        change = jnp.where(speed > 0.0, left.preceding(b), backward) + slope.get(b)
-        partial[first_cell + b] = linear[first_cell + b] - (0.5 * speed) * change
-
-
-def rows_pass(levels, cell, places, partial, result, coef, block, blocks):
-    c = [levels[cell + (i - 2) * blocks + block] for i in range(GROUP + 4)]
-    d = [c[i + 1] - c[i] for i in range(GROUP + 3)]
+def stencil(line, speeds):
+    d = [line[i + 1] - line[i] for i in range(GROUP + 3)]
     slope = [None] + [limited(d[i - 1], d[i]) for i in range(1, GROUP + 3)]
     twice = [None] + [d[i] + d[i] for i in range(1, GROUP + 2)]
+    results = []
     for i in range(2, GROUP + 2):
-        speed = everywhere(coef, block, places[i - 2][0])
+        speed = speeds[i - 2]
         forward = twice[i - 1] - slope[i - 1]
         backward = twice[i] - slope[i + 1]
-        change = everywhere(coef, block, places[i - 2][2]) * (d[i] - d[i - 1])
-        change = change - (0.5 * speed) * (jnp.where(speed > 0.0, forward, backward) + slope[i])
-        here = (i - 2) * blocks + block
-        result[here] = partial[here] + change
-
-
-def advance_group(level, row, levels, work, result, coef, params, blocks):
-    diff, slopes, linear, partial = work
+        flux = speed * (jnp.where(speed > 0.0, forward, backward) + slope[i])
+        results.append((flux, d[i] - d[i - 1]))
+    return results
+
+
+def advance_tile(cell, places, part, parts, levels, coef, params, blocks):
+    start = part * FOLD
+    before = lax.rem(part + parts - 1, parts) * FOLD
+    after = lax.rem(part + 1, parts) * FOLD
+    first, last = edge_lanes()
+    own = [
+        [levels[cell + (i - 2) * blocks + start + p] for p in range(FOLD)] for i in range(GROUP + 4)
+    ]
+    along_rows = [
+        stencil(
+            [own[i][p] for i in range(GROUP + 4)],
+            [everywhere(coef, start + p, places[i][0]) for i in range(GROUP)],
+        )
+        for p in range(FOLD)
+    ]
+    values = []
+    for i in range(GROUP):
+        row = own[i + 2]
+        here = cell + i * blocks
+        left = [
+            jnp.where(first, pltpu.roll(levels[here + before + p], 1, 1), pltpu.roll(row[p], 1, 1))
+            for p in (FOLD - 2, FOLD - 1)
+        ]
+        right = [
+            jnp.where(
+                last,
+                pltpu.roll(levels[here + after + p], LANES - 1, 1),
+                pltpu.roll(row[p], LANES - 1, 1),
+            )
+            for p in (0, 1)
+        ]
+        along_columns = stencil(
+            [*left, *row, *right], [everywhere(coef, start + p, places[i][1]) for p in range(FOLD)]
+        )
+        for p in range(FOLD):
+            flux_x, lap_x = along_rows[p][i]
+            flux_y, lap_y = along_columns[p]
+            value = row[p] - 0.5 * (flux_x + flux_y)
+            value = value + everywhere(coef, start + p, places[i][2]) * (lap_x + lap_y)
+            source = params[:, block_at(start + p)] * everywhere(coef, start + p, places[i][3])
+            values.append((here + start + p, value + source))
+    for place, value in values:
+        levels[place + ALL_ROWS * blocks] = value
+
+
+def advance_group(level, row, levels, coef, params, blocks):
     cell = (level * ALL_ROWS + row) * blocks
     places = [[coef_row(array, row + i) for array in range(4)] for i in range(GROUP)]
-
-    def over_rows(one_row):
-        @pl.loop(0, GROUP // TOGETHER)
-        def _(pair):
-            for k in range(TOGETHER):
-                i = pair * TOGETHER + k
-                one_row([coef_row(array, row + i) for array in range(4)], i * blocks)
-
-    over_rows(lambda _, at: difference_pass(levels, cell + at, at, diff, blocks))
-    over_rows(
-        lambda where, at: slope_pass(
-            levels, cell + at, where, at, diff, slopes, linear, coef, params, blocks
-        )
-    )
-    over_rows(
-        lambda where, at: flux_pass(where, at, diff, slopes, linear, partial, coef, blocks)
-    )
-
-    @pl.loop(0, blocks // WIDE)
-    def _(wide_block):
-        for i in range(WIDE):
-            rows_pass(levels, cell, places, partial, result, coef, wide_block * WIDE + i, blocks)
-
-    @pl.loop(0, GROUP * blocks // MOVED)
-    def _(i):
-        first = i * MOVED
-        moved = [result[first + k] for k in range(MOVED)]
-        for k in range(MOVED):
-            levels[cell + ALL_ROWS * blocks + first + k] = moved[k]
+    parts = blocks // FOLD
+
+    @pl.loop(0, parts)
+    def _(part):
+        advance_tile(cell, places, part, parts, levels, coef, params, blocks)
 
 
 class Copies:
@@ -283,7 +242,7 @@
 
 
 def interior_kernel(blocks, own0, own1, own2, own3, own_coef, params, *rest):
-    outs, (levels, *work, result, coef, sems) = rest[:5], rest[5:]
+    outs, (levels, coef, sems) = rest[:5], rest[5:]
     copies = Copies(sems)
     waits = [
         copies.start(own, region(levels, 0, GROUP * i, blocks))
@@ -297,7 +256,7 @@
     def _(i):
         level = jnp.where(i < 3, 0, jnp.where(i < 5, 1, 2))
         row = jnp.where(i < 3, 2 + 4 * i, jnp.where(i < 5, 4 * i - 8, 6))
-        advance_group(level, row + HALO, levels, work, result, coef, params, blocks)
+        advance_group(level, row + HALO, levels, coef, params, blocks)
 
     waits = [
         copies.start(region(levels, level, row, blocks), out)
@@ -307,7 +266,7 @@
         copy.wait()
 
 
-def edge_steps(outer, blocks, waits, sends, levels, work, result, coef, params):
+def edge_steps(outer, blocks, waits, sends, levels, coef, params):
     @pl.loop(0, 2 * STEPS)
     def _(step):
         level, side = lax.div(step, 2), lax.rem(step, 2)
@@ -320,7 +279,7 @@
         low = 2 * level - outer
         high = ROWS + outer - GROUP - 2 * level
         row = jnp.where(side == 0, low, high) + HALO
-        advance_group(level, row, levels, work, result, coef, params, blocks)
+        advance_group(level, row, levels, coef, params, blocks)
         for k, copy in enumerate(sends):
             pl.when(step == k)(copy.start)
 
@@ -345,7 +304,7 @@
 def middle_kernel(blocks, *refs):
     sources, refs = refs[:9], refs[9:]
     own_coef, pair, other, params, place_of = refs[:5]
-    outs, (levels, *work, result, coef, sems) = refs[5:13], refs[13:]
+    outs, (levels, coef, sems) = refs[5:13], refs[13:]
     copies = Copies(sems)
     places = ((0, -4), (0, 0), (0, 12), (0, 16), (1, 2), (1, 10), (2, 4), (2, 8), (3, 6))
     waits = [[] for _ in range(STEPS)]
@@ -357,7 +316,7 @@
         copies.make(region(levels, level, row, blocks), out)
         for out, (level, row) in zip(outs, places)
     ]
-    edge_steps(2, blocks, waits, sends, levels, work, result, coef, params)
+    edge_steps(2, blocks, waits, sends, levels, coef, params)
     for copy in sends:
         copy.wait()
 
@@ -365,7 +324,7 @@
 def last_kernel(blocks, *refs):
     sources, refs = refs[:12], refs[12:]
     own_coef, pair, other, params, place_of, cell_of, shift_of = refs[:7]
-    low_out, high_out, predicted, levels, *work, result, coef, sems = refs[7:]
+    low_out, high_out, predicted, levels, coef, sems = refs[7:]
     copies = Copies(sems)
     places = (
         (0, -8), (0, -4), (0, 16), (0, 20),
@@ -375,7 +334,7 @@
     for source, (level, row) in zip(sources, places):
         waits[level].append(copies.start(source, region(levels, level, row, blocks)))
     waits[0] += load_coef(copies, own_coef, pair, other, place_of, coef)
-    edge_steps(6, blocks, waits, (), levels, work, result, coef, params)
+    edge_steps(6, blocks, waits, (), levels, coef, params)
     for copy in waits[STEPS]:
         copy.wait()
     sends = [
@@ -444,10 +403,8 @@
 
 def scratch(columns, *more):
     blocks = columns // LANES
-    group = pltpu.VMEM((GROUP * blocks, SUBLANES, LANES), jnp.float32)
     return [
         pltpu.VMEM(((STEPS + 1) * ALL_ROWS * blocks, SUBLANES, LANES), jnp.float32),
-        *[group] * 5,
         pltpu.VMEM((blocks, 4 * ALL_ROWS, LANES), jnp.float32),
         *more,
     ]
@@ -506,11 +463,10 @@
     flat = (members * rows, columns)
     dma = pltpu.SemaphoreType.DMA
     staged = pltpu.VMEM((blocks, members * rows, LANES), jnp.float32)
-    gated, pair = lax.optimization_barrier((params, pair))
     inner = kernel_call(
         functools.partial(interior_kernel, blocks), "interior",
         [group] * 5, [ANYWHERE] * 5 + [IN_VMEM], (ANYWHERE,) * 5,
-        scratch(columns, dma((16,))), 8, [*own, own_coef, gated],
+        scratch(columns, dma((16,))), 8, [*own, own_coef, params],
     )
     upper, lower, low0, high0, *_ = lax.optimization_barrier(
         (own[2], own[1], low0, high0, inner[0])

time: 120 us -> 112 us (0.933)
  waiting for transfers between devices: 11.4 us -> 7.06 us
  Pallas kernels: 64.2 us -> 60.8 us
    ppermute x3, waiting for transfers between devices: 4.26 us -> 0.47 us  [halos(): lax.ppermute(upper, 'slab', forward)]
    pallas_call x6, Pallas kernels: 61.5 us -> 58.1 us  [kernel_call(): pl.pallas_call(body, out_shape=tuple((jax.ShapeDtypeStruct(shape, jnp.flo...]
    ppermute x3, waiting for transfers between devices: 1.76 us -> 0.01 us  [halos(): lax.ppermute(lower, 'slab', backward)]
  transfers between devices with their start and end apart: 13 -> 13, of which waited for: 6 -> 5; matrix products, arithmetic and copies ran while one was open for 3% -> 3% of each run, Pallas kernels for 49% -> 49%
where the time goes in v10:
time: 112 us
  Pallas kernels  60.8 us (54%)
  starting transfers between devices  31.8 us (28%)
  waiting for transfers between devices  7.06 us (6%)
  blocking collectives  6 us (5%)
  other arithmetic  2.7 us (2%)
  local copies, waits for them, and re-layouts  1.89 us (2%)
    pallas_call x6, Pallas kernels, kernel_call(): pl.pallas_call(body, out_shape=tuple((jax.ShapeDtypeStruct(shape, jnp.flo...  58.1 us
    ppermute x3, starting transfers between devices, halos(): lax.ppermute(upper, 'slab', forward)  15.4 us
    ppermute x3, starting transfers between devices, local(): products = products + lax.ppermute(products, 'slab', pairs)  8.8 us
    all_gather x1, blocking collectives, local(): everyone = lax.all_gather(predicted, 'ens', axis=0, tiled=True)  6 us
    ppermute x3, starting transfers between devices, halos(): lax.ppermute(lower, 'slab', backward)  3.86 us
    ppermute x2, waiting for transfers between devices, over_ens(): lax.ppermute(pair, 'ens', [(i, i ^ 2) for i in range(ens_count)])  3.74 us
    ppermute x2, starting transfers between devices, over_ens(): lax.ppermute(pair, 'ens', [(i, i ^ 2) for i in range(ens_count)])  3.12 us
    ppermute x3, waiting for transfers between devices, local(): products = products + lax.ppermute(products, 'slab', pairs)  2.4 us
  transfers between devices with their start and end apart: 13, of which 5 were waited for; matrix products, arithmetic and copies ran while one was open for 3% of the time, Pallas kernels for 49%

profile of v10, /device:TPU:0, one launch (start us, length us, event | category | flops | bytes accessed | tf_op | source)
XLA Modules:
  0.0 111.7 jit_solution(2392498162476683222)
XLA Ops:
  0.6 4.3 %outer_rows.1 = (f32[128,8,128]{2,1,0:T(8,128)}, f32[128,8,128]{2,1,0:T(8,128)}, f32[32,8,128]{2,1,0:T(8,128)}, f32[32,8,128]{2,1,0:T(8,128)}) custom-call(f32[128,4096]{1,0:T(8,128)} %bitcast.28, f32[4,16,4096]{2,1,0:T(8,128)} %own_coef.3, s32[1]{0:T(128)} %bitcast.1.place_of.refs_13_.refs_16_), custom_call_target="tpu_custom_call" | custom-call | bytes 600000 | tf_op jit(solution)/shard_map/outer_rows/pallas_call | solution.py:414
  5.0 1.3 %collective-permute-start.5 = (f32[32,8,128]{2,1,0:T(8,128)}, f32[32,8,128]{2,1,0:T(8,128)S(1)}, u32[]{:S(2)}, u32[]{:S(2)}) collective-permute-start(f32[32,8,128]{2,1,0:T(8,128)} %get-tuple-element.47), channel_id=1, source_target_pairs={{1,0},{2,1},{3,2},{4,3},{5,4},{6,5},{7,6},{9,8},{10,9},{11,10},{12... | collective-permute-start | bytes 393224 | tf_op jit(solution)/shard_map/ppermute | solution.py:568
  6.3 5.5 %collective-permute-start.4 = (f32[32,8,128]{2,1,0:T(8,128)}, f32[32,8,128]{2,1,0:T(8,128)S(1)}, u32[]{:S(2)}, u32[]{:S(2)}) collective-permute-start(f32[32,8,128]{2,1,0:T(8,128)} %get-tuple-element.46), channel_id=1, source_target_pairs={{0,1},{1,2},{2,3},{3,4},{4,5},{5,6},{6,7},{8,9},{9,10},{10,11},{11... | collective-permute-start | bytes 393224 | tf_op jit(solution)/shard_map/ppermute | solution.py:568
  11.8 4.8 %collective-permute-start = (f32[128,8,128]{2,1,0:T(8,128)}, f32[128,8,128]{2,1,0:T(8,128)S(1)}, u32[]{:S(2)}, u32[]{:S(2)}) collective-permute-start(f32[128,8,128]{2,1,0:T(8,128)} %get-tuple-element.31.outer.own3.refs_2_), channel_id=1, source_target_pairs={{0,1},{1,2},{2,3},{3,4},{4,5},{5,6},{6,7},{8,9},{9,10},{10,11},{11... | collective-permute-start | bytes 1572872 | tf_op jit(solution)/shard_map/ppermute | solution.py:568
  16.6 1.3 %collective-permute-start.1 = (f32[128,8,128]{2,1,0:T(8,128)}, f32[128,8,128]{2,1,0:T(8,128)S(1)}, u32[]{:S(2)}, u32[]{:S(2)}) collective-permute-start(f32[128,8,128]{2,1,0:T(8,128)} %get-tuple-element.34.own0.refs_1_), channel_id=1, source_target_pairs={{1,0},{2,1},{3,2},{4,3},{5,4},{6,5},{7,6},{9,8},{10,9},{11,10},{12... | collective-permute-start | bytes 1572872 | tf_op jit(solution)/shard_map/ppermute | solution.py:568
  17.9 6.4 %inner_rows.1 = (f32[128,8,128]{2,1,0:T(8,128)}, f32[128,8,128]{2,1,0:T(8,128)}, f32[32,64,128]{2,1,0:T(8,128)}, f32[8,4096]{1,0:T(8,128)}) custom-call(f32[128,4096]{1,0:T(8,128)} %bitcast.29, f32[4,16,4096]{2,1,0:T(8,128)} %own_coef.3, f32[8,4096]{1,0:T(8,128)} %own.1, f32[128,8,128]{2,1,0:T(8,128)} %get-tuple-element.31.outer.own3.refs_2_), custom_call_target="tpu_custom_call" | custom-call | bytes 600000 | tf_op jit(solution)/shard_map/inner_rows/pallas_call | solution.py:414
  24.3 0.0 copy-start
  24.3 0.0 copy-start.10
  24.3 0.0 copy-start.11
  24.4 0.0 copy-start.9
  24.4 0.0 copy-start.8
  24.4 10.7 %interior.1 = (f32[128,8,128]{2,1,0:T(8,128)}, f32[128,8,128]{2,1,0:T(8,128)}, f32[128,8,128]{2,1,0:T(8,128)}, f32[128,8,128]{2,1,0:T(8,128)}, f32[128,8,128]{2,1,0:T(8,128)}) custom-call(f32[128,8,128]{2,1,0:T(8,128)} %get-tuple-element.34.own0.refs_1_, f32[128,8,128]{2,1,0:T(8,128)} %get-tuple-element.41.own1, f32[128,8,128]{2,1,0:T(8,128)} %get-tuple-element.38.own2, ...), custom_call_target="tpu_custom_call" | custom-call | bytes 1600000 | tf_op jit(solution)/shard_map/interior/pallas_call | solution.py:414
  35.1 0.0 copy-done
  35.1 0.1 collective-permute-start.11
  35.2 0.0 collective-permute-done.5
  35.2 0.0 collective-permute-done.4
  35.2 0.5 collective-permute-start.6
  35.8 0.0 copy-done.10
  35.8 0.6 add_select_fusion
  36.4 0.0 copy-done.11
  36.4 0.1 compare_convert_fusion.same
  36.5 0.4 collective-permute-done.6
  37.0 0.0 copy-start.4
  37.0 1.6 %collective-permute-start.7 = (f32[2,2,32,8,128]{4,3,2,1,0:T(8,128)S(1)}, f32[2,2,32,8,128]{4,3,2,1,0:T(8,128)S(1)}, u32[]{:S(2)}, u32[]{:S(2)}) collective-permute-start(f32[2,2,32,8,128]{4,3,2,1,0:T(8,128)S(1)} %pad_maximum_fusion.refs_10_.refs_13_), channel_id=1, source_target_pairs={{0,16},{8,24},{16,0},{24,8},{1,17},{9,25},{17,1},{25,9},{2,18},{10... | collective-permute-start | bytes 1572872 | tf_op jit(solution)/shard_map/ppermute | solution.py:565
  38.6 0.5 collective-permute-done.refs_0_.refs_1_
  39.1 0.0 copy-start.5
  39.1 0.0 collective-permute-done.1.refs_3_.refs_2_
  39.1 0.0 copy-done.9
  39.1 5.1 %collective-permute-start.2 = (f32[128,8,128]{2,1,0:T(8,128)S(1)}, f32[128,8,128]{2,1,0:T(8,128)}, u32[]{:S(2)}, u32[]{:S(2)}) collective-permute-start(f32[128,8,128]{2,1,0:T(8,128)S(1)} %copy-done.9), channel_id=1, source_target_pairs={{0,1},{1,2},{2,3},{3,4},{4,5},{5,6},{6,7},{8,9},{9,10},{10,11},{11... | collective-permute-start | bytes 1572872 | tf_op jit(solution)/shard_map/ppermute | solution.py:568
  44.2 0.0 copy-done.8
  44.2 1.3 %collective-permute-start.3 = (f32[128,8,128]{2,1,0:T(8,128)S(1)}, f32[128,8,128]{2,1,0:T(8,128)}, u32[]{:S(2)}, u32[]{:S(2)}) collective-permute-start(f32[128,8,128]{2,1,0:T(8,128)S(1)} %copy-done.8), channel_id=1, source_target_pairs={{1,0},{2,1},{3,2},{4,3},{5,4},{6,5},{7,6},{9,8},{10,9},{11,10},{12... | collective-permute-start | bytes 1572872 | tf_op jit(solution)/shard_map/ppermute | solution.py:568
  45.5 0.0 collective-permute-done.11
  45.5 0.7 pad_maximum_fusion.3
  46.2 1.5 %collective-permute-start.12 = (f32[2,8,4096]{2,1,0:T(8,128)}, f32[2,8,4096]{2,1,0:T(8,128)}, u32[]{:S(2)}, u32[]{:S(2)}) collective-permute-start(f32[2,8,4096]{2,1,0:T(8,128)} %pad_maximum_fusion.3), channel_id=1, source_target_pairs={{0,16},{8,24},{16,0},{24,8},{1,17},{9,25},{17,1},{25,9},{2,18},{10... | collective-permute-start | bytes 786440 | tf_op jit(solution)/shard_map/ppermute | solution.py:565
  47.7 0.2 convert_reduce_fusion
  47.9 0.1 copy.9.rank_col
  48.0 0.1 constant_dynamic-slice_fusion.own_same
  48.1 3.7 %collective-permute-done.7.refs_11_.refs_14_ = f32[2,2,32,8,128]{4,3,2,1,0:T(8,128)S(1)} collective-permute-done((f32[2,2,32,8,128]{4,3,2,1,0:T(8,128)S(1)}, f32[2,2,32,8,128]{4,3,2,1,0:T(8,128)S(1)}, u32[]{:S(2)}, u32[]{:S(2)}) %collective-permute-start.7) | collective-permute-done | bytes 524320 | tf_op jit(solution)/shard_map/ppermute | solution.py:565
  51.8 0.0 copy-done.4
  51.8 0.0 copy-done.5
  51.8 0.0 copy-done.6
  51.8 0.8 copy-done.7
  52.6 13.3 %edge_first.1 = (f32[128,8,128]{2,1,0:T(8,128)}, f32[128,8,128]{2,1,0:T(8,128)}, f32[128,8,128]{2,1,0:T(8,128)}, f32[128,8,128]{2,1,0:T(8,128)}, f32[128,8,128]{...) custom-call(f32[128,8,128]{2,1,0:T(8,128)} %copy-done.5, ...), custom_call_target="tpu_custom_call" | custom-call | bytes 2000000 | tf_op jit(solution)/shard_map/edge_first/pallas_call | solution.py:414
  66.0 0.0 collective-permute-done.2.refs_0_
  66.0 0.0 collective-permute-done.3.refs_3_
  66.0 0.0 copy-start.2
  66.0 0.0 copy-start.3
  66.0 18.0 %edge_last.1 = (f32[128,8,128]{2,1,0:T(8,128)}, f32[128,8,128]{2,1,0:T(8,128)}, f32[8,2048]{1,0:T(8,128)}) custom-call(f32[128,8,128]{2,1,0:T(8,128)} %collective-permute-done.2.refs_0_, f32[128,8,128]{2,1,0:T(8,128)} %copy-done.5, f32[128,8,128]{2,1,0:T(8,128)} %copy-done.6, f32[128,8,128]{2,1,0:T(8,128)} %collective-permute-done.3.refs_3_, ...), custom_call_target="tpu_custom_call" | custom-call | bytes 3000000 | tf_op jit(solution)/shard_map/edge_last/pallas_call | solution.py:414
  84.0 6.0 %all_gather.3.everyone = f32[32,2048]{1,0:T(8,128)S(1)} all-gather(f32[8,2048]{1,0:T(8,128)} %get-tuple-element.58.own), channel_id=1, replica_groups=mesh['ens'=4,'slab'=8] {'ens'}, dimensions={0}, use_global_device_ids=true | all-gather | bytes 327680 | tf_op jit(solution)/shard_map/all_gather | solution.py:598
  90.0 0.0 copy-done.2
  90.0 0.0 copy-done.3
  90.1 0.8 copy-done.1
  90.9 0.6 products.1
  91.5 2.7 %collective-permute-start.8 = (f32[32,40]{1,0:T(8,128)S(1)}, f32[32,40]{1,0:T(8,128)S(1)}, u32[]{:S(2)}, u32[]{:S(2)}) collective-permute-start(f32[32,40]{1,0:T(8,128)S(1)} %products.1), channel_id=1, source_target_pairs={{0,1},{1,0},{2,3},{3,2},{4,5},{5,4},{6,7},{7,6},{8,9},{9,8},{10,11... | collective-permute-start | bytes 15368 | tf_op jit(solution)/shard_map/ppermute | solution.py:609
  94.2 0.0 collective-permute-done.12
  94.2 1.0 pad_maximum_fusion.1
  95.2 0.7 collective-permute-done.8
  96.0 3.1 %collective-permute-start.9 = (f32[32,40]{1,0:T(8,128)S(1)}, f32[32,40]{1,0:T(8,128)S(1)}, u32[]{:S(2)}, u32[]{:S(2)}) collective-permute-start(f32[32,40]{1,0:T(8,128)S(1)} %add.66), channel_id=1, source_target_pairs={{0,2},{1,3},{2,0},{3,1},{4,6},{5,7},{6,4},{7,5},{8,10},{9,11},{10,... | collective-permute-start | bytes 15368 | tf_op jit(solution)/shard_map/ppermute | solution.py:609
  99.1 1.7 %collective-permute-done.9 = f32[32,40]{1,0:T(8,128)S(1)} collective-permute-done((f32[32,40]{1,0:T(8,128)S(1)}, f32[32,40]{1,0:T(8,128)S(1)}, u32[]{:S(2)}, u32[]{:S(2)}) %collective-permute-start.9) | collective-permute-done | bytes 5152 | tf_op jit(solution)/shard_map/ppermute | solution.py:609
  100.7 3.0 %collective-permute-start.10 = (f32[32,40]{1,0:T(8,128)S(1)}, f32[32,40]{1,0:T(8,128)S(1)}, u32[]{:S(2)}, u32[]{:S(2)}) collective-permute-start(f32[32,40]{1,0:T(8,128)S(1)} %add.67), channel_id=1, source_target_pairs={{0,4},{1,5},{2,6},{3,7},{4,0},{5,1},{6,2},{7,3},{8,12},{9,13},{10,... | collective-permute-start | bytes 15368 | tf_op jit(solution)/shard_map/ppermute | solution.py:609
  103.8 0.4 fusion.1.anomalies
  104.2 5.3 %field.1 = f32[128,4096]{1,0:T(8,128)} custom-call(f32[128,8,128]{2,1,0:T(8,128)} %get-tuple-element.56.refs_0_, f32[128,8,128]{2,1,0:T(8,128)} %get-tuple-element.54.refs_10_.refs_1_, f32[128,8,128]{2,1,0:T(8,128)} %get-tuple-element.55.refs_11_.refs_2_, f32[128,8,128]{2,1,0:T(8,128)} %get-tuple-element.57.refs_3_), custom_call_target="tpu_custom_call" | custom-call | bytes 800000 | tf_op jit(solution)/shard_map/field/pallas_call | solution.py:414
  109.5 0.0 collective-permute-done.10
  109.6 2.1 %update.1 = f32[8,4096]{1,0:T(8,128)} custom-call(f32[1,32,40]{2,1,0:T(8,128)S(1)} %add_bitcast_fusion.summands, f32[32,32]{1,0:T(8,128)S(1)} %compare_convert_fusion.same, f32[32,8]{1,0:T(8,128)S(1)} %constant_dynamic-slice_fusion.own_same, s32[1,32]{1,0:T(1,128)S(1)} %bitcast.27, s32[32,1]{1,0:T(8,128)S(1)} %copy.9.rank_col, ...), custom_call_target="tpu_custom_call" | custom-call | tf_op jit(solution)/shard_map/update/pallas_call | solution.py:611
  (9 shorter events, 0.1 us)
Async XLA Ops:
  5.0 30.2 %collective-permute-start.5 = (f32[32,8,128]{2,1,0:T(8,128)}, f32[32,8,128]{2,1,0:T(8,128)S(1)}, u32[]{:S(2)}, u32[]{:S(2)}) collective-permute-start(f32[32,8,128]{2,1,0:T(8,128)} %get-tuple-element.47), channel_id=1, source_target_pairs={{1,0},{2,1},{3,2},{4,3},{5,4},{6,5},{7,6},{9,8},{10,9},{11,10},{12... | collective-permute-start | bytes 393224 | tf_op jit(solution)/shard_map/ppermute | solution.py:568
  6.3 28.9 %collective-permute-start.4 = (f32[32,8,128]{2,1,0:T(8,128)}, f32[32,8,128]{2,1,0:T(8,128)S(1)}, u32[]{:S(2)}, u32[]{:S(2)}) collective-permute-start(f32[32,8,128]{2,1,0:T(8,128)} %get-tuple-element.46), channel_id=1, source_target_pairs={{0,1},{1,2},{2,3},{3,4},{4,5},{5,6},{6,7},{8,9},{9,10},{10,11},{11... | collective-permute-start | bytes 393224 | tf_op jit(solution)/shard_map/ppermute | solution.py:568
  11.8 27.3 %collective-permute-start = (f32[128,8,128]{2,1,0:T(8,128)}, f32[128,8,128]{2,1,0:T(8,128)S(1)}, u32[]{:S(2)}, u32[]{:S(2)}) collective-permute-start(f32[128,8,128]{2,1,0:T(8,128)} %get-tuple-element.31.outer.own3.refs_2_), channel_id=1, source_target_pairs={{0,1},{1,2},{2,3},{3,4},{4,5},{5,6},{6,7},{8,9},{9,10},{10,11},{11... | collective-permute-start | bytes 1572872 | tf_op jit(solution)/shard_map/ppermute | solution.py:568
  16.6 22.4 %collective-permute-start.1 = (f32[128,8,128]{2,1,0:T(8,128)}, f32[128,8,128]{2,1,0:T(8,128)S(1)}, u32[]{:S(2)}, u32[]{:S(2)}) collective-permute-start(f32[128,8,128]{2,1,0:T(8,128)} %get-tuple-element.34.own0.refs_1_), channel_id=1, source_target_pairs={{1,0},{2,1},{3,2},{4,3},{5,4},{6,5},{7,6},{9,8},{10,9},{11,10},{12... | collective-permute-start | bytes 1572872 | tf_op jit(solution)/shard_map/ppermute | solution.py:568
  24.3 10.8 %copy-start = (f32[8,4096]{1,0:T(8,128)S(1)}, f32[8,4096]{1,0:T(8,128)}, u32[]{:S(2)}) copy-start(f32[8,4096]{1,0:T(8,128)} %own.1) | copy-start | bytes 393220
  24.3 11.5 %copy-start.10 = (s32[2048]{0:T(1024)S(1)}, s32[2048]{0:T(1024)}, u32[]{:S(2)}) copy-start(s32[2048]{0:T(1024)} %param.10) | copy-start | bytes 24580
  24.3 12.1 %copy-start.11 = (s32[32]{0:T(128)S(1)}, s32[32]{0:T(128)}, u32[]{:S(2)}) copy-start(s32[32]{0:T(128)} %param.13) | copy-start | bytes 388
  24.4 14.7 %copy-start.9 = (f32[128,8,128]{2,1,0:T(8,128)S(1)}, f32[128,8,128]{2,1,0:T(8,128)}, u32[]{:S(2)}) copy-start(f32[128,8,128]{2,1,0:T(8,128)} %get-tuple-element.38.own2) | copy-start | bytes 1572868
  24.4 19.8 %copy-start.8 = (f32[128,8,128]{2,1,0:T(8,128)S(1)}, f32[128,8,128]{2,1,0:T(8,128)}, u32[]{:S(2)}) copy-start(f32[128,8,128]{2,1,0:T(8,128)} %get-tuple-element.41.own1) | copy-start | bytes 1572868
  35.1 10.4 %collective-permute-start.11 = (f32[8,4096]{1,0:T(8,128)S(1)}, f32[8,4096]{1,0:T(8,128)S(1)}, u32[]{:S(2)}, u32[]{:S(2)}) collective-permute-start(f32[8,4096]{1,0:T(8,128)S(1)} %copy-done), channel_id=1, source_target_pairs={{0,8},{8,0},{16,24},{24,16},{1,9},{9,1},{17,25},{25,17},{2,10},{10... | collective-permute-start | bytes 393224 | tf_op jit(solution)/shard_map/ppermute | solution.py:564
  35.2 1.7 %collective-permute-start.6 = (f32[2,32,8,128]{3,2,1,0:T(8,128)S(1)}, f32[2,32,8,128]{3,2,1,0:T(8,128)S(1)}, u32[]{:S(2)}, u32[]{:S(2)}) collective-permute-start(f32[2,32,8,128]{3,2,1,0:T(8,128)S(1)} %get-tuple-element.65), channel_id=1, source_target_pairs={{0,8},{8,0},{16,24},{24,16},{1,9},{9,1},{17,25},{25,17},{2,10},{10... | collective-permute-start | bytes 786440 | tf_op jit(solution)/shard_map/ppermute | solution.py:564
  37.0 14.8 %copy-start.4 = (f32[2,2,32,8,128]{4,3,2,1,0:T(8,128)}, f32[2,2,32,8,128]{4,3,2,1,0:T(8,128)S(1)}, u32[]{:S(2)}) copy-start(f32[2,2,32,8,128]{4,3,2,1,0:T(8,128)S(1)} %pad_maximum_fusion.refs_10_.refs_13_) | copy-start | bytes 1572868
  37.0 14.8 %collective-permute-start.7 = (f32[2,2,32,8,128]{4,3,2,1,0:T(8,128)S(1)}, f32[2,2,32,8,128]{4,3,2,1,0:T(8,128)S(1)}, u32[]{:S(2)}, u32[]{:S(2)}) collective-permute-start(f32[2,2,32,8,128]{4,3,2,1,0:T(8,128)S(1)} %pad_maximum_fusion.refs_10_.refs_13_), channel_id=1, source_target_pairs={{0,16},{8,24},{16,0},{24,8},{1,17},{9,25},{17,1},{25,9},{2,18},{10... | collective-permute-start | bytes 1572872 | tf_op jit(solution)/shard_map/ppermute | solution.py:565
  39.1 12.8 %copy-start.5 = (f32[128,8,128]{2,1,0:T(8,128)}, f32[128,8,128]{2,1,0:T(8,128)S(1)}, u32[]{:S(2)}) copy-start(f32[128,8,128]{2,1,0:T(8,128)S(1)} %collective-permute-done.refs_0_.refs_1_) | copy-start | bytes 1572868
  39.1 12.8 %copy-start.6 = (f32[128,8,128]{2,1,0:T(8,128)}, f32[128,8,128]{2,1,0:T(8,128)S(1)}, u32[]{:S(2)}) copy-start(f32[128,8,128]{2,1,0:T(8,128)S(1)} %collective-permute-done.1.refs_3_.refs_2_) | copy-start | bytes 1572868
  39.1 26.9 %collective-permute-start.2 = (f32[128,8,128]{2,1,0:T(8,128)S(1)}, f32[128,8,128]{2,1,0:T(8,128)}, u32[]{:S(2)}, u32[]{:S(2)}) collective-permute-start(f32[128,8,128]{2,1,0:T(8,128)S(1)} %copy-done.9), channel_id=1, source_target_pairs={{0,1},{1,2},{2,3},{3,4},{4,5},{5,6},{6,7},{8,9},{9,10},{10,11},{11... | collective-permute-start | bytes 1572872 | tf_op jit(solution)/shard_map/ppermute | solution.py:568
  44.2 21.8 %collective-permute-start.3 = (f32[128,8,128]{2,1,0:T(8,128)S(1)}, f32[128,8,128]{2,1,0:T(8,128)}, u32[]{:S(2)}, u32[]{:S(2)}) collective-permute-start(f32[128,8,128]{2,1,0:T(8,128)S(1)} %copy-done.8), channel_id=1, source_target_pairs={{1,0},{2,1},{3,2},{4,3},{5,4},{6,5},{7,6},{9,8},{10,9},{11,10},{12... | collective-permute-start | bytes 1572872 | tf_op jit(solution)/shard_map/ppermute | solution.py:568
  46.2 48.0 %collective-permute-start.12 = (f32[2,8,4096]{2,1,0:T(8,128)}, f32[2,8,4096]{2,1,0:T(8,128)}, u32[]{:S(2)}, u32[]{:S(2)}) collective-permute-start(f32[2,8,4096]{2,1,0:T(8,128)} %pad_maximum_fusion.3), channel_id=1, source_target_pairs={{0,16},{8,24},{16,0},{24,8},{1,17},{9,25},{17,1},{25,9},{2,18},{10... | collective-permute-start | bytes 786440 | tf_op jit(solution)/shard_map/ppermute | solution.py:565
  51.8 0.8 copy-start.7
  66.0 24.1 %copy-start.2 = (f32[8,2048]{1,0:T(8,128)S(1)}, f32[8,2048]{1,0:T(8,128)}, u32[]{:S(2)}) copy-start(f32[8,2048]{1,0:T(8,128)} %values.1) | copy-start | bytes 196612
  66.0 24.0 %copy-start.3 = (f32[2048]{0:T(1024)S(1)}, f32[2048]{0:T(1024)}, u32[]{:S(2)}) copy-start(f32[2048]{0:T(1024)} %param.12) | copy-start | bytes 24580
  90.1 0.8 copy-start.1
  91.5 4.4 %collective-permute-start.8 = (f32[32,40]{1,0:T(8,128)S(1)}, f32[32,40]{1,0:T(8,128)S(1)}, u32[]{:S(2)}, u32[]{:S(2)}) collective-permute-start(f32[32,40]{1,0:T(8,128)S(1)} %products.1), channel_id=1, source_target_pairs={{0,1},{1,0},{2,3},{3,2},{4,5},{5,4},{6,7},{7,6},{8,9},{9,8},{10,11... | collective-permute-start | bytes 15368 | tf_op jit(solution)/shard_map/ppermute | solution.py:609
  96.0 4.8 %collective-permute-start.9 = (f32[32,40]{1,0:T(8,128)S(1)}, f32[32,40]{1,0:T(8,128)S(1)}, u32[]{:S(2)}, u32[]{:S(2)}) collective-permute-start(f32[32,40]{1,0:T(8,128)S(1)} %add.66), channel_id=1, source_target_pairs={{0,2},{1,3},{2,0},{3,1},{4,6},{5,7},{6,4},{7,5},{8,10},{9,11},{10,... | collective-permute-start | bytes 15368 | tf_op jit(solution)/shard_map/ppermute | solution.py:609
  100.7 8.8 %collective-permute-start.10 = (f32[32,40]{1,0:T(8,128)S(1)}, f32[32,40]{1,0:T(8,128)S(1)}, u32[]{:S(2)}, u32[]{:S(2)}) collective-permute-start(f32[32,40]{1,0:T(8,128)S(1)} %add.67), channel_id=1, source_target_pairs={{0,4},{1,5},{2,6},{3,7},{4,0},{5,1},{6,2},{7,3},{8,12},{9,13},{10,... | collective-permute-start | bytes 15368 | tf_op jit(solution)/shard_map/ppermute | solution.py:609

commit v11 on v10

--- a/solution.py
+++ b/solution.py
@@ -17,6 +17,8 @@
 GROUP = 4
 FOLD = 4
 PICKED = 128
+TILES = 2
+FIELD_CALLS = 3
 ALL_ROWS = ROWS + 2 * HALO
 VMEM_LIMIT = 16 * 1024 * 1024
 TALL_LIMIT = 58 * 1024 * 1024
@@ -75,13 +77,13 @@
     return results
 
 
-def advance_tile(cell, places, part, parts, levels, coef, params, blocks):
+def advance_tile(cell, places, part, parts, source, target, coef, params, blocks):
     start = part * FOLD
     before = lax.rem(part + parts - 1, parts) * FOLD
     after = lax.rem(part + 1, parts) * FOLD
     first, last = edge_lanes()
     own = [
-        [levels[cell + (i - 2) * blocks + start + p] for p in range(FOLD)] for i in range(GROUP + 4)
+        [source[cell + (i - 2) * blocks + start + p] for p in range(FOLD)] for i in range(GROUP + 4)
     ]
     along_rows = [
         stencil(
@@ -90,18 +92,17 @@
         )
         for p in range(FOLD)
     ]
-    values = []
     for i in range(GROUP):
         row = own[i + 2]
         here = cell + i * blocks
         left = [
-            jnp.where(first, pltpu.roll(levels[here + before + p], 1, 1), pltpu.roll(row[p], 1, 1))
+            jnp.where(first, pltpu.roll(source[here + before + p], 1, 1), pltpu.roll(row[p], 1, 1))
             for p in (FOLD - 2, FOLD - 1)
         ]
         right = [
             jnp.where(
                 last,
-                pltpu.roll(levels[here + after + p], LANES - 1, 1),
+                pltpu.roll(source[here + after + p], LANES - 1, 1),
                 pltpu.roll(row[p], LANES - 1, 1),
             )
             for p in (0, 1)
@@ -114,20 +115,21 @@
             flux_y, lap_y = along_columns[p]
             value = row[p] - 0.5 * (flux_x + flux_y)
             value = value + everywhere(coef, start + p, places[i][2]) * (lap_x + lap_y)
-            source = params[:, block_at(start + p)] * everywhere(coef, start + p, places[i][3])
-            values.append((here + start + p, value + source))
-    for place, value in values:
-        levels[place + ALL_ROWS * blocks] = value
-
-
-def advance_group(level, row, levels, coef, params, blocks):
-    cell = (level * ALL_ROWS + row) * blocks
+            value = value + params[:, block_at(start + p)] * everywhere(coef, start + p, places[i][3])
+            target[here + start + p] = value
+
+
+def advance_group(source, target, row, coef, params, blocks):
+    cell = row * blocks
     places = [[coef_row(array, row + i) for array in range(4)] for i in range(GROUP)]
     parts = blocks // FOLD
 
-    @pl.loop(0, parts)
-    def _(part):
-        advance_tile(cell, places, part, parts, levels, coef, params, blocks)
+    @pl.loop(0, parts // TILES)
+    def _(some):
+        for k in range(TILES):
+            advance_tile(
+                cell, places, some * TILES + k, parts, source, target, coef, params, blocks
+            )
 
 
 class Copies:
@@ -147,7 +149,7 @@
 
 
 def region(levels, level, row, blocks):
-    return levels.at[pl.ds((level * ALL_ROWS + HALO + row) * blocks, GROUP * blocks)]
+    return levels[level].at[pl.ds((HALO + row) * blocks, GROUP * blocks)]
 
 
 def fill_rows(blocks, first_rows, tracer, mixed, staged, sems):
@@ -242,7 +244,7 @@
 
 
 def interior_kernel(blocks, own0, own1, own2, own3, own_coef, params, *rest):
-    outs, (levels, coef, sems) = rest[:5], rest[5:]
+    outs, (*levels, coef, sems) = rest[:5], rest[5:]
     copies = Copies(sems)
     waits = [
         copies.start(own, region(levels, 0, GROUP * i, blocks))
@@ -252,11 +254,11 @@
     for copy in waits:
         copy.wait()
 
-    @pl.loop(0, 6)
-    def _(i):
-        level = jnp.where(i < 3, 0, jnp.where(i < 5, 1, 2))
-        row = jnp.where(i < 3, 2 + 4 * i, jnp.where(i < 5, 4 * i - 8, 6))
-        advance_group(level, row + HALO, levels, coef, params, blocks)
+    for level, start, count in ((0, 2, 3), (1, 4, 2), (2, 6, 1)):
+        @pl.loop(0, count)
+        def _(i):
+            row = start + HALO + GROUP * i
+            advance_group(levels[level], levels[level + 1], row, coef, params, blocks)
 
     waits = [
         copies.start(region(levels, level, row, blocks), out)
@@ -267,21 +269,18 @@
 
 
 def edge_steps(outer, blocks, waits, sends, levels, coef, params):
-    @pl.loop(0, 2 * STEPS)
-    def _(step):
-        level, side = lax.div(step, 2), lax.rem(step, 2)
-        for k in range(STEPS):
-            @pl.when(step == 2 * k)
-            def _():
-                for copy in waits[k]:
-                    copy.wait()
-
-        low = 2 * level - outer
-        high = ROWS + outer - GROUP - 2 * level
-        row = jnp.where(side == 0, low, high) + HALO
-        advance_group(level, row, levels, coef, params, blocks)
-        for k, copy in enumerate(sends):
-            pl.when(step == k)(copy.start)
+    for level in range(STEPS):
+        for copy in waits[level]:
+            copy.wait()
+        low, high = 2 * level - outer, ROWS + outer - GROUP - 2 * level
+
+        @pl.loop(0, 2)
+        def _(side):
+            row = low + HALO + side * (high - low)
+            advance_group(levels[level], levels[level + 1], row, coef, params, blocks)
+
+        for copy in sends[2 * level : 2 * level + 2]:
+            copy.start()
 
 
 def coef_row(array, row):
@@ -304,7 +303,7 @@
 def middle_kernel(blocks, *refs):
     sources, refs = refs[:9], refs[9:]
     own_coef, pair, other, params, place_of = refs[:5]
-    outs, (levels, coef, sems) = refs[5:13], refs[13:]
+    outs, (*levels, coef, sems) = refs[5:13], refs[13:]
     copies = Copies(sems)
     places = ((0, -4), (0, 0), (0, 12), (0, 16), (1, 2), (1, 10), (2, 4), (2, 8), (3, 6))
     waits = [[] for _ in range(STEPS)]
@@ -324,7 +323,7 @@
 def last_kernel(blocks, *refs):
     sources, refs = refs[:12], refs[12:]
     own_coef, pair, other, params, place_of, cell_of, shift_of = refs[:7]
-    low_out, high_out, predicted, levels, coef, sems = refs[7:]
+    low_out, high_out, predicted, *levels, coef, sems = refs[7:]
     copies = Copies(sems)
     places = (
         (0, -8), (0, -4), (0, 16), (0, 20),
@@ -350,7 +349,7 @@
         def some(part, found):
             for i in range(PICKED):
                 o = part * PICKED + i
-                value = pltpu.roll(levels[cell_of[base + o]], shift_of[base + o], 1)
+                value = pltpu.roll(levels[STEPS][cell_of[base + o]], shift_of[base + o], 1)
                 found = jnp.where(lane == o, value, found)
             return found
 
@@ -361,12 +360,18 @@
         copy.wait()
 
 
-def field_kernel(blocks, *refs):
-    parts, (out, cells, mixed, staged, sems, out_sems) = refs[: ROWS // GROUP], refs[ROWS // GROUP :]
+def field_kernel(blocks, first_part, count, *refs):
+    sources, refs = refs[: ROWS // GROUP], refs[-6:]
+    out, cells, mixed, staged, sems, out_sems = refs
     copies = Copies(sems)
-    size = GROUP * blocks
+    width = count * FOLD
     waits = [
-        copies.start(part, cells.at[pl.ds(i * size, size)]) for i, part in enumerate(parts)
+        copies.start(
+            source.at[pl.ds(row * blocks + first_part * FOLD, width)],
+            cells.at[pl.ds((i * GROUP + row) * width, width)],
+        )
+        for i, source in enumerate(sources)
+        for row in range(GROUP)
     ]
     for copy in waits:
         copy.wait()
@@ -375,18 +380,20 @@
     def line_at(part, row):
         return pl.ds(pl.multiple_of(part * lines + row * SUBLANES, SUBLANES), SUBLANES)
 
-    @pl.loop(0, blocks // FOLD)
+    @pl.loop(0, count)
     def _(part):
         for row in range(ROWS):
             for p in range(FOLD):
-                mixed[line_at(part, row), block_at(p)] = cells[row * blocks + part * FOLD + p]
+                mixed[line_at(part, row), block_at(p)] = cells[row * width + part * FOLD + p]
 
     mixed[...] = dealt(mixed[...], back=True)
 
     def out_copy(block):
-        return pltpu.make_async_copy(staged.at[block], out.at[:, block_at(block)], out_sems.at[block])
-
-    @pl.loop(0, blocks // FOLD)
+        return pltpu.make_async_copy(
+            staged.at[block], out.at[:, block_at(first_part * FOLD + block)], out_sems.at[block]
+        )
+
+    @pl.loop(0, count)
     def _(part):
         for q in range(FOLD):
             block = part * FOLD + q
@@ -396,7 +403,7 @@
                 ]
             out_copy(block).start()
 
-    @pl.loop(0, blocks)
+    @pl.loop(0, width)
     def _(block):
         out_copy(block).wait()
 
@@ -404,13 +411,13 @@
 def scratch(columns, *more):
     blocks = columns // LANES
     return [
-        pltpu.VMEM(((STEPS + 1) * ALL_ROWS * blocks, SUBLANES, LANES), jnp.float32),
+        *[pltpu.VMEM((ALL_ROWS * blocks, SUBLANES, LANES), jnp.float32)] * (STEPS + 1),
         pltpu.VMEM((blocks, 4 * ALL_ROWS, LANES), jnp.float32),
         *more,
     ]
 
 
-def kernel_call(body, name, outs, specs, out_specs, scratches, cost, operands):
+def kernel_call(body, name, outs, specs, out_specs, scratches, cost, operands, aliases={}):
     return pl.pallas_call(
         body,
         out_shape=tuple(jax.ShapeDtypeStruct(shape, jnp.float32) for shape in outs),
@@ -419,6 +426,7 @@
         scratch_shapes=scratches,
         compiler_params=pltpu.CompilerParams(vmem_limit_bytes=TALL_LIMIT),
         cost_estimate=pl.CostEstimate(flops=0, bytes_accessed=cost * COST_BYTES, transcendentals=0),
+        input_output_aliases=aliases,
         name=name,
     )(*operands)
 
@@ -462,7 +470,6 @@
     group = (GROUP * blocks, members, LANES)
     flat = (members * rows, columns)
     dma = pltpu.SemaphoreType.DMA
-    staged = pltpu.VMEM((blocks, members * rows, LANES), jnp.float32)
     inner = kernel_call(
         functools.partial(interior_kernel, blocks), "interior",
         [group] * 5, [ANYWHERE] * 5 + [IN_VMEM], (ANYWHERE,) * 5,
@@ -481,7 +488,7 @@
     obs_row, obs_col = obs_index // columns, obs_index % columns
     width = FOLD * LANES
     obs_block = obs_col // width * FOLD + obs_col % FOLD
-    cell_of = (STEPS * ALL_ROWS + HALO + obs_row) * blocks + obs_block
+    cell_of = (HALO + obs_row) * blocks + obs_block
     lane_of = obs_col % width // FOLD
     shift_of = (jnp.arange(obs_index.shape[0], dtype=jnp.int32) - lane_of) % LANES
     low4, high4, predicted = kernel_call(
@@ -491,16 +498,23 @@
         scratch(columns, dma((31,))), 15,
         [low1, low0, high0, high1, *first, own_coef, pair, other, params, place_of, cell_of, shift_of],
     )
-    (field,) = kernel_call(
-        functools.partial(field_kernel, blocks), "field",
-        [flat], [ANYWHERE] * 4, (ANYWHERE,),
-        [
-            pltpu.VMEM((rows * blocks, members, LANES), jnp.float32),
-            pltpu.VMEM((members * rows * blocks // FOLD, FOLD * LANES), jnp.float32),
-            staged, dma((4,)), dma((blocks,)),
-        ],
-        4, [low4, first[6], first[7], high4],
-    )
+    field, first_part, parts = None, 0, blocks // FOLD
+    for i in range(FIELD_CALLS):
+        count = parts * (i + 1) // FIELD_CALLS - first_part
+        width = count * FOLD
+        previous = [] if field is None else [field]
+        (field,) = kernel_call(
+            functools.partial(field_kernel, blocks, first_part, count), "field_%d" % i,
+            [flat], [ANYWHERE] * (4 + len(previous)), (ANYWHERE,),
+            [
+                pltpu.VMEM((rows * width, members, LANES), jnp.float32),
+                pltpu.VMEM((members * rows * count, FOLD * LANES), jnp.float32),
+                pltpu.VMEM((width, members * rows, LANES), jnp.float32),
+                dma((rows,)), dma((width,)),
+            ],
+            4, [low4, first[6], first[7], high4, *previous], {4: 0} if previous else {},
+        )
+        first_part += count
     return field.reshape(shape), predicted, inner[0]
 
 

time: 112 us -> 115 us (1.027)
  starting transfers between devices: 31.8 us -> 33.2 us
    ppermute x3, waiting for transfers between devices: 0.47 us -> 2.78 us  [halos(): lax.ppermute(upper, 'slab', forward)]
    ppermute x3, starting transfers between devices: 8.8 us -> 10.2 us  [local(): products = products + lax.ppermute(products, 'slab', pairs)]
    ppermute x2, waiting for transfers between devices: 3.74 us -> 2.53 us  [over_ens(): lax.ppermute(pair, 'ens', [(i, i ^ 2) for i in range(ens_count)])]
    pallas_call x6 -> x8, Pallas kernels: 58.1 us -> 58 us  [kernel_call(): pl.pallas_call(body, out_shape=tuple((jax.ShapeDtypeStruct(shape, jnp.flo...]
  transfers between devices with their start and end apart: 13 -> 13, of which waited for: 5 -> 6; matrix products, arithmetic and copies ran while one was open for 3% -> 3% of each run, Pallas kernels for 49% -> 48%
where the time goes in v11:
time: 115 us; the launch traced here: 114 us
  Pallas kernels  60.7 us (53%)
  starting transfers between devices  33.2 us (29%)
  waiting for transfers between devices  8.17 us (7%)
  blocking collectives  6 us (5%)
  other arithmetic  2.7 us (2%)
  local copies, waits for them, and re-layouts  1.89 us (2%)
    pallas_call x8, Pallas kernels, kernel_call(): pl.pallas_call(body, out_shape=tuple((jax.ShapeDtypeStruct(shape, jnp.flo...  58 us
    ppermute x3, starting transfers between devices, halos(): lax.ppermute(upper, 'slab', forward)  15.4 us
    ppermute x3, starting transfers between devices, local(): products = products + lax.ppermute(products, 'slab', pairs)  10.2 us
    all_gather x1, blocking collectives, local(): everyone = lax.all_gather(predicted, 'ens', axis=0, tiled=True)  6 us
    ppermute x3, starting transfers between devices, halos(): lax.ppermute(lower, 'slab', backward)  3.86 us
    ppermute x2, starting transfers between devices, over_ens(): lax.ppermute(pair, 'ens', [(i, i ^ 2) for i in range(ens_count)])  3.12 us
    ppermute x3, waiting for transfers between devices, halos(): lax.ppermute(upper, 'slab', forward)  2.78 us
    ppermute x2, waiting for transfers between devices, over_ens(): lax.ppermute(pair, 'ens', [(i, i ^ 2) for i in range(ens_count)])  2.53 us
  transfers between devices with their start and end apart: 13, of which 6 were waited for; matrix products, arithmetic and copies ran while one was open for 3% of the time, Pallas kernels for 48%

profile of v11, /device:TPU:0, one launch (start us, length us, event | category | flops | bytes accessed | tf_op | source)
XLA Modules:
  0.0 114.1 jit_solution(11498225848602776825)
XLA Ops:
  0.6 4.3 %outer_rows.1 = (f32[128,8,128]{2,1,0:T(8,128)}, f32[128,8,128]{2,1,0:T(8,128)}, f32[32,8,128]{2,1,0:T(8,128)}, f32[32,8,128]{2,1,0:T(8,128)}) custom-call(f32[128,4096]{1,0:T(8,128)} %bitcast.29, f32[4,16,4096]{2,1,0:T(8,128)} %own_coef.3, s32[1]{0:T(128)} %bitcast.1.place_of.refs_13_.refs_16_), custom_call_target="tpu_custom_call" | custom-call | bytes 600000 | tf_op jit(solution)/shard_map/outer_rows/pallas_call | solution.py:421
  5.0 1.3 %collective-permute-start.5 = (f32[32,8,128]{2,1,0:T(8,128)}, f32[32,8,128]{2,1,0:T(8,128)S(1)}, u32[]{:S(2)}, u32[]{:S(2)}) collective-permute-start(f32[32,8,128]{2,1,0:T(8,128)} %get-tuple-element.47), channel_id=1, source_target_pairs={{1,0},{2,1},{3,2},{4,3},{5,4},{6,5},{7,6},{9,8},{10,9},{11,10},{12... | collective-permute-start | bytes 393224 | tf_op jit(solution)/shard_map/ppermute | solution.py:582
  6.3 5.5 %collective-permute-start.4 = (f32[32,8,128]{2,1,0:T(8,128)}, f32[32,8,128]{2,1,0:T(8,128)S(1)}, u32[]{:S(2)}, u32[]{:S(2)}) collective-permute-start(f32[32,8,128]{2,1,0:T(8,128)} %get-tuple-element.46), channel_id=1, source_target_pairs={{0,1},{1,2},{2,3},{3,4},{4,5},{5,6},{6,7},{8,9},{9,10},{10,11},{11... | collective-permute-start | bytes 393224 | tf_op jit(solution)/shard_map/ppermute | solution.py:582
  11.8 4.8 %collective-permute-start = (f32[128,8,128]{2,1,0:T(8,128)}, f32[128,8,128]{2,1,0:T(8,128)S(1)}, u32[]{:S(2)}, u32[]{:S(2)}) collective-permute-start(f32[128,8,128]{2,1,0:T(8,128)} %get-tuple-element.31.outer.own3.refs_2_), channel_id=1, source_target_pairs={{0,1},{1,2},{2,3},{3,4},{4,5},{5,6},{6,7},{8,9},{9,10},{10,11},{11... | collective-permute-start | bytes 1572872 | tf_op jit(solution)/shard_map/ppermute | solution.py:582
  16.6 1.3 %collective-permute-start.1 = (f32[128,8,128]{2,1,0:T(8,128)}, f32[128,8,128]{2,1,0:T(8,128)S(1)}, u32[]{:S(2)}, u32[]{:S(2)}) collective-permute-start(f32[128,8,128]{2,1,0:T(8,128)} %get-tuple-element.34.own0.refs_1_), channel_id=1, source_target_pairs={{1,0},{2,1},{3,2},{4,3},{5,4},{6,5},{7,6},{9,8},{10,9},{11,10},{12... | collective-permute-start | bytes 1572872 | tf_op jit(solution)/shard_map/ppermute | solution.py:582
  17.9 6.4 %inner_rows.1 = (f32[128,8,128]{2,1,0:T(8,128)}, f32[128,8,128]{2,1,0:T(8,128)}, f32[32,64,128]{2,1,0:T(8,128)}, f32[8,4096]{1,0:T(8,128)}) custom-call(f32[128,4096]{1,0:T(8,128)} %bitcast.30, f32[4,16,4096]{2,1,0:T(8,128)} %own_coef.3, f32[8,4096]{1,0:T(8,128)} %own.1, f32[128,8,128]{2,1,0:T(8,128)} %get-tuple-element.31.outer.own3.refs_2_), custom_call_target="tpu_custom_call" | custom-call | bytes 600000 | tf_op jit(solution)/shard_map/inner_rows/pallas_call | solution.py:421
  24.3 0.0 copy-start
  24.3 0.0 copy-start.10
  24.3 0.0 copy-start.11
  24.4 0.0 copy-start.9
  24.4 0.0 copy-start.8
  24.4 9.5 %interior.1 = (f32[128,8,128]{2,1,0:T(8,128)}, f32[128,8,128]{2,1,0:T(8,128)}, f32[128,8,128]{2,1,0:T(8,128)}, f32[128,8,128]{2,1,0:T(8,128)}, f32[128,8,128]{2,1,0:T(8,128)}) custom-call(f32[128,8,128]{2,1,0:T(8,128)} %get-tuple-element.34.own0.refs_1_, f32[128,8,128]{2,1,0:T(8,128)} %get-tuple-element.41.own1, f32[128,8,128]{2,1,0:T(8,128)} %get-tuple-element.38.own2, ...), custom_call_target="tpu_custom_call" | custom-call | bytes 1600000 | tf_op jit(solution)/shard_map/interior/pallas_call | solution.py:421
  33.9 0.0 copy-done
  33.9 0.1 collective-permute-start.11
  34.0 0.0 collective-permute-done.5
  34.0 0.0 collective-permute-done.4
  34.0 0.5 collective-permute-start.6
  34.6 0.0 copy-done.10
  34.6 0.6 add_select_fusion
  35.2 0.0 copy-done.11
  35.2 0.1 compare_convert_fusion.same
  35.3 0.4 collective-permute-done.6
  35.8 0.0 copy-start.4
  35.8 1.6 %collective-permute-start.7 = (f32[2,2,32,8,128]{4,3,2,1,0:T(8,128)S(1)}, f32[2,2,32,8,128]{4,3,2,1,0:T(8,128)S(1)}, u32[]{:S(2)}, u32[]{:S(2)}) collective-permute-start(f32[2,2,32,8,128]{4,3,2,1,0:T(8,128)S(1)} %pad_maximum_fusion.refs_10_.refs_13_), channel_id=1, source_target_pairs={{0,16},{8,24},{16,0},{24,8},{1,17},{9,25},{17,1},{25,9},{2,18},{10... | collective-permute-start | bytes 1572872 | tf_op jit(solution)/shard_map/ppermute | solution.py:579
  37.4 1.7 %collective-permute-done.refs_0_.refs_1_ = f32[128,8,128]{2,1,0:T(8,128)S(1)} collective-permute-done((f32[128,8,128]{2,1,0:T(8,128)}, f32[128,8,128]{2,1,0:T(8,128)S(1)}, u32[]{:S(2)}, u32[]{:S(2)}) %collective-permute-start) | collective-permute-done | bytes 524320 | tf_op jit(solution)/shard_map/ppermute | solution.py:582
  39.1 0.0 copy-start.5
  39.1 0.0 collective-permute-done.1.refs_3_.refs_2_
  39.1 0.0 copy-done.9
  39.1 5.1 %collective-permute-start.2 = (f32[128,8,128]{2,1,0:T(8,128)S(1)}, f32[128,8,128]{2,1,0:T(8,128)}, u32[]{:S(2)}, u32[]{:S(2)}) collective-permute-start(f32[128,8,128]{2,1,0:T(8,128)S(1)} %copy-done.9), channel_id=1, source_target_pairs={{0,1},{1,2},{2,3},{3,4},{4,5},{5,6},{6,7},{8,9},{9,10},{10,11},{11... | collective-permute-start | bytes 1572872 | tf_op jit(solution)/shard_map/ppermute | solution.py:582
  44.2 0.0 copy-done.8
  44.2 1.3 %collective-permute-start.3 = (f32[128,8,128]{2,1,0:T(8,128)S(1)}, f32[128,8,128]{2,1,0:T(8,128)}, u32[]{:S(2)}, u32[]{:S(2)}) collective-permute-start(f32[128,8,128]{2,1,0:T(8,128)S(1)} %copy-done.8), channel_id=1, source_target_pairs={{1,0},{2,1},{3,2},{4,3},{5,4},{6,5},{7,6},{9,8},{10,9},{11,10},{12... | collective-permute-start | bytes 1572872 | tf_op jit(solution)/shard_map/ppermute | solution.py:582
  45.5 0.0 collective-permute-done.11
  45.5 0.7 pad_maximum_fusion.3
  46.2 1.5 %collective-permute-start.12 = (f32[2,8,4096]{2,1,0:T(8,128)}, f32[2,8,4096]{2,1,0:T(8,128)}, u32[]{:S(2)}, u32[]{:S(2)}) collective-permute-start(f32[2,8,4096]{2,1,0:T(8,128)} %pad_maximum_fusion.3), channel_id=1, source_target_pairs={{0,16},{8,24},{16,0},{24,8},{1,17},{9,25},{17,1},{25,9},{2,18},{10... | collective-permute-start | bytes 786440 | tf_op jit(solution)/shard_map/ppermute | solution.py:579
  47.7 0.2 convert_reduce_fusion
  47.9 0.1 copy.11.rank_col
  48.0 0.1 constant_dynamic-slice_fusion.own_same
  48.1 2.5 %collective-permute-done.7.refs_11_.refs_14_ = f32[2,2,32,8,128]{4,3,2,1,0:T(8,128)S(1)} collective-permute-done((f32[2,2,32,8,128]{4,3,2,1,0:T(8,128)S(1)}, f32[2,2,32,8,128]{4,3,2,1,0:T(8,128)S(1)}, u32[]{:S(2)}, u32[]{:S(2)}) %collective-permute-start.7) | collective-permute-done | bytes 524320 | tf_op jit(solution)/shard_map/ppermute | solution.py:579
  50.6 0.0 copy-done.4
  50.6 0.0 copy-done.5
  50.6 0.0 copy-done.6
  50.6 0.8 copy-done.7
  51.4 12.1 %edge_first.1 = (f32[128,8,128]{2,1,0:T(8,128)}, f32[128,8,128]{2,1,0:T(8,128)}, f32[128,8,128]{2,1,0:T(8,128)}, f32[128,8,128]{2,1,0:T(8,128)}, f32[128,8,128]{...) custom-call(f32[128,8,128]{2,1,0:T(8,128)} %copy-done.5, ...), custom_call_target="tpu_custom_call" | custom-call | bytes 2000000 | tf_op jit(solution)/shard_map/edge_first/pallas_call | solution.py:421
  63.5 1.1 collective-permute-done.2.refs_0_
  64.6 0.0 collective-permute-done.3.refs_3_
  64.6 16.6 %edge_last.1 = (f32[128,8,128]{2,1,0:T(8,128)}, f32[128,8,128]{2,1,0:T(8,128)}, f32[8,2048]{1,0:T(8,128)}) custom-call(f32[128,8,128]{2,1,0:T(8,128)} %collective-permute-done.2.refs_0_, f32[128,8,128]{2,1,0:T(8,128)} %copy-done.5, f32[128,8,128]{2,1,0:T(8,128)} %copy-done.6, f32[128,8,128]{2,1,0:T(8,128)} %collective-permute-done.3.refs_3_, ...), custom_call_target="tpu_custom_call" | custom-call | bytes 3000000 | tf_op jit(solution)/shard_map/edge_last/pallas_call | solution.py:421
  81.2 6.0 %all_gather.3.everyone = f32[32,2048]{1,0:T(8,128)S(1)} all-gather(f32[8,2048]{1,0:T(8,128)} %get-tuple-element.58.own), channel_id=1, replica_groups=mesh['ens'=4,'slab'=8] {'ens'}, dimensions={0}, use_global_device_ids=true | all-gather | bytes 327680 | tf_op jit(solution)/shard_map/all_gather | solution.py:612
  87.2 0.0 copy-done.2
  87.2 0.0 copy-done.3
  87.2 0.8 copy-done.1
  88.1 0.6 products.1
  88.7 2.6 %collective-permute-start.8 = (f32[32,40]{1,0:T(8,128)S(1)}, f32[32,40]{1,0:T(8,128)S(1)}, u32[]{:S(2)}, u32[]{:S(2)}) collective-permute-start(f32[32,40]{1,0:T(8,128)S(1)} %products.1), channel_id=1, source_target_pairs={{0,1},{1,0},{2,3},{3,2},{4,5},{5,4},{6,7},{7,6},{8,9},{9,8},{10,11... | collective-permute-start | bytes 15368 | tf_op jit(solution)/shard_map/ppermute | solution.py:623
  91.3 0.0 collective-permute-done.12
  91.3 1.0 pad_maximum_fusion.1
  92.3 0.7 collective-permute-done.8
  93.1 4.5 %collective-permute-start.9 = (f32[32,40]{1,0:T(8,128)S(1)}, f32[32,40]{1,0:T(8,128)S(1)}, u32[]{:S(2)}, u32[]{:S(2)}) collective-permute-start(f32[32,40]{1,0:T(8,128)S(1)} %add.66), channel_id=1, source_target_pairs={{0,2},{1,3},{2,0},{3,1},{4,6},{5,7},{6,4},{7,5},{8,10},{9,11},{10,... | collective-permute-start | bytes 15368 | tf_op jit(solution)/shard_map/ppermute | solution.py:623
  97.6 1.7 %collective-permute-done.9 = f32[32,40]{1,0:T(8,128)S(1)} collective-permute-done((f32[32,40]{1,0:T(8,128)S(1)}, f32[32,40]{1,0:T(8,128)S(1)}, u32[]{:S(2)}, u32[]{:S(2)}) %collective-permute-start.9) | collective-permute-done | bytes 5152 | tf_op jit(solution)/shard_map/ppermute | solution.py:623
  99.3 3.0 %collective-permute-start.10 = (f32[32,40]{1,0:T(8,128)S(1)}, f32[32,40]{1,0:T(8,128)S(1)}, u32[]{:S(2)}, u32[]{:S(2)}) collective-permute-start(f32[32,40]{1,0:T(8,128)S(1)} %add.67), channel_id=1, source_target_pairs={{0,4},{1,5},{2,6},{3,7},{4,0},{5,1},{6,2},{7,3},{8,12},{9,13},{10,... | collective-permute-start | bytes 15368 | tf_op jit(solution)/shard_map/ppermute | solution.py:623
  102.3 0.4 fusion.1.anomalies
  102.8 2.7 %field_0.1.refs_4_ = f32[128,4096]{1,0:T(8,128)} custom-call(f32[128,8,128]{2,1,0:T(8,128)} %get-tuple-element.56.refs_0_, f32[128,8,128]{2,1,0:T(8,128)} %get-tuple-element.54.refs_10_.refs_1_, f32[128,8,128]{2,1,0:T(8,128)} %get-tuple-element.55.refs_11_.refs_2_, f32[128,8,128]{2,1,0:T(8,128)} %get-tuple-element.57.refs_3_), custom_call_target="tpu_custom_call" | custom-call | bytes 800000 | tf_op jit(solution)/shard_map/field_0/pallas_call | solution.py:421
  105.5 3.2 %field_1.1.refs_4_ = f32[128,4096]{1,0:T(8,128)} custom-call(f32[128,8,128]{2,1,0:T(8,128)} %get-tuple-element.56.refs_0_, f32[128,8,128]{2,1,0:T(8,128)} %get-tuple-element.54.refs_10_.refs_1_, f32[128,8,128]{2,1,0:T(8,128)} %get-tuple-element.55.refs_11_.refs_2_, f32[128,8,128]{2,1,0:T(8,128)} %get-tuple-element.57.refs_3_, ...), custom_call_target="tpu_custom_call", output_to_operand_aliasing={{}: (4, {})} | custom-call | bytes 800000 | tf_op jit(solution)/shard_map/field_1/pallas_call | solution.py:421
  108.7 3.2 %field_2.1 = f32[128,4096]{1,0:T(8,128)} custom-call(f32[128,8,128]{2,1,0:T(8,128)} %get-tuple-element.56.refs_0_, f32[128,8,128]{2,1,0:T(8,128)} %get-tuple-element.54.refs_10_.refs_1_, f32[128,8,128]{2,1,0:T(8,128)} %get-tuple-element.55.refs_11_.refs_2_, f32[128,8,128]{2,1,0:T(8,128)} %get-tuple-element.57.refs_3_, ...), custom_call_target="tpu_custom_call", output_to_operand_aliasing={{}: (4, {})} | custom-call | bytes 800000 | tf_op jit(solution)/shard_map/field_2/pallas_call | solution.py:421
  111.9 0.0 collective-permute-done.10
  111.9 2.1 %update.1 = f32[8,4096]{1,0:T(8,128)} custom-call(f32[1,32,40]{2,1,0:T(8,128)S(1)} %add_bitcast_fusion.summands, f32[32,32]{1,0:T(8,128)S(1)} %compare_convert_fusion.same, f32[32,8]{1,0:T(8,128)S(1)} %constant_dynamic-slice_fusion.own_same, s32[1,32]{1,0:T(1,128)S(1)} %bitcast.27, s32[32,1]{1,0:T(8,128)S(1)} %copy.11.rank_col, ...), custom_call_target="tpu_custom_call" | custom-call | tf_op jit(solution)/shard_map/update/pallas_call | solution.py:625
  (11 shorter events, 0.1 us)
Async XLA Ops:
  5.0 29.0 %collective-permute-start.5 = (f32[32,8,128]{2,1,0:T(8,128)}, f32[32,8,128]{2,1,0:T(8,128)S(1)}, u32[]{:S(2)}, u32[]{:S(2)}) collective-permute-start(f32[32,8,128]{2,1,0:T(8,128)} %get-tuple-element.47), channel_id=1, source_target_pairs={{1,0},{2,1},{3,2},{4,3},{5,4},{6,5},{7,6},{9,8},{10,9},{11,10},{12... | collective-permute-start | bytes 393224 | tf_op jit(solution)/shard_map/ppermute | solution.py:582
  6.3 27.7 %collective-permute-start.4 = (f32[32,8,128]{2,1,0:T(8,128)}, f32[32,8,128]{2,1,0:T(8,128)S(1)}, u32[]{:S(2)}, u32[]{:S(2)}) collective-permute-start(f32[32,8,128]{2,1,0:T(8,128)} %get-tuple-element.46), channel_id=1, source_target_pairs={{0,1},{1,2},{2,3},{3,4},{4,5},{5,6},{6,7},{8,9},{9,10},{10,11},{11... | collective-permute-start | bytes 393224 | tf_op jit(solution)/shard_map/ppermute | solution.py:582
  11.8 27.3 %collective-permute-start = (f32[128,8,128]{2,1,0:T(8,128)}, f32[128,8,128]{2,1,0:T(8,128)S(1)}, u32[]{:S(2)}, u32[]{:S(2)}) collective-permute-start(f32[128,8,128]{2,1,0:T(8,128)} %get-tuple-element.31.outer.own3.refs_2_), channel_id=1, source_target_pairs={{0,1},{1,2},{2,3},{3,4},{4,5},{5,6},{6,7},{8,9},{9,10},{10,11},{11... | collective-permute-start | bytes 1572872 | tf_op jit(solution)/shard_map/ppermute | solution.py:582
  16.6 22.4 %collective-permute-start.1 = (f32[128,8,128]{2,1,0:T(8,128)}, f32[128,8,128]{2,1,0:T(8,128)S(1)}, u32[]{:S(2)}, u32[]{:S(2)}) collective-permute-start(f32[128,8,128]{2,1,0:T(8,128)} %get-tuple-element.34.own0.refs_1_), channel_id=1, source_target_pairs={{1,0},{2,1},{3,2},{4,3},{5,4},{6,5},{7,6},{9,8},{10,9},{11,10},{12... | collective-permute-start | bytes 1572872 | tf_op jit(solution)/shard_map/ppermute | solution.py:582
  24.3 9.6 %copy-start = (f32[8,4096]{1,0:T(8,128)S(1)}, f32[8,4096]{1,0:T(8,128)}, u32[]{:S(2)}) copy-start(f32[8,4096]{1,0:T(8,128)} %own.1) | copy-start | bytes 393220
  24.3 10.3 %copy-start.10 = (s32[2048]{0:T(1024)S(1)}, s32[2048]{0:T(1024)}, u32[]{:S(2)}) copy-start(s32[2048]{0:T(1024)} %param.10) | copy-start | bytes 24580
  24.3 10.9 %copy-start.11 = (s32[32]{0:T(128)S(1)}, s32[32]{0:T(128)}, u32[]{:S(2)}) copy-start(s32[32]{0:T(128)} %param.13) | copy-start | bytes 388
  24.4 14.7 %copy-start.9 = (f32[128,8,128]{2,1,0:T(8,128)S(1)}, f32[128,8,128]{2,1,0:T(8,128)}, u32[]{:S(2)}) copy-start(f32[128,8,128]{2,1,0:T(8,128)} %get-tuple-element.38.own2) | copy-start | bytes 1572868
  24.4 19.8 %copy-start.8 = (f32[128,8,128]{2,1,0:T(8,128)S(1)}, f32[128,8,128]{2,1,0:T(8,128)}, u32[]{:S(2)}) copy-start(f32[128,8,128]{2,1,0:T(8,128)} %get-tuple-element.41.own1) | copy-start | bytes 1572868
  33.9 11.6 %collective-permute-start.11 = (f32[8,4096]{1,0:T(8,128)S(1)}, f32[8,4096]{1,0:T(8,128)S(1)}, u32[]{:S(2)}, u32[]{:S(2)}) collective-permute-start(f32[8,4096]{1,0:T(8,128)S(1)} %copy-done), channel_id=1, source_target_pairs={{0,8},{8,0},{16,24},{24,16},{1,9},{9,1},{17,25},{25,17},{2,10},{10... | collective-permute-start | bytes 393224 | tf_op jit(solution)/shard_map/ppermute | solution.py:578
  34.0 1.7 %collective-permute-start.6 = (f32[2,32,8,128]{3,2,1,0:T(8,128)S(1)}, f32[2,32,8,128]{3,2,1,0:T(8,128)S(1)}, u32[]{:S(2)}, u32[]{:S(2)}) collective-permute-start(f32[2,32,8,128]{3,2,1,0:T(8,128)S(1)} %get-tuple-element.65), channel_id=1, source_target_pairs={{0,8},{8,0},{16,24},{24,16},{1,9},{9,1},{17,25},{25,17},{2,10},{10... | collective-permute-start | bytes 786440 | tf_op jit(solution)/shard_map/ppermute | solution.py:578
  35.8 14.8 %copy-start.4 = (f32[2,2,32,8,128]{4,3,2,1,0:T(8,128)}, f32[2,2,32,8,128]{4,3,2,1,0:T(8,128)S(1)}, u32[]{:S(2)}) copy-start(f32[2,2,32,8,128]{4,3,2,1,0:T(8,128)S(1)} %pad_maximum_fusion.refs_10_.refs_13_) | copy-start | bytes 1572868
  35.8 14.8 %collective-permute-start.7 = (f32[2,2,32,8,128]{4,3,2,1,0:T(8,128)S(1)}, f32[2,2,32,8,128]{4,3,2,1,0:T(8,128)S(1)}, u32[]{:S(2)}, u32[]{:S(2)}) collective-permute-start(f32[2,2,32,8,128]{4,3,2,1,0:T(8,128)S(1)} %pad_maximum_fusion.refs_10_.refs_13_), channel_id=1, source_target_pairs={{0,16},{8,24},{16,0},{24,8},{1,17},{9,25},{17,1},{25,9},{2,18},{10... | collective-permute-start | bytes 1572872 | tf_op jit(solution)/shard_map/ppermute | solution.py:579
  39.1 11.6 %copy-start.5 = (f32[128,8,128]{2,1,0:T(8,128)}, f32[128,8,128]{2,1,0:T(8,128)S(1)}, u32[]{:S(2)}) copy-start(f32[128,8,128]{2,1,0:T(8,128)S(1)} %collective-permute-done.refs_0_.refs_1_) | copy-start | bytes 1572868
  39.1 11.6 %copy-start.6 = (f32[128,8,128]{2,1,0:T(8,128)}, f32[128,8,128]{2,1,0:T(8,128)S(1)}, u32[]{:S(2)}) copy-start(f32[128,8,128]{2,1,0:T(8,128)S(1)} %collective-permute-done.1.refs_3_.refs_2_) | copy-start | bytes 1572868
  39.1 25.5 %collective-permute-start.2 = (f32[128,8,128]{2,1,0:T(8,128)S(1)}, f32[128,8,128]{2,1,0:T(8,128)}, u32[]{:S(2)}, u32[]{:S(2)}) collective-permute-start(f32[128,8,128]{2,1,0:T(8,128)S(1)} %copy-done.9), channel_id=1, source_target_pairs={{0,1},{1,2},{2,3},{3,4},{4,5},{5,6},{6,7},{8,9},{9,10},{10,11},{11... | collective-permute-start | bytes 1572872 | tf_op jit(solution)/shard_map/ppermute | solution.py:582
  44.2 20.4 %collective-permute-start.3 = (f32[128,8,128]{2,1,0:T(8,128)S(1)}, f32[128,8,128]{2,1,0:T(8,128)}, u32[]{:S(2)}, u32[]{:S(2)}) collective-permute-start(f32[128,8,128]{2,1,0:T(8,128)S(1)} %copy-done.8), channel_id=1, source_target_pairs={{1,0},{2,1},{3,2},{4,3},{5,4},{6,5},{7,6},{9,8},{10,9},{11,10},{12... | collective-permute-start | bytes 1572872 | tf_op jit(solution)/shard_map/ppermute | solution.py:582
  46.2 45.1 %collective-permute-start.12 = (f32[2,8,4096]{2,1,0:T(8,128)}, f32[2,8,4096]{2,1,0:T(8,128)}, u32[]{:S(2)}, u32[]{:S(2)}) collective-permute-start(f32[2,8,4096]{2,1,0:T(8,128)} %pad_maximum_fusion.3), channel_id=1, source_target_pairs={{0,16},{8,24},{16,0},{24,8},{1,17},{9,25},{17,1},{25,9},{2,18},{10... | collective-permute-start | bytes 786440 | tf_op jit(solution)/shard_map/ppermute | solution.py:579
  50.6 0.8 copy-start.7
  64.6 22.6 %copy-start.2 = (f32[8,2048]{1,0:T(8,128)S(1)}, f32[8,2048]{1,0:T(8,128)}, u32[]{:S(2)}) copy-start(f32[8,2048]{1,0:T(8,128)} %values.1) | copy-start | bytes 196612
  64.6 22.6 %copy-start.3 = (f32[2048]{0:T(1024)S(1)}, f32[2048]{0:T(1024)}, u32[]{:S(2)}) copy-start(f32[2048]{0:T(1024)} %param.12) | copy-start | bytes 24580
  87.2 0.8 copy-start.1
  88.7 4.4 %collective-permute-start.8 = (f32[32,40]{1,0:T(8,128)S(1)}, f32[32,40]{1,0:T(8,128)S(1)}, u32[]{:S(2)}, u32[]{:S(2)}) collective-permute-start(f32[32,40]{1,0:T(8,128)S(1)} %products.1), channel_id=1, source_target_pairs={{0,1},{1,0},{2,3},{3,2},{4,5},{5,4},{6,7},{7,6},{8,9},{9,8},{10,11... | collective-permute-start | bytes 15368 | tf_op jit(solution)/shard_map/ppermute | solution.py:623
  93.1 6.2 %collective-permute-start.9 = (f32[32,40]{1,0:T(8,128)S(1)}, f32[32,40]{1,0:T(8,128)S(1)}, u32[]{:S(2)}, u32[]{:S(2)}) collective-permute-start(f32[32,40]{1,0:T(8,128)S(1)} %add.66), channel_id=1, source_target_pairs={{0,2},{1,3},{2,0},{3,1},{4,6},{5,7},{6,4},{7,5},{8,10},{9,11},{10,... | collective-permute-start | bytes 15368 | tf_op jit(solution)/shard_map/ppermute | solution.py:623
  99.3 12.6 %collective-permute-start.10 = (f32[32,40]{1,0:T(8,128)S(1)}, f32[32,40]{1,0:T(8,128)S(1)}, u32[]{:S(2)}, u32[]{:S(2)}) collective-permute-start(f32[32,40]{1,0:T(8,128)S(1)} %add.67), channel_id=1, source_target_pairs={{0,4},{1,5},{2,6},{3,7},{4,0},{5,1},{6,2},{7,3},{8,12},{9,13},{10,... | collective-permute-start | bytes 15368 | tf_op jit(solution)/shard_map/ppermute | solution.py:623

commit v12 on v11

--- a/solution.py
+++ b/solution.py
@@ -17,8 +17,8 @@
 GROUP = 4
 FOLD = 4
 PICKED = 128
-TILES = 2
-FIELD_CALLS = 3
+TILES = 4
+FIELD_CALLS = 2
 ALL_ROWS = ROWS + 2 * HALO
 VMEM_LIMIT = 16 * 1024 * 1024
 TALL_LIMIT = 58 * 1024 * 1024
@@ -464,7 +464,7 @@
     return (down, low, high, up), (up_coef, down_coef), by_block, dealt_params
 
 
-def transport(shape, own, low0, high0, own_coef, pair, other, params, place_of, obs_index, halos):
+def transport(shape, own, low0, high0, own_coef, pair, other, params, place_of, obs_index, halos, share_params):
     members, rows, columns = shape
     blocks = columns // LANES
     group = (GROUP * blocks, members, LANES)
@@ -475,9 +475,7 @@
         [group] * 5, [ANYWHERE] * 5 + [IN_VMEM], (ANYWHERE,) * 5,
         scratch(columns, dma((16,))), 8, [*own, own_coef, params],
     )
-    upper, lower, low0, high0, *_ = lax.optimization_barrier(
-        (own[2], own[1], low0, high0, inner[0])
-    )
+    upper, lower, *_ = lax.optimization_barrier((own[2], own[1], inner[0], pair))
     low1, high1 = halos(upper, lower)
     first = kernel_call(
         functools.partial(middle_kernel, blocks), "edge_first",
@@ -485,6 +483,7 @@
         scratch(columns, dma((29,))), 10,
         [low0, own[0], own[3], high0, *inner, own_coef, pair, other, params, place_of],
     )
+    high1, *all_params = lax.optimization_barrier((high1, *share_params(inner[0])))
     obs_row, obs_col = obs_index // columns, obs_index % columns
     width = FOLD * LANES
     obs_block = obs_col // width * FOLD + obs_col % FOLD
@@ -498,13 +497,15 @@
         scratch(columns, dma((31,))), 15,
         [low1, low0, high0, high1, *first, own_coef, pair, other, params, place_of, cell_of, shift_of],
     )
-    field, first_part, parts = None, 0, blocks // FOLD
-    for i in range(FIELD_CALLS):
-        count = parts * (i + 1) // FIELD_CALLS - first_part
+
+    def write_field(index, field):
+        parts = blocks // FOLD
+        first_part = parts * index // FIELD_CALLS
+        count = parts * (index + 1) // FIELD_CALLS - first_part
         width = count * FOLD
         previous = [] if field is None else [field]
-        (field,) = kernel_call(
-            functools.partial(field_kernel, blocks, first_part, count), "field_%d" % i,
+        return kernel_call(
+            functools.partial(field_kernel, blocks, first_part, count), "field_%d" % index,
             [flat], [ANYWHERE] * (4 + len(previous)), (ANYWHERE,),
             [
                 pltpu.VMEM((rows * width, members, LANES), jnp.float32),
@@ -513,15 +514,15 @@
                 dma((rows,)), dma((width,)),
             ],
             4, [low4, first[6], first[7], high4, *previous], {4: 0} if previous else {},
-        )
-        first_part += count
-    return field.reshape(shape), predicted, inner[0]
-
-
-def products_kernel(total_obs, per_group, spread, everyone, own, values, variance, same, out):
+        )[0]
+
+    return write_field, predicted, all_params
+
+
+def products_kernel(total_obs, per_group, spread, pair, other, values, variance, same, out):
     weight = 1.0 / (variance[...] * total_obs)
-    innovation = (values[...] - own[...]) * weight
-    predicted = everyone[...]
+    predicted = jnp.concatenate([pair[0], pair[1], other[0], other[1]], axis=0)
+    innovation = (values[...] - pair[0]) * weight
     anomalies = (predicted - hdot(same[...], predicted) / per_group) * spread
     right = jnp.concatenate([anomalies * weight, innovation], axis=0)
     out[...] = lax.dot_general(
@@ -574,9 +575,15 @@
     forward = [(i, i + 1) for i in range(slab_count - 1)]
     backward = [(target, source) for source, target in forward]
 
+    def next_core(value):
+        return lax.ppermute(value, "ens", [(i, i ^ 1) for i in range(ens_count)])
+
+    def next_chip(value):
+        return lax.ppermute(value, "ens", [(i, i ^ 2) for i in range(ens_count)])
+
     def over_ens(mine):
-        pair = jnp.stack([mine, lax.ppermute(mine, "ens", [(i, i ^ 1) for i in range(ens_count)])])
-        return pair, lax.ppermute(pair, "ens", [(i, i ^ 2) for i in range(ens_count)])
+        pair = jnp.stack([mine, next_core(mine)])
+        return pair, next_chip(pair)
 
     def halos(upper, lower):
         return lax.ppermute(upper, "slab", forward), lax.ppermute(lower, "slab", backward)
@@ -593,30 +600,39 @@
     members = member_group.shape[0]
     per_group = members // GROUPS
     spread = 1.0 / math.sqrt(per_group - 1)
-    same_bool = member_group[:, None] == member_group[None, :]
+    blocks_of = member_group.reshape(ens_count, local_members)
+    group_of = jnp.concatenate(
+        [lax.dynamic_index_in_dim(blocks_of, ens_pos ^ i, 0, False) for i in range(ens_count)]
+    )
+    same_bool = group_of[:, None] == group_of[None, :]
     same = same_bool.astype(jnp.float32)
     earlier = jnp.arange(members)[None, :] < jnp.arange(members)[:, None]
     rank = jnp.sum((same_bool & earlier).astype(jnp.int32), axis=1)
-    own_same = lax.dynamic_slice_in_dim(same, ens_pos * local_members, local_members, 1)
-    field, predicted, first_done = transport(
+
+    def share_params(after):
+        later, _ = lax.optimization_barrier((parameters, after))
+        return over_ens(later)
+
+    write_field, predicted, all_params = transport(
         tracer.shape, own, low0, high0,
-        own_coef, pair, other, dealt_params, place_of, obs_index, halos,
-    )
-
-    later, _ = lax.optimization_barrier((parameters, first_done))
-    shared = jnp.concatenate(over_ens(later), axis=0)
-    all_params = jnp.concatenate(
-        [lax.dynamic_index_in_dim(shared, ens_pos ^ i, 0, False) for i in range(ens_count)], axis=0
-    )
+        own_coef, pair, other, dealt_params, place_of, obs_index, halos, share_params,
+    )
+    all_params = jnp.concatenate(all_params, axis=0).reshape(members, columns)
     param_anomalies = (all_params - hdot(same, all_params) / per_group) * spread
-    everyone = lax.all_gather(predicted, "ens", axis=0, tiled=True)
+
+    near = jnp.stack([predicted, next_core(predicted)])
+    field = write_field(0, None)
+    near, field = lax.optimization_barrier((near, field))
+    far = next_chip(near)
+    field = write_field(1, field)
+    far, field = lax.optimization_barrier((far, field))
     total_obs = obs_variance.shape[0] * slab_count
     products = pl.pallas_call(
         functools.partial(products_kernel, float(total_obs), per_group, spread),
         out_shape=jax.ShapeDtypeStruct((members, members + local_members), jnp.float32),
         compiler_params=pltpu.CompilerParams(vmem_limit_bytes=VMEM_LIMIT),
         name="products",
-    )(everyone, predicted, obs_values, obs_variance[None, :], same)
+    )(near, far, obs_values, obs_variance[None, :], same)
     distance = 1
     while distance < slab_count:
         pairs = [(i, i ^ distance) for i in range(slab_count)]
@@ -627,8 +643,11 @@
         out_shape=jax.ShapeDtypeStruct(parameters.shape, jnp.float32),
         compiler_params=pltpu.CompilerParams(vmem_limit_bytes=VMEM_LIMIT),
         name="update",
-    )(products[None], same, own_same, rank[None, :], rank[:, None], param_anomalies, parameters)
-    return (field, updated)
+    )(
+        products[None], same, same[:, :local_members], rank[None, :], rank[:, None],
+        param_anomalies, parameters,
+    )
+    return (field.reshape(tracer.shape), updated)
 
 
 def solution(mesh):

time: 115 us -> 135 us (1.17)
  waiting for transfers between devices: 8.17 us -> 29.8 us
  starting transfers between devices: 33.2 us -> 42.4 us
  blocking collectives: 6 us -> 0 us
  Pallas kernels: 60.7 us -> 58.1 us
  other arithmetic: 2.7 us -> 1.09 us
    ppermute x3, waiting for transfers between devices: 2.78 us -> 21.8 us  [halos(): lax.ppermute(upper, 'slab', forward)]
    ppermute x3, starting transfers between devices: 10.2 us -> 17.6 us  [local(): products = products + lax.ppermute(products, 'slab', pairs)]
    all_gather x1 -> x0, blocking collectives: 6 us -> none  [local(): everyone = lax.all_gather(predicted, 'ens', axis=0, tiled=True)]
    pallas_call x8 -> x7, Pallas kernels: 58 us -> 55.3 us  [kernel_call(): pl.pallas_call(body, out_shape=tuple((jax.ShapeDtypeStruct(shape, jnp.flo...]
    ppermute x3, waiting for transfers between devices: 2.4 us -> 4.43 us  [local(): products = products + lax.ppermute(products, 'slab', pairs)]
    ppermute x3, waiting for transfers between devices: 0.01 us -> 1.54 us  [halos(): lax.ppermute(lower, 'slab', backward)]
    ppermute x4 -> x6, waiting for transfers between devices: 2.98 us -> 1.98 us  [the longest x3 1.24 us: next_chip(): return lax.ppermute(value, 'ens', [(i, i ^ 2) for i in range(ens_count)])]
    ppermute x4 -> x6, starting transfers between devices: 3.73 us -> 4.25 us  [the longest x3 3.56 us: next_chip(): return lax.ppermute(value, 'ens', [(i, i ^ 2) for i in range(ens_count)])]
  transfers between devices with their start and end apart: 13 -> 15, of which waited for: 6 -> 7; matrix products, arithmetic and copies ran while one was open for 3% -> 1% of each run, Pallas kernels for 48% -> 26%
where the time goes in v12:
time: 135 us
  Pallas kernels  58.1 us (43%)
  starting transfers between devices  42.4 us (31%)
  waiting for transfers between devices  29.8 us (22%)
  local copies, waits for them, and re-layouts  2.06 us (2%)
    pallas_call x7, Pallas kernels, kernel_call(): pl.pallas_call(body, out_shape=tuple((jax.ShapeDtypeStruct(shape, jnp.flo...  55.3 us
    ppermute x3, waiting for transfers between devices, halos(): lax.ppermute(upper, 'slab', forward)  21.8 us
    ppermute x3, starting transfers between devices, local(): products = products + lax.ppermute(products, 'slab', pairs)  17.6 us
    ppermute x3, starting transfers between devices, halos(): lax.ppermute(upper, 'slab', forward)  16.6 us
    ppermute x3, waiting for transfers between devices, local(): products = products + lax.ppermute(products, 'slab', pairs)  4.43 us
    ppermute x3, starting transfers between devices, halos(): lax.ppermute(lower, 'slab', backward)  3.88 us
    ppermute x3, starting transfers between devices, next_chip(): return lax.ppermute(value, 'ens', [(i, i ^ 2) for i in range(ens_count)])  3.56 us
  transfers between devices with their start and end apart: 15, of which 7 were waited for; matrix products, arithmetic and copies ran while one was open for 1% of the time, Pallas kernels for 26%

profile of v12, /device:TPU:0, one launch (start us, length us, event | category | flops | bytes accessed | tf_op | source)
XLA Modules:
  0.0 134.8 jit_solution(6196392997591310676)
XLA Ops:
  0.6 4.3 %outer_rows.1 = (f32[128,8,128]{2,1,0:T(8,128)}, f32[128,8,128]{2,1,0:T(8,128)}, f32[32,8,128]{2,1,0:T(8,128)}, f32[32,8,128]{2,1,0:T(8,128)}) custom-call(f32[128,4096]{1,0:T(8,128)} %bitcast.38, f32[4,16,4096]{2,1,0:T(8,128)} %own_coef.3, s32[1]{0:T(128)} %bitcast.1.place_of.refs_13_.refs_16_), custom_call_target="tpu_custom_call" | custom-call | bytes 600000 | tf_op jit(solution)/shard_map/outer_rows/pallas_call | solution.py:421
  5.0 1.3 collective-permute-start.1
  6.3 5.5 %collective-permute-start = (f32[32,8,128]{2,1,0:T(8,128)}, f32[32,8,128]{2,1,0:T(8,128)S(1)}, u32[]{:S(2)}, u32[]{:S(2)}) collective-permute-start(f32[32,8,128]{2,1,0:T(8,128)} %get-tuple-element.43), channel_id=1, source_target_pairs={{0,1},{1,2},{2,3},{3,4},{4,5},{5,6},{6,7},{8,9},{9,10},{10,11},{11... | collective-permute-start | bytes 393224 | tf_op jit(solution)/shard_map/ppermute | solution.py:589
  11.8 6.4 %inner_rows.1 = (f32[128,8,128]{2,1,0:T(8,128)}, f32[128,8,128]{2,1,0:T(8,128)}, f32[32,64,128]{2,1,0:T(8,128)}, f32[8,4096]{1,0:T(8,128)}) custom-call(f32[128,4096]{1,0:T(8,128)} %bitcast.39, f32[4,16,4096]{2,1,0:T(8,128)} %own_coef.3, f32[8,4096]{1,0:T(8,128)} %own.1, f32[128,8,128]{2,1,0:T(8,128)} %get-tuple-element.36.outer.own3.refs_2_), custom_call_target="tpu_custom_call" | custom-call | bytes 600000 | tf_op jit(solution)/shard_map/inner_rows/pallas_call | solution.py:421
  18.2 0.0 copy-start
  18.2 0.0 copy-start.4
  18.2 0.0 copy-start.5
  18.2 0.0 copy-start.13
  18.2 0.0 copy-start.12
  18.2 9.3 %interior.1 = (f32[128,8,128]{2,1,0:T(8,128)}, f32[128,8,128]{2,1,0:T(8,128)}, f32[128,8,128]{2,1,0:T(8,128)}, f32[128,8,128]{2,1,0:T(8,128)}, f32[128,8,128]{2,1,0:T(8,128)}) custom-call(f32[128,8,128]{2,1,0:T(8,128)} %get-tuple-element.39.own0.refs_1_, f32[128,8,128]{2,1,0:T(8,128)} %get-tuple-element.46.own1, f32[128,8,128]{2,1,0:T(8,128)} %get-tuple-element.45.own2, ...), custom_call_target="tpu_custom_call" | custom-call | bytes 1600000 | tf_op jit(solution)/shard_map/interior/pallas_call | solution.py:421
  27.5 0.0 copy-done
  27.5 0.1 collective-permute-start.7
  27.6 0.0 collective-permute-done.1
  27.6 0.0 collective-permute-done
  27.7 0.5 collective-permute-start.2
  28.2 0.7 collective-permute-done.7
  29.0 2.1 %collective-permute-start.8 = (f32[2,8,4096]{2,1,0:T(8,128)S(1)}, f32[2,8,4096]{2,1,0:T(8,128)S(1)}, u32[]{:S(2)}, u32[]{:S(2)}) collective-permute-start(f32[2,8,4096]{2,1,0:T(8,128)S(1)} %pad_maximum_fusion.2), channel_id=1, source_target_pairs={{0,16},{8,24},{16,0},{24,8},{1,17},{9,25},{17,1},{25,9},{2,18},{10... | collective-permute-start | bytes 786440 | tf_op jit(solution)/shard_map/ppermute | solution.py:582
  31.1 0.0 collective-permute-done.2
  31.1 0.0 copy-start.3
  31.1 1.3 collective-permute-start.6
  32.4 0.0 copy-done.4
  32.4 4.9 %collective-permute-start.4 = (f32[128,8,128]{2,1,0:T(8,128)S(1)}, f32[128,8,128]{2,1,0:T(8,128)S(1)}, u32[]{:S(2)}, u32[]{:S(2)}) collective-permute-start(f32[128,8,128]{2,1,0:T(8,128)S(1)} %copy-done.4), channel_id=1, source_target_pairs={{0,1},{1,2},{2,3},{3,4},{4,5},{5,6},{6,7},{8,9},{9,10},{10,11},{11... | collective-permute-start | bytes 1572872 | tf_op jit(solution)/shard_map/ppermute | solution.py:589
  37.4 0.0 copy-done.5
  37.4 1.3 collective-permute-start.5
  38.7 0.6 collective-permute-start.9
  39.3 0.0 collective-permute-done.8
  39.3 0.7 copy-done.9
  40.0 6.2 %collective-permute-start.3 = (f32[128,8,128]{2,1,0:T(8,128)}, f32[128,8,128]{2,1,0:T(8,128)}, u32[]{:S(2)}, u32[]{:S(2)}) collective-permute-start(f32[128,8,128]{2,1,0:T(8,128)} %get-tuple-element.45.own2), channel_id=1, source_target_pairs={{0,1},{1,2},{2,3},{3,4},{4,5},{5,6},{6,7},{8,9},{9,10},{10,11},{11... | collective-permute-start | bytes 1572872 | tf_op jit(solution)/shard_map/ppermute | solution.py:589
  46.2 0.0 copy-done.13
  46.2 0.1 reshape.24
  46.3 0.0 copy-done.12
  46.3 0.6 add_select_fusion
  46.9 1.5 %collective-permute-done.6.refs_3_ = f32[128,8,128]{2,1,0:T(8,128)} collective-permute-done((f32[128,8,128]{2,1,0:T(8,128)}, f32[128,8,128]{2,1,0:T(8,128)}, u32[]{:S(2)}, u32[]{:S(2)}) %collective-permute-start.6) | collective-permute-done | bytes 524320 | tf_op jit(solution)/shard_map/ppermute | solution.py:589
  48.5 21.8 %collective-permute-done.4.refs_0_.refs_1_ = f32[128,8,128]{2,1,0:T(8,128)S(1)} collective-permute-done((f32[128,8,128]{2,1,0:T(8,128)S(1)}, f32[128,8,128]{2,1,0:T(8,128)S(1)}, u32[]{:S(2)}, u32[]{:S(2)}) %collective-permute-start.4) | collective-permute-done | bytes 524320 | tf_op jit(solution)/shard_map/ppermute | solution.py:589
  70.3 0.0 collective-permute-done.5.refs_3_.refs_2_
  70.3 0.0 collective-permute-done.9.refs_11_.refs_14_
  70.3 0.8 copy-done.6
  71.1 0.2 copy-done.7
  71.3 0.2 copy-done.8
  71.4 11.7 %edge_first.1 = (f32[128,8,128]{2,1,0:T(8,128)}, f32[128,8,128]{2,1,0:T(8,128)}, f32[128,8,128]{2,1,0:T(8,128)}, f32[128,8,128]{2,1,0:T(8,128)}, f32[128,8,128]{...) custom-call(f32[128,8,128]{2,1,0:T(8,128)} %copy-done.6, ...), custom_call_target="tpu_custom_call" | custom-call | bytes 2000000 | tf_op jit(solution)/shard_map/edge_first/pallas_call | solution.py:421
  83.1 0.0 collective-permute-done.3.refs_0_
  83.2 16.2 %edge_last.1 = (f32[128,8,128]{2,1,0:T(8,128)}, f32[128,8,128]{2,1,0:T(8,128)}, f32[8,2048]{1,0:T(8,128)}) custom-call(f32[128,8,128]{2,1,0:T(8,128)} %collective-permute-done.3.refs_0_, f32[128,8,128]{2,1,0:T(8,128)} %copy-done.6, f32[128,8,128]{2,1,0:T(8,128)} %copy-done.7, f32[128,8,128]{2,1,0:T(8,128)} %collective-permute-done.6.refs_3_, ...), custom_call_target="tpu_custom_call" | custom-call | bytes 3000000 | tf_op jit(solution)/shard_map/edge_last/pallas_call | solution.py:421
  99.3 0.1 collective-permute-start.10
  99.4 0.1 pad_add_fusion
  99.5 3.7 %field_0.1.refs_4_ = f32[128,4096]{1,0:T(8,128)} custom-call(f32[128,8,128]{2,1,0:T(8,128)} %get-tuple-element.62.refs_0_, f32[128,8,128]{2,1,0:T(8,128)} %get-tuple-element.59.refs_10_.refs_1_, f32[128,8,128]{2,1,0:T(8,128)} %get-tuple-element.60.refs_11_.refs_2_, f32[128,8,128]{2,1,0:T(8,128)} %get-tuple-element.63.refs_3_), custom_call_target="tpu_custom_call" | custom-call | bytes 800000 | tf_op jit(solution)/shard_map/field_0/pallas_call | solution.py:421
  103.2 0.0 collective-permute-done.10
  103.2 0.0 copy-done.11
  103.3 0.9 collective-permute-start.11
  104.2 0.1 compare_convert_fusion.same
  104.2 3.7 %field_1.1 = f32[128,4096]{1,0:T(8,128)} custom-call(f32[128,8,128]{2,1,0:T(8,128)} %get-tuple-element.62.refs_0_, f32[128,8,128]{2,1,0:T(8,128)} %get-tuple-element.59.refs_10_.refs_1_, f32[128,8,128]{2,1,0:T(8,128)} %get-tuple-element.60.refs_11_.refs_2_, f32[128,8,128]{2,1,0:T(8,128)} %get-tuple-element.63.refs_3_, ...), custom_call_target="tpu_custom_call", output_to_operand_aliasing={{}: (4, {})} | custom-call | bytes 800000 | tf_op jit(solution)/shard_map/field_1/pallas_call | solution.py:421
  108.0 1.2 collective-permute-done.11.other
  109.2 0.0 copy-done.2
  109.2 0.6 products.1
  109.9 2.5 %collective-permute-start.12 = (f32[32,40]{1,0:T(8,128)S(1)}, f32[32,40]{1,0:T(8,128)S(1)}, u32[]{:S(2)}, u32[]{:S(2)}) collective-permute-start(f32[32,40]{1,0:T(8,128)S(1)} %products.1), channel_id=1, source_target_pairs={{0,1},{1,0},{2,3},{3,2},{4,5},{5,4},{6,7},{7,6},{8,9},{9,8},{10,11... | collective-permute-start | bytes 15368 | tf_op jit(solution)/shard_map/ppermute | solution.py:639
  112.4 1.7 %collective-permute-done.12 = f32[32,40]{1,0:T(8,128)S(1)} collective-permute-done((f32[32,40]{1,0:T(8,128)S(1)}, f32[32,40]{1,0:T(8,128)S(1)}, u32[]{:S(2)}, u32[]{:S(2)}) %collective-permute-start.12) | collective-permute-done | bytes 5152 | tf_op jit(solution)/shard_map/ppermute | solution.py:639
  114.1 11.9 %collective-permute-start.13 = (f32[32,40]{1,0:T(8,128)S(1)}, f32[32,40]{1,0:T(8,128)S(1)}, u32[]{:S(2)}, u32[]{:S(2)}) collective-permute-start(f32[32,40]{1,0:T(8,128)S(1)} %add.67), channel_id=1, source_target_pairs={{0,2},{1,3},{2,0},{3,1},{4,6},{5,7},{6,4},{7,5},{8,10},{9,11},{10,... | collective-permute-start | bytes 15368 | tf_op jit(solution)/shard_map/ppermute | solution.py:639
  126.1 0.2 convert_reduce_fusion
  126.2 0.1 copy.10.rank_col
  126.3 1.4 %collective-permute-done.13 = f32[32,40]{1,0:T(8,128)S(1)} collective-permute-done((f32[32,40]{1,0:T(8,128)S(1)}, f32[32,40]{1,0:T(8,128)S(1)}, u32[]{:S(2)}, u32[]{:S(2)}) %collective-permute-start.13) | collective-permute-done | bytes 5152 | tf_op jit(solution)/shard_map/ppermute | solution.py:639
  127.8 3.1 %collective-permute-start.14 = (f32[32,40]{1,0:T(8,128)S(1)}, f32[32,40]{1,0:T(8,128)S(1)}, u32[]{:S(2)}, u32[]{:S(2)}) collective-permute-start(f32[32,40]{1,0:T(8,128)S(1)} %add.68), channel_id=1, source_target_pairs={{0,4},{1,5},{2,6},{3,7},{4,0},{5,1},{6,2},{7,3},{8,12},{9,13},{10,... | collective-permute-start | bytes 15368 | tf_op jit(solution)/shard_map/ppermute | solution.py:639
  130.9 0.0 copy-done.10
  130.9 0.4 fusion.1.anomalies
  131.4 1.3 collective-permute-done.14
  132.7 2.1 %update.1 = f32[8,4096]{1,0:T(8,128)} custom-call(f32[1,32,40]{2,1,0:T(8,128)S(1)} %add_bitcast_fusion.summands, f32[32,32]{1,0:T(8,128)S(1)} %compare_convert_fusion.same, f32[32,8]{1,0:T(8,128)S(1)} %bitcast.33, s32[1,32]{1,0:T(1,128)S(1)} %bitcast.36, s32[32,1]{1,0:T(8,128)S(1)} %copy.10.rank_col, f32[32,4096]{1,0:T(8,128)S(1)} %fusion.1.anomalies, ...), custom_call_target="tpu_custom_call" | custom-call | tf_op jit(solution)/shard_map/update/pallas_call | solution.py:641
  (18 shorter events, 0.2 us)
Async XLA Ops:
  5.0 22.6 %collective-permute-start.1 = (f32[32,8,128]{2,1,0:T(8,128)}, f32[32,8,128]{2,1,0:T(8,128)S(1)}, u32[]{:S(2)}, u32[]{:S(2)}) collective-permute-start(f32[32,8,128]{2,1,0:T(8,128)} %get-tuple-element.44), channel_id=1, source_target_pairs={{1,0},{2,1},{3,2},{4,3},{5,4},{6,5},{7,6},{9,8},{10,9},{11,10},{12... | collective-permute-start | bytes 393224 | tf_op jit(solution)/shard_map/ppermute | solution.py:589
  6.3 21.3 %collective-permute-start = (f32[32,8,128]{2,1,0:T(8,128)}, f32[32,8,128]{2,1,0:T(8,128)S(1)}, u32[]{:S(2)}, u32[]{:S(2)}) collective-permute-start(f32[32,8,128]{2,1,0:T(8,128)} %get-tuple-element.43), channel_id=1, source_target_pairs={{0,1},{1,2},{2,3},{3,4},{4,5},{5,6},{6,7},{8,9},{9,10},{10,11},{11... | collective-permute-start | bytes 393224 | tf_op jit(solution)/shard_map/ppermute | solution.py:589
  18.2 9.3 %copy-start = (f32[8,4096]{1,0:T(8,128)S(1)}, f32[8,4096]{1,0:T(8,128)}, u32[]{:S(2)}) copy-start(f32[8,4096]{1,0:T(8,128)} %own.1) | copy-start | bytes 393220
  18.2 14.2 %copy-start.4 = (f32[128,8,128]{2,1,0:T(8,128)S(1)}, f32[128,8,128]{2,1,0:T(8,128)}, u32[]{:S(2)}) copy-start(f32[128,8,128]{2,1,0:T(8,128)} %get-tuple-element.36.outer.own3.refs_2_) | copy-start | bytes 1572868
  18.2 19.2 %copy-start.5 = (f32[128,8,128]{2,1,0:T(8,128)S(1)}, f32[128,8,128]{2,1,0:T(8,128)}, u32[]{:S(2)}) copy-start(f32[128,8,128]{2,1,0:T(8,128)} %get-tuple-element.39.own0.refs_1_) | copy-start | bytes 1572868
  18.2 28.0 %copy-start.13 = (s32[32]{0:T(128)S(1)}, s32[32]{0:T(128)}, u32[]{:S(2)}) copy-start(s32[32]{0:T(128)} %param.13) | copy-start | bytes 388
  18.2 28.1 %copy-start.12 = (s32[2048]{0:T(1024)S(1)}, s32[2048]{0:T(1024)}, u32[]{:S(2)}) copy-start(s32[2048]{0:T(1024)} %param.10) | copy-start | bytes 24580
  27.5 1.4 %collective-permute-start.7 = (f32[8,4096]{1,0:T(8,128)S(1)}, f32[8,4096]{1,0:T(8,128)S(1)}, u32[]{:S(2)}, u32[]{:S(2)}) collective-permute-start(f32[8,4096]{1,0:T(8,128)S(1)} %copy-done), channel_id=1, source_target_pairs={{0,8},{8,0},{16,24},{24,16},{1,9},{9,1},{17,25},{25,17},{2,10},{10... | collective-permute-start | bytes 393224 | tf_op jit(solution)/shard_map/ppermute | solution.py:579
  27.7 3.4 %collective-permute-start.2 = (f32[2,32,8,128]{3,2,1,0:T(8,128)S(1)}, f32[2,32,8,128]{3,2,1,0:T(8,128)S(1)}, u32[]{:S(2)}, u32[]{:S(2)}) collective-permute-start(f32[2,32,8,128]{3,2,1,0:T(8,128)S(1)} %get-tuple-element.71), channel_id=1, source_target_pairs={{0,8},{8,0},{16,24},{24,16},{1,9},{9,1},{17,25},{25,17},{2,10},{10... | collective-permute-start | bytes 786440 | tf_op jit(solution)/shard_map/ppermute | solution.py:579
  29.0 10.3 %collective-permute-start.8 = (f32[2,8,4096]{2,1,0:T(8,128)S(1)}, f32[2,8,4096]{2,1,0:T(8,128)S(1)}, u32[]{:S(2)}, u32[]{:S(2)}) collective-permute-start(f32[2,8,4096]{2,1,0:T(8,128)S(1)} %pad_maximum_fusion.2), channel_id=1, source_target_pairs={{0,16},{8,24},{16,0},{24,8},{1,17},{9,25},{17,1},{25,9},{2,18},{10... | collective-permute-start | bytes 786440 | tf_op jit(solution)/shard_map/ppermute | solution.py:582
  31.1 39.2 %copy-start.3 = (f32[2,2,32,8,128]{4,3,2,1,0:T(8,128)}, f32[2,2,32,8,128]{4,3,2,1,0:T(8,128)S(1)}, u32[]{:S(2)}) copy-start(f32[2,2,32,8,128]{4,3,2,1,0:T(8,128)S(1)} %pad_maximum_fusion.refs_10_.refs_13_) | copy-start | bytes 1572868
  31.1 17.3 %collective-permute-start.6 = (f32[128,8,128]{2,1,0:T(8,128)}, f32[128,8,128]{2,1,0:T(8,128)}, u32[]{:S(2)}, u32[]{:S(2)}) collective-permute-start(f32[128,8,128]{2,1,0:T(8,128)} %get-tuple-element.46.own1), channel_id=1, source_target_pairs={{1,0},{2,1},{3,2},{4,3},{5,4},{6,5},{7,6},{9,8},{10,9},{11,10},{12... | collective-permute-start | bytes 1572872 | tf_op jit(solution)/shard_map/ppermute | solution.py:589
  32.4 37.9 %collective-permute-start.4 = (f32[128,8,128]{2,1,0:T(8,128)S(1)}, f32[128,8,128]{2,1,0:T(8,128)S(1)}, u32[]{:S(2)}, u32[]{:S(2)}) collective-permute-start(f32[128,8,128]{2,1,0:T(8,128)S(1)} %copy-done.4), channel_id=1, source_target_pairs={{0,1},{1,2},{2,3},{3,4},{4,5},{5,6},{6,7},{8,9},{9,10},{10,11},{11... | collective-permute-start | bytes 1572872 | tf_op jit(solution)/shard_map/ppermute | solution.py:589
  37.4 32.9 %collective-permute-start.5 = (f32[128,8,128]{2,1,0:T(8,128)S(1)}, f32[128,8,128]{2,1,0:T(8,128)S(1)}, u32[]{:S(2)}, u32[]{:S(2)}) collective-permute-start(f32[128,8,128]{2,1,0:T(8,128)S(1)} %copy-done.5), channel_id=1, source_target_pairs={{1,0},{2,1},{3,2},{4,3},{5,4},{6,5},{7,6},{9,8},{10,9},{11,10},{12... | collective-permute-start | bytes 1572872 | tf_op jit(solution)/shard_map/ppermute | solution.py:589
  38.7 31.6 %collective-permute-start.9 = (f32[2,2,32,8,128]{4,3,2,1,0:T(8,128)S(1)}, f32[2,2,32,8,128]{4,3,2,1,0:T(8,128)S(1)}, u32[]{:S(2)}, u32[]{:S(2)}) collective-permute-start(f32[2,2,32,8,128]{4,3,2,1,0:T(8,128)S(1)} %pad_maximum_fusion.refs_10_.refs_13_), channel_id=1, source_target_pairs={{0,16},{8,24},{16,0},{24,8},{1,17},{9,25},{17,1},{25,9},{2,18},{10... | collective-permute-start | bytes 1572872 | tf_op jit(solution)/shard_map/ppermute | solution.py:582
  39.3 0.7 copy-start.9
  40.0 43.2 %collective-permute-start.3 = (f32[128,8,128]{2,1,0:T(8,128)}, f32[128,8,128]{2,1,0:T(8,128)}, u32[]{:S(2)}, u32[]{:S(2)}) collective-permute-start(f32[128,8,128]{2,1,0:T(8,128)} %get-tuple-element.45.own2), channel_id=1, source_target_pairs={{0,1},{1,2},{2,3},{3,4},{4,5},{5,6},{6,7},{8,9},{9,10},{10,11},{11... | collective-permute-start | bytes 1572872 | tf_op jit(solution)/shard_map/ppermute | solution.py:589
  70.3 0.8 copy-start.6
  70.3 1.0 copy-start.7
  70.3 1.1 copy-start.8
  99.3 3.9 %collective-permute-start.10 = (f32[8,2048]{1,0:T(8,128)}, f32[8,2048]{1,0:T(8,128)S(1)}, u32[]{:S(2)}, u32[]{:S(2)}) collective-permute-start(f32[8,2048]{1,0:T(8,128)} %get-tuple-element.61), channel_id=1, source_target_pairs={{0,8},{8,0},{16,24},{24,16},{1,9},{9,1},{17,25},{25,17},{2,10},{10... | collective-permute-start | bytes 196616 | tf_op jit(solution)/shard_map/ppermute | solution.py:579
  99.5 3.8 %copy-start.11 = (f32[8,2048]{1,0:T(8,128)S(1)}, f32[8,2048]{1,0:T(8,128)}, u32[]{:S(2)}) copy-start(f32[8,2048]{1,0:T(8,128)} %get-tuple-element.61) | copy-start | bytes 196612
  103.3 5.9 %collective-permute-start.11 = (f32[2,8,2048]{2,1,0:T(8,128)S(1)}, f32[2,8,2048]{2,1,0:T(8,128)S(1)}, u32[]{:S(2)}, u32[]{:S(2)}) collective-permute-start(f32[2,8,2048]{2,1,0:T(8,128)S(1)} %pad_maximum_fusion.3.pair), channel_id=1, source_target_pairs={{0,16},{8,24},{16,0},{24,8},{1,17},{9,25},{17,1},{25,9},{2,18},{10... | collective-permute-start | bytes 393224 | tf_op jit(solution)/shard_map/ppermute | solution.py:582
  104.2 5.0 %copy-start.1 = (f32[8,2048]{1,0:T(8,128)S(1)}, f32[8,2048]{1,0:T(8,128)}, u32[]{:S(2)}) copy-start(f32[8,2048]{1,0:T(8,128)} %values.1) | copy-start | bytes 196612
  104.2 5.0 %copy-start.2 = (f32[2048]{0:T(1024)S(1)}, f32[2048]{0:T(1024)}, u32[]{:S(2)}) copy-start(f32[2048]{0:T(1024)} %param.12) | copy-start | bytes 24580
  104.2 26.7 %copy-start.10 = (f32[2,8,4096]{2,1,0:T(8,128)S(1)}, f32[2,8,4096]{2,1,0:T(8,128)}, u32[]{:S(2)}) copy-start(f32[2,8,4096]{2,1,0:T(8,128)} %copy-done.9) | copy-start | bytes 786436
  109.9 4.2 %collective-permute-start.12 = (f32[32,40]{1,0:T(8,128)S(1)}, f32[32,40]{1,0:T(8,128)S(1)}, u32[]{:S(2)}, u32[]{:S(2)}) collective-permute-start(f32[32,40]{1,0:T(8,128)S(1)} %products.1), channel_id=1, source_target_pairs={{0,1},{1,0},{2,3},{3,2},{4,5},{5,4},{6,7},{7,6},{8,9},{9,8},{10,11... | collective-permute-start | bytes 15368 | tf_op jit(solution)/shard_map/ppermute | solution.py:639
  114.1 13.7 %collective-permute-start.13 = (f32[32,40]{1,0:T(8,128)S(1)}, f32[32,40]{1,0:T(8,128)S(1)}, u32[]{:S(2)}, u32[]{:S(2)}) collective-permute-start(f32[32,40]{1,0:T(8,128)S(1)} %add.67), channel_id=1, source_target_pairs={{0,2},{1,3},{2,0},{3,1},{4,6},{5,7},{6,4},{7,5},{8,10},{9,11},{10,... | collective-permute-start | bytes 15368 | tf_op jit(solution)/shard_map/ppermute | solution.py:639
  127.8 4.9 %collective-permute-start.14 = (f32[32,40]{1,0:T(8,128)S(1)}, f32[32,40]{1,0:T(8,128)S(1)}, u32[]{:S(2)}, u32[]{:S(2)}) collective-permute-start(f32[32,40]{1,0:T(8,128)S(1)} %add.68), channel_id=1, source_target_pairs={{0,4},{1,5},{2,6},{3,7},{4,0},{5,1},{6,2},{7,3},{8,12},{9,13},{10,... | collective-permute-start | bytes 15368 | tf_op jit(solution)/shard_map/ppermute | solution.py:639

commit v13 on v12

--- a/solution.py
+++ b/solution.py
@@ -475,7 +475,9 @@
         [group] * 5, [ANYWHERE] * 5 + [IN_VMEM], (ANYWHERE,) * 5,
         scratch(columns, dma((16,))), 8, [*own, own_coef, params],
     )
-    upper, lower, *_ = lax.optimization_barrier((own[2], own[1], inner[0], pair))
+    upper, lower, low0, high0, *_ = lax.optimization_barrier(
+        (own[2], own[1], low0, high0, inner[0])
+    )
     low1, high1 = halos(upper, lower)
     first = kernel_call(
         functools.partial(middle_kernel, blocks), "edge_first",
@@ -624,8 +626,6 @@
     field = write_field(0, None)
     near, field = lax.optimization_barrier((near, field))
     far = next_chip(near)
-    field = write_field(1, field)
-    far, field = lax.optimization_barrier((far, field))
     total_obs = obs_variance.shape[0] * slab_count
     products = pl.pallas_call(
         functools.partial(products_kernel, float(total_obs), per_group, spread),
@@ -636,7 +636,10 @@
     distance = 1
     while distance < slab_count:
         pairs = [(i, i ^ distance) for i in range(slab_count)]
-        products = products + lax.ppermute(products, "slab", pairs)
+        arrived = lax.ppermute(products, "slab", pairs)
+        if distance == 1:
+            arrived, field = lax.optimization_barrier((arrived, write_field(1, field)))
+        products = products + arrived
         distance *= 2
     updated = pl.pallas_call(
         functools.partial(update_kernel, per_group),

time: 135 us -> 112 us (0.83)
  starting transfers between devices: 42.4 us -> 30.7 us
  waiting for transfers between devices: 29.8 us -> 18.5 us
    ppermute x3, waiting for transfers between devices: 21.8 us -> 10.7 us  [halos(): lax.ppermute(upper, 'slab', forward)]
    ppermute x3, starting transfers between devices: 17.6 us -> 6.75 us  [local(): arrived = lax.ppermute(products, 'slab', pairs)]
    ppermute x3, waiting for transfers between devices: 1.24 us -> 4.29 us  [next_chip(): return lax.ppermute(value, 'ens', [(i, i ^ 2) for i in range(ens_count)])]
    ppermute x3, starting transfers between devices: 16.6 us -> 14.6 us  [halos(): lax.ppermute(upper, 'slab', forward)]
    ppermute x3, waiting for transfers between devices: 1.54 us -> 0.01 us  [halos(): lax.ppermute(lower, 'slab', backward)]
  transfers between devices with their start and end apart: 15 -> 15, of which waited for: 7 -> 5; matrix products, arithmetic and copies ran while one was open for 1% -> 2% of each run, Pallas kernels for 26% -> 31%
where the time goes in v13:
time: 112 us
  Pallas kernels  58.1 us (52%)
  starting transfers between devices  30.7 us (27%)
  waiting for transfers between devices  18.5 us (17%)
  local copies, waits for them, and re-layouts  1.83 us (2%)
    pallas_call x7, Pallas kernels, kernel_call(): pl.pallas_call(body, out_shape=tuple((jax.ShapeDtypeStruct(shape, jnp.flo...  55.3 us
    ppermute x3, starting transfers between devices, halos(): lax.ppermute(upper, 'slab', forward)  14.6 us
    ppermute x3, waiting for transfers between devices, halos(): lax.ppermute(upper, 'slab', forward)  10.7 us
    ppermute x3, starting transfers between devices, local(): arrived = lax.ppermute(products, 'slab', pairs)  6.75 us
    ppermute x3, starting transfers between devices, next_chip(): return lax.ppermute(value, 'ens', [(i, i ^ 2) for i in range(ens_count)])  4.76 us
    ppermute x3, waiting for transfers between devices, next_chip(): return lax.ppermute(value, 'ens', [(i, i ^ 2) for i in range(ens_count)])  4.29 us
    ppermute x3, starting transfers between devices, halos(): lax.ppermute(lower, 'slab', backward)  3.88 us
    ppermute x3, waiting for transfers between devices, local(): arrived = lax.ppermute(products, 'slab', pairs)  3.5 us
  transfers between devices with their start and end apart: 15, of which 5 were waited for; matrix products, arithmetic and copies ran while one was open for 2% of the time, Pallas kernels for 31%

profile of v13, /device:TPU:0, one launch (start us, length us, event | category | flops | bytes accessed | tf_op | source)
XLA Modules:
  0.0 111.6 jit_solution(4363945922273317388)
XLA Ops:
  0.6 4.3 %outer_rows.1 = (f32[128,8,128]{2,1,0:T(8,128)}, f32[128,8,128]{2,1,0:T(8,128)}, f32[32,8,128]{2,1,0:T(8,128)}, f32[32,8,128]{2,1,0:T(8,128)}) custom-call(f32[128,4096]{1,0:T(8,128)} %bitcast.38, f32[4,16,4096]{2,1,0:T(8,128)} %own_coef.3, s32[1]{0:T(128)} %bitcast.1.place_of.refs_13_.refs_16_), custom_call_target="tpu_custom_call" | custom-call | bytes 600000 | tf_op jit(solution)/shard_map/outer_rows/pallas_call | solution.py:421
  5.0 4.8 %collective-permute-start.6 = (f32[32,8,128]{2,1,0:T(8,128)}, f32[32,8,128]{2,1,0:T(8,128)S(1)}, u32[]{:S(2)}, u32[]{:S(2)}) collective-permute-start(f32[32,8,128]{2,1,0:T(8,128)} %get-tuple-element.55), channel_id=1, source_target_pairs={{0,1},{1,2},{2,3},{3,4},{4,5},{5,6},{6,7},{8,9},{9,10},{10,11},{11... | collective-permute-start | bytes 393224 | tf_op jit(solution)/shard_map/ppermute | solution.py:591
  9.8 1.3 %collective-permute-start.7 = (f32[32,8,128]{2,1,0:T(8,128)}, f32[32,8,128]{2,1,0:T(8,128)S(1)}, u32[]{:S(2)}, u32[]{:S(2)}) collective-permute-start(f32[32,8,128]{2,1,0:T(8,128)} %get-tuple-element.56), channel_id=1, source_target_pairs={{1,0},{2,1},{3,2},{4,3},{5,4},{6,5},{7,6},{9,8},{10,9},{11,10},{12... | collective-permute-start | bytes 393224 | tf_op jit(solution)/shard_map/ppermute | solution.py:591
  11.1 4.6 %collective-permute-start = (f32[128,8,128]{2,1,0:T(8,128)}, f32[128,8,128]{2,1,0:T(8,128)S(1)}, u32[]{:S(2)}, u32[]{:S(2)}) collective-permute-start(f32[128,8,128]{2,1,0:T(8,128)} %get-tuple-element.38.outer.own3.refs_2_), channel_id=1, source_target_pairs={{0,1},{1,2},{2,3},{3,4},{4,5},{5,6},{6,7},{8,9},{9,10},{10,11},{11... | collective-permute-start | bytes 1572872 | tf_op jit(solution)/shard_map/ppermute | solution.py:591
  15.7 1.3 %collective-permute-start.1 = (f32[128,8,128]{2,1,0:T(8,128)}, f32[128,8,128]{2,1,0:T(8,128)S(1)}, u32[]{:S(2)}, u32[]{:S(2)}) collective-permute-start(f32[128,8,128]{2,1,0:T(8,128)} %get-tuple-element.41.own0.refs_1_), channel_id=1, source_target_pairs={{1,0},{2,1},{3,2},{4,3},{5,4},{6,5},{7,6},{9,8},{10,9},{11,10},{12... | collective-permute-start | bytes 1572872 | tf_op jit(solution)/shard_map/ppermute | solution.py:591
  17.0 0.0 collective-permute-done.6
  17.0 0.0 collective-permute-done.7
  17.1 0.1 collective-permute-start.8
  17.2 6.4 %inner_rows.1 = (f32[128,8,128]{2,1,0:T(8,128)}, f32[128,8,128]{2,1,0:T(8,128)}, f32[32,64,128]{2,1,0:T(8,128)}, f32[8,4096]{1,0:T(8,128)}) custom-call(f32[128,4096]{1,0:T(8,128)} %bitcast.39, f32[4,16,4096]{2,1,0:T(8,128)} %own_coef.3, f32[8,4096]{1,0:T(8,128)} %own.1, f32[128,8,128]{2,1,0:T(8,128)} %get-tuple-element.38.outer.own3.refs_2_), custom_call_target="tpu_custom_call" | custom-call | bytes 600000 | tf_op jit(solution)/shard_map/inner_rows/pallas_call | solution.py:421
  23.6 0.0 copy-start
  23.6 0.0 copy-start.13
  23.6 0.0 copy-start.8
  23.6 0.0 copy-start.7
  23.6 0.0 copy-start.12
  23.6 9.3 %interior.1 = (f32[128,8,128]{2,1,0:T(8,128)}, f32[128,8,128]{2,1,0:T(8,128)}, f32[128,8,128]{2,1,0:T(8,128)}, f32[128,8,128]{2,1,0:T(8,128)}, f32[128,8,128]{2,1,0:T(8,128)}) custom-call(f32[128,8,128]{2,1,0:T(8,128)} %get-tuple-element.41.own0.refs_1_, f32[128,8,128]{2,1,0:T(8,128)} %get-tuple-element.48.own1, f32[128,8,128]{2,1,0:T(8,128)} %get-tuple-element.45.own2, ...), custom_call_target="tpu_custom_call" | custom-call | bytes 1600000 | tf_op jit(solution)/shard_map/interior/pallas_call | solution.py:421
  33.0 0.0 copy-done
  33.0 0.6 collective-permute-start.4
  33.5 0.0 copy-done.13
  33.6 0.1 reshape.23
  33.6 0.0 collective-permute-done.8
  33.6 0.1 pad_maximum_fusion.refs_10_.refs_13_
  33.7 1.6 %collective-permute-start.9 = (f32[2,2,32,8,128]{4,3,2,1,0:T(8,128)S(1)}, f32[2,2,32,8,128]{4,3,2,1,0:T(8,128)S(1)}, u32[]{:S(2)}, u32[]{:S(2)}) collective-permute-start(f32[2,2,32,8,128]{4,3,2,1,0:T(8,128)S(1)} %pad_maximum_fusion.refs_10_.refs_13_), channel_id=1, source_target_pairs={{0,16},{8,24},{16,0},{24,8},{1,17},{9,25},{17,1},{25,9},{2,18},{10... | collective-permute-start | bytes 1572872 | tf_op jit(solution)/shard_map/ppermute | solution.py:584
  35.3 4.1 %collective-permute-done.refs_0_.refs_1_ = f32[128,8,128]{2,1,0:T(8,128)S(1)} collective-permute-done((f32[128,8,128]{2,1,0:T(8,128)}, f32[128,8,128]{2,1,0:T(8,128)S(1)}, u32[]{:S(2)}, u32[]{:S(2)}) %collective-permute-start) | collective-permute-done | bytes 524320 | tf_op jit(solution)/shard_map/ppermute | solution.py:591
  39.4 0.0 collective-permute-done.1.refs_3_.refs_2_
  39.4 0.0 copy-done.8
  39.5 1.3 %collective-permute-start.3 = (f32[128,8,128]{2,1,0:T(8,128)S(1)}, f32[128,8,128]{2,1,0:T(8,128)S(1)}, u32[]{:S(2)}, u32[]{:S(2)}) collective-permute-start(f32[128,8,128]{2,1,0:T(8,128)S(1)} %copy-done.8), channel_id=1, source_target_pairs={{1,0},{2,1},{3,2},{4,3},{5,4},{6,5},{7,6},{9,8},{10,9},{11,10},{12... | collective-permute-start | bytes 1572872 | tf_op jit(solution)/shard_map/ppermute | solution.py:591
  40.8 0.0 copy-done.7
  40.8 5.1 %collective-permute-start.2 = (f32[128,8,128]{2,1,0:T(8,128)S(1)}, f32[128,8,128]{2,1,0:T(8,128)S(1)}, u32[]{:S(2)}, u32[]{:S(2)}) collective-permute-start(f32[128,8,128]{2,1,0:T(8,128)S(1)} %copy-done.7), channel_id=1, source_target_pairs={{0,1},{1,2},{2,3},{3,4},{4,5},{5,6},{6,7},{8,9},{9,10},{10,11},{11... | collective-permute-start | bytes 1572872 | tf_op jit(solution)/shard_map/ppermute | solution.py:591
  45.9 0.0 collective-permute-done.4
  45.9 1.6 %collective-permute-start.5 = (f32[2,8,4096]{2,1,0:T(8,128)S(1)}, f32[2,8,4096]{2,1,0:T(8,128)S(1)}, u32[]{:S(2)}, u32[]{:S(2)}) collective-permute-start(f32[2,8,4096]{2,1,0:T(8,128)S(1)} %pad_maximum_fusion.1), channel_id=1, source_target_pairs={{0,16},{8,24},{16,0},{24,8},{1,17},{9,25},{17,1},{25,9},{2,18},{10... | collective-permute-start | bytes 786440 | tf_op jit(solution)/shard_map/ppermute | solution.py:584
  47.5 0.0 copy-done.12
  47.5 0.6 add_select_fusion
  48.2 0.0 collective-permute-done.9.refs_11_.refs_14_
  48.2 0.0 copy-done.3
  48.2 0.0 copy-done.4
  48.2 0.0 copy-done.5
  48.2 0.8 copy-done.6
  49.0 11.7 %edge_first.1 = (f32[128,8,128]{2,1,0:T(8,128)}, f32[128,8,128]{2,1,0:T(8,128)}, f32[128,8,128]{2,1,0:T(8,128)}, f32[128,8,128]{2,1,0:T(8,128)}, f32[128,8,128]{...) custom-call(f32[128,8,128]{2,1,0:T(8,128)} %copy-done.4, ...), custom_call_target="tpu_custom_call" | custom-call | bytes 2000000 | tf_op jit(solution)/shard_map/edge_first/pallas_call | solution.py:421
  60.6 0.0 collective-permute-done.5
  60.7 0.0 collective-permute-done.3.refs_3_
  60.7 0.0 copy-start.9
  60.7 6.5 %collective-permute-done.2.refs_0_ = f32[128,8,128]{2,1,0:T(8,128)S(1)} collective-permute-done((f32[128,8,128]{2,1,0:T(8,128)S(1)}, f32[128,8,128]{2,1,0:T(8,128)S(1)}, u32[]{:S(2)}, u32[]{:S(2)}) %collective-permute-start.2) | collective-permute-done | bytes 524320 | tf_op jit(solution)/shard_map/ppermute | solution.py:591
  67.2 0.8 copy-done.10
  68.0 16.2 %edge_last.1 = (f32[128,8,128]{2,1,0:T(8,128)}, f32[128,8,128]{2,1,0:T(8,128)}, f32[8,2048]{1,0:T(8,128)}) custom-call(f32[128,8,128]{2,1,0:T(8,128)} %copy-done.10, f32[128,8,128]{2,1,0:T(8,128)} %copy-done.4, f32[128,8,128]{2,1,0:T(8,128)} %copy-done.5, f32[128,8,128]{2,1,0:T(8,128)} %copy-done.9, f32[128,8,128]{2,1,0:T(8,128)} %get-tuple-element.57.refs_4_, ...), custom_call_target="tpu_custom_call" | custom-call | bytes 3000000 | tf_op jit(solution)/shard_map/edge_last/pallas_call | solution.py:421
  84.2 0.1 collective-permute-start.10
  84.3 0.1 pad_add_fusion
  84.4 3.7 %field_0.1.refs_4_ = f32[128,4096]{1,0:T(8,128)} custom-call(f32[128,8,128]{2,1,0:T(8,128)} %get-tuple-element.66.refs_0_, f32[128,8,128]{2,1,0:T(8,128)} %get-tuple-element.63.refs_10_.refs_1_, f32[128,8,128]{2,1,0:T(8,128)} %get-tuple-element.64.refs_11_.refs_2_, f32[128,8,128]{2,1,0:T(8,128)} %get-tuple-element.67.refs_3_), custom_call_target="tpu_custom_call" | custom-call | bytes 800000 | tf_op jit(solution)/shard_map/field_0/pallas_call | solution.py:421
  88.2 0.0 collective-permute-done.10
  88.2 1.6 %collective-permute-start.11 = (f32[2,8,2048]{2,1,0:T(8,128)S(1)}, f32[2,8,2048]{2,1,0:T(8,128)S(1)}, u32[]{:S(2)}, u32[]{:S(2)}) collective-permute-start(f32[2,8,2048]{2,1,0:T(8,128)S(1)} %pad_maximum_fusion.3.pair), channel_id=1, source_target_pairs={{0,16},{8,24},{16,0},{24,8},{1,17},{9,25},{17,1},{25,9},{2,18},{10... | collective-permute-start | bytes 393224 | tf_op jit(solution)/shard_map/ppermute | solution.py:584
  89.8 0.1 compare_convert_fusion.same
  89.9 4.3 %collective-permute-done.11.other = f32[2,8,2048]{2,1,0:T(8,128)S(1)} collective-permute-done((f32[2,8,2048]{2,1,0:T(8,128)S(1)}, f32[2,8,2048]{2,1,0:T(8,128)S(1)}, u32[]{:S(2)}, u32[]{:S(2)}) %collective-permute-start.11) | collective-permute-done | bytes 131104 | tf_op jit(solution)/shard_map/ppermute | solution.py:584
  94.1 0.0 copy-done.2
  94.1 0.6 products.1
  94.8 2.5 %collective-permute-start.12 = (f32[32,40]{1,0:T(8,128)S(1)}, f32[32,40]{1,0:T(8,128)S(1)}, u32[]{:S(2)}, u32[]{:S(2)}) collective-permute-start(f32[32,40]{1,0:T(8,128)S(1)} %products.1), channel_id=1, source_target_pairs={{0,1},{1,0},{2,3},{3,2},{4,5},{5,4},{6,7},{7,6},{8,9},{9,8},{10,11... | collective-permute-start | bytes 15368 | tf_op jit(solution)/shard_map/ppermute | solution.py:639
  97.3 3.7 %field_1.1 = f32[128,4096]{1,0:T(8,128)} custom-call(f32[128,8,128]{2,1,0:T(8,128)} %get-tuple-element.66.refs_0_, f32[128,8,128]{2,1,0:T(8,128)} %get-tuple-element.63.refs_10_.refs_1_, f32[128,8,128]{2,1,0:T(8,128)} %get-tuple-element.64.refs_11_.refs_2_, f32[128,8,128]{2,1,0:T(8,128)} %get-tuple-element.67.refs_3_, ...), custom_call_target="tpu_custom_call", output_to_operand_aliasing={{}: (4, {})} | custom-call | bytes 800000 | tf_op jit(solution)/shard_map/field_1/pallas_call | solution.py:421
  101.0 0.0 collective-permute-done.12
  101.0 1.6 %collective-permute-start.13 = (f32[32,40]{1,0:T(8,128)S(1)}, f32[32,40]{1,0:T(8,128)S(1)}, u32[]{:S(2)}, u32[]{:S(2)}) collective-permute-start(f32[32,40]{1,0:T(8,128)S(1)} %add.67), channel_id=1, source_target_pairs={{0,2},{1,3},{2,0},{3,1},{4,6},{5,7},{6,4},{7,5},{8,10},{9,11},{10,... | collective-permute-start | bytes 15368 | tf_op jit(solution)/shard_map/ppermute | solution.py:639
  102.7 0.2 convert_reduce_fusion
  102.9 0.1 copy.10.rank_col
  102.9 1.9 %collective-permute-done.13 = f32[32,40]{1,0:T(8,128)S(1)} collective-permute-done((f32[32,40]{1,0:T(8,128)S(1)}, f32[32,40]{1,0:T(8,128)S(1)}, u32[]{:S(2)}, u32[]{:S(2)}) %collective-permute-start.13) | collective-permute-done | bytes 5152 | tf_op jit(solution)/shard_map/ppermute | solution.py:639
  104.9 2.6 %collective-permute-start.14 = (f32[32,40]{1,0:T(8,128)S(1)}, f32[32,40]{1,0:T(8,128)S(1)}, u32[]{:S(2)}, u32[]{:S(2)}) collective-permute-start(f32[32,40]{1,0:T(8,128)S(1)} %add.68), channel_id=1, source_target_pairs={{0,4},{1,5},{2,6},{3,7},{4,0},{5,1},{6,2},{7,3},{8,12},{9,13},{10,... | collective-permute-start | bytes 15368 | tf_op jit(solution)/shard_map/ppermute | solution.py:639
  107.4 0.4 fusion.1.anomalies
  107.9 1.6 %collective-permute-done.14 = f32[32,40]{1,0:T(8,128)S(1)} collective-permute-done((f32[32,40]{1,0:T(8,128)S(1)}, f32[32,40]{1,0:T(8,128)S(1)}, u32[]{:S(2)}, u32[]{:S(2)}) %collective-permute-start.14) | collective-permute-done | bytes 5152 | tf_op jit(solution)/shard_map/ppermute | solution.py:639
  109.5 2.1 %update.1 = f32[8,4096]{1,0:T(8,128)} custom-call(f32[1,32,40]{2,1,0:T(8,128)S(1)} %add_bitcast_fusion.summands, f32[32,32]{1,0:T(8,128)S(1)} %compare_convert_fusion.same, f32[32,8]{1,0:T(8,128)S(1)} %bitcast.33, s32[1,32]{1,0:T(1,128)S(1)} %bitcast.36, s32[32,1]{1,0:T(8,128)S(1)} %copy.10.rank_col, f32[32,4096]{1,0:T(8,128)S(1)} %fusion.1.anomalies, ...), custom_call_target="tpu_custom_call" | custom-call | tf_op jit(solution)/shard_map/update/pallas_call | solution.py:644
  (18 shorter events, 0.1 us)
Async XLA Ops:
  5.0 12.0 %collective-permute-start.6 = (f32[32,8,128]{2,1,0:T(8,128)}, f32[32,8,128]{2,1,0:T(8,128)S(1)}, u32[]{:S(2)}, u32[]{:S(2)}) collective-permute-start(f32[32,8,128]{2,1,0:T(8,128)} %get-tuple-element.55), channel_id=1, source_target_pairs={{0,1},{1,2},{2,3},{3,4},{4,5},{5,6},{6,7},{8,9},{9,10},{10,11},{11... | collective-permute-start | bytes 393224 | tf_op jit(solution)/shard_map/ppermute | solution.py:591
  9.8 7.2 %collective-permute-start.7 = (f32[32,8,128]{2,1,0:T(8,128)}, f32[32,8,128]{2,1,0:T(8,128)S(1)}, u32[]{:S(2)}, u32[]{:S(2)}) collective-permute-start(f32[32,8,128]{2,1,0:T(8,128)} %get-tuple-element.56), channel_id=1, source_target_pairs={{1,0},{2,1},{3,2},{4,3},{5,4},{6,5},{7,6},{9,8},{10,9},{11,10},{12... | collective-permute-start | bytes 393224 | tf_op jit(solution)/shard_map/ppermute | solution.py:591
  11.1 28.3 %collective-permute-start = (f32[128,8,128]{2,1,0:T(8,128)}, f32[128,8,128]{2,1,0:T(8,128)S(1)}, u32[]{:S(2)}, u32[]{:S(2)}) collective-permute-start(f32[128,8,128]{2,1,0:T(8,128)} %get-tuple-element.38.outer.own3.refs_2_), channel_id=1, source_target_pairs={{0,1},{1,2},{2,3},{3,4},{4,5},{5,6},{6,7},{8,9},{9,10},{10,11},{11... | collective-permute-start | bytes 1572872 | tf_op jit(solution)/shard_map/ppermute | solution.py:591
  15.7 23.7 %collective-permute-start.1 = (f32[128,8,128]{2,1,0:T(8,128)}, f32[128,8,128]{2,1,0:T(8,128)S(1)}, u32[]{:S(2)}, u32[]{:S(2)}) collective-permute-start(f32[128,8,128]{2,1,0:T(8,128)} %get-tuple-element.41.own0.refs_1_), channel_id=1, source_target_pairs={{1,0},{2,1},{3,2},{4,3},{5,4},{6,5},{7,6},{9,8},{10,9},{11,10},{12... | collective-permute-start | bytes 1572872 | tf_op jit(solution)/shard_map/ppermute | solution.py:591
  17.1 16.5 %collective-permute-start.8 = (f32[2,32,8,128]{3,2,1,0:T(8,128)S(1)}, f32[2,32,8,128]{3,2,1,0:T(8,128)S(1)}, u32[]{:S(2)}, u32[]{:S(2)}) collective-permute-start(f32[2,32,8,128]{3,2,1,0:T(8,128)S(1)} %get-tuple-element.75), channel_id=1, source_target_pairs={{0,8},{8,0},{16,24},{24,16},{1,9},{9,1},{17,25},{25,17},{2,10},{10... | collective-permute-start | bytes 786440 | tf_op jit(solution)/shard_map/ppermute | solution.py:581
  23.6 9.4 %copy-start = (f32[8,4096]{1,0:T(8,128)S(1)}, f32[8,4096]{1,0:T(8,128)}, u32[]{:S(2)}) copy-start(f32[8,4096]{1,0:T(8,128)} %own.1) | copy-start | bytes 393220
  23.6 10.0 %copy-start.13 = (s32[32]{0:T(128)S(1)}, s32[32]{0:T(128)}, u32[]{:S(2)}) copy-start(s32[32]{0:T(128)} %param.13) | copy-start | bytes 388
  23.6 15.8 %copy-start.8 = (f32[128,8,128]{2,1,0:T(8,128)S(1)}, f32[128,8,128]{2,1,0:T(8,128)}, u32[]{:S(2)}) copy-start(f32[128,8,128]{2,1,0:T(8,128)} %get-tuple-element.48.own1) | copy-start | bytes 1572868
  23.6 17.1 %copy-start.7 = (f32[128,8,128]{2,1,0:T(8,128)S(1)}, f32[128,8,128]{2,1,0:T(8,128)}, u32[]{:S(2)}) copy-start(f32[128,8,128]{2,1,0:T(8,128)} %get-tuple-element.45.own2) | copy-start | bytes 1572868
  23.6 23.9 %copy-start.12 = (s32[2048]{0:T(1024)S(1)}, s32[2048]{0:T(1024)}, u32[]{:S(2)}) copy-start(s32[2048]{0:T(1024)} %param.10) | copy-start | bytes 24580
  33.0 12.9 %collective-permute-start.4 = (f32[8,4096]{1,0:T(8,128)S(1)}, f32[8,4096]{1,0:T(8,128)S(1)}, u32[]{:S(2)}, u32[]{:S(2)}) collective-permute-start(f32[8,4096]{1,0:T(8,128)S(1)} %copy-done), channel_id=1, source_target_pairs={{0,8},{8,0},{16,24},{24,16},{1,9},{9,1},{17,25},{25,17},{2,10},{10... | collective-permute-start | bytes 393224 | tf_op jit(solution)/shard_map/ppermute | solution.py:581
  33.7 14.5 %copy-start.3 = (f32[2,2,32,8,128]{4,3,2,1,0:T(8,128)}, f32[2,2,32,8,128]{4,3,2,1,0:T(8,128)S(1)}, u32[]{:S(2)}) copy-start(f32[2,2,32,8,128]{4,3,2,1,0:T(8,128)S(1)} %pad_maximum_fusion.refs_10_.refs_13_) | copy-start | bytes 1572868
  33.7 14.5 %collective-permute-start.9 = (f32[2,2,32,8,128]{4,3,2,1,0:T(8,128)S(1)}, f32[2,2,32,8,128]{4,3,2,1,0:T(8,128)S(1)}, u32[]{:S(2)}, u32[]{:S(2)}) collective-permute-start(f32[2,2,32,8,128]{4,3,2,1,0:T(8,128)S(1)} %pad_maximum_fusion.refs_10_.refs_13_), channel_id=1, source_target_pairs={{0,16},{8,24},{16,0},{24,8},{1,17},{9,25},{17,1},{25,9},{2,18},{10... | collective-permute-start | bytes 1572872 | tf_op jit(solution)/shard_map/ppermute | solution.py:584
  39.4 8.8 %copy-start.4 = (f32[128,8,128]{2,1,0:T(8,128)}, f32[128,8,128]{2,1,0:T(8,128)S(1)}, u32[]{:S(2)}) copy-start(f32[128,8,128]{2,1,0:T(8,128)S(1)} %collective-permute-done.refs_0_.refs_1_) | copy-start | bytes 1572868
  39.4 8.8 %copy-start.5 = (f32[128,8,128]{2,1,0:T(8,128)}, f32[128,8,128]{2,1,0:T(8,128)S(1)}, u32[]{:S(2)}) copy-start(f32[128,8,128]{2,1,0:T(8,128)S(1)} %collective-permute-done.1.refs_3_.refs_2_) | copy-start | bytes 1572868
  39.5 21.2 %collective-permute-start.3 = (f32[128,8,128]{2,1,0:T(8,128)S(1)}, f32[128,8,128]{2,1,0:T(8,128)S(1)}, u32[]{:S(2)}, u32[]{:S(2)}) collective-permute-start(f32[128,8,128]{2,1,0:T(8,128)S(1)} %copy-done.8), channel_id=1, source_target_pairs={{1,0},{2,1},{3,2},{4,3},{5,4},{6,5},{7,6},{9,8},{10,9},{11,10},{12... | collective-permute-start | bytes 1572872 | tf_op jit(solution)/shard_map/ppermute | solution.py:591
  40.8 26.5 %collective-permute-start.2 = (f32[128,8,128]{2,1,0:T(8,128)S(1)}, f32[128,8,128]{2,1,0:T(8,128)S(1)}, u32[]{:S(2)}, u32[]{:S(2)}) collective-permute-start(f32[128,8,128]{2,1,0:T(8,128)S(1)} %copy-done.7), channel_id=1, source_target_pairs={{0,1},{1,2},{2,3},{3,4},{4,5},{5,6},{6,7},{8,9},{9,10},{10,11},{11... | collective-permute-start | bytes 1572872 | tf_op jit(solution)/shard_map/ppermute | solution.py:591
  45.9 14.7 %collective-permute-start.5 = (f32[2,8,4096]{2,1,0:T(8,128)S(1)}, f32[2,8,4096]{2,1,0:T(8,128)S(1)}, u32[]{:S(2)}, u32[]{:S(2)}) collective-permute-start(f32[2,8,4096]{2,1,0:T(8,128)S(1)} %pad_maximum_fusion.1), channel_id=1, source_target_pairs={{0,16},{8,24},{16,0},{24,8},{1,17},{9,25},{17,1},{25,9},{2,18},{10... | collective-permute-start | bytes 786440 | tf_op jit(solution)/shard_map/ppermute | solution.py:584
  48.2 0.8 copy-start.6
  60.7 6.6 %copy-start.9 = (f32[128,8,128]{2,1,0:T(8,128)}, f32[128,8,128]{2,1,0:T(8,128)S(1)}, u32[]{:S(2)}) copy-start(f32[128,8,128]{2,1,0:T(8,128)S(1)} %collective-permute-done.3.refs_3_) | copy-start | bytes 1572868
  67.2 0.8 copy-start.10
  84.2 3.9 %collective-permute-start.10 = (f32[8,2048]{1,0:T(8,128)}, f32[8,2048]{1,0:T(8,128)S(1)}, u32[]{:S(2)}, u32[]{:S(2)}) collective-permute-start(f32[8,2048]{1,0:T(8,128)} %get-tuple-element.65), channel_id=1, source_target_pairs={{0,8},{8,0},{16,24},{24,16},{1,9},{9,1},{17,25},{25,17},{2,10},{10... | collective-permute-start | bytes 196616 | tf_op jit(solution)/shard_map/ppermute | solution.py:581
  84.4 3.8 %copy-start.11 = (f32[8,2048]{1,0:T(8,128)S(1)}, f32[8,2048]{1,0:T(8,128)}, u32[]{:S(2)}) copy-start(f32[8,2048]{1,0:T(8,128)} %get-tuple-element.65) | copy-start | bytes 196612
  84.4 9.7 %copy-start.1 = (f32[8,2048]{1,0:T(8,128)S(1)}, f32[8,2048]{1,0:T(8,128)}, u32[]{:S(2)}) copy-start(f32[8,2048]{1,0:T(8,128)} %values.1) | copy-start | bytes 196612
  84.4 9.7 %copy-start.2 = (f32[2048]{0:T(1024)S(1)}, f32[2048]{0:T(1024)}, u32[]{:S(2)}) copy-start(f32[2048]{0:T(1024)} %param.12) | copy-start | bytes 24580
  88.2 6.0 %collective-permute-start.11 = (f32[2,8,2048]{2,1,0:T(8,128)S(1)}, f32[2,8,2048]{2,1,0:T(8,128)S(1)}, u32[]{:S(2)}, u32[]{:S(2)}) collective-permute-start(f32[2,8,2048]{2,1,0:T(8,128)S(1)} %pad_maximum_fusion.3.pair), channel_id=1, source_target_pairs={{0,16},{8,24},{16,0},{24,8},{1,17},{9,25},{17,1},{25,9},{2,18},{10... | collective-permute-start | bytes 393224 | tf_op jit(solution)/shard_map/ppermute | solution.py:584
  94.8 6.2 %collective-permute-start.12 = (f32[32,40]{1,0:T(8,128)S(1)}, f32[32,40]{1,0:T(8,128)S(1)}, u32[]{:S(2)}, u32[]{:S(2)}) collective-permute-start(f32[32,40]{1,0:T(8,128)S(1)} %products.1), channel_id=1, source_target_pairs={{0,1},{1,0},{2,3},{3,2},{4,5},{5,4},{6,7},{7,6},{8,9},{9,8},{10,11... | collective-permute-start | bytes 15368 | tf_op jit(solution)/shard_map/ppermute | solution.py:639
  101.0 3.8 %collective-permute-start.13 = (f32[32,40]{1,0:T(8,128)S(1)}, f32[32,40]{1,0:T(8,128)S(1)}, u32[]{:S(2)}, u32[]{:S(2)}) collective-permute-start(f32[32,40]{1,0:T(8,128)S(1)} %add.67), channel_id=1, source_target_pairs={{0,2},{1,3},{2,0},{3,1},{4,6},{5,7},{6,4},{7,5},{8,10},{9,11},{10,... | collective-permute-start | bytes 15368 | tf_op jit(solution)/shard_map/ppermute | solution.py:639
  104.9 4.6 %collective-permute-start.14 = (f32[32,40]{1,0:T(8,128)S(1)}, f32[32,40]{1,0:T(8,128)S(1)}, u32[]{:S(2)}, u32[]{:S(2)}) collective-permute-start(f32[32,40]{1,0:T(8,128)S(1)} %add.68), channel_id=1, source_target_pairs={{0,4},{1,5},{2,6},{3,7},{4,0},{5,1},{6,2},{7,3},{8,12},{9,13},{10,... | collective-permute-start | bytes 15368 | tf_op jit(solution)/shard_map/ppermute | solution.py:639

commit v14 on v13

--- a/solution.py
+++ b/solution.py
@@ -485,7 +485,7 @@
         scratch(columns, dma((29,))), 10,
         [low0, own[0], own[3], high0, *inner, own_coef, pair, other, params, place_of],
     )
-    high1, *all_params = lax.optimization_barrier((high1, *share_params(inner[0])))
+    place_of, *all_params = lax.optimization_barrier((place_of, *share_params(inner[0])))
     obs_row, obs_col = obs_index // columns, obs_index % columns
     width = FOLD * LANES
     obs_block = obs_col // width * FOLD + obs_col % FOLD
@@ -521,10 +521,12 @@
     return write_field, predicted, all_params
 
 
-def products_kernel(total_obs, per_group, spread, pair, other, values, variance, same, out):
+def products_kernel(
+    total_obs, per_group, spread, own, second, third, fourth, values, variance, same, out
+):
     weight = 1.0 / (variance[...] * total_obs)
-    predicted = jnp.concatenate([pair[0], pair[1], other[0], other[1]], axis=0)
-    innovation = (values[...] - pair[0]) * weight
+    predicted = jnp.concatenate([own[...], second[...], third[...], fourth[...]], axis=0)
+    innovation = (values[...] - own[...]) * weight
     anomalies = (predicted - hdot(same[...], predicted) / per_group) * spread
     right = jnp.concatenate([anomalies * weight, innovation], axis=0)
     out[...] = lax.dot_general(
@@ -622,25 +624,31 @@
     all_params = jnp.concatenate(all_params, axis=0).reshape(members, columns)
     param_anomalies = (all_params - hdot(same, all_params) / per_group) * spread
 
-    near = jnp.stack([predicted, next_core(predicted)])
-    field = write_field(0, None)
-    near, field = lax.optimization_barrier((near, field))
-    far = next_chip(near)
+    others = [
+        lax.ppermute(predicted, "ens", [(i, i ^ step) for i in range(ens_count)])
+        for step in range(1, ens_count)
+    ]
+    *others, field = lax.optimization_barrier((*others, write_field(0, None)))
     total_obs = obs_variance.shape[0] * slab_count
     products = pl.pallas_call(
         functools.partial(products_kernel, float(total_obs), per_group, spread),
         out_shape=jax.ShapeDtypeStruct((members, members + local_members), jnp.float32),
         compiler_params=pltpu.CompilerParams(vmem_limit_bytes=VMEM_LIMIT),
         name="products",
-    )(near, far, obs_values, obs_variance[None, :], same)
+    )(predicted, *others, obs_values, obs_variance[None, :], same)
     distance = 1
     while distance < slab_count:
-        pairs = [(i, i ^ distance) for i in range(slab_count)]
-        arrived = lax.ppermute(products, "slab", pairs)
+        radix = 4 if slab_count // distance % 4 == 0 else 2
+        arrived = [
+            lax.ppermute(products, "slab", [(i, i ^ (step * distance)) for i in range(slab_count)])
+            for step in range(1, radix)
+        ]
         if distance == 1:
-            arrived, field = lax.optimization_barrier((arrived, write_field(1, field)))
-        products = products + arrived
-        distance *= 2
+            *arrived, field = lax.optimization_barrier((*arrived, write_field(1, field)))
+        products = products + arrived[0]
+        if radix == 4:
+            products = products + (arrived[1] + arrived[2])
+        distance *= radix
     updated = pl.pallas_call(
         functools.partial(update_kernel, per_group),
         out_shape=jax.ShapeDtypeStruct(parameters.shape, jnp.float32),

time: 112 us -> 107 us (0.955)
  waiting for transfers between devices: 18.5 us -> 12.4 us
    ppermute x3, waiting for transfers between devices: 10.7 us -> 2.87 us  [halos(): lax.ppermute(upper, 'slab', forward)]
    ppermute x3 -> x2, waiting for transfers between devices: 4.29 us -> 6.92 us  [next_chip(): return lax.ppermute(value, 'ens', [(i, i ^ 2) for i in range(ens_count)])]
    ppermute x3 -> x7, starting transfers between devices: 6.75 us -> 8.72 us  [the longest x4 6.78 us: local(): lax.ppermute(products, 'slab', [(i, i ^ step * distance) for i in range(s...]
    ppermute x3 -> x2, starting transfers between devices: 4.76 us -> 3.17 us  [next_chip(): return lax.ppermute(value, 'ens', [(i, i ^ 2) for i in range(ens_count)])]
    ppermute x3 -> x7, waiting for transfers between devices: 3.5 us -> 2.62 us  [the longest x4 2.37 us: local(): lax.ppermute(products, 'slab', [(i, i ^ step * distance) for i in range(s...]
  transfers between devices with their start and end apart: 15 -> 17, of which waited for: 5 -> 5; matrix products, arithmetic and copies ran while one was open for 2% -> 2% of each run, Pallas kernels for 31% -> 33%
where the time goes in v14:
time: 107 us; the launch traced here: 106 us
  Pallas kernels  58 us (54%)
  starting transfers between devices  31.2 us (29%)
  waiting for transfers between devices  12.4 us (12%)
  local copies, waits for them, and re-layouts  2.06 us (2%)
  other arithmetic  1.1 us (1%)
    pallas_call x7, Pallas kernels, kernel_call(): pl.pallas_call(body, out_shape=tuple((jax.ShapeDtypeStruct(shape, jnp.flo...  55.3 us
    ppermute x3, starting transfers between devices, halos(): lax.ppermute(upper, 'slab', forward)  14.6 us
    ppermute x2, waiting for transfers between devices, next_chip(): return lax.ppermute(value, 'ens', [(i, i ^ 2) for i in range(ens_count)])  6.92 us
    ppermute x4, starting transfers between devices, local(): lax.ppermute(products, 'slab', [(i, i ^ step * distance) for i in range(s...  6.78 us
    ppermute x3, starting transfers between devices, halos(): lax.ppermute(lower, 'slab', backward)  4.06 us
    ppermute x2, starting transfers between devices, next_chip(): return lax.ppermute(value, 'ens', [(i, i ^ 2) for i in range(ens_count)])  3.17 us
    ppermute x3, waiting for transfers between devices, halos(): lax.ppermute(upper, 'slab', forward)  2.87 us
    ppermute x4, waiting for transfers between devices, local(): lax.ppermute(products, 'slab', [(i, i ^ step * distance) for i in range(s...  2.37 us
  transfers between devices with their start and end apart: 17, of which 5 were waited for; matrix products, arithmetic and copies ran while one was open for 2% of the time, Pallas kernels for 33%

profile of v14, /device:TPU:0, one launch (start us, length us, event | category | flops | bytes accessed | tf_op | source)
XLA Modules:
  0.0 106.2 jit_solution(13364424304545692845)
XLA Ops:
  0.6 4.3 %outer_rows.1 = (f32[128,8,128]{2,1,0:T(8,128)}, f32[128,8,128]{2,1,0:T(8,128)}, f32[32,8,128]{2,1,0:T(8,128)}, f32[32,8,128]{2,1,0:T(8,128)}) custom-call(f32[128,4096]{1,0:T(8,128)} %bitcast.36, f32[4,16,4096]{2,1,0:T(8,128)} %own_coef.3, s32[1]{0:T(128)} %bitcast.1.place_of.refs_13_.refs_16_), custom_call_target="tpu_custom_call" | custom-call | bytes 600000 | tf_op jit(solution)/shard_map/outer_rows/pallas_call | solution.py:421
  5.0 1.3 %collective-permute-start.5 = (f32[32,8,128]{2,1,0:T(8,128)}, f32[32,8,128]{2,1,0:T(8,128)S(1)}, u32[]{:S(2)}, u32[]{:S(2)}) collective-permute-start(f32[32,8,128]{2,1,0:T(8,128)} %get-tuple-element.58), channel_id=1, source_target_pairs={{1,0},{2,1},{3,2},{4,3},{5,4},{6,5},{7,6},{9,8},{10,9},{11,10},{12... | collective-permute-start | bytes 393224 | tf_op jit(solution)/shard_map/ppermute | solution.py:593
  6.3 5.5 %collective-permute-start.4 = (f32[32,8,128]{2,1,0:T(8,128)}, f32[32,8,128]{2,1,0:T(8,128)S(1)}, u32[]{:S(2)}, u32[]{:S(2)}) collective-permute-start(f32[32,8,128]{2,1,0:T(8,128)} %get-tuple-element.57), channel_id=1, source_target_pairs={{0,1},{1,2},{2,3},{3,4},{4,5},{5,6},{6,7},{8,9},{9,10},{10,11},{11... | collective-permute-start | bytes 393224 | tf_op jit(solution)/shard_map/ppermute | solution.py:593
  11.8 4.8 %collective-permute-start = (f32[128,8,128]{2,1,0:T(8,128)}, f32[128,8,128]{2,1,0:T(8,128)S(1)}, u32[]{:S(2)}, u32[]{:S(2)}) collective-permute-start(f32[128,8,128]{2,1,0:T(8,128)} %get-tuple-element.42.outer.own3.refs_2_), channel_id=1, source_target_pairs={{0,1},{1,2},{2,3},{3,4},{4,5},{5,6},{6,7},{8,9},{9,10},{10,11},{11... | collective-permute-start | bytes 1572872 | tf_op jit(solution)/shard_map/ppermute | solution.py:593
  16.6 1.3 %collective-permute-start.1 = (f32[128,8,128]{2,1,0:T(8,128)}, f32[128,8,128]{2,1,0:T(8,128)S(1)}, u32[]{:S(2)}, u32[]{:S(2)}) collective-permute-start(f32[128,8,128]{2,1,0:T(8,128)} %get-tuple-element.45.own0.refs_1_), channel_id=1, source_target_pairs={{1,0},{2,1},{3,2},{4,3},{5,4},{6,5},{7,6},{9,8},{10,9},{11,10},{12... | collective-permute-start | bytes 1572872 | tf_op jit(solution)/shard_map/ppermute | solution.py:593
  17.9 0.0 collective-permute-done.5
  17.9 0.0 collective-permute-done.4
  18.0 0.1 collective-permute-start.6
  18.1 6.4 %inner_rows.1 = (f32[128,8,128]{2,1,0:T(8,128)}, f32[128,8,128]{2,1,0:T(8,128)}, f32[32,64,128]{2,1,0:T(8,128)}, f32[8,4096]{1,0:T(8,128)}) custom-call(f32[128,4096]{1,0:T(8,128)} %bitcast.37, f32[4,16,4096]{2,1,0:T(8,128)} %own_coef.3, f32[8,4096]{1,0:T(8,128)} %own.1, f32[128,8,128]{2,1,0:T(8,128)} %get-tuple-element.42.outer.own3.refs_2_), custom_call_target="tpu_custom_call" | custom-call | bytes 600000 | tf_op jit(solution)/shard_map/inner_rows/pallas_call | solution.py:421
  24.5 0.0 copy-start
  24.5 0.0 copy-start.13
  24.5 0.0 copy-start.9
  24.5 0.0 copy-start.8
  24.5 0.0 copy-start.12
  24.5 9.3 %interior.1 = (f32[128,8,128]{2,1,0:T(8,128)}, f32[128,8,128]{2,1,0:T(8,128)}, f32[128,8,128]{2,1,0:T(8,128)}, f32[128,8,128]{2,1,0:T(8,128)}, f32[128,8,128]{2,1,0:T(8,128)}) custom-call(f32[128,8,128]{2,1,0:T(8,128)} %get-tuple-element.45.own0.refs_1_, f32[128,8,128]{2,1,0:T(8,128)} %get-tuple-element.52.own1, f32[128,8,128]{2,1,0:T(8,128)} %get-tuple-element.49.own2, ...), custom_call_target="tpu_custom_call" | custom-call | bytes 1600000 | tf_op jit(solution)/shard_map/interior/pallas_call | solution.py:421
  33.9 0.0 copy-done
  33.9 0.6 collective-permute-start.8
  34.4 0.0 copy-done.13
  34.4 0.1 reshape.23
  34.5 0.0 collective-permute-done.6
  34.5 0.1 pad_maximum_fusion.refs_10_.refs_13_
  34.6 1.6 %collective-permute-start.7 = (f32[2,2,32,8,128]{4,3,2,1,0:T(8,128)S(1)}, f32[2,2,32,8,128]{4,3,2,1,0:T(8,128)S(1)}, u32[]{:S(2)}, u32[]{:S(2)}) collective-permute-start(f32[2,2,32,8,128]{4,3,2,1,0:T(8,128)S(1)} %pad_maximum_fusion.refs_10_.refs_13_), channel_id=1, source_target_pairs={{0,16},{8,24},{16,0},{24,8},{1,17},{9,25},{17,1},{25,9},{2,18},{10... | collective-permute-start | bytes 1572872 | tf_op jit(solution)/shard_map/ppermute | solution.py:586
  36.2 2.9 %collective-permute-done.refs_0_.refs_1_ = f32[128,8,128]{2,1,0:T(8,128)S(1)} collective-permute-done((f32[128,8,128]{2,1,0:T(8,128)}, f32[128,8,128]{2,1,0:T(8,128)S(1)}, u32[]{:S(2)}, u32[]{:S(2)}) %collective-permute-start) | collective-permute-done | bytes 524320 | tf_op jit(solution)/shard_map/ppermute | solution.py:593
  39.1 0.0 collective-permute-done.1.refs_3_.refs_2_
  39.1 0.0 copy-done.9
  39.1 4.3 %collective-permute-start.2 = (f32[128,8,128]{2,1,0:T(8,128)S(1)}, f32[128,8,128]{2,1,0:T(8,128)S(1)}, u32[]{:S(2)}, u32[]{:S(2)}) collective-permute-start(f32[128,8,128]{2,1,0:T(8,128)S(1)} %copy-done.9), channel_id=1, source_target_pairs={{0,1},{1,2},{2,3},{3,4},{4,5},{5,6},{6,7},{8,9},{9,10},{10,11},{11... | collective-permute-start | bytes 1572872 | tf_op jit(solution)/shard_map/ppermute | solution.py:593
  43.4 0.0 copy-done.8
  43.4 1.5 %collective-permute-start.3 = (f32[128,8,128]{2,1,0:T(8,128)S(1)}, f32[128,8,128]{2,1,0:T(8,128)S(1)}, u32[]{:S(2)}, u32[]{:S(2)}) collective-permute-start(f32[128,8,128]{2,1,0:T(8,128)S(1)} %copy-done.8), channel_id=1, source_target_pairs={{1,0},{2,1},{3,2},{4,3},{5,4},{6,5},{7,6},{9,8},{10,9},{11,10},{12... | collective-permute-start | bytes 1572872 | tf_op jit(solution)/shard_map/ppermute | solution.py:593
  44.9 0.0 collective-permute-done.8
  44.9 1.6 %collective-permute-start.9 = (f32[2,8,4096]{2,1,0:T(8,128)S(1)}, f32[2,8,4096]{2,1,0:T(8,128)S(1)}, u32[]{:S(2)}, u32[]{:S(2)}) collective-permute-start(f32[2,8,4096]{2,1,0:T(8,128)S(1)} %pad_maximum_fusion.2), channel_id=1, source_target_pairs={{0,16},{8,24},{16,0},{24,8},{1,17},{9,25},{17,1},{25,9},{2,18},{10... | collective-permute-start | bytes 786440 | tf_op jit(solution)/shard_map/ppermute | solution.py:586
  46.5 0.1 pad_add_fusion
  46.6 0.6 add_select_fusion
  47.2 6.9 %collective-permute-done.9 = f32[2,8,4096]{2,1,0:T(8,128)S(1)} collective-permute-done((f32[2,8,4096]{2,1,0:T(8,128)S(1)}, f32[2,8,4096]{2,1,0:T(8,128)S(1)}, u32[]{:S(2)}, u32[]{:S(2)}) %collective-permute-start.9) | collective-permute-done | bytes 262176 | tf_op jit(solution)/shard_map/ppermute | solution.py:586
  54.2 0.0 collective-permute-done.7.refs_11_.refs_14_
  54.2 0.8 copy-done.7
  54.9 11.6 %edge_first.1 = (f32[128,8,128]{2,1,0:T(8,128)}, f32[128,8,128]{2,1,0:T(8,128)}, f32[128,8,128]{2,1,0:T(8,128)}, f32[128,8,128]{2,1,0:T(8,128)}, f32[128,8,128]{...) custom-call(f32[128,8,128]{2,1,0:T(8,128)} %copy-done.5, ...), custom_call_target="tpu_custom_call" | custom-call | bytes 2000000 | tf_op jit(solution)/shard_map/edge_first/pallas_call | solution.py:421
  66.6 0.0 collective-permute-done.2.refs_0_
  66.6 0.0 copy-start.10
  66.6 0.0 collective-permute-done.3.refs_3_
  66.6 0.8 copy-done.10
  67.4 0.3 copy-done.11
  67.7 16.2 %edge_last.1 = (f32[128,8,128]{2,1,0:T(8,128)}, f32[128,8,128]{2,1,0:T(8,128)}, f32[8,2048]{1,0:T(8,128)}) custom-call(f32[128,8,128]{2,1,0:T(8,128)} %copy-done.10, f32[128,8,128]{2,1,0:T(8,128)} %copy-done.5, f32[128,8,128]{2,1,0:T(8,128)} %copy-done.6, f32[128,8,128]{2,1,0:T(8,128)} %copy-done.11, f32[128,8,128]{2,1,0:T(8,128)} %get-tuple-element.59.refs_4_, ...), custom_call_target="tpu_custom_call" | custom-call | bytes 3000000 | tf_op jit(solution)/shard_map/edge_last/pallas_call | solution.py:421
  83.9 0.1 collective-permute-start.10
  83.9 1.6 %collective-permute-start.11 = (f32[8,2048]{1,0:T(8,128)}, f32[8,2048]{1,0:T(8,128)S(1)}, u32[]{:S(2)}, u32[]{:S(2)}) collective-permute-start(f32[8,2048]{1,0:T(8,128)} %get-tuple-element.69.own), channel_id=1, source_target_pairs={{0,16},{8,24},{16,0},{24,8},{1,17},{9,25},{17,1},{25,9},{2,18},{10... | collective-permute-start | bytes 196616 | tf_op jit(solution)/shard_map/ppermute | solution.py:628
  85.5 0.3 collective-permute-start.12
  85.8 0.1 compare_convert_fusion.same
  85.9 3.7 %field_0.1.refs_4_ = f32[128,4096]{1,0:T(8,128)} custom-call(f32[128,8,128]{2,1,0:T(8,128)} %get-tuple-element.70.refs_0_, f32[128,8,128]{2,1,0:T(8,128)} %get-tuple-element.65.refs_10_.refs_1_, f32[128,8,128]{2,1,0:T(8,128)} %get-tuple-element.66.refs_11_.refs_2_, f32[128,8,128]{2,1,0:T(8,128)} %get-tuple-element.71.refs_3_), custom_call_target="tpu_custom_call" | custom-call | bytes 800000 | tf_op jit(solution)/shard_map/field_0/pallas_call | solution.py:421
  89.6 0.0 collective-permute-done.10.second
  89.6 0.0 collective-permute-done.11.third
  89.6 0.2 collective-permute-done.12.fourth
  89.9 0.6 products.1
  90.5 2.7 %collective-permute-start.13 = (f32[32,40]{1,0:T(8,128)S(1)}, f32[32,40]{1,0:T(8,128)S(1)}, u32[]{:S(2)}, u32[]{:S(2)}) collective-permute-start(f32[32,40]{1,0:T(8,128)S(1)} %products.1), channel_id=1, source_target_pairs={{0,1},{1,0},{2,3},{3,2},{4,5},{5,4},{6,7},{7,6},{8,9},{9,8},{10,11... | collective-permute-start | bytes 15368 | tf_op jit(solution)/shard_map/ppermute | solution.py:643
  93.2 1.6 %collective-permute-start.14 = (f32[32,40]{1,0:T(8,128)S(1)}, f32[32,40]{1,0:T(8,128)S(1)}, u32[]{:S(2)}, u32[]{:S(2)}) collective-permute-start(f32[32,40]{1,0:T(8,128)S(1)} %products.1), channel_id=1, source_target_pairs={{0,2},{1,3},{2,0},{3,1},{4,6},{5,7},{6,4},{7,5},{8,10},{9,11},{10,... | collective-permute-start | bytes 15368 | tf_op jit(solution)/shard_map/ppermute | solution.py:643
  94.8 0.0 collective-permute-start.15
  94.8 0.2 convert_reduce_fusion
  95.0 0.1 copy.10.rank_col
  95.1 3.7 %field_1.1 = f32[128,4096]{1,0:T(8,128)} custom-call(f32[128,8,128]{2,1,0:T(8,128)} %get-tuple-element.70.refs_0_, f32[128,8,128]{2,1,0:T(8,128)} %get-tuple-element.65.refs_10_.refs_1_, f32[128,8,128]{2,1,0:T(8,128)} %get-tuple-element.66.refs_11_.refs_2_, f32[128,8,128]{2,1,0:T(8,128)} %get-tuple-element.71.refs_3_, ...), custom_call_target="tpu_custom_call", output_to_operand_aliasing={{}: (4, {})} | custom-call | bytes 800000 | tf_op jit(solution)/shard_map/field_1/pallas_call | solution.py:421
  98.8 0.0 collective-permute-done.13
  98.8 0.0 collective-permute-done.14
  98.8 0.6 collective-permute-done.15
  99.4 2.5 %collective-permute-start.16 = (f32[32,40]{1,0:T(8,128)S(1)}, f32[32,40]{1,0:T(8,128)S(1)}, u32[]{:S(2)}, u32[]{:S(2)}) collective-permute-start(f32[32,40]{1,0:T(8,128)S(1)} %add_add_fusion), channel_id=1, source_target_pairs={{0,4},{1,5},{2,6},{3,7},{4,0},{5,1},{6,2},{7,3},{8,12},{9,13},{10,... | collective-permute-start | bytes 15368 | tf_op jit(solution)/shard_map/ppermute | solution.py:643
  101.9 0.4 fusion.1.anomalies
  102.4 1.7 %collective-permute-done.16 = f32[32,40]{1,0:T(8,128)S(1)} collective-permute-done((f32[32,40]{1,0:T(8,128)S(1)}, f32[32,40]{1,0:T(8,128)S(1)}, u32[]{:S(2)}, u32[]{:S(2)}) %collective-permute-start.16) | collective-permute-done | bytes 5152 | tf_op jit(solution)/shard_map/ppermute | solution.py:643
  104.1 2.1 %update.1 = f32[8,4096]{1,0:T(8,128)} custom-call(f32[1,32,40]{2,1,0:T(8,128)S(1)} %add_bitcast_fusion.summands, f32[32,32]{1,0:T(8,128)S(1)} %compare_convert_fusion.same, f32[32,8]{1,0:T(8,128)S(1)} %bitcast.31, s32[1,32]{1,0:T(1,128)S(1)} %bitcast.34, s32[32,1]{1,0:T(8,128)S(1)} %copy.10.rank_col, f32[32,4096]{1,0:T(8,128)S(1)} %fusion.1.anomalies, ...), custom_call_target="tpu_custom_call" | custom-call | tf_op jit(solution)/shard_map/update/pallas_call | solution.py:652
  (20 shorter events, 0.1 us)
Async XLA Ops:
  5.0 12.9 %collective-permute-start.5 = (f32[32,8,128]{2,1,0:T(8,128)}, f32[32,8,128]{2,1,0:T(8,128)S(1)}, u32[]{:S(2)}, u32[]{:S(2)}) collective-permute-start(f32[32,8,128]{2,1,0:T(8,128)} %get-tuple-element.58), channel_id=1, source_target_pairs={{1,0},{2,1},{3,2},{4,3},{5,4},{6,5},{7,6},{9,8},{10,9},{11,10},{12... | collective-permute-start | bytes 393224 | tf_op jit(solution)/shard_map/ppermute | solution.py:593
  6.3 11.7 %collective-permute-start.4 = (f32[32,8,128]{2,1,0:T(8,128)}, f32[32,8,128]{2,1,0:T(8,128)S(1)}, u32[]{:S(2)}, u32[]{:S(2)}) collective-permute-start(f32[32,8,128]{2,1,0:T(8,128)} %get-tuple-element.57), channel_id=1, source_target_pairs={{0,1},{1,2},{2,3},{3,4},{4,5},{5,6},{6,7},{8,9},{9,10},{10,11},{11... | collective-permute-start | bytes 393224 | tf_op jit(solution)/shard_map/ppermute | solution.py:593
  11.8 27.3 %collective-permute-start = (f32[128,8,128]{2,1,0:T(8,128)}, f32[128,8,128]{2,1,0:T(8,128)S(1)}, u32[]{:S(2)}, u32[]{:S(2)}) collective-permute-start(f32[128,8,128]{2,1,0:T(8,128)} %get-tuple-element.42.outer.own3.refs_2_), channel_id=1, source_target_pairs={{0,1},{1,2},{2,3},{3,4},{4,5},{5,6},{6,7},{8,9},{9,10},{10,11},{11... | collective-permute-start | bytes 1572872 | tf_op jit(solution)/shard_map/ppermute | solution.py:593
  16.6 22.4 %collective-permute-start.1 = (f32[128,8,128]{2,1,0:T(8,128)}, f32[128,8,128]{2,1,0:T(8,128)S(1)}, u32[]{:S(2)}, u32[]{:S(2)}) collective-permute-start(f32[128,8,128]{2,1,0:T(8,128)} %get-tuple-element.45.own0.refs_1_), channel_id=1, source_target_pairs={{1,0},{2,1},{3,2},{4,3},{5,4},{6,5},{7,6},{9,8},{10,9},{11,10},{12... | collective-permute-start | bytes 1572872 | tf_op jit(solution)/shard_map/ppermute | solution.py:593
  18.0 16.5 %collective-permute-start.6 = (f32[2,32,8,128]{3,2,1,0:T(8,128)S(1)}, f32[2,32,8,128]{3,2,1,0:T(8,128)S(1)}, u32[]{:S(2)}, u32[]{:S(2)}) collective-permute-start(f32[2,32,8,128]{3,2,1,0:T(8,128)S(1)} %get-tuple-element.83), channel_id=1, source_target_pairs={{0,8},{8,0},{16,24},{24,16},{1,9},{9,1},{17,25},{25,17},{2,10},{10... | collective-permute-start | bytes 786440 | tf_op jit(solution)/shard_map/ppermute | solution.py:583
  24.5 9.4 %copy-start = (f32[8,4096]{1,0:T(8,128)S(1)}, f32[8,4096]{1,0:T(8,128)}, u32[]{:S(2)}) copy-start(f32[8,4096]{1,0:T(8,128)} %own.1) | copy-start | bytes 393220
  24.5 9.9 %copy-start.13 = (s32[32]{0:T(128)S(1)}, s32[32]{0:T(128)}, u32[]{:S(2)}) copy-start(s32[32]{0:T(128)} %param.13) | copy-start | bytes 388
  24.5 14.6 %copy-start.9 = (f32[128,8,128]{2,1,0:T(8,128)S(1)}, f32[128,8,128]{2,1,0:T(8,128)}, u32[]{:S(2)}) copy-start(f32[128,8,128]{2,1,0:T(8,128)} %get-tuple-element.49.own2) | copy-start | bytes 1572868
  24.5 18.9 %copy-start.8 = (f32[128,8,128]{2,1,0:T(8,128)S(1)}, f32[128,8,128]{2,1,0:T(8,128)}, u32[]{:S(2)}) copy-start(f32[128,8,128]{2,1,0:T(8,128)} %get-tuple-element.52.own1) | copy-start | bytes 1572868
  24.5 22.1 %copy-start.12 = (s32[2048]{0:T(1024)S(1)}, s32[2048]{0:T(1024)}, u32[]{:S(2)}) copy-start(s32[2048]{0:T(1024)} %param.10) | copy-start | bytes 24580
  33.9 11.0 %collective-permute-start.8 = (f32[8,4096]{1,0:T(8,128)S(1)}, f32[8,4096]{1,0:T(8,128)S(1)}, u32[]{:S(2)}, u32[]{:S(2)}) collective-permute-start(f32[8,4096]{1,0:T(8,128)S(1)} %copy-done), channel_id=1, source_target_pairs={{0,8},{8,0},{16,24},{24,16},{1,9},{9,1},{17,25},{25,17},{2,10},{10... | collective-permute-start | bytes 393224 | tf_op jit(solution)/shard_map/ppermute | solution.py:583
  34.6 19.6 %copy-start.4 = (f32[2,2,32,8,128]{4,3,2,1,0:T(8,128)}, f32[2,2,32,8,128]{4,3,2,1,0:T(8,128)S(1)}, u32[]{:S(2)}) copy-start(f32[2,2,32,8,128]{4,3,2,1,0:T(8,128)S(1)} %pad_maximum_fusion.refs_10_.refs_13_) | copy-start | bytes 1572868
  34.6 19.6 %collective-permute-start.7 = (f32[2,2,32,8,128]{4,3,2,1,0:T(8,128)S(1)}, f32[2,2,32,8,128]{4,3,2,1,0:T(8,128)S(1)}, u32[]{:S(2)}, u32[]{:S(2)}) collective-permute-start(f32[2,2,32,8,128]{4,3,2,1,0:T(8,128)S(1)} %pad_maximum_fusion.refs_10_.refs_13_), channel_id=1, source_target_pairs={{0,16},{8,24},{16,0},{24,8},{1,17},{9,25},{17,1},{25,9},{2,18},{10... | collective-permute-start | bytes 1572872 | tf_op jit(solution)/shard_map/ppermute | solution.py:586
  39.1 15.1 %copy-start.5 = (f32[128,8,128]{2,1,0:T(8,128)}, f32[128,8,128]{2,1,0:T(8,128)S(1)}, u32[]{:S(2)}) copy-start(f32[128,8,128]{2,1,0:T(8,128)S(1)} %collective-permute-done.refs_0_.refs_1_) | copy-start | bytes 1572868
  39.1 15.1 %copy-start.6 = (f32[128,8,128]{2,1,0:T(8,128)}, f32[128,8,128]{2,1,0:T(8,128)S(1)}, u32[]{:S(2)}) copy-start(f32[128,8,128]{2,1,0:T(8,128)S(1)} %collective-permute-done.1.refs_3_.refs_2_) | copy-start | bytes 1572868
  39.1 27.5 %collective-permute-start.2 = (f32[128,8,128]{2,1,0:T(8,128)S(1)}, f32[128,8,128]{2,1,0:T(8,128)S(1)}, u32[]{:S(2)}, u32[]{:S(2)}) collective-permute-start(f32[128,8,128]{2,1,0:T(8,128)S(1)} %copy-done.9), channel_id=1, source_target_pairs={{0,1},{1,2},{2,3},{3,4},{4,5},{5,6},{6,7},{8,9},{9,10},{10,11},{11... | collective-permute-start | bytes 1572872 | tf_op jit(solution)/shard_map/ppermute | solution.py:593
  43.4 23.2 %collective-permute-start.3 = (f32[128,8,128]{2,1,0:T(8,128)S(1)}, f32[128,8,128]{2,1,0:T(8,128)S(1)}, u32[]{:S(2)}, u32[]{:S(2)}) collective-permute-start(f32[128,8,128]{2,1,0:T(8,128)S(1)} %copy-done.8), channel_id=1, source_target_pairs={{1,0},{2,1},{3,2},{4,3},{5,4},{6,5},{7,6},{9,8},{10,9},{11,10},{12... | collective-permute-start | bytes 1572872 | tf_op jit(solution)/shard_map/ppermute | solution.py:593
  44.9 9.2 %collective-permute-start.9 = (f32[2,8,4096]{2,1,0:T(8,128)S(1)}, f32[2,8,4096]{2,1,0:T(8,128)S(1)}, u32[]{:S(2)}, u32[]{:S(2)}) collective-permute-start(f32[2,8,4096]{2,1,0:T(8,128)S(1)} %pad_maximum_fusion.2), channel_id=1, source_target_pairs={{0,16},{8,24},{16,0},{24,8},{1,17},{9,25},{17,1},{25,9},{2,18},{10... | collective-permute-start | bytes 786440 | tf_op jit(solution)/shard_map/ppermute | solution.py:586
  54.2 0.8 copy-start.7
  66.6 0.8 copy-start.10
  66.6 1.1 %copy-start.11 = (f32[128,8,128]{2,1,0:T(8,128)}, f32[128,8,128]{2,1,0:T(8,128)S(1)}, u32[]{:S(2)}) copy-start(f32[128,8,128]{2,1,0:T(8,128)S(1)} %collective-permute-done.3.refs_3_) | copy-start | bytes 1572868
  83.9 5.8 %collective-permute-start.10 = (f32[8,2048]{1,0:T(8,128)}, f32[8,2048]{1,0:T(8,128)S(1)}, u32[]{:S(2)}, u32[]{:S(2)}) collective-permute-start(f32[8,2048]{1,0:T(8,128)} %get-tuple-element.69.own), channel_id=1, source_target_pairs={{0,8},{8,0},{16,24},{24,16},{1,9},{9,1},{17,25},{25,17},{2,10},{10... | collective-permute-start | bytes 196616 | tf_op jit(solution)/shard_map/ppermute | solution.py:628
  83.9 5.7 %collective-permute-start.11 = (f32[8,2048]{1,0:T(8,128)}, f32[8,2048]{1,0:T(8,128)S(1)}, u32[]{:S(2)}, u32[]{:S(2)}) collective-permute-start(f32[8,2048]{1,0:T(8,128)} %get-tuple-element.69.own), channel_id=1, source_target_pairs={{0,16},{8,24},{16,0},{24,8},{1,17},{9,25},{17,1},{25,9},{2,18},{10... | collective-permute-start | bytes 196616 | tf_op jit(solution)/shard_map/ppermute | solution.py:628
  85.5 4.3 %collective-permute-start.12 = (f32[8,2048]{1,0:T(8,128)}, f32[8,2048]{1,0:T(8,128)S(1)}, u32[]{:S(2)}, u32[]{:S(2)}) collective-permute-start(f32[8,2048]{1,0:T(8,128)} %get-tuple-element.69.own), channel_id=1, source_target_pairs={{0,24},{8,16},{16,8},{24,0},{1,25},{9,17},{17,9},{25,1},{2,26},{10... | collective-permute-start | bytes 196616 | tf_op jit(solution)/shard_map/ppermute | solution.py:628
  85.9 4.0 %copy-start.1 = (f32[8,2048]{1,0:T(8,128)S(1)}, f32[8,2048]{1,0:T(8,128)}, u32[]{:S(2)}) copy-start(f32[8,2048]{1,0:T(8,128)} %values.1) | copy-start | bytes 196612
  85.9 4.0 %copy-start.2 = (f32[8,2048]{1,0:T(8,128)S(1)}, f32[8,2048]{1,0:T(8,128)}, u32[]{:S(2)}) copy-start(f32[8,2048]{1,0:T(8,128)} %get-tuple-element.69.own) | copy-start | bytes 196612
  85.9 4.0 %copy-start.3 = (f32[2048]{0:T(1024)S(1)}, f32[2048]{0:T(1024)}, u32[]{:S(2)}) copy-start(f32[2048]{0:T(1024)} %param.12) | copy-start | bytes 24580
  90.5 8.2 %collective-permute-start.13 = (f32[32,40]{1,0:T(8,128)S(1)}, f32[32,40]{1,0:T(8,128)S(1)}, u32[]{:S(2)}, u32[]{:S(2)}) collective-permute-start(f32[32,40]{1,0:T(8,128)S(1)} %products.1), channel_id=1, source_target_pairs={{0,1},{1,0},{2,3},{3,2},{4,5},{5,4},{6,7},{7,6},{8,9},{9,8},{10,11... | collective-permute-start | bytes 15368 | tf_op jit(solution)/shard_map/ppermute | solution.py:643
  93.2 5.6 %collective-permute-start.14 = (f32[32,40]{1,0:T(8,128)S(1)}, f32[32,40]{1,0:T(8,128)S(1)}, u32[]{:S(2)}, u32[]{:S(2)}) collective-permute-start(f32[32,40]{1,0:T(8,128)S(1)} %products.1), channel_id=1, source_target_pairs={{0,2},{1,3},{2,0},{3,1},{4,6},{5,7},{6,4},{7,5},{8,10},{9,11},{10,... | collective-permute-start | bytes 15368 | tf_op jit(solution)/shard_map/ppermute | solution.py:643
  94.8 4.6 %collective-permute-start.15 = (f32[32,40]{1,0:T(8,128)S(1)}, f32[32,40]{1,0:T(8,128)S(1)}, u32[]{:S(2)}, u32[]{:S(2)}) collective-permute-start(f32[32,40]{1,0:T(8,128)S(1)} %products.1), channel_id=1, source_target_pairs={{0,3},{1,2},{2,1},{3,0},{4,7},{5,6},{6,5},{7,4},{8,11},{9,10},{10,... | collective-permute-start | bytes 15368 | tf_op jit(solution)/shard_map/ppermute | solution.py:643
  99.4 4.7 %collective-permute-start.16 = (f32[32,40]{1,0:T(8,128)S(1)}, f32[32,40]{1,0:T(8,128)S(1)}, u32[]{:S(2)}, u32[]{:S(2)}) collective-permute-start(f32[32,40]{1,0:T(8,128)S(1)} %add_add_fusion), channel_id=1, source_target_pairs={{0,4},{1,5},{2,6},{3,7},{4,0},{5,1},{6,2},{7,3},{8,12},{9,13},{10,... | collective-permute-start | bytes 15368 | tf_op jit(solution)/shard_map/ppermute | solution.py:643

commit v15 on v14

--- a/solution.py
+++ b/solution.py
@@ -21,7 +21,7 @@
 FIELD_CALLS = 2
 ALL_ROWS = ROWS + 2 * HALO
 VMEM_LIMIT = 16 * 1024 * 1024
-TALL_LIMIT = 58 * 1024 * 1024
+TALL_LIMIT = 60 * 1024 * 1024
 COST_BYTES = 200000
 ANYWHERE = pl.BlockSpec(memory_space=pltpu.HBM)
 IN_VMEM = pl.BlockSpec(memory_space=pltpu.VMEM)
@@ -485,7 +485,8 @@
         scratch(columns, dma((29,))), 10,
         [low0, own[0], own[3], high0, *inner, own_coef, pair, other, params, place_of],
     )
-    place_of, *all_params = lax.optimization_barrier((place_of, *share_params(inner[0])))
+    *first, share_0, share_1 = lax.optimization_barrier((*first, *share_params(inner[0])))
+    all_params = (share_0, share_1)
     obs_row, obs_col = obs_index // columns, obs_index % columns
     width = FOLD * LANES
     obs_block = obs_col // width * FOLD + obs_col % FOLD

time: 107 us -> 106 us (level)
  waiting for transfers between devices: 12.4 us -> 8.53 us
  starting transfers between devices: 31.2 us -> 34.9 us
    ppermute x2, waiting for transfers between devices: 6.92 us -> 1.49 us  [next_chip(): return lax.ppermute(value, 'ens', [(i, i ^ 2) for i in range(ens_count)])]
    ppermute x4, starting transfers between devices: 6.78 us -> 9.71 us  [local(): lax.ppermute(products, 'slab', [(i, i ^ step * distance) for i in range(s...]
    ppermute x3, waiting for transfers between devices: 2.87 us -> 5.51 us  [halos(): lax.ppermute(upper, 'slab', forward)]
    ppermute x4, waiting for transfers between devices: 2.37 us -> 1.28 us  [local(): lax.ppermute(products, 'slab', [(i, i ^ step * distance) for i in range(s...]
where the time goes in v15:
time: 106 us; the launch traced here: 105 us
  Pallas kernels  58.1 us (55%)
  starting transfers between devices  34.9 us (33%)
  waiting for transfers between devices  8.53 us (8%)
  other arithmetic  1.11 us (1%)
    pallas_call x7, Pallas kernels, kernel_call(): pl.pallas_call(body, out_shape=tuple((jax.ShapeDtypeStruct(shape, jnp.flo...  55.3 us
    ppermute x3, starting transfers between devices, halos(): lax.ppermute(upper, 'slab', forward)  15.4 us
    ppermute x4, starting transfers between devices, local(): lax.ppermute(products, 'slab', [(i, i ^ step * distance) for i in range(s...  9.71 us
    ppermute x3, waiting for transfers between devices, halos(): lax.ppermute(upper, 'slab', forward)  5.51 us
    ppermute x3, starting transfers between devices, halos(): lax.ppermute(lower, 'slab', backward)  4.05 us
    ppermute x2, starting transfers between devices, next_chip(): return lax.ppermute(value, 'ens', [(i, i ^ 2) for i in range(ens_count)])  3.17 us
  transfers between devices with their start and end apart: 17, of which 5 were waited for; matrix products, arithmetic and copies ran while one was open for 2% of the time, Pallas kernels for 33%

profile of v15, /device:TPU:0, one launch (start us, length us, event | category | flops | bytes accessed | tf_op | source)
XLA Modules:
  0.0 105.0 jit_solution(17075814383561611225)
XLA Ops:
  0.6 4.3 %outer_rows.1 = (f32[128,8,128]{2,1,0:T(8,128)}, f32[128,8,128]{2,1,0:T(8,128)}, f32[32,8,128]{2,1,0:T(8,128)}, f32[32,8,128]{2,1,0:T(8,128)}) custom-call(f32[128,4096]{1,0:T(8,128)} %bitcast.36, f32[4,16,4096]{2,1,0:T(8,128)} %own_coef.3, s32[1]{0:T(128)} %bitcast.1.place_of.refs_13_.refs_16_), custom_call_target="tpu_custom_call" | custom-call | bytes 600000 | tf_op jit(solution)/shard_map/outer_rows/pallas_call | solution.py:421
  5.0 1.3 %collective-permute-start.5 = (f32[32,8,128]{2,1,0:T(8,128)}, f32[32,8,128]{2,1,0:T(8,128)S(1)}, u32[]{:S(2)}, u32[]{:S(2)}) collective-permute-start(f32[32,8,128]{2,1,0:T(8,128)} %get-tuple-element.65), channel_id=1, source_target_pairs={{1,0},{2,1},{3,2},{4,3},{5,4},{6,5},{7,6},{9,8},{10,9},{11,10},{12... | collective-permute-start | bytes 393224 | tf_op jit(solution)/shard_map/ppermute | solution.py:594
  6.3 5.5 %collective-permute-start.4 = (f32[32,8,128]{2,1,0:T(8,128)}, f32[32,8,128]{2,1,0:T(8,128)S(1)}, u32[]{:S(2)}, u32[]{:S(2)}) collective-permute-start(f32[32,8,128]{2,1,0:T(8,128)} %get-tuple-element.64), channel_id=1, source_target_pairs={{0,1},{1,2},{2,3},{3,4},{4,5},{5,6},{6,7},{8,9},{9,10},{10,11},{11... | collective-permute-start | bytes 393224 | tf_op jit(solution)/shard_map/ppermute | solution.py:594
  11.8 4.8 %collective-permute-start = (f32[128,8,128]{2,1,0:T(8,128)}, f32[128,8,128]{2,1,0:T(8,128)S(1)}, u32[]{:S(2)}, u32[]{:S(2)}) collective-permute-start(f32[128,8,128]{2,1,0:T(8,128)} %get-tuple-element.49.outer.own3.refs_2_), channel_id=1, source_target_pairs={{0,1},{1,2},{2,3},{3,4},{4,5},{5,6},{6,7},{8,9},{9,10},{10,11},{11... | collective-permute-start | bytes 1572872 | tf_op jit(solution)/shard_map/ppermute | solution.py:594
  16.6 1.3 %collective-permute-start.1 = (f32[128,8,128]{2,1,0:T(8,128)}, f32[128,8,128]{2,1,0:T(8,128)S(1)}, u32[]{:S(2)}, u32[]{:S(2)}) collective-permute-start(f32[128,8,128]{2,1,0:T(8,128)} %get-tuple-element.52.own0.refs_1_), channel_id=1, source_target_pairs={{1,0},{2,1},{3,2},{4,3},{5,4},{6,5},{7,6},{9,8},{10,9},{11,10},{12... | collective-permute-start | bytes 1572872 | tf_op jit(solution)/shard_map/ppermute | solution.py:594
  17.9 0.0 collective-permute-done.5
  17.9 0.0 collective-permute-done.4
  18.0 0.1 collective-permute-start.6
  18.1 6.4 %inner_rows.1 = (f32[128,8,128]{2,1,0:T(8,128)}, f32[128,8,128]{2,1,0:T(8,128)}, f32[32,64,128]{2,1,0:T(8,128)}, f32[8,4096]{1,0:T(8,128)}) custom-call(f32[128,4096]{1,0:T(8,128)} %bitcast.37, f32[4,16,4096]{2,1,0:T(8,128)} %own_coef.3, f32[8,4096]{1,0:T(8,128)} %own.1, f32[128,8,128]{2,1,0:T(8,128)} %get-tuple-element.49.outer.own3.refs_2_), custom_call_target="tpu_custom_call" | custom-call | bytes 600000 | tf_op jit(solution)/shard_map/inner_rows/pallas_call | solution.py:421
  24.5 0.0 copy-start
  24.5 0.0 copy-start.11
  24.5 0.0 copy-start.9
  24.5 0.0 copy-start.8
  24.5 0.0 copy-start.10
  24.5 9.3 %interior.1 = (f32[128,8,128]{2,1,0:T(8,128)}, f32[128,8,128]{2,1,0:T(8,128)}, f32[128,8,128]{2,1,0:T(8,128)}, f32[128,8,128]{2,1,0:T(8,128)}, f32[128,8,128]{2,1,0:T(8,128)}) custom-call(f32[128,8,128]{2,1,0:T(8,128)} %get-tuple-element.52.own0.refs_1_, f32[128,8,128]{2,1,0:T(8,128)} %get-tuple-element.59.own1, f32[128,8,128]{2,1,0:T(8,128)} %get-tuple-element.56.own2, ...), custom_call_target="tpu_custom_call" | custom-call | bytes 1600000 | tf_op jit(solution)/shard_map/interior/pallas_call | solution.py:421
  33.9 0.0 copy-done
  33.9 0.6 collective-permute-start.8
  34.4 0.0 copy-done.11
  34.4 0.1 reshape.23
  34.5 0.0 collective-permute-done.6
  34.6 0.1 pad_maximum_fusion.refs_10_.refs_13_
  34.6 1.6 %collective-permute-start.7 = (f32[2,2,32,8,128]{4,3,2,1,0:T(8,128)S(1)}, f32[2,2,32,8,128]{4,3,2,1,0:T(8,128)S(1)}, u32[]{:S(2)}, u32[]{:S(2)}) collective-permute-start(f32[2,2,32,8,128]{4,3,2,1,0:T(8,128)S(1)} %pad_maximum_fusion.refs_10_.refs_13_), channel_id=1, source_target_pairs={{0,16},{8,24},{16,0},{24,8},{1,17},{9,25},{17,1},{25,9},{2,18},{10... | collective-permute-start | bytes 1572872 | tf_op jit(solution)/shard_map/ppermute | solution.py:587
  36.2 2.9 %collective-permute-done.refs_0_.refs_1_ = f32[128,8,128]{2,1,0:T(8,128)S(1)} collective-permute-done((f32[128,8,128]{2,1,0:T(8,128)}, f32[128,8,128]{2,1,0:T(8,128)S(1)}, u32[]{:S(2)}, u32[]{:S(2)}) %collective-permute-start) | collective-permute-done | bytes 524320 | tf_op jit(solution)/shard_map/ppermute | solution.py:594
  39.1 0.0 collective-permute-done.1.refs_3_.refs_2_
  39.1 0.0 copy-done.9
  39.1 5.1 %collective-permute-start.2 = (f32[128,8,128]{2,1,0:T(8,128)S(1)}, f32[128,8,128]{2,1,0:T(8,128)}, u32[]{:S(2)}, u32[]{:S(2)}) collective-permute-start(f32[128,8,128]{2,1,0:T(8,128)S(1)} %copy-done.9), channel_id=1, source_target_pairs={{0,1},{1,2},{2,3},{3,4},{4,5},{5,6},{6,7},{8,9},{9,10},{10,11},{11... | collective-permute-start | bytes 1572872 | tf_op jit(solution)/shard_map/ppermute | solution.py:594
  44.2 0.0 copy-done.8
  44.2 1.5 %collective-permute-start.3 = (f32[128,8,128]{2,1,0:T(8,128)S(1)}, f32[128,8,128]{2,1,0:T(8,128)}, u32[]{:S(2)}, u32[]{:S(2)}) collective-permute-start(f32[128,8,128]{2,1,0:T(8,128)S(1)} %copy-done.8), channel_id=1, source_target_pairs={{1,0},{2,1},{3,2},{4,3},{5,4},{6,5},{7,6},{9,8},{10,9},{11,10},{12... | collective-permute-start | bytes 1572872 | tf_op jit(solution)/shard_map/ppermute | solution.py:594
  45.6 0.0 collective-permute-done.8
  45.7 1.6 %collective-permute-start.9 = (f32[2,8,4096]{2,1,0:T(8,128)S(1)}, f32[2,8,4096]{2,1,0:T(8,128)S(1)}, u32[]{:S(2)}, u32[]{:S(2)}) collective-permute-start(f32[2,8,4096]{2,1,0:T(8,128)S(1)} %pad_maximum_fusion.2), channel_id=1, source_target_pairs={{0,16},{8,24},{16,0},{24,8},{1,17},{9,25},{17,1},{25,9},{2,18},{10... | collective-permute-start | bytes 786440 | tf_op jit(solution)/shard_map/ppermute | solution.py:587
  47.3 0.1 pad_add_fusion
  47.3 0.0 copy-done.10
  47.3 0.6 add_select_fusion
  48.0 1.5 %collective-permute-done.7.refs_11_.refs_14_ = f32[2,2,32,8,128]{4,3,2,1,0:T(8,128)S(1)} collective-permute-done((f32[2,2,32,8,128]{4,3,2,1,0:T(8,128)S(1)}, f32[2,2,32,8,128]{4,3,2,1,0:T(8,128)S(1)}, u32[]{:S(2)}, u32[]{:S(2)}) %collective-permute-start.7) | collective-permute-done | bytes 524320 | tf_op jit(solution)/shard_map/ppermute | solution.py:587
  49.5 0.0 copy-done.4
  49.5 0.0 copy-done.5
  49.5 0.8 copy-done.7
  50.3 11.6 %edge_first.1 = (f32[128,8,128]{2,1,0:T(8,128)}, f32[128,8,128]{2,1,0:T(8,128)}, f32[128,8,128]{2,1,0:T(8,128)}, f32[128,8,128]{2,1,0:T(8,128)}, f32[128,8,128]{...) custom-call(f32[128,8,128]{2,1,0:T(8,128)} %copy-done.5, ...), custom_call_target="tpu_custom_call" | custom-call | bytes 2000000 | tf_op jit(solution)/shard_map/edge_first/pallas_call | solution.py:421
  62.0 0.0 collective-permute-done.9
  62.0 2.6 %collective-permute-done.2.refs_0_ = f32[128,8,128]{2,1,0:T(8,128)} collective-permute-done((f32[128,8,128]{2,1,0:T(8,128)S(1)}, f32[128,8,128]{2,1,0:T(8,128)}, u32[]{:S(2)}, u32[]{:S(2)}) %collective-permute-start.2) | collective-permute-done | bytes 524320 | tf_op jit(solution)/shard_map/ppermute | solution.py:594
  64.6 0.0 collective-permute-done.3.refs_3_
  64.6 16.2 %edge_last.1 = (f32[128,8,128]{2,1,0:T(8,128)}, f32[128,8,128]{2,1,0:T(8,128)}, f32[8,2048]{1,0:T(8,128)}) custom-call(f32[128,8,128]{2,1,0:T(8,128)} %collective-permute-done.2.refs_0_, f32[128,8,128]{2,1,0:T(8,128)} %copy-done.5, f32[128,8,128]{2,1,0:T(8,128)} %copy-done.6, f32[128,8,128]{2,1,0:T(8,128)} %collective-permute-done.3.refs_3_, ...), custom_call_target="tpu_custom_call" | custom-call | bytes 3000000 | tf_op jit(solution)/shard_map/edge_last/pallas_call | solution.py:421
  80.8 0.1 collective-permute-start.10
  80.9 1.6 %collective-permute-start.11 = (f32[8,2048]{1,0:T(8,128)}, f32[8,2048]{1,0:T(8,128)S(1)}, u32[]{:S(2)}, u32[]{:S(2)}) collective-permute-start(f32[8,2048]{1,0:T(8,128)} %get-tuple-element.83.own), channel_id=1, source_target_pairs={{0,16},{8,24},{16,0},{24,8},{1,17},{9,25},{17,1},{25,9},{2,18},{10... | collective-permute-start | bytes 196616 | tf_op jit(solution)/shard_map/ppermute | solution.py:629
  82.5 0.3 collective-permute-start.12
  82.7 0.1 compare_convert_fusion.same
  82.8 3.7 %field_0.1.refs_4_ = f32[128,4096]{1,0:T(8,128)} custom-call(f32[128,8,128]{2,1,0:T(8,128)} %get-tuple-element.84.refs_0_, f32[128,8,128]{2,1,0:T(8,128)} %get-tuple-element.81.refs_10_.refs_1_, f32[128,8,128]{2,1,0:T(8,128)} %get-tuple-element.82.refs_11_.refs_2_, f32[128,8,128]{2,1,0:T(8,128)} %get-tuple-element.85.refs_3_), custom_call_target="tpu_custom_call" | custom-call | bytes 800000 | tf_op jit(solution)/shard_map/field_0/pallas_call | solution.py:421
  86.5 0.0 collective-permute-done.10.second
  86.6 0.0 collective-permute-done.11.third
  86.6 0.2 collective-permute-done.12.fourth
  86.8 0.6 products.1
  87.5 2.6 %collective-permute-start.13 = (f32[32,40]{1,0:T(8,128)S(1)}, f32[32,40]{1,0:T(8,128)S(1)}, u32[]{:S(2)}, u32[]{:S(2)}) collective-permute-start(f32[32,40]{1,0:T(8,128)S(1)} %products.1), channel_id=1, source_target_pairs={{0,1},{1,0},{2,3},{3,2},{4,5},{5,4},{6,7},{7,6},{8,9},{9,8},{10,11... | collective-permute-start | bytes 15368 | tf_op jit(solution)/shard_map/ppermute | solution.py:644
  90.1 2.6 %collective-permute-start.14 = (f32[32,40]{1,0:T(8,128)S(1)}, f32[32,40]{1,0:T(8,128)S(1)}, u32[]{:S(2)}, u32[]{:S(2)}) collective-permute-start(f32[32,40]{1,0:T(8,128)S(1)} %products.1), channel_id=1, source_target_pairs={{0,2},{1,3},{2,0},{3,1},{4,6},{5,7},{6,4},{7,5},{8,10},{9,11},{10,... | collective-permute-start | bytes 15368 | tf_op jit(solution)/shard_map/ppermute | solution.py:644
  92.7 1.4 %collective-permute-start.15 = (f32[32,40]{1,0:T(8,128)S(1)}, f32[32,40]{1,0:T(8,128)S(1)}, u32[]{:S(2)}, u32[]{:S(2)}) collective-permute-start(f32[32,40]{1,0:T(8,128)S(1)} %products.1), channel_id=1, source_target_pairs={{0,3},{1,2},{2,1},{3,0},{4,7},{5,6},{6,5},{7,4},{8,11},{9,10},{10,... | collective-permute-start | bytes 15368 | tf_op jit(solution)/shard_map/ppermute | solution.py:644
  94.1 0.2 convert_reduce_fusion
  94.3 0.1 copy.10.rank_col
  94.3 3.7 %field_1.1 = f32[128,4096]{1,0:T(8,128)} custom-call(f32[128,8,128]{2,1,0:T(8,128)} %get-tuple-element.84.refs_0_, f32[128,8,128]{2,1,0:T(8,128)} %get-tuple-element.81.refs_10_.refs_1_, f32[128,8,128]{2,1,0:T(8,128)} %get-tuple-element.82.refs_11_.refs_2_, f32[128,8,128]{2,1,0:T(8,128)} %get-tuple-element.85.refs_3_, ...), custom_call_target="tpu_custom_call", output_to_operand_aliasing={{}: (4, {})} | custom-call | bytes 800000 | tf_op jit(solution)/shard_map/field_1/pallas_call | solution.py:421
  98.0 0.0 collective-permute-done.13
  98.1 0.0 collective-permute-done.14
  98.1 0.0 collective-permute-done.15
  98.1 3.1 %collective-permute-start.16 = (f32[32,40]{1,0:T(8,128)S(1)}, f32[32,40]{1,0:T(8,128)S(1)}, u32[]{:S(2)}, u32[]{:S(2)}) collective-permute-start(f32[32,40]{1,0:T(8,128)S(1)} %add_add_fusion), channel_id=1, source_target_pairs={{0,4},{1,5},{2,6},{3,7},{4,0},{5,1},{6,2},{7,3},{8,12},{9,13},{10,... | collective-permute-start | bytes 15368 | tf_op jit(solution)/shard_map/ppermute | solution.py:644
  101.2 0.4 fusion.1.anomalies
  101.6 1.3 %collective-permute-done.16 = f32[32,40]{1,0:T(8,128)S(1)} collective-permute-done((f32[32,40]{1,0:T(8,128)S(1)}, f32[32,40]{1,0:T(8,128)S(1)}, u32[]{:S(2)}, u32[]{:S(2)}) %collective-permute-start.16) | collective-permute-done | bytes 5152 | tf_op jit(solution)/shard_map/ppermute | solution.py:644
  102.9 2.1 %update.1 = f32[8,4096]{1,0:T(8,128)} custom-call(f32[1,32,40]{2,1,0:T(8,128)S(1)} %add_bitcast_fusion.summands, f32[32,32]{1,0:T(8,128)S(1)} %compare_convert_fusion.same, f32[32,8]{1,0:T(8,128)S(1)} %bitcast.31, s32[1,32]{1,0:T(1,128)S(1)} %bitcast.34, s32[32,1]{1,0:T(8,128)S(1)} %copy.10.rank_col, f32[32,4096]{1,0:T(8,128)S(1)} %fusion.1.anomalies, ...), custom_call_target="tpu_custom_call" | custom-call | tf_op jit(solution)/shard_map/update/pallas_call | solution.py:653
  (16 shorter events, 0.1 us)
Async XLA Ops:
  5.0 12.9 %collective-permute-start.5 = (f32[32,8,128]{2,1,0:T(8,128)}, f32[32,8,128]{2,1,0:T(8,128)S(1)}, u32[]{:S(2)}, u32[]{:S(2)}) collective-permute-start(f32[32,8,128]{2,1,0:T(8,128)} %get-tuple-element.65), channel_id=1, source_target_pairs={{1,0},{2,1},{3,2},{4,3},{5,4},{6,5},{7,6},{9,8},{10,9},{11,10},{12... | collective-permute-start | bytes 393224 | tf_op jit(solution)/shard_map/ppermute | solution.py:594
  6.3 11.7 %collective-permute-start.4 = (f32[32,8,128]{2,1,0:T(8,128)}, f32[32,8,128]{2,1,0:T(8,128)S(1)}, u32[]{:S(2)}, u32[]{:S(2)}) collective-permute-start(f32[32,8,128]{2,1,0:T(8,128)} %get-tuple-element.64), channel_id=1, source_target_pairs={{0,1},{1,2},{2,3},{3,4},{4,5},{5,6},{6,7},{8,9},{9,10},{10,11},{11... | collective-permute-start | bytes 393224 | tf_op jit(solution)/shard_map/ppermute | solution.py:594
  11.8 27.3 %collective-permute-start = (f32[128,8,128]{2,1,0:T(8,128)}, f32[128,8,128]{2,1,0:T(8,128)S(1)}, u32[]{:S(2)}, u32[]{:S(2)}) collective-permute-start(f32[128,8,128]{2,1,0:T(8,128)} %get-tuple-element.49.outer.own3.refs_2_), channel_id=1, source_target_pairs={{0,1},{1,2},{2,3},{3,4},{4,5},{5,6},{6,7},{8,9},{9,10},{10,11},{11... | collective-permute-start | bytes 1572872 | tf_op jit(solution)/shard_map/ppermute | solution.py:594
  16.6 22.4 %collective-permute-start.1 = (f32[128,8,128]{2,1,0:T(8,128)}, f32[128,8,128]{2,1,0:T(8,128)S(1)}, u32[]{:S(2)}, u32[]{:S(2)}) collective-permute-start(f32[128,8,128]{2,1,0:T(8,128)} %get-tuple-element.52.own0.refs_1_), channel_id=1, source_target_pairs={{1,0},{2,1},{3,2},{4,3},{5,4},{6,5},{7,6},{9,8},{10,9},{11,10},{12... | collective-permute-start | bytes 1572872 | tf_op jit(solution)/shard_map/ppermute | solution.py:594
  18.0 16.6 %collective-permute-start.6 = (f32[2,32,8,128]{3,2,1,0:T(8,128)S(1)}, f32[2,32,8,128]{3,2,1,0:T(8,128)S(1)}, u32[]{:S(2)}, u32[]{:S(2)}) collective-permute-start(f32[2,32,8,128]{3,2,1,0:T(8,128)S(1)} %get-tuple-element.97), channel_id=1, source_target_pairs={{0,8},{8,0},{16,24},{24,16},{1,9},{9,1},{17,25},{25,17},{2,10},{10... | collective-permute-start | bytes 786440 | tf_op jit(solution)/shard_map/ppermute | solution.py:584
  24.5 9.4 %copy-start = (f32[8,4096]{1,0:T(8,128)S(1)}, f32[8,4096]{1,0:T(8,128)}, u32[]{:S(2)}) copy-start(f32[8,4096]{1,0:T(8,128)} %own.1) | copy-start | bytes 393220
  24.5 10.0 %copy-start.11 = (s32[32]{0:T(128)S(1)}, s32[32]{0:T(128)}, u32[]{:S(2)}) copy-start(s32[32]{0:T(128)} %param.13) | copy-start | bytes 388
  24.5 14.6 %copy-start.9 = (f32[128,8,128]{2,1,0:T(8,128)S(1)}, f32[128,8,128]{2,1,0:T(8,128)}, u32[]{:S(2)}) copy-start(f32[128,8,128]{2,1,0:T(8,128)} %get-tuple-element.56.own2) | copy-start | bytes 1572868
  24.5 19.7 %copy-start.8 = (f32[128,8,128]{2,1,0:T(8,128)S(1)}, f32[128,8,128]{2,1,0:T(8,128)}, u32[]{:S(2)}) copy-start(f32[128,8,128]{2,1,0:T(8,128)} %get-tuple-element.59.own1) | copy-start | bytes 1572868
  24.5 22.8 %copy-start.10 = (s32[2048]{0:T(1024)S(1)}, s32[2048]{0:T(1024)}, u32[]{:S(2)}) copy-start(s32[2048]{0:T(1024)} %param.10) | copy-start | bytes 24580
  33.9 11.8 %collective-permute-start.8 = (f32[8,4096]{1,0:T(8,128)S(1)}, f32[8,4096]{1,0:T(8,128)S(1)}, u32[]{:S(2)}, u32[]{:S(2)}) collective-permute-start(f32[8,4096]{1,0:T(8,128)S(1)} %copy-done), channel_id=1, source_target_pairs={{0,8},{8,0},{16,24},{24,16},{1,9},{9,1},{17,25},{25,17},{2,10},{10... | collective-permute-start | bytes 393224 | tf_op jit(solution)/shard_map/ppermute | solution.py:584
  34.6 14.9 %copy-start.4 = (f32[2,2,32,8,128]{4,3,2,1,0:T(8,128)}, f32[2,2,32,8,128]{4,3,2,1,0:T(8,128)S(1)}, u32[]{:S(2)}) copy-start(f32[2,2,32,8,128]{4,3,2,1,0:T(8,128)S(1)} %pad_maximum_fusion.refs_10_.refs_13_) | copy-start | bytes 1572868
  34.6 14.9 %collective-permute-start.7 = (f32[2,2,32,8,128]{4,3,2,1,0:T(8,128)S(1)}, f32[2,2,32,8,128]{4,3,2,1,0:T(8,128)S(1)}, u32[]{:S(2)}, u32[]{:S(2)}) collective-permute-start(f32[2,2,32,8,128]{4,3,2,1,0:T(8,128)S(1)} %pad_maximum_fusion.refs_10_.refs_13_), channel_id=1, source_target_pairs={{0,16},{8,24},{16,0},{24,8},{1,17},{9,25},{17,1},{25,9},{2,18},{10... | collective-permute-start | bytes 1572872 | tf_op jit(solution)/shard_map/ppermute | solution.py:587
  39.1 10.4 %copy-start.5 = (f32[128,8,128]{2,1,0:T(8,128)}, f32[128,8,128]{2,1,0:T(8,128)S(1)}, u32[]{:S(2)}) copy-start(f32[128,8,128]{2,1,0:T(8,128)S(1)} %collective-permute-done.refs_0_.refs_1_) | copy-start | bytes 1572868
  39.1 10.4 %copy-start.6 = (f32[128,8,128]{2,1,0:T(8,128)}, f32[128,8,128]{2,1,0:T(8,128)S(1)}, u32[]{:S(2)}) copy-start(f32[128,8,128]{2,1,0:T(8,128)S(1)} %collective-permute-done.1.refs_3_.refs_2_) | copy-start | bytes 1572868
  39.1 25.5 %collective-permute-start.2 = (f32[128,8,128]{2,1,0:T(8,128)S(1)}, f32[128,8,128]{2,1,0:T(8,128)}, u32[]{:S(2)}, u32[]{:S(2)}) collective-permute-start(f32[128,8,128]{2,1,0:T(8,128)S(1)} %copy-done.9), channel_id=1, source_target_pairs={{0,1},{1,2},{2,3},{3,4},{4,5},{5,6},{6,7},{8,9},{9,10},{10,11},{11... | collective-permute-start | bytes 1572872 | tf_op jit(solution)/shard_map/ppermute | solution.py:594
  44.2 20.4 %collective-permute-start.3 = (f32[128,8,128]{2,1,0:T(8,128)S(1)}, f32[128,8,128]{2,1,0:T(8,128)}, u32[]{:S(2)}, u32[]{:S(2)}) collective-permute-start(f32[128,8,128]{2,1,0:T(8,128)S(1)} %copy-done.8), channel_id=1, source_target_pairs={{1,0},{2,1},{3,2},{4,3},{5,4},{6,5},{7,6},{9,8},{10,9},{11,10},{12... | collective-permute-start | bytes 1572872 | tf_op jit(solution)/shard_map/ppermute | solution.py:594
  45.7 16.3 %collective-permute-start.9 = (f32[2,8,4096]{2,1,0:T(8,128)S(1)}, f32[2,8,4096]{2,1,0:T(8,128)S(1)}, u32[]{:S(2)}, u32[]{:S(2)}) collective-permute-start(f32[2,8,4096]{2,1,0:T(8,128)S(1)} %pad_maximum_fusion.2), channel_id=1, source_target_pairs={{0,16},{8,24},{16,0},{24,8},{1,17},{9,25},{17,1},{25,9},{2,18},{10... | collective-permute-start | bytes 786440 | tf_op jit(solution)/shard_map/ppermute | solution.py:587
  49.5 0.8 copy-start.7
  80.8 5.8 %collective-permute-start.10 = (f32[8,2048]{1,0:T(8,128)}, f32[8,2048]{1,0:T(8,128)S(1)}, u32[]{:S(2)}, u32[]{:S(2)}) collective-permute-start(f32[8,2048]{1,0:T(8,128)} %get-tuple-element.83.own), channel_id=1, source_target_pairs={{0,8},{8,0},{16,24},{24,16},{1,9},{9,1},{17,25},{25,17},{2,10},{10... | collective-permute-start | bytes 196616 | tf_op jit(solution)/shard_map/ppermute | solution.py:629
  80.9 5.7 %collective-permute-start.11 = (f32[8,2048]{1,0:T(8,128)}, f32[8,2048]{1,0:T(8,128)S(1)}, u32[]{:S(2)}, u32[]{:S(2)}) collective-permute-start(f32[8,2048]{1,0:T(8,128)} %get-tuple-element.83.own), channel_id=1, source_target_pairs={{0,16},{8,24},{16,0},{24,8},{1,17},{9,25},{17,1},{25,9},{2,18},{10... | collective-permute-start | bytes 196616 | tf_op jit(solution)/shard_map/ppermute | solution.py:629
  82.5 4.3 %collective-permute-start.12 = (f32[8,2048]{1,0:T(8,128)}, f32[8,2048]{1,0:T(8,128)S(1)}, u32[]{:S(2)}, u32[]{:S(2)}) collective-permute-start(f32[8,2048]{1,0:T(8,128)} %get-tuple-element.83.own), channel_id=1, source_target_pairs={{0,24},{8,16},{16,8},{24,0},{1,25},{9,17},{17,9},{25,1},{2,26},{10... | collective-permute-start | bytes 196616 | tf_op jit(solution)/shard_map/ppermute | solution.py:629
  82.8 4.0 %copy-start.1 = (f32[8,2048]{1,0:T(8,128)S(1)}, f32[8,2048]{1,0:T(8,128)}, u32[]{:S(2)}) copy-start(f32[8,2048]{1,0:T(8,128)} %values.1) | copy-start | bytes 196612
  82.8 4.0 %copy-start.2 = (f32[8,2048]{1,0:T(8,128)S(1)}, f32[8,2048]{1,0:T(8,128)}, u32[]{:S(2)}) copy-start(f32[8,2048]{1,0:T(8,128)} %get-tuple-element.83.own) | copy-start | bytes 196612
  82.8 4.0 %copy-start.3 = (f32[2048]{0:T(1024)S(1)}, f32[2048]{0:T(1024)}, u32[]{:S(2)}) copy-start(f32[2048]{0:T(1024)} %param.12) | copy-start | bytes 24580
  87.5 10.6 %collective-permute-start.13 = (f32[32,40]{1,0:T(8,128)S(1)}, f32[32,40]{1,0:T(8,128)S(1)}, u32[]{:S(2)}, u32[]{:S(2)}) collective-permute-start(f32[32,40]{1,0:T(8,128)S(1)} %products.1), channel_id=1, source_target_pairs={{0,1},{1,0},{2,3},{3,2},{4,5},{5,4},{6,7},{7,6},{8,9},{9,8},{10,11... | collective-permute-start | bytes 15368 | tf_op jit(solution)/shard_map/ppermute | solution.py:644
  90.1 8.0 %collective-permute-start.14 = (f32[32,40]{1,0:T(8,128)S(1)}, f32[32,40]{1,0:T(8,128)S(1)}, u32[]{:S(2)}, u32[]{:S(2)}) collective-permute-start(f32[32,40]{1,0:T(8,128)S(1)} %products.1), channel_id=1, source_target_pairs={{0,2},{1,3},{2,0},{3,1},{4,6},{5,7},{6,4},{7,5},{8,10},{9,11},{10,... | collective-permute-start | bytes 15368 | tf_op jit(solution)/shard_map/ppermute | solution.py:644
  92.7 5.4 %collective-permute-start.15 = (f32[32,40]{1,0:T(8,128)S(1)}, f32[32,40]{1,0:T(8,128)S(1)}, u32[]{:S(2)}, u32[]{:S(2)}) collective-permute-start(f32[32,40]{1,0:T(8,128)S(1)} %products.1), channel_id=1, source_target_pairs={{0,3},{1,2},{2,1},{3,0},{4,7},{5,6},{6,5},{7,4},{8,11},{9,10},{10,... | collective-permute-start | bytes 15368 | tf_op jit(solution)/shard_map/ppermute | solution.py:644
  98.1 4.8 %collective-permute-start.16 = (f32[32,40]{1,0:T(8,128)S(1)}, f32[32,40]{1,0:T(8,128)S(1)}, u32[]{:S(2)}, u32[]{:S(2)}) collective-permute-start(f32[32,40]{1,0:T(8,128)S(1)} %add_add_fusion), channel_id=1, source_target_pairs={{0,4},{1,5},{2,6},{3,7},{4,0},{5,1},{6,2},{7,3},{8,12},{9,13},{10,... | collective-permute-start | bytes 15368 | tf_op jit(solution)/shard_map/ppermute | solution.py:644

commit v16 on v15

--- a/solution.py
+++ b/solution.py
@@ -16,7 +16,7 @@
 ROWS = 16
 GROUP = 4
 FOLD = 4
-PICKED = 128
+CHAINS = 4
 TILES = 4
 FIELD_CALLS = 2
 ALL_ROWS = ROWS + 2 * HALO
@@ -346,15 +346,14 @@
     def _(block):
         base = block * LANES
 
-        def some(part, found):
-            for i in range(PICKED):
-                o = part * PICKED + i
-                value = pltpu.roll(levels[STEPS][cell_of[base + o]], shift_of[base + o], 1)
-                found = jnp.where(lane == o, value, found)
-            return found
-
-        empty = jnp.zeros((SUBLANES, LANES), jnp.float32)
-        predicted[:, block_at(block)] = lax.fori_loop(0, LANES // PICKED, some, empty)
+        found = [jnp.zeros((SUBLANES, LANES), jnp.float32)] * CHAINS
+        for o in range(LANES):
+            value = pltpu.roll(levels[STEPS][cell_of[base + o]], shift_of[base + o], 1)
+            found[o % CHAINS] = jnp.where(lane == o, value, found[o % CHAINS])
+        picked = found[0]
+        for k in range(1, CHAINS):
+            picked = jnp.where(lax.rem(lane, CHAINS) == k, found[k], picked)
+        predicted[:, block_at(block)] = picked
 
     for copy in sends:
         copy.wait()

time: 106 us -> 106 us (level)
  no operation moved by 1% of the time
where the time goes in v16:
time: 106 us; the launch traced here: 105 us
  Pallas kernels  58.1 us (55%)
  starting transfers between devices  34.9 us (33%)
  waiting for transfers between devices  8.53 us (8%)
  other arithmetic  1.11 us (1%)
    pallas_call x7, Pallas kernels, kernel_call(): pl.pallas_call(body, out_shape=tuple((jax.ShapeDtypeStruct(shape, jnp.flo...  55.3 us
    ppermute x3, starting transfers between devices, halos(): lax.ppermute(upper, 'slab', forward)  15.4 us
    ppermute x4, starting transfers between devices, local(): lax.ppermute(products, 'slab', [(i, i ^ step * distance) for i in range(s...  9.72 us
    ppermute x3, waiting for transfers between devices, halos(): lax.ppermute(upper, 'slab', forward)  5.51 us
    ppermute x3, starting transfers between devices, halos(): lax.ppermute(lower, 'slab', backward)  4.05 us
    ppermute x2, starting transfers between devices, next_chip(): return lax.ppermute(value, 'ens', [(i, i ^ 2) for i in range(ens_count)])  3.17 us
  transfers between devices with their start and end apart: 17, of which 5 were waited for; matrix products, arithmetic and copies ran while one was open for 2% of the time, Pallas kernels for 33%

profile of v16, /device:TPU:0, one launch (start us, length us, event | category | flops | bytes accessed | tf_op | source)
XLA Modules:
  0.0 105.0 jit_solution(14907022253399629630)
XLA Ops:
  0.6 4.3 %outer_rows.1 = (f32[128,8,128]{2,1,0:T(8,128)}, f32[128,8,128]{2,1,0:T(8,128)}, f32[32,8,128]{2,1,0:T(8,128)}, f32[32,8,128]{2,1,0:T(8,128)}) custom-call(f32[128,4096]{1,0:T(8,128)} %bitcast.36, f32[4,16,4096]{2,1,0:T(8,128)} %own_coef.3, s32[1]{0:T(128)} %bitcast.1.place_of.refs_13_.refs_16_), custom_call_target="tpu_custom_call" | custom-call | bytes 600000 | tf_op jit(solution)/shard_map/outer_rows/pallas_call | solution.py:420
  5.0 1.3 %collective-permute-start.5 = (f32[32,8,128]{2,1,0:T(8,128)}, f32[32,8,128]{2,1,0:T(8,128)S(1)}, u32[]{:S(2)}, u32[]{:S(2)}) collective-permute-start(f32[32,8,128]{2,1,0:T(8,128)} %get-tuple-element.65), channel_id=1, source_target_pairs={{1,0},{2,1},{3,2},{4,3},{5,4},{6,5},{7,6},{9,8},{10,9},{11,10},{12... | collective-permute-start | bytes 393224 | tf_op jit(solution)/shard_map/ppermute | solution.py:593
  6.3 5.5 %collective-permute-start.4 = (f32[32,8,128]{2,1,0:T(8,128)}, f32[32,8,128]{2,1,0:T(8,128)S(1)}, u32[]{:S(2)}, u32[]{:S(2)}) collective-permute-start(f32[32,8,128]{2,1,0:T(8,128)} %get-tuple-element.64), channel_id=1, source_target_pairs={{0,1},{1,2},{2,3},{3,4},{4,5},{5,6},{6,7},{8,9},{9,10},{10,11},{11... | collective-permute-start | bytes 393224 | tf_op jit(solution)/shard_map/ppermute | solution.py:593
  11.8 4.8 %collective-permute-start = (f32[128,8,128]{2,1,0:T(8,128)}, f32[128,8,128]{2,1,0:T(8,128)S(1)}, u32[]{:S(2)}, u32[]{:S(2)}) collective-permute-start(f32[128,8,128]{2,1,0:T(8,128)} %get-tuple-element.49.outer.own3.refs_2_), channel_id=1, source_target_pairs={{0,1},{1,2},{2,3},{3,4},{4,5},{5,6},{6,7},{8,9},{9,10},{10,11},{11... | collective-permute-start | bytes 1572872 | tf_op jit(solution)/shard_map/ppermute | solution.py:593
  16.6 1.3 %collective-permute-start.1 = (f32[128,8,128]{2,1,0:T(8,128)}, f32[128,8,128]{2,1,0:T(8,128)S(1)}, u32[]{:S(2)}, u32[]{:S(2)}) collective-permute-start(f32[128,8,128]{2,1,0:T(8,128)} %get-tuple-element.52.own0.refs_1_), channel_id=1, source_target_pairs={{1,0},{2,1},{3,2},{4,3},{5,4},{6,5},{7,6},{9,8},{10,9},{11,10},{12... | collective-permute-start | bytes 1572872 | tf_op jit(solution)/shard_map/ppermute | solution.py:593
  17.9 0.0 collective-permute-done.5
  17.9 0.0 collective-permute-done.4
  18.0 0.1 collective-permute-start.6
  18.1 6.4 %inner_rows.1 = (f32[128,8,128]{2,1,0:T(8,128)}, f32[128,8,128]{2,1,0:T(8,128)}, f32[32,64,128]{2,1,0:T(8,128)}, f32[8,4096]{1,0:T(8,128)}) custom-call(f32[128,4096]{1,0:T(8,128)} %bitcast.37, f32[4,16,4096]{2,1,0:T(8,128)} %own_coef.3, f32[8,4096]{1,0:T(8,128)} %own.1, f32[128,8,128]{2,1,0:T(8,128)} %get-tuple-element.49.outer.own3.refs_2_), custom_call_target="tpu_custom_call" | custom-call | bytes 600000 | tf_op jit(solution)/shard_map/inner_rows/pallas_call | solution.py:420
  24.5 0.0 copy-start
  24.5 0.0 copy-start.11
  24.5 0.0 copy-start.9
  24.5 0.0 copy-start.8
  24.5 0.0 copy-start.10
  24.5 9.3 %interior.1 = (f32[128,8,128]{2,1,0:T(8,128)}, f32[128,8,128]{2,1,0:T(8,128)}, f32[128,8,128]{2,1,0:T(8,128)}, f32[128,8,128]{2,1,0:T(8,128)}, f32[128,8,128]{2,1,0:T(8,128)}) custom-call(f32[128,8,128]{2,1,0:T(8,128)} %get-tuple-element.52.own0.refs_1_, f32[128,8,128]{2,1,0:T(8,128)} %get-tuple-element.59.own1, f32[128,8,128]{2,1,0:T(8,128)} %get-tuple-element.56.own2, ...), custom_call_target="tpu_custom_call" | custom-call | bytes 1600000 | tf_op jit(solution)/shard_map/interior/pallas_call | solution.py:420
  33.9 0.0 copy-done
  33.9 0.6 collective-permute-start.8
  34.4 0.0 copy-done.11
  34.4 0.1 reshape.23
  34.5 0.0 collective-permute-done.6
  34.6 0.1 pad_maximum_fusion.refs_10_.refs_13_
  34.6 1.6 %collective-permute-start.7 = (f32[2,2,32,8,128]{4,3,2,1,0:T(8,128)S(1)}, f32[2,2,32,8,128]{4,3,2,1,0:T(8,128)S(1)}, u32[]{:S(2)}, u32[]{:S(2)}) collective-permute-start(f32[2,2,32,8,128]{4,3,2,1,0:T(8,128)S(1)} %pad_maximum_fusion.refs_10_.refs_13_), channel_id=1, source_target_pairs={{0,16},{8,24},{16,0},{24,8},{1,17},{9,25},{17,1},{25,9},{2,18},{10... | collective-permute-start | bytes 1572872 | tf_op jit(solution)/shard_map/ppermute | solution.py:586
  36.2 2.9 %collective-permute-done.refs_0_.refs_1_ = f32[128,8,128]{2,1,0:T(8,128)S(1)} collective-permute-done((f32[128,8,128]{2,1,0:T(8,128)}, f32[128,8,128]{2,1,0:T(8,128)S(1)}, u32[]{:S(2)}, u32[]{:S(2)}) %collective-permute-start) | collective-permute-done | bytes 524320 | tf_op jit(solution)/shard_map/ppermute | solution.py:593
  39.1 0.0 collective-permute-done.1.refs_3_.refs_2_
  39.1 0.0 copy-done.9
  39.1 5.1 %collective-permute-start.2 = (f32[128,8,128]{2,1,0:T(8,128)S(1)}, f32[128,8,128]{2,1,0:T(8,128)}, u32[]{:S(2)}, u32[]{:S(2)}) collective-permute-start(f32[128,8,128]{2,1,0:T(8,128)S(1)} %copy-done.9), channel_id=1, source_target_pairs={{0,1},{1,2},{2,3},{3,4},{4,5},{5,6},{6,7},{8,9},{9,10},{10,11},{11... | collective-permute-start | bytes 1572872 | tf_op jit(solution)/shard_map/ppermute | solution.py:593
  44.2 0.0 copy-done.8
  44.2 1.5 %collective-permute-start.3 = (f32[128,8,128]{2,1,0:T(8,128)S(1)}, f32[128,8,128]{2,1,0:T(8,128)}, u32[]{:S(2)}, u32[]{:S(2)}) collective-permute-start(f32[128,8,128]{2,1,0:T(8,128)S(1)} %copy-done.8), channel_id=1, source_target_pairs={{1,0},{2,1},{3,2},{4,3},{5,4},{6,5},{7,6},{9,8},{10,9},{11,10},{12... | collective-permute-start | bytes 1572872 | tf_op jit(solution)/shard_map/ppermute | solution.py:593
  45.6 0.0 collective-permute-done.8
  45.7 1.6 %collective-permute-start.9 = (f32[2,8,4096]{2,1,0:T(8,128)S(1)}, f32[2,8,4096]{2,1,0:T(8,128)S(1)}, u32[]{:S(2)}, u32[]{:S(2)}) collective-permute-start(f32[2,8,4096]{2,1,0:T(8,128)S(1)} %pad_maximum_fusion.2), channel_id=1, source_target_pairs={{0,16},{8,24},{16,0},{24,8},{1,17},{9,25},{17,1},{25,9},{2,18},{10... | collective-permute-start | bytes 786440 | tf_op jit(solution)/shard_map/ppermute | solution.py:586
  47.3 0.1 pad_add_fusion
  47.3 0.0 copy-done.10
  47.3 0.6 add_select_fusion
  48.0 1.5 %collective-permute-done.7.refs_11_.refs_14_ = f32[2,2,32,8,128]{4,3,2,1,0:T(8,128)S(1)} collective-permute-done((f32[2,2,32,8,128]{4,3,2,1,0:T(8,128)S(1)}, f32[2,2,32,8,128]{4,3,2,1,0:T(8,128)S(1)}, u32[]{:S(2)}, u32[]{:S(2)}) %collective-permute-start.7) | collective-permute-done | bytes 524320 | tf_op jit(solution)/shard_map/ppermute | solution.py:586
  49.5 0.0 copy-done.4
  49.5 0.8 copy-done.7
  50.3 11.6 %edge_first.1 = (f32[128,8,128]{2,1,0:T(8,128)}, f32[128,8,128]{2,1,0:T(8,128)}, f32[128,8,128]{2,1,0:T(8,128)}, f32[128,8,128]{2,1,0:T(8,128)}, f32[128,8,128]{...) custom-call(f32[128,8,128]{2,1,0:T(8,128)} %copy-done.5, ...), custom_call_target="tpu_custom_call" | custom-call | bytes 2000000 | tf_op jit(solution)/shard_map/edge_first/pallas_call | solution.py:420
  62.0 0.0 collective-permute-done.9
  62.0 2.6 %collective-permute-done.2.refs_0_ = f32[128,8,128]{2,1,0:T(8,128)} collective-permute-done((f32[128,8,128]{2,1,0:T(8,128)S(1)}, f32[128,8,128]{2,1,0:T(8,128)}, u32[]{:S(2)}, u32[]{:S(2)}) %collective-permute-start.2) | collective-permute-done | bytes 524320 | tf_op jit(solution)/shard_map/ppermute | solution.py:593
  64.6 0.0 collective-permute-done.3.refs_3_
  64.6 16.2 %edge_last.1 = (f32[128,8,128]{2,1,0:T(8,128)}, f32[128,8,128]{2,1,0:T(8,128)}, f32[8,2048]{1,0:T(8,128)}) custom-call(f32[128,8,128]{2,1,0:T(8,128)} %collective-permute-done.2.refs_0_, f32[128,8,128]{2,1,0:T(8,128)} %copy-done.5, f32[128,8,128]{2,1,0:T(8,128)} %copy-done.6, f32[128,8,128]{2,1,0:T(8,128)} %collective-permute-done.3.refs_3_, ...), custom_call_target="tpu_custom_call" | custom-call | bytes 3000000 | tf_op jit(solution)/shard_map/edge_last/pallas_call | solution.py:420
  80.8 0.1 collective-permute-start.10
  80.9 1.6 %collective-permute-start.11 = (f32[8,2048]{1,0:T(8,128)}, f32[8,2048]{1,0:T(8,128)S(1)}, u32[]{:S(2)}, u32[]{:S(2)}) collective-permute-start(f32[8,2048]{1,0:T(8,128)} %get-tuple-element.83.own), channel_id=1, source_target_pairs={{0,16},{8,24},{16,0},{24,8},{1,17},{9,25},{17,1},{25,9},{2,18},{10... | collective-permute-start | bytes 196616 | tf_op jit(solution)/shard_map/ppermute | solution.py:628
  82.5 0.3 collective-permute-start.12
  82.7 0.1 compare_convert_fusion.same
  82.8 3.7 %field_0.1.refs_4_ = f32[128,4096]{1,0:T(8,128)} custom-call(f32[128,8,128]{2,1,0:T(8,128)} %get-tuple-element.84.refs_0_, f32[128,8,128]{2,1,0:T(8,128)} %get-tuple-element.81.refs_10_.refs_1_, f32[128,8,128]{2,1,0:T(8,128)} %get-tuple-element.82.refs_11_.refs_2_, f32[128,8,128]{2,1,0:T(8,128)} %get-tuple-element.85.refs_3_), custom_call_target="tpu_custom_call" | custom-call | bytes 800000 | tf_op jit(solution)/shard_map/field_0/pallas_call | solution.py:420
  86.5 0.0 collective-permute-done.10.second
  86.6 0.0 collective-permute-done.11.third
  86.6 0.2 collective-permute-done.12.fourth
  86.8 0.0 copy-done.2
  86.8 0.6 products.1
  87.5 2.6 %collective-permute-start.13 = (f32[32,40]{1,0:T(8,128)S(1)}, f32[32,40]{1,0:T(8,128)S(1)}, u32[]{:S(2)}, u32[]{:S(2)}) collective-permute-start(f32[32,40]{1,0:T(8,128)S(1)} %products.1), channel_id=1, source_target_pairs={{0,1},{1,0},{2,3},{3,2},{4,5},{5,4},{6,7},{7,6},{8,9},{9,8},{10,11... | collective-permute-start | bytes 15368 | tf_op jit(solution)/shard_map/ppermute | solution.py:643
  90.1 2.6 %collective-permute-start.14 = (f32[32,40]{1,0:T(8,128)S(1)}, f32[32,40]{1,0:T(8,128)S(1)}, u32[]{:S(2)}, u32[]{:S(2)}) collective-permute-start(f32[32,40]{1,0:T(8,128)S(1)} %products.1), channel_id=1, source_target_pairs={{0,2},{1,3},{2,0},{3,1},{4,6},{5,7},{6,4},{7,5},{8,10},{9,11},{10,... | collective-permute-start | bytes 15368 | tf_op jit(solution)/shard_map/ppermute | solution.py:643
  92.7 1.4 %collective-permute-start.15 = (f32[32,40]{1,0:T(8,128)S(1)}, f32[32,40]{1,0:T(8,128)S(1)}, u32[]{:S(2)}, u32[]{:S(2)}) collective-permute-start(f32[32,40]{1,0:T(8,128)S(1)} %products.1), channel_id=1, source_target_pairs={{0,3},{1,2},{2,1},{3,0},{4,7},{5,6},{6,5},{7,4},{8,11},{9,10},{10,... | collective-permute-start | bytes 15368 | tf_op jit(solution)/shard_map/ppermute | solution.py:643
  94.1 0.2 convert_reduce_fusion
  94.3 0.1 copy.10.rank_col
  94.3 3.7 %field_1.1 = f32[128,4096]{1,0:T(8,128)} custom-call(f32[128,8,128]{2,1,0:T(8,128)} %get-tuple-element.84.refs_0_, f32[128,8,128]{2,1,0:T(8,128)} %get-tuple-element.81.refs_10_.refs_1_, f32[128,8,128]{2,1,0:T(8,128)} %get-tuple-element.82.refs_11_.refs_2_, f32[128,8,128]{2,1,0:T(8,128)} %get-tuple-element.85.refs_3_, ...), custom_call_target="tpu_custom_call", output_to_operand_aliasing={{}: (4, {})} | custom-call | bytes 800000 | tf_op jit(solution)/shard_map/field_1/pallas_call | solution.py:420
  98.0 0.0 collective-permute-done.13
  98.1 0.0 collective-permute-done.14
  98.1 0.0 collective-permute-done.15
  98.1 3.1 %collective-permute-start.16 = (f32[32,40]{1,0:T(8,128)S(1)}, f32[32,40]{1,0:T(8,128)S(1)}, u32[]{:S(2)}, u32[]{:S(2)}) collective-permute-start(f32[32,40]{1,0:T(8,128)S(1)} %add_add_fusion), channel_id=1, source_target_pairs={{0,4},{1,5},{2,6},{3,7},{4,0},{5,1},{6,2},{7,3},{8,12},{9,13},{10,... | collective-permute-start | bytes 15368 | tf_op jit(solution)/shard_map/ppermute | solution.py:643
  101.2 0.4 fusion.1.anomalies
  101.6 1.3 %collective-permute-done.16 = f32[32,40]{1,0:T(8,128)S(1)} collective-permute-done((f32[32,40]{1,0:T(8,128)S(1)}, f32[32,40]{1,0:T(8,128)S(1)}, u32[]{:S(2)}, u32[]{:S(2)}) %collective-permute-start.16) | collective-permute-done | bytes 5152 | tf_op jit(solution)/shard_map/ppermute | solution.py:643
  102.9 2.1 %update.1 = f32[8,4096]{1,0:T(8,128)} custom-call(f32[1,32,40]{2,1,0:T(8,128)S(1)} %add_bitcast_fusion.summands, f32[32,32]{1,0:T(8,128)S(1)} %compare_convert_fusion.same, f32[32,8]{1,0:T(8,128)S(1)} %bitcast.31, s32[1,32]{1,0:T(1,128)S(1)} %bitcast.34, s32[32,1]{1,0:T(8,128)S(1)} %copy.10.rank_col, f32[32,4096]{1,0:T(8,128)S(1)} %fusion.1.anomalies, ...), custom_call_target="tpu_custom_call" | custom-call | tf_op jit(solution)/shard_map/update/pallas_call | solution.py:652
  (16 shorter events, 0.1 us)
Async XLA Ops:
  5.0 12.9 %collective-permute-start.5 = (f32[32,8,128]{2,1,0:T(8,128)}, f32[32,8,128]{2,1,0:T(8,128)S(1)}, u32[]{:S(2)}, u32[]{:S(2)}) collective-permute-start(f32[32,8,128]{2,1,0:T(8,128)} %get-tuple-element.65), channel_id=1, source_target_pairs={{1,0},{2,1},{3,2},{4,3},{5,4},{6,5},{7,6},{9,8},{10,9},{11,10},{12... | collective-permute-start | bytes 393224 | tf_op jit(solution)/shard_map/ppermute | solution.py:593
  6.3 11.7 %collective-permute-start.4 = (f32[32,8,128]{2,1,0:T(8,128)}, f32[32,8,128]{2,1,0:T(8,128)S(1)}, u32[]{:S(2)}, u32[]{:S(2)}) collective-permute-start(f32[32,8,128]{2,1,0:T(8,128)} %get-tuple-element.64), channel_id=1, source_target_pairs={{0,1},{1,2},{2,3},{3,4},{4,5},{5,6},{6,7},{8,9},{9,10},{10,11},{11... | collective-permute-start | bytes 393224 | tf_op jit(solution)/shard_map/ppermute | solution.py:593
  11.8 27.3 %collective-permute-start = (f32[128,8,128]{2,1,0:T(8,128)}, f32[128,8,128]{2,1,0:T(8,128)S(1)}, u32[]{:S(2)}, u32[]{:S(2)}) collective-permute-start(f32[128,8,128]{2,1,0:T(8,128)} %get-tuple-element.49.outer.own3.refs_2_), channel_id=1, source_target_pairs={{0,1},{1,2},{2,3},{3,4},{4,5},{5,6},{6,7},{8,9},{9,10},{10,11},{11... | collective-permute-start | bytes 1572872 | tf_op jit(solution)/shard_map/ppermute | solution.py:593
  16.6 22.4 %collective-permute-start.1 = (f32[128,8,128]{2,1,0:T(8,128)}, f32[128,8,128]{2,1,0:T(8,128)S(1)}, u32[]{:S(2)}, u32[]{:S(2)}) collective-permute-start(f32[128,8,128]{2,1,0:T(8,128)} %get-tuple-element.52.own0.refs_1_), channel_id=1, source_target_pairs={{1,0},{2,1},{3,2},{4,3},{5,4},{6,5},{7,6},{9,8},{10,9},{11,10},{12... | collective-permute-start | bytes 1572872 | tf_op jit(solution)/shard_map/ppermute | solution.py:593
  18.0 16.6 %collective-permute-start.6 = (f32[2,32,8,128]{3,2,1,0:T(8,128)S(1)}, f32[2,32,8,128]{3,2,1,0:T(8,128)S(1)}, u32[]{:S(2)}, u32[]{:S(2)}) collective-permute-start(f32[2,32,8,128]{3,2,1,0:T(8,128)S(1)} %get-tuple-element.97), channel_id=1, source_target_pairs={{0,8},{8,0},{16,24},{24,16},{1,9},{9,1},{17,25},{25,17},{2,10},{10... | collective-permute-start | bytes 786440 | tf_op jit(solution)/shard_map/ppermute | solution.py:583
  24.5 9.4 %copy-start = (f32[8,4096]{1,0:T(8,128)S(1)}, f32[8,4096]{1,0:T(8,128)}, u32[]{:S(2)}) copy-start(f32[8,4096]{1,0:T(8,128)} %own.1) | copy-start | bytes 393220
  24.5 10.0 %copy-start.11 = (s32[32]{0:T(128)S(1)}, s32[32]{0:T(128)}, u32[]{:S(2)}) copy-start(s32[32]{0:T(128)} %param.13) | copy-start | bytes 388
  24.5 14.6 %copy-start.9 = (f32[128,8,128]{2,1,0:T(8,128)S(1)}, f32[128,8,128]{2,1,0:T(8,128)}, u32[]{:S(2)}) copy-start(f32[128,8,128]{2,1,0:T(8,128)} %get-tuple-element.56.own2) | copy-start | bytes 1572868
  24.5 19.7 %copy-start.8 = (f32[128,8,128]{2,1,0:T(8,128)S(1)}, f32[128,8,128]{2,1,0:T(8,128)}, u32[]{:S(2)}) copy-start(f32[128,8,128]{2,1,0:T(8,128)} %get-tuple-element.59.own1) | copy-start | bytes 1572868
  24.5 22.8 %copy-start.10 = (s32[2048]{0:T(1024)S(1)}, s32[2048]{0:T(1024)}, u32[]{:S(2)}) copy-start(s32[2048]{0:T(1024)} %param.10) | copy-start | bytes 24580
  33.9 11.8 %collective-permute-start.8 = (f32[8,4096]{1,0:T(8,128)S(1)}, f32[8,4096]{1,0:T(8,128)S(1)}, u32[]{:S(2)}, u32[]{:S(2)}) collective-permute-start(f32[8,4096]{1,0:T(8,128)S(1)} %copy-done), channel_id=1, source_target_pairs={{0,8},{8,0},{16,24},{24,16},{1,9},{9,1},{17,25},{25,17},{2,10},{10... | collective-permute-start | bytes 393224 | tf_op jit(solution)/shard_map/ppermute | solution.py:583
  34.6 14.9 %copy-start.4 = (f32[2,2,32,8,128]{4,3,2,1,0:T(8,128)}, f32[2,2,32,8,128]{4,3,2,1,0:T(8,128)S(1)}, u32[]{:S(2)}) copy-start(f32[2,2,32,8,128]{4,3,2,1,0:T(8,128)S(1)} %pad_maximum_fusion.refs_10_.refs_13_) | copy-start | bytes 1572868
  34.6 14.9 %collective-permute-start.7 = (f32[2,2,32,8,128]{4,3,2,1,0:T(8,128)S(1)}, f32[2,2,32,8,128]{4,3,2,1,0:T(8,128)S(1)}, u32[]{:S(2)}, u32[]{:S(2)}) collective-permute-start(f32[2,2,32,8,128]{4,3,2,1,0:T(8,128)S(1)} %pad_maximum_fusion.refs_10_.refs_13_), channel_id=1, source_target_pairs={{0,16},{8,24},{16,0},{24,8},{1,17},{9,25},{17,1},{25,9},{2,18},{10... | collective-permute-start | bytes 1572872 | tf_op jit(solution)/shard_map/ppermute | solution.py:586
  39.1 10.4 %copy-start.5 = (f32[128,8,128]{2,1,0:T(8,128)}, f32[128,8,128]{2,1,0:T(8,128)S(1)}, u32[]{:S(2)}) copy-start(f32[128,8,128]{2,1,0:T(8,128)S(1)} %collective-permute-done.refs_0_.refs_1_) | copy-start | bytes 1572868
  39.1 10.4 %copy-start.6 = (f32[128,8,128]{2,1,0:T(8,128)}, f32[128,8,128]{2,1,0:T(8,128)S(1)}, u32[]{:S(2)}) copy-start(f32[128,8,128]{2,1,0:T(8,128)S(1)} %collective-permute-done.1.refs_3_.refs_2_) | copy-start | bytes 1572868
  39.1 25.5 %collective-permute-start.2 = (f32[128,8,128]{2,1,0:T(8,128)S(1)}, f32[128,8,128]{2,1,0:T(8,128)}, u32[]{:S(2)}, u32[]{:S(2)}) collective-permute-start(f32[128,8,128]{2,1,0:T(8,128)S(1)} %copy-done.9), channel_id=1, source_target_pairs={{0,1},{1,2},{2,3},{3,4},{4,5},{5,6},{6,7},{8,9},{9,10},{10,11},{11... | collective-permute-start | bytes 1572872 | tf_op jit(solution)/shard_map/ppermute | solution.py:593
  44.2 20.4 %collective-permute-start.3 = (f32[128,8,128]{2,1,0:T(8,128)S(1)}, f32[128,8,128]{2,1,0:T(8,128)}, u32[]{:S(2)}, u32[]{:S(2)}) collective-permute-start(f32[128,8,128]{2,1,0:T(8,128)S(1)} %copy-done.8), channel_id=1, source_target_pairs={{1,0},{2,1},{3,2},{4,3},{5,4},{6,5},{7,6},{9,8},{10,9},{11,10},{12... | collective-permute-start | bytes 1572872 | tf_op jit(solution)/shard_map/ppermute | solution.py:593
  45.7 16.3 %collective-permute-start.9 = (f32[2,8,4096]{2,1,0:T(8,128)S(1)}, f32[2,8,4096]{2,1,0:T(8,128)S(1)}, u32[]{:S(2)}, u32[]{:S(2)}) collective-permute-start(f32[2,8,4096]{2,1,0:T(8,128)S(1)} %pad_maximum_fusion.2), channel_id=1, source_target_pairs={{0,16},{8,24},{16,0},{24,8},{1,17},{9,25},{17,1},{25,9},{2,18},{10... | collective-permute-start | bytes 786440 | tf_op jit(solution)/shard_map/ppermute | solution.py:586
  49.5 0.8 copy-start.7
  80.8 5.8 %collective-permute-start.10 = (f32[8,2048]{1,0:T(8,128)}, f32[8,2048]{1,0:T(8,128)S(1)}, u32[]{:S(2)}, u32[]{:S(2)}) collective-permute-start(f32[8,2048]{1,0:T(8,128)} %get-tuple-element.83.own), channel_id=1, source_target_pairs={{0,8},{8,0},{16,24},{24,16},{1,9},{9,1},{17,25},{25,17},{2,10},{10... | collective-permute-start | bytes 196616 | tf_op jit(solution)/shard_map/ppermute | solution.py:628
  80.9 5.7 %collective-permute-start.11 = (f32[8,2048]{1,0:T(8,128)}, f32[8,2048]{1,0:T(8,128)S(1)}, u32[]{:S(2)}, u32[]{:S(2)}) collective-permute-start(f32[8,2048]{1,0:T(8,128)} %get-tuple-element.83.own), channel_id=1, source_target_pairs={{0,16},{8,24},{16,0},{24,8},{1,17},{9,25},{17,1},{25,9},{2,18},{10... | collective-permute-start | bytes 196616 | tf_op jit(solution)/shard_map/ppermute | solution.py:628
  82.5 4.3 %collective-permute-start.12 = (f32[8,2048]{1,0:T(8,128)}, f32[8,2048]{1,0:T(8,128)S(1)}, u32[]{:S(2)}, u32[]{:S(2)}) collective-permute-start(f32[8,2048]{1,0:T(8,128)} %get-tuple-element.83.own), channel_id=1, source_target_pairs={{0,24},{8,16},{16,8},{24,0},{1,25},{9,17},{17,9},{25,1},{2,26},{10... | collective-permute-start | bytes 196616 | tf_op jit(solution)/shard_map/ppermute | solution.py:628
  82.8 4.0 %copy-start.1 = (f32[8,2048]{1,0:T(8,128)S(1)}, f32[8,2048]{1,0:T(8,128)}, u32[]{:S(2)}) copy-start(f32[8,2048]{1,0:T(8,128)} %values.1) | copy-start | bytes 196612
  82.8 4.0 %copy-start.2 = (f32[8,2048]{1,0:T(8,128)S(1)}, f32[8,2048]{1,0:T(8,128)}, u32[]{:S(2)}) copy-start(f32[8,2048]{1,0:T(8,128)} %get-tuple-element.83.own) | copy-start | bytes 196612
  82.8 4.0 %copy-start.3 = (f32[2048]{0:T(1024)S(1)}, f32[2048]{0:T(1024)}, u32[]{:S(2)}) copy-start(f32[2048]{0:T(1024)} %param.12) | copy-start | bytes 24580
  87.5 10.6 %collective-permute-start.13 = (f32[32,40]{1,0:T(8,128)S(1)}, f32[32,40]{1,0:T(8,128)S(1)}, u32[]{:S(2)}, u32[]{:S(2)}) collective-permute-start(f32[32,40]{1,0:T(8,128)S(1)} %products.1), channel_id=1, source_target_pairs={{0,1},{1,0},{2,3},{3,2},{4,5},{5,4},{6,7},{7,6},{8,9},{9,8},{10,11... | collective-permute-start | bytes 15368 | tf_op jit(solution)/shard_map/ppermute | solution.py:643
  90.1 8.0 %collective-permute-start.14 = (f32[32,40]{1,0:T(8,128)S(1)}, f32[32,40]{1,0:T(8,128)S(1)}, u32[]{:S(2)}, u32[]{:S(2)}) collective-permute-start(f32[32,40]{1,0:T(8,128)S(1)} %products.1), channel_id=1, source_target_pairs={{0,2},{1,3},{2,0},{3,1},{4,6},{5,7},{6,4},{7,5},{8,10},{9,11},{10,... | collective-permute-start | bytes 15368 | tf_op jit(solution)/shard_map/ppermute | solution.py:643
  92.7 5.4 %collective-permute-start.15 = (f32[32,40]{1,0:T(8,128)S(1)}, f32[32,40]{1,0:T(8,128)S(1)}, u32[]{:S(2)}, u32[]{:S(2)}) collective-permute-start(f32[32,40]{1,0:T(8,128)S(1)} %products.1), channel_id=1, source_target_pairs={{0,3},{1,2},{2,1},{3,0},{4,7},{5,6},{6,5},{7,4},{8,11},{9,10},{10,... | collective-permute-start | bytes 15368 | tf_op jit(solution)/shard_map/ppermute | solution.py:643
  98.1 4.8 %collective-permute-start.16 = (f32[32,40]{1,0:T(8,128)S(1)}, f32[32,40]{1,0:T(8,128)S(1)}, u32[]{:S(2)}, u32[]{:S(2)}) collective-permute-start(f32[32,40]{1,0:T(8,128)S(1)} %add_add_fusion), channel_id=1, source_target_pairs={{0,4},{1,5},{2,6},{3,7},{4,0},{5,1},{6,2},{7,3},{8,12},{9,13},{10,... | collective-permute-start | bytes 15368 | tf_op jit(solution)/shard_map/ppermute | solution.py:643
